TPU v7x, 32 devices: a whole 2x2x4 slice. The times are simulated.
32 devices in a mesh: expert: 16 (over z, x, core), shard: 2 (over y).
Axes of the slice: x: 2, y: 2, z: 4, core: 2. Of those that a mesh axis runs over, the one named last changes fastest.
Arguments:
- tokens: bfloat16 [8192, 1536], P(('expert', 'shard')), may hold values from -6 to 6
- segment_ids: int32 [8192], P(('expert', 'shard')), may hold values from 0 to 2, as said below
- routes: int32 [8192, 8], P(('expert', 'shard')), may hold values from 0 to 15, all different within a row; in each aligned block of 256 rows (0 to 255, 256 to 511, ...) at most 256 rows name the same one
- norm1_gain: bfloat16 [1536], P('shard'), may hold values from 0.099609375 to 1.8984375
- norm2_gain: bfloat16 [1536], P('shard'), may hold values from 0.099609375 to 1.8984375
- query_key_value_weight: bfloat16 [1536, 2560], P('shard'), may hold values from -0.4375 to 0.4375
- out_weight: bfloat16 [1536, 1536], P('shard'), may hold values from -2.5 to 2.5
- route_weight: bfloat16 [1536, 16], P('shard'), may hold values from -0.078125 to 0.078125
- expert_in: bfloat16 [16, 1536, 1024], P('expert', 'shard'), may hold values from -0.15625 to 0.15625
- expert_down: bfloat16 [16, 512, 1536], P('expert', None, 'shard'), may hold values from -6 to 6
- cotangent: bfloat16 [8192, 1536], P(('expert', 'shard')), may hold values from -6 to 6
Outputs:
- block_out: bfloat16 [8192, 1536], P(('expert', 'shard'))
- grad_tokens: float32 [8192, 1536], P(('expert', 'shard'))
- grad_norm1: float32 [1536], P('shard')
- grad_norm2: float32 [1536], P('shard')
- grad_qkv: float32 [1536, 2560], P('shard')
- grad_out: float32 [1536, 1536], P('shard')
- grad_route: float32 [1536, 16], P('shard')
- grad_in: float32 [16, 1536, 1024], P('expert', 'shard')
- grad_down: float32 [16, 512, 1536], P('expert', None, 'shard')
Inputs may be any that keep to these rules, and one draw needn't show every extreme that they name: `segment_ids`: within each sequence of 512 consecutive rows the ids number its documents from 0 and never fall. `routes`: each row names 8 different experts; among the 256 rows of one device no expert is named more than 256 times.
All inputs are finite; a program needn't handle non-finite values.
Results may differ from a plain program's by a relative error of at most 0.02.
Values may be sent and summed in bfloat16 or wider, within the bound.
No kernel may reach another device: no remote copies, remote signals or barrier semaphores. Data moves between devices by JAX's collectives and lax.ppermute only.
A program may use at most 256 MiB of HBM per device.

v0:
```python
import jax
import jax.numpy as jnp
from jax import lax
from jax.sharding import PartitionSpec as P

QUERY_HEADS = 24
KEY_VALUE_HEADS = 8
HEAD_SIZE = 64


RES_SCALE = 0.22
ATT_SCALE = 0.015625
EPSILON = 1e-06
ROPE_BASE = 10000.0
MASKED = -1000000000.0


def norm_apply(value_rows, scaling):
    return (
        value_rows
        * lax.rsqrt(jnp.mean(value_rows * value_rows, axis=-1, keepdims=True) + EPSILON)
        * scaling
    )


def rotation(positions, half_dim):
    inverse = jnp.power(ROPE_BASE, -(jnp.arange(half_dim) * 2.0 / (2 * half_dim)))
    angles = positions.astype(jnp.float32)[:, None] * inverse[None, :]
    return (jnp.cos(angles), jnp.sin(angles))


def table_shape(value_rows, table):
    half_dim = value_rows.shape[-1] // 2
    return table.reshape((value_rows.shape[0],) + (1,) * (value_rows.ndim - 2) + (half_dim,))


def apply_rotary(value_rows, cosine_table, sine_lookup):
    half_dim = value_rows.shape[-1] // 2
    cosine_table = table_shape(value_rows, cosine_table)
    sine_lookup = table_shape(value_rows, sine_lookup)
    first_half = value_rows[..., :half_dim]
    second_half = value_rows[..., half_dim:]
    return jnp.concatenate(
        [
            first_half * cosine_table - second_half * sine_lookup,
            second_half * cosine_table + first_half * sine_lookup,
        ],
        axis=-1,
    )


def invert_rotary(value_rows, cosine_table, sine_lookup):
    half_dim = value_rows.shape[-1] // 2
    cosine_table = table_shape(value_rows, cosine_table)
    sine_lookup = table_shape(value_rows, sine_lookup)
    first_half = value_rows[..., :half_dim]
    second_half = value_rows[..., half_dim:]
    return jnp.concatenate(
        [
            first_half * cosine_table + second_half * sine_lookup,
            second_half * cosine_table - first_half * sine_lookup,
        ],
        axis=-1,
    )


def swish_gate(gate_part, up_part):
    return jax.nn.silu(gate_part) * up_part


def body(
    tokens,
    segment_ids,
    routes,
    norm1_gain,
    norm2_gain,
    query_key_value_weight,
    out_weight,
    route_weight,
    expert_in,
    expert_down,
    cotangent,
):
    token_rows, model_dim = tokens.shape
    sequence_length = token_rows * lax.axis_size("shard")
    topk_routes = routes.shape[1]
    query_width = QUERY_HEADS * HEAD_SIZE
    pair_width = KEY_VALUE_HEADS * HEAD_SIZE
    queries_per_group = QUERY_HEADS // KEY_VALUE_HEADS
    dense_full = (
        lax.all_gather(norm1_gain, "shard", axis=0, tiled=True),
        lax.all_gather(norm2_gain, "shard", axis=0, tiled=True),
        lax.all_gather(query_key_value_weight, "shard", axis=0, tiled=True),
        lax.all_gather(out_weight, "shard", axis=0, tiled=True),
        lax.all_gather(route_weight, "shard", axis=0, tiled=True),
    )
    gain_one = dense_full[0].astype(jnp.float32)
    gain_two = dense_full[1].astype(jnp.float32)
    inputs = tokens.astype(jnp.float32)
    normed = norm_apply(inputs, gain_one).astype(jnp.bfloat16)
    projected_rows = jnp.dot(normed, dense_full[2], preferred_element_type=jnp.float32)
    positions = lax.axis_index("shard") * token_rows + jnp.arange(token_rows)
    cosine_table, sine_lookup = rotation(positions, HEAD_SIZE // 2)
    query_rows = apply_rotary(
        projected_rows[:, :query_width].reshape(
            token_rows, KEY_VALUE_HEADS, queries_per_group, HEAD_SIZE
        ),
        cosine_table,
        sine_lookup,
    ).astype(jnp.bfloat16)
    own_keys = apply_rotary(
        projected_rows[:, query_width : query_width + pair_width].reshape(
            token_rows, KEY_VALUE_HEADS, HEAD_SIZE
        ),
        cosine_table,
        sine_lookup,
    )
    own_pairs = jnp.concatenate(
        [own_keys.reshape(token_rows, pair_width), projected_rows[:, query_width + pair_width :]],
        axis=1,
    ).astype(jnp.bfloat16)
    gathered_pairs, all_segments = (
        lax.all_gather(own_pairs, "shard", axis=0, tiled=True),
        lax.all_gather(segment_ids, "shard", axis=0, tiled=True),
    )
    gathered_keys = gathered_pairs[:, :pair_width].reshape(
        sequence_length, KEY_VALUE_HEADS, HEAD_SIZE
    )
    gathered_values = gathered_pairs[:, pair_width:].reshape(
        sequence_length, KEY_VALUE_HEADS, HEAD_SIZE
    )
    allowed = (segment_ids[:, None] == all_segments[None, :]) & (
        positions[:, None] >= jnp.arange(sequence_length)[None, :]
    )

    def scores_of():
        raw_scores = (
            jnp.einsum(
                "qgjd,kgd->gjqk", query_rows, gathered_keys, preferred_element_type=jnp.float32
            )
            * ATT_SCALE
        )
        return jnp.where(allowed[None, None], raw_scores, MASKED)

    scores = scores_of()
    highest = jnp.max(scores, axis=-1, keepdims=True)
    shifted = jnp.exp(scores - highest)
    totals = jnp.sum(shifted, axis=-1, keepdims=True)
    log_total = highest + jnp.log(totals)
    attn_probs = (shifted / totals).astype(jnp.bfloat16)
    head_out = (
        jnp.einsum(
            "gjqk,kgd->qgjd", attn_probs, gathered_values, preferred_element_type=jnp.float32
        )
        .reshape(token_rows, query_width)
        .astype(jnp.bfloat16)
    )
    middle = inputs + RES_SCALE * jnp.dot(
        head_out, dense_full[3], preferred_element_type=jnp.float32
    )
    second = norm_apply(middle, gain_two).astype(jnp.bfloat16)
    logits = jnp.dot(second, dense_full[4], preferred_element_type=jnp.float32)
    chosen = jnp.take_along_axis(logits, routes, axis=1)
    gate_probs = jax.nn.softmax(chosen, axis=-1)
    num_experts = route_weight.shape[1]
    capacity = min(token_rows, 2 * token_rows * topk_routes // num_experts)
    flat_routes = routes.reshape(-1)
    one_hot = (flat_routes[:, None] == jnp.arange(num_experts)[None, :]).astype(jnp.int32)
    slot_of = jnp.sum(jnp.cumsum(one_hot, axis=0) * one_hot, axis=1) - 1
    copies = jnp.broadcast_to(second[:, None, :], (token_rows, topk_routes, model_dim)).reshape(
        -1, model_dim
    )
    outgoing = (
        jnp.zeros((num_experts, capacity, model_dim), jnp.bfloat16)
        .at[flat_routes, slot_of]
        .set(copies)
    )
    arrived = lax.all_to_all(outgoing, "expert", split_axis=0, concat_axis=0, tiled=True).reshape(
        -1, model_dim
    )
    expert_full = (
        lax.all_gather(expert_in, "shard", axis=1, tiled=True),
        lax.all_gather(expert_down, "shard", axis=2, tiled=True),
    )
    weight_in = expert_full[0][0]
    weight_down = expert_full[1][0]
    ffe_dim = weight_down.shape[0]
    gate_up_rows = jnp.dot(arrived, weight_in, preferred_element_type=jnp.float32)
    hidden_rows = swish_gate(gate_up_rows[:, :ffe_dim], gate_up_rows[:, ffe_dim:]).astype(
        jnp.bfloat16
    )
    produced = (
        jnp.dot(hidden_rows, weight_down, preferred_element_type=jnp.float32)
        .astype(jnp.bfloat16)
        .reshape(-1, capacity, model_dim)
    )
    returned = lax.all_to_all(produced, "expert", split_axis=0, concat_axis=0, tiled=True)
    picked = (
        returned[flat_routes, slot_of]
        .astype(jnp.float32)
        .reshape(token_rows, topk_routes, model_dim)
    )
    combined = jnp.sum(gate_probs[:, :, None] * picked, axis=1)
    block_out = (middle + RES_SCALE * combined).astype(jnp.bfloat16)
    upstream = cotangent.astype(jnp.float32)
    scaled_up = RES_SCALE * upstream
    route_grads = (
        (gate_probs[:, :, None] * scaled_up[:, None, :]).astype(jnp.bfloat16).reshape(-1, model_dim)
    )
    gate_grads = jnp.sum(picked * scaled_up[:, None, :], axis=-1)
    grad_buffer = (
        jnp.zeros((num_experts, capacity, model_dim), jnp.bfloat16)
        .at[flat_routes, slot_of]
        .set(route_grads)
    )
    grad_arrived = lax.all_to_all(
        grad_buffer, "expert", split_axis=0, concat_axis=0, tiled=True
    ).reshape(-1, model_dim)
    hidden_grads = jnp.einsum(
        "rd,fd->rf", grad_arrived, weight_down, preferred_element_type=jnp.float32
    )
    _, swish_pull = jax.vjp(swish_gate, gate_up_rows[:, :ffe_dim], gate_up_rows[:, ffe_dim:])
    gate_part_grad, up_part_grad = swish_pull(hidden_grads)
    gate_up_grads = jnp.concatenate([gate_part_grad, up_part_grad], axis=1).astype(jnp.bfloat16)
    grad_down_local = jnp.einsum(
        "rf,rd->fd", hidden_rows, grad_arrived, preferred_element_type=jnp.float32
    )
    grad_in_local = jnp.einsum(
        "rd,rf->df", arrived, gate_up_grads, preferred_element_type=jnp.float32
    )
    back_rows = (
        jnp.einsum("rf,df->rd", gate_up_grads, weight_in, preferred_element_type=jnp.float32)
        .astype(jnp.bfloat16)
        .reshape(-1, capacity, model_dim)
    )
    back_home = lax.all_to_all(back_rows, "expert", split_axis=0, concat_axis=0, tiled=True)
    from_experts = jnp.sum(
        back_home[flat_routes, slot_of]
        .astype(jnp.float32)
        .reshape(token_rows, topk_routes, model_dim),
        axis=1,
    )
    expert_grads = (
        lax.psum_scatter(
            grad_in_local[None].astype(jnp.bfloat16), "shard", scatter_dimension=1, tiled=True
        ).astype(jnp.float32),
        lax.psum_scatter(
            grad_down_local[None].astype(jnp.bfloat16), "shard", scatter_dimension=2, tiled=True
        ).astype(jnp.float32),
    )
    chosen_grads = gate_probs * (
        gate_grads - jnp.sum(gate_probs * gate_grads, axis=-1, keepdims=True)
    )
    route_hits = routes[:, :, None] == jnp.arange(num_experts)[None, None, :]
    logit_grads = jnp.sum(chosen_grads[:, :, None] * route_hits, axis=1).astype(jnp.bfloat16)
    grad_route_local = jnp.einsum(
        "td,te->de", second, logit_grads, preferred_element_type=jnp.float32
    )
    second_grads = from_experts + jnp.einsum(
        "te,de->td", logit_grads, dense_full[4], preferred_element_type=jnp.float32
    )
    _, second_pull = jax.vjp(norm_apply, middle, dense_full[1].astype(jnp.float32))
    middle_norm_grads, grad_gain_two = second_pull(second_grads)
    middle_grads = upstream + middle_norm_grads
    attn_grads = (RES_SCALE * middle_grads).astype(jnp.bfloat16)
    grad_out_local = jnp.einsum(
        "tq,td->qd", head_out, attn_grads, preferred_element_type=jnp.float32
    )
    head_grads = (
        jnp.einsum("td,qd->tq", attn_grads, dense_full[3], preferred_element_type=jnp.float32)
        .astype(jnp.bfloat16)
        .reshape(token_rows, KEY_VALUE_HEADS, queries_per_group, HEAD_SIZE)
    )
    probs_again = jnp.exp(scores_of() - log_total)
    prob_grads = jnp.einsum(
        "qgjd,kgd->gjqk", head_grads, gathered_values, preferred_element_type=jnp.float32
    )
    row_dots = jnp.sum(probs_again * prob_grads, axis=-1, keepdims=True)
    score_grads = (probs_again * (prob_grads - row_dots)).astype(jnp.bfloat16)
    query_grads = (
        jnp.einsum("gjqk,kgd->qgjd", score_grads, gathered_keys, preferred_element_type=jnp.float32)
        * ATT_SCALE
    )
    key_grads = (
        jnp.einsum("gjqk,qgjd->kgd", score_grads, query_rows, preferred_element_type=jnp.float32)
        * ATT_SCALE
    )
    value_grads = jnp.einsum(
        "gjqk,qgjd->kgd", attn_probs, head_grads, preferred_element_type=jnp.float32
    )
    local_key_grads, own_value_grads = (
        lax.psum_scatter(
            key_grads.reshape(sequence_length, pair_width).astype(jnp.bfloat16),
            "shard",
            scatter_dimension=0,
            tiled=True,
        ).astype(jnp.float32),
        lax.psum_scatter(
            value_grads.reshape(sequence_length, pair_width).astype(jnp.bfloat16),
            "shard",
            scatter_dimension=0,
            tiled=True,
        ).astype(jnp.float32),
    )
    query_pre = invert_rotary(query_grads, cosine_table, sine_lookup).reshape(
        token_rows, query_width
    )
    key_unrotated = invert_rotary(
        local_key_grads.reshape(token_rows, KEY_VALUE_HEADS, HEAD_SIZE), cosine_table, sine_lookup
    ).reshape(token_rows, pair_width)
    projected_grads = jnp.concatenate([query_pre, key_unrotated, own_value_grads], axis=1).astype(
        jnp.bfloat16
    )
    grad_qkv_local = jnp.einsum(
        "td,tc->dc", normed, projected_grads, preferred_element_type=jnp.float32
    )
    normed_grads = jnp.einsum(
        "tc,dc->td", projected_grads, dense_full[2], preferred_element_type=jnp.float32
    )
    _, first_pull = jax.vjp(norm_apply, inputs, dense_full[0].astype(jnp.float32))
    input_norm_grads, grad_gain_one = first_pull(normed_grads)
    grad_tokens = middle_grads + input_norm_grads
    partial_grads = (
        lax.psum_scatter(grad_gain_one, "shard", scatter_dimension=0, tiled=True),
        lax.psum_scatter(grad_gain_two, "shard", scatter_dimension=0, tiled=True),
        lax.psum_scatter(grad_qkv_local, "shard", scatter_dimension=0, tiled=True),
        lax.psum_scatter(grad_out_local, "shard", scatter_dimension=0, tiled=True),
        lax.psum_scatter(grad_route_local, "shard", scatter_dimension=0, tiled=True),
    )
    summed = (
        lax.psum(partial_grads[0].astype(jnp.bfloat16), "expert").astype(jnp.float32),
        lax.psum(partial_grads[1].astype(jnp.bfloat16), "expert").astype(jnp.float32),
        lax.psum(partial_grads[2].astype(jnp.bfloat16), "expert").astype(jnp.float32),
        lax.psum(partial_grads[3].astype(jnp.bfloat16), "expert").astype(jnp.float32),
        lax.psum(partial_grads[4].astype(jnp.bfloat16), "expert").astype(jnp.float32),
    )
    return (
        block_out,
        grad_tokens,
        summed[0],
        summed[1],
        summed[2],
        summed[3],
        summed[4],
        expert_grads[0],
        expert_grads[1],
    )


def solution(mesh):
    in_specs = (
        P(("expert", "shard"), None),
        P(("expert", "shard")),
        P(("expert", "shard"), None),
        P("shard"),
        P("shard"),
        P("shard", None),
        P("shard", None),
        P("shard", None),
        P("expert", "shard", None),
        P("expert", None, "shard"),
        P(("expert", "shard"), None),
    )
    out_specs = (
        P(("expert", "shard"), None),
        P(("expert", "shard"), None),
        P("shard"),
        P("shard"),
        P("shard", None),
        P("shard", None),
        P("shard", None),
        P("expert", "shard", None),
        P("expert", None, "shard"),
    )
    return jax.shard_map(body, mesh=mesh, in_specs=in_specs, out_specs=out_specs, check_vma=False)
```

profile of v0, /device:TPU:0, one launch (start us, length us, event | category | flops | bytes accessed | tf_op | source)
XLA Modules:
  0.0 2038.1 jit_solution(1049015000892088502)
XLA Ops:
  8.7 5.2 all-gather
  15.0 95.4 %all-gather.9.cloned.1.call-done = bf16[1536,2560]{1,0:T(8,128)(2,1)} async-done(((bf16[768,2560]{1,0:T(8,128)(2,1)}), bf16[1536,2560]{1,0:T(8,128)(2,1)}) %all-gather.9.cloned.1.call-update) | async-done | bytes 7864336 | tf_op jit(solution)/shard_map/all_gather | solution.py:93
  110.4 5.5 fusion.47
  120.1 4.3 all-gather.2
  124.5 4.5 reduce-window.6
  131.3 4.2 all-gather.1
  135.7 2.7 slice.83
  145.2 2.6 fusion.6
  147.9 2.8 copy-done.1
  150.7 3.2 divide_convert_fusion
  153.9 2.6 copy-done.2
  157.7 46.9 %all-gather.13.cloned.1.call-done = bf16[1536,1536]{1,0:T(8,128)(2,1)} async-done(((bf16[768,1536]{1,0:T(8,128)(2,1)}), bf16[1536,1536]{1,0:T(8,128)(2,1)}) %all-gather.13.cloned.1.call-update) | async-done | bytes 4718608 | tf_op jit(solution)/shard_map/all_gather | solution.py:94
  204.6 3.9 multiply_reduce_fusion.2
  209.9 17.2 scatter_custom_fusion
  227.1 5.8 all-to-all-start
  233.2 4.5 all_gather.33
  238.6 16.8 gather_fusion.2
  255.9 18.1 scatter_custom_fusion.1
  274.1 182.6 %all-to-all-done = bf16[16,256,1536]{2,1,0:T(8,128)(2,1)} async-done(((bf16[16,256,1536]{2,1,0:T(8,128)(2,1)}), bf16[16,256,1536]{2,1,0:T(8,128)(2,1)}, u32[]{:S(2)}, u32[]{:S(2)}) %all-to-all-start) | async-done | bytes 12582944 | tf_op jit(solution)/shard_map/all_to_all | solution.py:178
  456.7 53.4 %all-to-all-start.2 = ((bf16[16,256,1536]{2,1,0:T(8,128)(2,1)}), bf16[16,256,1536]{2,1,0:T(8,128)(2,1)}, u32[]{:S(2)}, u32[]{:S(2)}) async-start(bf16[16,256,1536]{2,1,0:T(8,128)(2,1)} %bitcast.158), calls=%async_computation.2 | async-start | bytes 25165824 | tf_op jit(solution)/shard_map/all_to_all | solution.py:216
  511.2 46.2 %all-gather.15.cloned.1.call-done = bf16[1,1536,1024]{2,1,0:T(8,128)(2,1)} async-done(((bf16[1,768,1024]{2,1,0:T(8,128)(2,1)}), bf16[1,1536,1024]{2,1,0:T(8,128)(2,1)}) %all-gather.15.cloned.1.call-update) | async-done | bytes 3145744 | tf_op jit(solution)/shard_map/all_gather | solution.py:182
  557.5 20.5 %fusion.24 = f32[4096,1024]{0,1:T(8,128)} fusion(bf16[4096,1536]{1,0:T(8,128)(2,1)} %bitcast.20, bf16[1,1536,1024]{2,1,0:T(8,128)(2,1)} %all-gather.15.cloned.1.call-done), kind=kOutput, calls=%fused_computation.45 | convolution fusion | flops 12884901888 | bytes 32505856 | tf_op jit(solution)/shard_map/dot_general | solution.py:188
  578.0 8.1 all-gather.17.cloned.1.call-done
  586.1 147.7 %all-to-all-done.2 = bf16[16,256,1536]{2,1,0:T(8,128)(2,1)} async-done(((bf16[16,256,1536]{2,1,0:T(8,128)(2,1)}), bf16[16,256,1536]{2,1,0:T(8,128)(2,1)}, u32[]{:S(2)}, u32[]{:S(2)}) %all-to-all-start.2) | async-done | bytes 12582944 | tf_op jit(solution)/shard_map/all_to_all | solution.py:216
  733.8 19.3 fusion.9
  753.1 19.6 convolution_convert_fusion
  772.7 53.5 %all-to-all-start.3 = ((bf16[16,256,1536]{2,1,0:T(8,128)(2,1)}), bf16[16,256,1536]{2,1,0:T(8,128)(2,1)}, u32[]{:S(2)}, u32[]{:S(2)}) async-start(bf16[16,256,1536]{2,1,0:T(8,128)(2,1)} %bitcast.164), calls=%async_computation.3 | async-start | bytes 25165824 | tf_op jit(solution)/shard_map/all_to_all | solution.py:236
  826.3 12.1 convolution_convert_fusion.1
  838.3 211.6 %all-to-all-done.3 = bf16[16,256,1536]{2,1,0:T(8,128)(2,1)} async-done(((bf16[16,256,1536]{2,1,0:T(8,128)(2,1)}), bf16[16,256,1536]{2,1,0:T(8,128)(2,1)}, u32[]{:S(2)}, u32[]{:S(2)}) %all-to-all-start.3) | async-done | bytes 12582944 | tf_op jit(solution)/shard_map/all_to_all | solution.py:236
  1050.0 53.5 %all-to-all-start.1 = ((bf16[16,256,1536]{2,1,0:T(8,128)(2,1)}), bf16[16,256,1536]{2,1,0:T(8,128)(2,1)}, u32[]{:S(2)}, u32[]{:S(2)}) async-start(bf16[16,256,1536]{2,1,0:T(8,128)(2,1)} %bitcast.163), calls=%async_computation.1 | async-start | bytes 25165824 | tf_op jit(solution)/shard_map/all_to_all | solution.py:197
  1103.6 46.3 %gather_fusion.1 = bf16[2048,1536]{1,0:T(8,128)(2,1)} fusion(bf16[16,256,1536]{2,1,0:T(8,128)(2,1)} %all-to-all-done.3, s32[2048]{0:T(1024)S(1)} %bitcast.153), kind=kCustom, calls=%fused_computation.1 | custom fusion | bytes 12599296 | tf_op jit(solution)/shard_map/gather | solution.py:238
  1149.9 8.1 convert_reduce_fusion
  1158.0 169.2 %all-to-all-done.1 = bf16[16,256,1536]{2,1,0:T(8,128)(2,1)} async-done(((bf16[16,256,1536]{2,1,0:T(8,128)(2,1)}), bf16[16,256,1536]{2,1,0:T(8,128)(2,1)}, u32[]{:S(2)}, u32[]{:S(2)}) %all-to-all-start.1) | async-done | bytes 12582944 | tf_op jit(solution)/shard_map/all_to_all | solution.py:197
  1327.3 46.0 %gather_fusion = bf16[2048,1536]{1,0:T(8,128)(2,1)} fusion(bf16[16,256,1536]{2,1,0:T(8,128)(2,1)} %all-to-all-done.1, s32[2048]{0:T(1024)S(1)} %bitcast.154), kind=kCustom, calls=%fused_computation | custom fusion | bytes 12599296 | tf_op jit(solution)/shard_map/gather | solution.py:199
  1373.3 9.8 fusion.1
  1385.5 2.6 convert_add_fusion.1
  1391.9 11.0 fusion.2
  1404.5 6.7 fusion.4
  1411.2 2.7 copy-done.3
  1413.9 2.8 fusion.39
  1416.7 5.6 fusion.40
  1422.5 4.9 fusion.45
  1428.4 3.9 multiply_bitcast_fusion
  1432.8 46.3 %reduce-scatter.8.cloned.1.call-done = bf16[256,512]{0,1:T(8,128)(2,1)} async-done(((bf16[512,512]{0,1:T(8,128)(2,1)}), bf16[256,512]{0,1:T(8,128)(2,1)}) %reduce-scatter.8.cloned.1.call-update) | async-done | bytes 262160 | tf_op jit(solution)/shard_map/reduce_scatter | solution.py:292
  1480.2 16.4 reduce-scatter.10.cloned.1.call-done
  1496.6 9.4 fusion.41
  1506.1 11.8 fusion.27
  1517.9 19.7 fusion.22
  1538.9 70.6 %reduce-scatter.14.cloned.1.call-done = f32[768,1536]{1,0:T(8,128)} async-done(((f32[1536,1536]{1,0:T(8,128)}), f32[768,1536]{1,0:T(8,128)}) %reduce-scatter.14.cloned.1.call-update) | async-done | bytes 4718608 | tf_op jit(solution)/shard_map/reduce_scatter | solution.py:327
  1609.4 4.0 convert_element_type.208
  1613.5 176.7 %reduce-scatter.12.cloned.1.call-done = f32[768,2560]{1,0:T(8,128)} async-done(((f32[1536,2560]{1,0:T(8,128)}), f32[768,2560]{1,0:T(8,128)}) %reduce-scatter.12.cloned.1.call-update) | async-done | bytes 7864336 | tf_op jit(solution)/shard_map/reduce_scatter | solution.py:326
  1790.2 5.6 convert_element_type.206
  1797.7 21.3 %reduce-scatter.20.cloned.1.call-done = bf16[1,512,768]{2,1,0:T(8,128)(2,1)} async-done(((bf16[1,512,1536]{2,1,0:T(8,128)(2,1)}), bf16[1,512,768]{2,1,0:T(8,128)(2,1)}) %reduce-scatter.20.cloned.1.call-update) | async-done | bytes 786448 | tf_op jit(solution)/shard_map/reduce_scatter | solution.py:247
  1819.0 2.4 convert_element_type.217
  1821.4 43.9 %reduce-scatter.18.cloned.1.call-done = bf16[1,768,1024]{2,1,0:T(8,128)(2,1)} async-done(((bf16[1,1536,1024]{2,1,0:T(8,128)(2,1)}), bf16[1,768,1024]{2,1,0:T(8,128)(2,1)}) %reduce-scatter.18.cloned.1.call-update) | async-done | bytes 1572880 | tf_op jit(solution)/shard_map/reduce_scatter | solution.py:244
  1865.3 3.5 convert_element_type.214
  1868.7 8.6 reduce-scatter.16.cloned.1.call-done
  1878.2 6.8 fusion.31
  1885.0 6.8 all-reduce.2
  1892.0 62.4 %all-reduce.3 = (bf16[768]{0:T(1024)(128)(2,1)S(1)}, bf16[768]{0:T(1024)(128)(2,1)S(1)}, bf16[768,16]{0,1:T(8,128)(2,1)S(1)}) all-reduce(bf16[768]{0:T(1024)(128)(2,1)S(1)} %dynamic-slice.7, bf16[768]{0:T(1024)(128)(2,1)S(1)} %dynamic-slice.6, ...), channel_id=1, replica_groups=mesh['expert'=16,'shard'=2] {'expert'}, use_global_device_ids=true, to_apply=%region_23.24 | all-reduce | flops 13824 | bytes 55296 | tf_op jit(solution)/shard_map/psum | solution.py:331
  1956.2 3.0 fusion.32
  1959.2 62.5 %all-reduce.7.cloned.1.call-done = (bf16[768,2560]{1,0:T(8,128)(2,1)}, bf16[768,1536]{1,0:T(8,128)(2,1)}) async-done(((bf16[768,2560]{1,0:T(8,128)(2,1)}, bf16[768,1536]{1,0:T(8,128)(2,1)}), (bf16[768,2560]{1,0:T(8,128)(2,1)}, bf16[768,1536]{1,0:T(8,128)(2,1)})) %all-reduce.7.cloned.1.call-update) | async-done | bytes 6291472 | tf_op jit(solution)/shard_map/psum | solution.py:333
  2021.7 6.6 convert_element_type.207
  2028.2 2.8 convert_element_type.209
  (250 shorter events, 36.6 us)
Async XLA Ops:
  7.2 6.8 copy-start.8
  7.2 103.2 %all-gather.9.cloned.1.call-start = ((), (), s32[]{:S(2)}) async-start(), calls=%async_computation.11 | async-start | bytes 11796480 | tf_op jit(solution)/shard_map/all_gather | solution.py:93
  7.9 133.4 %all-gather.11.cloned.1.call-start = ((), (), s32[]{:S(2)}) async-start(), calls=%async_computation.12 | async-start | bytes 1572864 | tf_op jit(solution)/shard_map/all_gather | solution.py:123
  13.9 102.0 %copy-start.46 = (f32[1536]{0:T(1024)}, f32[1536]{0:T(1024)S(1)}, u32[]{:S(2)}) copy-start(f32[1536]{0:T(1024)S(1)} %reshape.507) | copy-start | bytes 18436
  14.8 101.1 %copy-start.52 = (f32[256]{0:T(256)}, f32[256]{0:T(256)S(1)}, u32[]{:S(2)}) copy-start(f32[256]{0:T(256)S(1)} %fusion.57) | copy-start | bytes 3076
  15.0 102.7 %copy-start.32 = (f32[256,32]{0,1:T(8,128)}, f32[256,32]{0,1:T(8,128)S(1)}, u32[]{:S(2)}) copy-start(f32[256,32]{0,1:T(8,128)S(1)} %get-tuple-element.42) | copy-start | bytes 98308
  15.0 102.7 %copy-start.35 = (f32[256,32]{0,1:T(8,128)}, f32[256,32]{0,1:T(8,128)S(1)}, u32[]{:S(2)}) copy-start(f32[256,32]{0,1:T(8,128)S(1)} %get-tuple-element.43) | copy-start | bytes 98308
  117.5 13.0 copy-start.64
  117.5 13.1 copy-start.63
  117.5 13.8 copy-start.61
  118.9 85.8 %all-gather.13.cloned.1.call-start = ((), (), s32[]{:S(2)}) async-start(), calls=%async_computation.13 | async-start | bytes 7077888 | tf_op jit(solution)/shard_map/all_gather | solution.py:94
  119.6 20.7 %copy-start.33 = (f32[256,32]{0,1:T(8,128)S(1)}, f32[256,32]{0,1:T(8,128)}, u32[]{:S(2)}) copy-start(f32[256,32]{0,1:T(8,128)} %copy-done.32) | copy-start | bytes 98308
  119.6 20.7 %copy-start.36 = (f32[256,32]{0,1:T(8,128)S(1)}, f32[256,32]{0,1:T(8,128)}, u32[]{:S(2)}) copy-start(f32[256,32]{0,1:T(8,128)} %copy-done.35) | copy-start | bytes 98308
  131.3 77.3 %copy-start.48 = (f32[1536]{0:T(1024)}, f32[1536]{0:T(1024)S(1)}, u32[]{:S(2)}) copy-start(f32[1536]{0:T(1024)S(1)} %reshape.508) | copy-start | bytes 18436
  135.7 12.1 copy-start.19
  143.2 10.6 copy-start.14
  157.7 50.8 %copy-start.6 = (bf16[8,64,3,256]{3,1,2,0:T(8,128)(2,1)}, bf16[8,64,3,256]{3,1,2,0:T(8,128)(2,1)S(1)}, u32[]{:S(2)}) copy-start(bf16[8,64,3,256]{3,1,2,0:T(8,128)(2,1)S(1)} %convolution_convert_fusion.4) | copy-start | bytes 2359300
  208.5 18.6 copy-start.59
  208.6 18.5 copy-start.55
  209.9 28.0 %copy-start.12 = (bf16[256,1536]{1,0:T(8,128)(2,1)}, bf16[256,1536]{1,0:T(8,128)(2,1)S(1)}, u32[]{:S(2)}) copy-start(bf16[256,1536]{1,0:T(8,128)(2,1)S(1)} %multiply_convert_fusion.3) | copy-start | bytes 2359300
  227.1 10.6 copy-start.27
  227.1 229.6 %all-to-all-start = ((bf16[16,256,1536]{2,1,0:T(8,128)(2,1)}), bf16[16,256,1536]{2,1,0:T(8,128)(2,1)}, u32[]{:S(2)}, u32[]{:S(2)}) async-start(bf16[16,256,1536]{2,1,0:T(8,128)(2,1)} %bitcast.157), calls=%async_computation | async-start | bytes 25165824 | tf_op jit(solution)/shard_map/all_to_all | solution.py:178
  238.3 17.6 copy-start.10
  255.7 18.4 copy-start.50
  255.8 18.3 copy-start.30
  456.7 277.1 %all-to-all-start.2 = ((bf16[16,256,1536]{2,1,0:T(8,128)(2,1)}), bf16[16,256,1536]{2,1,0:T(8,128)(2,1)}, u32[]{:S(2)}, u32[]{:S(2)}) async-start(bf16[16,256,1536]{2,1,0:T(8,128)(2,1)} %bitcast.158), calls=%async_computation.2 | async-start | bytes 25165824 | tf_op jit(solution)/shard_map/all_to_all | solution.py:216
  510.1 47.4 %all-gather.15.cloned.1.call-start = ((), (), s32[]{:S(2)}) async-start(), calls=%async_computation.14 | async-start | bytes 4718592 | tf_op jit(solution)/shard_map/all_gather | solution.py:182
  510.6 75.4 %all-gather.17.cloned.1.call-start = ((), (), s32[]{:S(2)}) async-start(), calls=%async_computation.15 | async-start | bytes 2359296 | tf_op jit(solution)/shard_map/all_gather | solution.py:183
  733.8 19.3 copy-start.65
  772.7 53.5 %copy-start.66 = (bf16[1,512,1536]{2,1,0:T(8,128)(2,1)S(1)}, bf16[1,512,1536]{2,1,0:T(8,128)(2,1)}, u32[]{:S(2)}) copy-start(bf16[1,512,1536]{2,1,0:T(8,128)(2,1)} %all-gather.17.cloned.1.call-done) | copy-start | bytes 4718596
  772.7 277.3 %all-to-all-start.3 = ((bf16[16,256,1536]{2,1,0:T(8,128)(2,1)}), bf16[16,256,1536]{2,1,0:T(8,128)(2,1)}, u32[]{:S(2)}, u32[]{:S(2)}) async-start(bf16[16,256,1536]{2,1,0:T(8,128)(2,1)} %bitcast.164), calls=%async_computation.3 | async-start | bytes 25165824 | tf_op jit(solution)/shard_map/all_to_all | solution.py:236
  1050.0 53.6 %copy-start.39 = (f32[8,3,256]{2,1,0:T(4,128)S(1)}, f32[8,3,256]{2,1,0:T(4,128)}, u32[]{:S(2)}) copy-start(f32[8,3,256]{2,1,0:T(4,128)} %copy-done.38) | copy-start | bytes 73732
  1050.0 53.6 %copy-start.43 = (f32[8,3,256]{2,1,0:T(4,128)S(1)}, f32[8,3,256]{2,1,0:T(4,128)}, u32[]{:S(2)}) copy-start(f32[8,3,256]{2,1,0:T(4,128)} %copy-done.42) | copy-start | bytes 73732
  1050.0 53.6 %copy-start = (s32[2048,1]{0,1:T(1,128)S(1)}, s32[2048,1]{0,1:T(1,128)}, u32[]{:S(2)}) copy-start(s32[2048,1]{0,1:T(1,128)} %get-tuple-element.22) | copy-start | bytes 24580
  1050.0 277.3 %all-to-all-start.1 = ((bf16[16,256,1536]{2,1,0:T(8,128)(2,1)}), bf16[16,256,1536]{2,1,0:T(8,128)(2,1)}, u32[]{:S(2)}, u32[]{:S(2)}) async-start(bf16[16,256,1536]{2,1,0:T(8,128)(2,1)} %bitcast.163), calls=%async_computation.1 | async-start | bytes 25165824 | tf_op jit(solution)/shard_map/all_to_all | solution.py:197
  1103.5 375.6 %reduce-scatter.8.cloned.1.call-start = ((), (), s32[]{:S(2)}) async-start(), calls=%async_computation.16 | async-start | bytes 786432 | tf_op jit(solution)/shard_map/reduce_scatter | solution.py:292
  1158.0 215.2 %copy-start.11 = (f32[256,1536]{1,0:T(8,128)S(1)}, f32[256,1536]{1,0:T(8,128)}, u32[]{:S(2)}) copy-start(f32[256,1536]{1,0:T(8,128)} %copy-done.10) | copy-start | bytes 4718596
  1158.0 215.2 %copy-start.31 = (f32[256,8]{1,0:T(8,128)S(1)}, f32[256,8]{1,0:T(8,128)}, u32[]{:S(2)}) copy-start(f32[256,8]{1,0:T(8,128)} %copy-done.30) | copy-start | bytes 24580
  1373.2 9.9 copy-start.51
  1373.2 9.9 copy-start.45
  1373.2 9.9 copy-start.5
  1373.3 9.9 copy-start.41
  1373.3 9.9 copy-start.49
  1373.3 9.9 copy-start.56
  1391.8 11.0 slice-start
  1391.8 11.0 slice-start.1
  1391.8 12.6 slice-start.2
  1404.5 9.4 copy-start.22
  1404.5 9.4 copy-start.24
  1416.7 79.9 %reduce-scatter.10.cloned.1.call-start = ((), (), s32[]{:S(2)}) async-start(), calls=%async_computation.17 | async-start | bytes 786432 | tf_op jit(solution)/shard_map/reduce_scatter | solution.py:298
  1422.4 187.0 %reduce-scatter.14.cloned.1.call-start = ((), (), s32[]{:S(2)}) async-start(), calls=%async_computation.19 | async-start | bytes 14155776 | tf_op jit(solution)/shard_map/reduce_scatter | solution.py:327
  1427.4 362.8 %reduce-scatter.12.cloned.1.call-start = ((), (), s32[]{:S(2)}) async-start(), calls=%async_computation.18 | async-start | bytes 23592960 | tf_op jit(solution)/shard_map/reduce_scatter | solution.py:326
  1432.4 64.2 %copy-start.9 = (bf16[256,1536]{1,0:T(8,128)(2,1)S(1)}, bf16[256,1536]{1,0:T(8,128)(2,1)}, u32[]{:S(2)}) copy-start(bf16[256,1536]{1,0:T(8,128)(2,1)} %param.11) | copy-start | bytes 2359300
  1432.4 64.2 %copy-start.47 = (f32[1536]{0:T(1024)S(1)}, f32[1536]{0:T(1024)}, u32[]{:S(2)}) copy-start(f32[1536]{0:T(1024)} %copy-done.46) | copy-start | bytes 18436
  1432.4 64.2 %copy-start.53 = (f32[256]{0:T(256)S(1)}, f32[256]{0:T(256)}, u32[]{:S(2)}) copy-start(f32[256]{0:T(256)} %copy-done.52) | copy-start | bytes 3076
  1432.7 73.2 %copy-start.25 = (bf16[256,8,3,64]{0,3,2,1:T(8,128)(2,1)}, bf16[256,8,3,64]{0,3,2,1:T(8,128)(2,1)S(1)}, u32[]{:S(2)}) copy-start(bf16[256,8,3,64]{0,3,2,1:T(8,128)(2,1)S(1)} %pad_maximum_fusion.9) | copy-start | bytes 2359300
  1506.0 313.0 %reduce-scatter.20.cloned.1.call-start = ((), (), s32[]{:S(2)}) async-start(), calls=%async_computation.22 | async-start | bytes 2359296 | tf_op jit(solution)/shard_map/reduce_scatter | solution.py:247
  1517.8 19.8 copy-start.13
  1517.8 347.4 %reduce-scatter.18.cloned.1.call-start = ((), (), s32[]{:S(2)}) async-start(), calls=%async_computation.21 | async-start | bytes 4718592 | tf_op jit(solution)/shard_map/reduce_scatter | solution.py:244
  1537.6 339.7 %reduce-scatter.16.cloned.1.call-start = ((), (), s32[]{:S(2)}) async-start(), calls=%async_computation.20 | async-start | bytes 147456 | tf_op jit(solution)/shard_map/reduce_scatter | solution.py:328
  1538.6 483.1 %all-reduce.7.cloned.1.call-start = ((), (), s32[]{:S(2)}) async-start(), calls=%async_computation.23 | async-start | bytes 12582912 | tf_op jit(solution)/shard_map/psum | solution.py:333
  1795.8 82.3 %copy-start.26 = (bf16[256,8,3,64]{0,3,2,1:T(8,128)(2,1)S(1)}, bf16[256,8,3,64]{0,3,2,1:T(8,128)(2,1)}, u32[]{:S(2)}) copy-start(bf16[256,8,3,64]{0,3,2,1:T(8,128)(2,1)} %copy-done.25) | copy-start | bytes 2359300
  1878.2 78.0 %copy-start.58 = (f32[256]{0:T(256)S(1)}, f32[256]{0:T(256)}, u32[]{:S(2)}) copy-start(f32[256]{0:T(256)} %copy-done.57) | copy-start | bytes 3076
  2021.7 6.6 copy-start.28
  (26 other events, 80.8 us)
Sparse Core Ops, SparseCore 0:
  9.6 100.7 all-gather.8
  119.0 21.3 all-gather.10
  141.9 62.6 all-gather.12
  512.1 45.2 all-gather.14
  558.8 27.2 all-gather.16
  1416.8 62.2 reduce-scatter.7
  1482.0 14.5 reduce-scatter.9
  1498.9 110.5 reduce-scatter.13
  1611.8 178.3 reduce-scatter.11
  1792.9 26.0 reduce-scatter.19
  1821.9 43.3 reduce-scatter.17
  1867.3 9.9 reduce-scatter.15
  1881.6 140.0 all-reduce.6
where the time goes:
time: 2050 us; the launch traced here: 2040 us
  waiting for transfers between devices  1360 us (66%)
  starting transfers between devices  167 us (8%)
  matrix products  166 us (8%)
  local copies, waits for them, and re-layouts  152 us (7%)
  other arithmetic  92.4 us (5%)
  blocking collectives  87.6 us (4%)
    all_to_all x1, waiting for transfers between devices, body(): lax.all_to_all(back_rows, 'expert', split_axis=0, concat_axis=0, tiled=True)  212 us
    all_to_all x1, waiting for transfers between devices, body(): lax.all_to_all(outgoing, 'expert', split_axis=0, concat_axis=0, tiled=True)  183 us
    reduce_scatter x1, waiting for transfers between devices, body(): lax.psum_scatter(grad_qkv_local, 'shard', scatter_dimension=0, tiled=True)  177 us
    all_to_all x1, waiting for transfers between devices, body(): lax.all_to_all(produced, 'expert', split_axis=0, concat_axis=0, tiled=True)  169 us
    all_to_all x1, waiting for transfers between devices, body(): lax.all_to_all(grad_buffer, 'expert', split_axis=0, concat_axis=0, tiled=...  148 us
    all_gather x1, waiting for transfers between devices, body(): lax.all_gather(query_key_value_weight, 'shard', axis=0, tiled=True)  95.4 us
    reduce_scatter x1, waiting for transfers between devices, body(): lax.psum_scatter(grad_out_local, 'shard', scatter_dimension=0, tiled=True)  70.6 us
    psum x1, waiting for transfers between devices, body(): lax.psum(partial_grads[2].astype(jnp.bfloat16), 'expert')  62.5 us
  transfers between devices with their start and end apart: 17, of which 16 were waited for; matrix products, arithmetic and copies ran while one was open for 11% of the time, Pallas kernels for 0%

commit v1 on v0

v1 whole, which is shorter than its diff:
```python
from functools import partial

import jax
import jax.numpy as jnp
import numpy as np
from jax import lax
from jax.experimental import pallas as pl
from jax.experimental.pallas import tpu as pltpu
from jax.sharding import Mesh, PartitionSpec as P

QUERY_HEADS = 24
KEY_VALUE_HEADS = 8
HEAD_SIZE = 64
GROUP = QUERY_HEADS // KEY_VALUE_HEADS
RES_SCALE = 0.22
ATT_SCALE = 0.015625
EPSILON = 1e-06
ROPE_BASE = 10000.0
MASKED = -1000000000.0
F32 = jnp.float32
BF16 = jnp.bfloat16
MIB = 1024 * 1024
BIG_VMEM = 60 * MIB


def mm(a, b, dims):
    return lax.dot_general(a, b, (dims, ((), ())), preferred_element_type=F32)


def nn(a, b):
    return mm(a, b, ((1,), (0,)))


def nt(a, b):
    return mm(a, b, ((1,), (1,)))


def tn(a, b):
    return mm(a, b, ((0,), (0,)))


def tie(values, after):
    return lax.optimization_barrier((values, after))[0]


def ring_chips(chips):
    depth = 4 if chips % 4 == 0 else 2
    width = max(1, chips // depth)
    walk = [(z, 0) for z in range(depth)]
    for z in reversed(range(depth)):
        line = range(1, width) if (depth - 1 - z) % 2 == 0 else reversed(range(1, width))
        walk += [(z, x) for x in line]
    return [z * width + x for z, x in walk]


def add_low(a, b):
    return (a.astype(F32) + b.astype(F32)).astype(BF16)


def rms_scale(rows):
    return lax.rsqrt(jnp.mean(rows * rows, axis=-1, keepdims=True) + EPSILON)


def rms_back(rows, scale, gain, grad):
    weighted = grad * gain
    dot = jnp.mean(weighted * rows, axis=-1, keepdims=True)
    return scale * weighted - rows * (scale * scale * scale * dot)


def turn(value, cosine, sine, first):
    swapped = jnp.where(first, pltpu.roll(value, 96, 1), pltpu.roll(value, 32, 1))
    return value * cosine + swapped * sine


def attend_kernel(
    q_ref, k_ref, v_ref, cos_ref, sin_ref, seg_col, seg_row, qkv_out, p_out, head_out, bias, turned
):
    pair, pairs = pl.program_id(0), pl.num_programs(0)
    length = q_ref.shape[0]
    block = min(256, length)
    q_cols = pairs * 2 * GROUP * HEAD_SIZE
    wide = 2 * GROUP * HEAD_SIZE
    first = lax.broadcasted_iota(jnp.int32, (length, 128), 1) % HEAD_SIZE < HEAD_SIZE // 2

    @pl.when(pair == 0)
    def _():
        keys = lax.broadcasted_iota(jnp.int32, (length, length), 0)
        rows = lax.broadcasted_iota(jnp.int32, (length, length), 1)
        allowed = (seg_col[...] == seg_row[...]) & (keys <= rows)
        bias[...] = jnp.where(allowed, 0.0, MASKED)

    cosine, sine = cos_ref[...], sin_ref[...]
    for c in range(wide // 128):
        at = pl.ds(c * 128, 128)
        turned[:, at] = turn(q_ref[:, at], cosine, sine, first).astype(BF16)
    key = turn(k_ref[...], cosine, sine, first).astype(BF16)
    value = v_ref[...].astype(BF16)
    qkv_out[:, pl.ds(pl.multiple_of(pair * wide, 128), wide)] = turned[...]
    qkv_out[:, pl.ds(pl.multiple_of(q_cols + pair * 128, 128), 128)] = key
    qkv_out[:, pl.ds(pl.multiple_of(q_cols + (pairs + pair) * 128, 128), 128)] = value
    value_t = jnp.transpose(v_ref[...]).astype(BF16)
    for r in range(length // block):
        rows = pl.ds(r * block, block)
        end = (r + 1) * block
        mask = bias[0:end, rows]
        mask = jnp.concatenate([mask] * GROUP, axis=1)
        both = []
        for g in range(2):
            query = jnp.concatenate(
                [
                    turned[rows, pl.ds((g * GROUP + j) * HEAD_SIZE, HEAD_SIZE)]
                    for j in range(GROUP)
                ],
                axis=0,
            )
            own_key = key[:end, g * HEAD_SIZE : (g + 1) * HEAD_SIZE]
            scores = nt(own_key, query) * ATT_SCALE + mask
            grown = jnp.exp(scores - jnp.max(scores, axis=0, keepdims=True))
            probs = grown * (1.0 / jnp.sum(grown, axis=0, keepdims=True))
            probs = probs.astype(BF16)
            p_out[g, 0:end, pl.ds(r * GROUP * block, GROUP * block)] = probs
            both.append(nn(value_t[g * HEAD_SIZE : (g + 1) * HEAD_SIZE, :end], probs))
        laid = jnp.transpose(jnp.concatenate(both, axis=0))
        for g in range(2):
            for j in range(GROUP):
                head_out[rows, pl.ds((g * GROUP + j) * HEAD_SIZE, HEAD_SIZE)] = laid[
                    j * block : (j + 1) * block, g * HEAD_SIZE : (g + 1) * HEAD_SIZE
                ].astype(BF16)


def attend(projected, cosine, sine, segments):
    length, cols = projected.shape
    q_cols = cols * 3 // 5
    pairs = q_cols // (2 * GROUP * HEAD_SIZE)
    wide = 2 * GROUP * HEAD_SIZE
    key_at = q_cols // 128
    return pl.pallas_call(
        attend_kernel,
        grid=(pairs,),
        in_specs=[
            pl.BlockSpec((length, wide), lambda i: (0, i)),
            pl.BlockSpec((length, 128), lambda i: (0, key_at + i)),
            pl.BlockSpec((length, 128), lambda i: (0, key_at + pairs + i)),
            pl.BlockSpec((length, 128), lambda i: (0, 0)),
            pl.BlockSpec((length, 128), lambda i: (0, 0)),
            pl.BlockSpec((length, 1), lambda i: (0, 0)),
            pl.BlockSpec((1, length), lambda i: (0, 0)),
        ],
        out_specs=[
            pl.BlockSpec((length, cols), lambda i: (0, 0)),
            pl.BlockSpec((2, length, GROUP * length), lambda i: (i, 0, 0)),
            pl.BlockSpec((length, wide), lambda i: (0, i)),
        ],
        out_shape=[
            jax.ShapeDtypeStruct((length, cols), BF16),
            jax.ShapeDtypeStruct((2 * pairs, length, GROUP * length), BF16),
            jax.ShapeDtypeStruct((length, q_cols), BF16),
        ],
        scratch_shapes=[pltpu.VMEM((length, length), F32), pltpu.VMEM((length, wide), BF16)],
        compiler_params=pltpu.CompilerParams(vmem_limit_bytes=40 * MIB),
        cost_estimate=pl.CostEstimate(
            flops=8 * pairs * GROUP * length * length * 256,
            bytes_accessed=4 * pairs * GROUP * length * length,
            transcendentals=2 * pairs * GROUP * length * length,
        ),
    )(projected, projected, projected, cosine, sine, segments[:, None], segments[None, :])


def attend_back_kernel(shards, info, q_ref, k_ref, v_ref, p_ref, w_ref, cos_ref, sin_ref, *refs):
    upstream, refs = refs[:shards], refs[shards:]
    grad_out, all_out, all_s, d_s, dq_s, dk_s, dv_s, sems = refs
    pair, pairs = pl.program_id(0), pl.num_programs(0)
    length = q_ref.shape[0]
    rows_of = length // shards

    def kept():
        return pltpu.make_async_copy(all_s, all_out, sems.at[shards])

    @pl.when(pair == 0)
    def _():
        made = [
            pltpu.make_async_copy(
                upstream[s],
                all_s.at[pl.ds(pl.multiple_of(info[2 + s] * rows_of, 16), rows_of)],
                sems.at[s],
            )
            for s in range(shards)
        ]
        for one in made:
            one.start()
        finish(made)
        kept().start()
        grads = nt(all_s[...], w_ref[...]).astype(BF16)
        for i in range(d_s.shape[0]):
            d_s[i] = grads[:, i * d_s.shape[2] : (i + 1) * d_s.shape[2]]

    @pl.when(pair == pairs - 1)
    def _():
        kept().wait()

    d_ref = d_s.at[pair]
    block = min(256, length)
    q_cols = pairs * 2 * GROUP * HEAD_SIZE
    wide = 2 * GROUP * HEAD_SIZE
    first = lax.broadcasted_iota(jnp.int32, (length, 128), 1) % HEAD_SIZE < HEAD_SIZE // 2
    key_t = jnp.transpose(k_ref[...].astype(F32)).astype(BF16)
    for r in reversed(range(length // block)):
        rows = pl.ds(r * block, block)
        end = (r + 1) * block
        both = []
        for g in range(2):
            own = pl.ds(g * HEAD_SIZE, HEAD_SIZE)
            heads = [
                pl.ds((g * GROUP + j) * HEAD_SIZE, HEAD_SIZE) for j in range(GROUP)
            ]
            query = jnp.concatenate([q_ref[rows, h] for h in heads], axis=0)
            grad = jnp.concatenate([d_ref[rows, h] for h in heads], axis=0)
            probs = p_ref[g, 0:end, pl.ds(r * GROUP * block, GROUP * block)]
            prob_grad = nt(v_ref[0:end, own], grad)
            wide_probs = probs.astype(F32)
            dots = jnp.sum(wide_probs * prob_grad, axis=0, keepdims=True)
            score_grad = (wide_probs * (prob_grad - dots)).astype(BF16)
            key_grad = nn(score_grad, query)
            value_grad = nn(probs, grad)
            if end == length:
                dk_s[0:end, own] = key_grad
                dv_s[0:end, own] = value_grad
            else:
                dk_s[0:end, own] += key_grad
                dv_s[0:end, own] += value_grad
            both.append(nn(key_t[g * HEAD_SIZE : (g + 1) * HEAD_SIZE, :end], score_grad))
        laid = jnp.transpose(jnp.concatenate(both, axis=0))
        for g in range(2):
            for j in range(GROUP):
                dq_s[rows, pl.ds((g * GROUP + j) * HEAD_SIZE, HEAD_SIZE)] = laid[
                    j * block : (j + 1) * block, g * HEAD_SIZE : (g + 1) * HEAD_SIZE
                ]
    cosine, sine = cos_ref[...] * ATT_SCALE, sin_ref[...] * -ATT_SCALE
    for c in range(wide // 128):
        at = pl.ds(c * 128, 128)
        grad_out[:, pl.ds(pl.multiple_of(pair * wide + c * 128, 128), 128)] = turn(
            dq_s[:, at], cosine, sine, first
        ).astype(BF16)
    grad_out[:, pl.ds(pl.multiple_of(q_cols + pair * 128, 128), 128)] = turn(
        dk_s[...], cosine, sine, first
    ).astype(BF16)
    grad_out[:, pl.ds(pl.multiple_of(q_cols + (pairs + pair) * 128, 128), 128)] = dv_s[
        ...
    ].astype(BF16)


def attend_back(info, qkv, probs, out_weight, cosine, sine, upstream):
    length, cols = qkv.shape
    q_cols = cols * 3 // 5
    pairs = q_cols // (2 * GROUP * HEAD_SIZE)
    wide = 2 * GROUP * HEAD_SIZE
    width = out_weight.shape[1]
    key_at = q_cols // 128
    shards = len(upstream)
    anywhere = pl.BlockSpec(memory_space=pltpu.HBM)
    return pl.pallas_call(
        partial(attend_back_kernel, shards),
        grid=(pairs,),
        in_specs=[
            pl.BlockSpec(memory_space=pltpu.SMEM),
            pl.BlockSpec((length, wide), lambda i: (0, i)),
            pl.BlockSpec((length, 128), lambda i: (0, key_at + i)),
            pl.BlockSpec((length, 128), lambda i: (0, key_at + pairs + i)),
            pl.BlockSpec((2, length, GROUP * length), lambda i: (i, 0, 0)),
            pl.BlockSpec((q_cols, width), lambda i: (0, 0)),
            pl.BlockSpec((length, 128), lambda i: (0, 0)),
            pl.BlockSpec((length, 128), lambda i: (0, 0)),
        ]
        + [anywhere] * shards,
        out_specs=[pl.BlockSpec((length, cols), lambda i: (0, 0)), anywhere],
        out_shape=[
            jax.ShapeDtypeStruct((length, cols), BF16),
            jax.ShapeDtypeStruct((length, width), BF16),
        ],
        scratch_shapes=[
            pltpu.VMEM((length, width), BF16),
            pltpu.VMEM((pairs, length, wide), BF16),
            pltpu.VMEM((length, wide), F32),
            pltpu.VMEM((length, 128), F32),
            pltpu.VMEM((length, 128), F32),
            pltpu.SemaphoreType.DMA((shards + 1,)),
        ],
        compiler_params=pltpu.CompilerParams(vmem_limit_bytes=40 * MIB),
        cost_estimate=pl.CostEstimate(
            flops=16 * pairs * GROUP * length * length * 256 + 2 * length * q_cols * width,
            bytes_accessed=4 * pairs * GROUP * length * length,
            transcendentals=0,
        ),
    )(info, qkv, qkv, qkv, probs, out_weight, cosine, sine, *upstream)


class Copies:
    def __init__(self, sems):
        self.sems, self.used = sems, 0

    def make(self, src, dst):
        made = pltpu.make_async_copy(src, dst, self.sems.at[self.used])
        self.used += 1
        return made

    def start(self, src, dst):
        made = self.make(src, dst)
        made.start()
        return made


def finish(copies):
    for made in copies:
        made.wait()


def load_weights(copies, info, refs, layout, scratch, base, cols):
    made = []
    for ref, (s, first, number, many) in zip(refs, layout):
        at = pl.ds(pl.multiple_of(info[2 + s] * many + first, 128 if cols else 16), number)
        if cols:
            made.append(copies.start(ref, scratch.at[pl.ds(base, ref.shape[0]), at]))
        else:
            made.append(copies.start(ref, scratch.at[at, pl.ds(base, ref.shape[1])]))
    return made


def expert_kernel(slots, in_layout, down_layout, info, *refs):
    parts = len(slots)
    refs = list(refs)
    take = lambda n: [refs.pop(0) for _ in range(n)]
    x_refs, d_refs = take(parts), take(parts)
    route_refs, (router_ref,) = take(parts), take(1)
    in_refs = [take(len(in_layout)), take(len(in_layout))]
    down_refs = [take(len(down_layout)), take(len(down_layout))]
    low_out, mixed_out = take(2)
    row_outs, gate_outs = take(parts), take(parts)
    (share_out,) = take(1)
    x_s, d_s, in_s, down_s, router_s, route_s, low_s, mixed_s, row_s, gate_s, pulled_s, sems = refs
    rows, width = x_refs[0].shape
    total = parts * rows
    ffe = in_s.shape[1] // 4
    tile = min(256, ffe)
    copies = Copies(sems)
    place = [pl.ds(p * rows, rows) for p in range(parts)]
    got_x = [copies.start(x_refs[p], x_s.at[place[p]]) for p in range(parts)]
    got_x.append(copies.start(router_ref, router_s))
    for p in range(parts):
        at, _, seen = slots[p]
        got_x.append(copies.start(route_refs[p].at[pl.ds(at, 16), pl.ds(0, seen)], route_s.at[p]))
    got_in, got_down = [], []
    for e in range(2):
        got_in.append(load_weights(copies, info, in_refs[e], in_layout, in_s, 2 * e * ffe, False))
        if e == 0:
            got_d = [copies.start(d_refs[p], d_s.at[place[p]]) for p in range(parts)]
        got_down.append(
            load_weights(copies, info, down_refs[e], down_layout, down_s, e * ffe, True)
        )
    lanes = lax.broadcasted_iota(jnp.int32, (rows, 128), 1)
    finish(got_x)
    bias = []
    for p in range(parts):
        first = slots[p][1]
        named = jnp.transpose(route_s[p].astype(F32))[first : first + rows].astype(jnp.int32)
        hit = named[:, 0:1] == lanes
        for k in range(1, 8):
            hit = hit | (named[:, k : k + 1] == lanes)
        bias.append(jnp.where(hit, 0.0, -1e30))
    logits = nn(x_s[...], router_s[...]) + jnp.concatenate(bias, axis=0)
    grown = jnp.exp(logits - jnp.max(logits, axis=-1, keepdims=True))
    shares = grown / jnp.sum(grown, axis=-1, keepdims=True)
    share_out[...] = shares
    lanes = lax.broadcasted_iota(jnp.int32, (total, 128), 1)
    gate_cols = jnp.zeros((total, 128), F32)
    sent = []
    for e in range(2):
        share = RES_SCALE * jnp.sum(
            jnp.where(lanes == info[e], shares, 0.0), axis=1, keepdims=True
        )
        gate_grad = jnp.zeros((total, 1), F32)
        finish(got_in[e])
        gate_s[...] = nn(x_s[...], in_s[:, pl.ds(2 * e * ffe, 2 * ffe)])
        finish((got_d if e == 0 else []) + got_down[e])
        pulled_s[...] = nt(d_s[...], down_s[pl.ds(e * ffe, ffe), :])
        for j in range(ffe // tile):
            gate_at = 2 * e * ffe + j * tile
            gate = gate_s[:, pl.ds(j * tile, tile)]
            up = gate_s[:, pl.ds(ffe + j * tile, tile)]
            pulled = pulled_s[:, pl.ds(j * tile, tile)]
            sigmoid = 0.5 * jnp.tanh(0.5 * gate) + 0.5
            swish = gate * sigmoid
            hidden = swish * up
            gate_grad = gate_grad + jnp.sum(hidden * pulled, axis=1, keepdims=True)
            hidden_grad = share * pulled
            low_s[:, pl.ds(gate_at, tile)] = (
                hidden_grad * up * (sigmoid * (1.0 + gate - swish))
            ).astype(BF16)
            low_s[:, pl.ds(gate_at + ffe, tile)] = (hidden_grad * swish).astype(BF16)
            mixed_s[:, pl.ds(e * ffe + j * tile, tile)] = (
                share * (1.0 / RES_SCALE) * hidden
            ).astype(BF16)
        gate_cols = gate_cols + jnp.where(lanes == e, RES_SCALE * gate_grad, 0.0)
    sent.append(copies.start(low_s, low_out))
    sent.append(copies.start(mixed_s, mixed_out))
    step = 768
    for n in range(width // step):
        at = pl.ds(n * step, step)
        row_s[:, at] = nt(low_s[...], in_s[at, :]).astype(BF16)
        for p in range(parts):
            sent.append(copies.start(row_s.at[place[p], at], row_outs[p].at[:, at]))
    for p in range(parts):
        gate_outs[p][...] = jnp.transpose(gate_cols[p * rows : (p + 1) * rows])[:8]
    finish(sent)


def run_experts(slots, info, x_list, d_list, routes, router, weights, layouts):
    parts = len(slots)
    rows, width = x_list[0].shape
    ffe = weights[0][0].shape[1] // 2
    total = parts * rows
    out_shape = [
        jax.ShapeDtypeStruct((total, 4 * ffe), BF16),
        jax.ShapeDtypeStruct((total, 2 * ffe), BF16),
    ]
    out_shape += [jax.ShapeDtypeStruct((rows, width), BF16)] * parts
    out_shape += [jax.ShapeDtypeStruct((8, rows), F32)] * parts
    out_shape += [jax.ShapeDtypeStruct((total, 128), F32)]
    operands = [*x_list, *d_list, *routes, router]
    for group in (weights[0], weights[2], weights[1], weights[3]):
        operands += list(group)
    here = pl.BlockSpec(memory_space=pltpu.VMEM)
    anywhere = pl.BlockSpec(memory_space=pltpu.HBM)
    copies = 3 * parts + 1 + sum(len(w) for w in weights) + 2 + parts * (width // 256)
    in_specs = [anywhere] * len(operands)
    outs = pl.pallas_call(
        partial(expert_kernel, slots, *layouts),
        in_specs=[pl.BlockSpec(memory_space=pltpu.SMEM)] + in_specs,
        out_specs=[anywhere] * (2 + parts) + [here] * (parts + 1),
        out_shape=out_shape,
        scratch_shapes=[
            pltpu.VMEM((total, width), BF16),
            pltpu.VMEM((total, width), BF16),
            pltpu.VMEM((width, 4 * ffe), BF16),
            pltpu.VMEM((2 * ffe, width), BF16),
            pltpu.VMEM((width, 128), BF16),
            pltpu.VMEM((parts, 16, slots[0][2]), BF16),
            pltpu.VMEM((total, 4 * ffe), BF16),
            pltpu.VMEM((total, 2 * ffe), BF16),
            pltpu.VMEM((total, width), BF16),
            pltpu.VMEM((total, 2 * ffe), F32),
            pltpu.VMEM((total, ffe), F32),
            pltpu.SemaphoreType.DMA((copies,)),
        ],
        compiler_params=pltpu.CompilerParams(vmem_limit_bytes=BIG_VMEM),
        cost_estimate=pl.CostEstimate(
            flops=20 * total * width * ffe,
            bytes_accessed=12 * ffe * width + 12 * total * width,
            transcendentals=total * ffe * 2,
        ),
    )(info, *operands)
    return outs[0], outs[1], outs[2 : 2 + parts], outs[2 + parts : 2 + 2 * parts], outs[-1]


def result_kernel(heights, out_heights, down_layout, info, *refs):
    refs = list(refs)
    take = lambda n: [refs.pop(0) for _ in range(n)]
    mixed_refs = take(len(heights))
    down_refs = [take(len(down_layout)), take(len(down_layout))]
    outs = take(len(out_heights))
    mixed_s, down_s, out_s, sems = refs
    ffe = down_s.shape[0] // 2
    copies = Copies(sems)
    got = [
        made
        for e in range(2)
        for made in load_weights(copies, info, down_refs[e], down_layout, down_s, e * ffe, True)
    ]
    start, waits = 0, []
    for ref, height in zip(mixed_refs, heights):
        waits.append(copies.start(ref, mixed_s.at[pl.ds(start, height)]))
        start += height
    finish(got)
    sent, start, place, at = [], 0, 0, 0
    for i, height in enumerate(heights):
        finish([waits[i]])
        rows = pl.ds(start, height)
        for n in range(down_s.shape[1] // 512):
            cols = pl.ds(n * 512, 512)
            out_s[rows, cols] = nn(mixed_s[rows, :], down_s[:, cols]).astype(BF16)
        start += height
        while place < len(outs) and at + out_heights[place] <= start:
            sent.append(copies.start(out_s.at[pl.ds(at, out_heights[place])], outs[place]))
            at += out_heights[place]
            place += 1
    finish(sent)


def run_results(info, mixeds, weights, layouts, out_heights):
    heights = [m.shape[0] for m in mixeds]
    total, cols = sum(heights), mixeds[0].shape[1]
    width = sum(number for _, _, number, _ in layouts[1])
    anywhere = pl.BlockSpec(memory_space=pltpu.HBM)
    operands = [*mixeds, *weights[1], *weights[3]]
    return pl.pallas_call(
        partial(result_kernel, heights, out_heights, layouts[1]),
        in_specs=[pl.BlockSpec(memory_space=pltpu.SMEM)] + [anywhere] * len(operands),
        out_specs=[anywhere] * len(out_heights),
        out_shape=[jax.ShapeDtypeStruct((h, width), BF16) for h in out_heights],
        scratch_shapes=[
            pltpu.VMEM((total, cols), BF16),
            pltpu.VMEM((cols, width), BF16),
            pltpu.VMEM((total, width), BF16),
            pltpu.SemaphoreType.DMA((len(operands) + len(out_heights),)),
        ],
        compiler_params=pltpu.CompilerParams(vmem_limit_bytes=BIG_VMEM),
        cost_estimate=pl.CostEstimate(
            flops=2 * total * cols * width,
            bytes_accessed=2 * (total * (cols + width) + cols * width),
            transcendentals=0,
        ),
    )(info, *operands)


def sort_gates_kernel(counts, info, *refs):
    out = refs[-1]
    for i, many in enumerate(counts):
        pieces = refs[sum(counts[:i]) : sum(counts[: i + 1])]
        at = 0
        for ref in pieces:
            cols = ref.shape[1]
            out[info[info.shape[0] - len(counts) + i], :, at : at + cols] = ref[0:2, :]
            at += cols


def sort_gates(info, parts, rows):
    flat = [ref for part in parts for ref in part]
    return pl.pallas_call(
        partial(sort_gates_kernel, [len(p) for p in parts]),
        in_specs=[pl.BlockSpec(memory_space=pltpu.SMEM)]
        + [pl.BlockSpec(memory_space=pltpu.VMEM)] * len(flat),
        out_specs=pl.BlockSpec(memory_space=pltpu.VMEM),
        out_shape=jax.ShapeDtypeStruct((len(parts), 2, rows), F32),
    )(info, *flat)


def spread_kernel(widths, kept, first, places, *refs):
    count = len(refs) - kept - 2 * len(widths) - 1
    blocks, refs = refs[:count], refs[count + kept :]
    outs, scratch, sems = refs[: len(widths)], refs[len(widths) : -1], refs[-1]
    copies, sent = Copies(sems), []
    for i, ref in enumerate(blocks):
        at = 0
        for out, buffer, wide in zip(outs, scratch, widths):
            buffer[i] = ref[:, at : at + wide].astype(F32)
            sent.append(copies.start(buffer.at[i], out.at[places[first + i]]))
            at += wide
    finish(sent)


def spread(places, first, blocks, widths, total, kept=()):
    count, height = len(blocks), blocks[0].shape[0]
    anywhere = pl.BlockSpec(memory_space=pltpu.HBM)
    return pl.pallas_call(
        partial(spread_kernel, widths, len(kept), first),
        in_specs=[pl.BlockSpec(memory_space=pltpu.SMEM)]
        + [pl.BlockSpec(memory_space=pltpu.VMEM)] * count
        + [anywhere] * len(kept),
        out_specs=[anywhere] * len(widths),
        out_shape=[jax.ShapeDtypeStruct((total, height, wide), F32) for wide in widths],
        scratch_shapes=[pltpu.VMEM((count, height, wide), F32) for wide in widths]
        + [pltpu.SemaphoreType.DMA((count * len(widths),))],
        input_output_aliases={1 + count + i: i for i in range(len(kept))},
        compiler_params=pltpu.CompilerParams(vmem_limit_bytes=40 * MIB),
    )(places, *blocks, *kept)


def weight_grad_kernel(heights, a_at, b_at, scale, by_rows, added, info, *refs):
    refs = list(refs)
    take = lambda n: [refs.pop(0) for _ in range(n)]
    a_refs, b_refs, more = take(len(heights[0])), take(len(heights[1])), take(added)
    a_s, b_s, sems = refs[-3:]
    outs = refs[:-3]
    step, steps = pl.program_id(0), pl.num_programs(0)
    tile = outs[0].shape[0 if by_rows else 1]

    def loads(parts, heights_of, scratch, at, tiled):
        made, start = [], 0
        for ref, height in zip(parts, heights_of):
            for t in range(steps_static if tiled else 1):
                wide = tile if tiled else scratch.shape[1]
                made.append(
                    (
                        t,
                        ref.at[:, pl.ds(at + t * wide, wide)],
                        scratch.at[pl.ds(start, height), pl.ds(t * wide, wide)],
                    )
                )
            start += height
        return made

    steps_static = (a_s if by_rows else b_s).shape[1] // tile
    first = loads(a_refs, heights[0], a_s, a_at, by_rows)
    second = loads(b_refs, heights[1], b_s, b_at, not by_rows)
    whole, tiled = (second, first) if by_rows else (first, second)
    tiled.sort(key=lambda entry: entry[0])
    copies = Copies(sems)
    made_whole = [copies.make(src, dst) for _, src, dst in whole]
    made_tiled = [(t, copies.make(src, dst)) for t, src, dst in tiled]

    @pl.when(step == 0)
    def _():
        for made in made_whole:
            made.start()
        for _, made in made_tiled:
            made.start()
        finish(made_whole)

    for t in range(steps_static):

        @pl.when(step == t)
        def _(t=t):
            finish([made for at, made in made_tiled if at == t])

    at = pl.ds(pl.multiple_of(step * tile, 128), tile)
    if by_rows:
        grad = tn(a_s[:, at], b_s[...])
    else:
        grad = tn(a_s[...], b_s[:, at])
    grad = scale * grad
    shards = len(outs) // (1 if by_rows else 2)
    place = lax.rem(step // (steps // shards) - info[2] + shards, shards)
    count = outs[0].shape[0]
    for i, out in enumerate(outs):
        value = grad if by_rows else grad[i // shards * count : (i // shards + 1) * count]

        @pl.when(place == i % shards)
        def _(i=i, out=out, value=value):
            if added:
                out[...] = (value + more[i][...].astype(F32)).astype(BF16)
            else:
                out[...] = value.astype(BF16)


def weight_grad(
    info, shards, a_list, a_at, a_cols, b_list, b_at, b_cols, scale=1.0, by_rows=True, more=()
):
    heights = ([a.shape[0] for a in a_list], [b.shape[0] for b in b_list])
    total = sum(heights[0])
    each = (a_cols if by_rows else b_cols) // shards
    tile = 256 if each % 256 == 0 else each
    tiles = each // tile
    shape = (each, b_cols) if by_rows else (a_cols // 2, each)
    many = shards if by_rows else 2 * shards
    anywhere = pl.BlockSpec(memory_space=pltpu.HBM)

    def tile_of(r):
        def index(i, info):
            at = jnp.clip(i - lax.rem(info[2] + r, shards) * tiles, 0, tiles - 1)
            return (at, 0) if by_rows else (0, at)

        block = (tile, b_cols) if by_rows else (a_cols // 2, tile)
        return pl.BlockSpec(block, index)

    parts_a = len(a_list) * (shards * tiles if by_rows else 1)
    parts_b = len(b_list) * (1 if by_rows else shards * tiles)
    return pl.pallas_call(
        partial(weight_grad_kernel, heights, a_at, b_at, scale, by_rows, len(more)),
        grid_spec=pltpu.PrefetchScalarGridSpec(
            num_scalar_prefetch=1,
            grid=(shards * tiles,),
            in_specs=[anywhere] * (len(a_list) + len(b_list))
            + [tile_of(r) for r in range(len(more))],
            out_specs=[tile_of(i % shards) for i in range(many)],
            scratch_shapes=[
                pltpu.VMEM((total, a_cols), BF16),
                pltpu.VMEM((total, b_cols), BF16),
                pltpu.SemaphoreType.DMA((parts_a + parts_b,)),
            ],
        ),
        out_shape=[jax.ShapeDtypeStruct(shape, BF16)] * many,
        compiler_params=pltpu.CompilerParams(vmem_limit_bytes=BIG_VMEM),
        cost_estimate=pl.CostEstimate(
            flops=2 * total * a_cols * b_cols,
            bytes_accessed=2 * (total * (a_cols + b_cols) + a_cols * b_cols),
            transcendentals=0,
        ),
    )(info, *a_list, *b_list, *more)


def dense_grad_kernel(unit, shards, small_too, info, places, *refs):
    sources, refs = refs[:2], refs[2:]
    extras, refs = (refs[:3], refs[3:]) if small_too else ((), refs)
    mine, theirs, a_s, b_s, scratch, sems = refs[:6]
    copies, sent = Copies(sems), []
    got = [copies.start(ref, to) for ref, to in zip(sources, (a_s, b_s))]
    flat = len(scratch.shape) == 2
    cols = b_s.shape[1]
    count = 2 * mine.shape[0]
    wide = mine.shape[2] // shards
    tile = 256 if flat else 384
    core = info[0] % 2
    if small_too:
        small, width = refs[6], a_s.shape[1]
        turned = jnp.transpose(
            jnp.concatenate([extras[0][...], extras[1][...], jnp.zeros((6, width), F32)], axis=0)
        )
        lanes = lax.broadcasted_iota(jnp.int32, (width, 128), 1)
        small[...] = jnp.where(
            lanes == count,
            turned[:, 0:1],
            jnp.where(lanes == count + 1, turned[:, 1:2], extras[2][...]),
        ).astype(BF16)
        if flat:
            scratch[:, cols:] = small[...]
    finish(got)
    ready = 0
    for t in range(a_s.shape[1] // tile):
        grad = tn(a_s[:, t * tile : (t + 1) * tile], b_s[...]).astype(BF16)
        if flat:
            scratch[t * tile : (t + 1) * tile, 0:cols] = grad
        while (ready + 1) * unit <= (t + 1) * tile:
            if flat:
                block = scratch.at[pl.ds(ready * unit, unit), :]
            else:
                first = ready * unit - t * tile
                scratch[ready, :, 0:cols] = grad[first : first + unit]
                if small_too:
                    scratch[ready, :, cols:] = small[ready * unit : (ready + 1) * unit, :]
                block = scratch.at[ready]
            name, turn = ready % count, ready // count
            place = places[name // 2]
            if shards > 1:
                turn = lax.rem(turn - info[2] + shards, shards)
            at = pl.ds(pl.multiple_of(turn * wide, 128), wide)
            to_mine = copies.make(block, mine.at[place, :, at])
            to_theirs = pltpu.make_async_copy(
                block, theirs.at[place, :, at], sems.at[copies.used - 1]
            )

            @pl.when(core == name % 2)
            def _(one=to_mine):
                one.start()

            @pl.when(core != name % 2)
            def _(one=to_theirs):
                one.start()

            sent.append(to_mine)
            ready += 1
    finish(sent)


def dense_grad(info, places, unit, shards, a, b, extras=()):
    length, rows = a.shape
    cols = b.shape[1]
    chips = places.shape[0]
    wide = cols + (128 if extras else 0)
    here = pl.BlockSpec(memory_space=pltpu.VMEM)
    anywhere = pl.BlockSpec(memory_space=pltpu.HBM)
    small = pl.BlockSpec(memory_space=pltpu.SMEM)
    flat = unit % 16 == 0
    many = rows // unit
    scratch = [
        pltpu.VMEM(a.shape, BF16),
        pltpu.VMEM(b.shape, BF16),
        pltpu.VMEM((rows, wide) if flat else (many, unit, wide), BF16),
        pltpu.SemaphoreType.DMA((2 + many,)),
    ]
    if extras:
        scratch.append(pltpu.VMEM((rows, 128), BF16))
    return pl.pallas_call(
        partial(dense_grad_kernel, unit, shards, bool(extras)),
        in_specs=[small] * 2 + [anywhere] * 2 + [here] * len(extras),
        out_specs=[anywhere] * 2,
        out_shape=[jax.ShapeDtypeStruct((chips, unit, shards * wide), BF16)] * 2,
        scratch_shapes=scratch,
        compiler_params=pltpu.CompilerParams(vmem_limit_bytes=BIG_VMEM),
        cost_estimate=pl.CostEstimate(
            flops=2 * length * rows * cols,
            bytes_accessed=2 * length * (rows + cols),
            transcendentals=0,
        ),
    )(info, places, a, b, *extras)


def normed_back_kernel(grads, weight, tokens, low_out, gain_out):
    grad = nt(grads[...], weight[...])
    rows = tokens[...].astype(F32)
    unit = rows * lax.rsqrt(jnp.mean(rows * rows, axis=-1, keepdims=True) + EPSILON)
    gain_out[...] = jnp.sum(grad * unit, axis=0, keepdims=True)
    low_out[...] = grad.astype(BF16)


def normed_back(grads, weight, tokens):
    length, width = tokens.shape
    here = pl.BlockSpec(memory_space=pltpu.VMEM)
    return pl.pallas_call(
        normed_back_kernel,
        in_specs=[here] * 3,
        out_specs=[here] * 2,
        out_shape=[
            jax.ShapeDtypeStruct((length, width), BF16),
            jax.ShapeDtypeStruct((1, width), F32),
        ],
        compiler_params=pltpu.CompilerParams(vmem_limit_bytes=40 * MIB),
        cost_estimate=pl.CostEstimate(
            flops=2 * length * width * grads.shape[1],
            bytes_accessed=2 * (grads.size + weight.size + 2 * tokens.size),
            transcendentals=0,
        ),
    )(grads, weight, tokens)


def project_kernel(shards, q_cols, k_cols, unit, info, places, own_ref, gain_ref, *refs):
    token_refs, refs = refs[:shards], refs[shards:]
    blocks, (normed_out, cols_out, out, tokens_out, w_s, t_s, sems) = refs[:-7], refs[-7:]
    count = own_ref.shape[0]
    rows = token_refs[0].shape[0]
    copies = Copies(sems)
    shard = info[2]
    key_at, value_at = q_cols * shards, (q_cols + k_cols) * shards
    made, to = [], 0
    for s in range(shards):
        at = pl.ds(pl.multiple_of(info[2 + s] * rows, 16), rows)
        made.append(copies.start(token_refs[s], t_s.at[at]))
    for at, wide in ((0, q_cols), (key_at, k_cols), (value_at, k_cols)):
        cols = pl.ds(pl.multiple_of(at + shard * wide, 128), wide)
        made.append(
            copies.start(
                own_ref.at[:, cols],
                w_s.at[pl.ds(pl.multiple_of(shard * count, 16), count), pl.ds(to, wide)],
            )
        )
        to += wide
    for i, ref in enumerate(blocks):
        at = pl.ds(pl.multiple_of(places[i] * unit, 16), unit)
        made.append(copies.start(ref.at[pl.ds(0, unit)], w_s.at[at]))
    finish(made[:shards])
    value = t_s[...].astype(F32)
    normed_out[...] = (
        value
        * lax.rsqrt(jnp.mean(value * value, axis=-1, keepdims=True) + EPSILON)
        * gain_ref[...]
    ).astype(BF16)
    finish(made[shards:])
    sent = [copies.start(w_s, cols_out), copies.start(t_s, tokens_out)]
    out[...] = nn(normed_out[...], w_s[...])
    finish(sent)


def project(info, places, own, gain, tokens, blocks, shards, q_cols, k_cols, unit):
    rows, width = tokens[0].shape
    cols = q_cols + 2 * k_cols
    anywhere = pl.BlockSpec(memory_space=pltpu.HBM)
    here = pl.BlockSpec(memory_space=pltpu.VMEM)
    small = pl.BlockSpec(memory_space=pltpu.SMEM)
    return pl.pallas_call(
        partial(project_kernel, shards, q_cols, k_cols, unit),
        in_specs=[small, small, anywhere, here] + [anywhere] * (shards + len(blocks)),
        out_specs=[here, anywhere, here, anywhere],
        out_shape=[
            jax.ShapeDtypeStruct((shards * rows, width), BF16),
            jax.ShapeDtypeStruct((width, cols), BF16),
            jax.ShapeDtypeStruct((shards * rows, cols), F32),
            jax.ShapeDtypeStruct((shards * rows, width), BF16),
        ],
        scratch_shapes=[
            pltpu.VMEM((width, cols), BF16),
            pltpu.VMEM((shards * rows, width), BF16),
            pltpu.SemaphoreType.DMA((shards + 5 + len(blocks),)),
        ],
        compiler_params=pltpu.CompilerParams(vmem_limit_bytes=BIG_VMEM),
        cost_estimate=pl.CostEstimate(
            flops=2 * shards * rows * width * cols,
            bytes_accessed=2 * (width * cols + shards * rows * (2 * width + 2 * cols)),
            transcendentals=0,
        ),
    )(info, places, own, gain, *tokens, *blocks)


def router_back_kernel(experts, info, gate_ref, share_ref, second_ref, router_ref, grad_ref, add_ref):
    core = info[0] % 2
    rows = second_ref.shape[0]
    turned = jnp.transpose(
        jnp.concatenate([gate_ref[c] for c in range(experts // 2)], axis=0)
    )
    kept = jnp.concatenate([turned, jnp.zeros((rows, 128 - experts), F32)], axis=1)
    lanes = lax.broadcasted_iota(jnp.int32, (rows, 128), 1)
    swapped = jnp.where(lanes % 2 == 0, pltpu.roll(kept, 127, 1), pltpu.roll(kept, 1, 1))
    gates = jnp.where(core == 0, kept, swapped)
    share = share_ref[...]
    dot = jnp.sum(share * gates, axis=1, keepdims=True)
    low = (share * (gates - dot)).astype(BF16)
    grad_ref[...] = tn(second_ref[...], low)
    add_ref[...] = nt(low, router_ref[...])


def router_back(info, gates, shares, second, router, experts):
    rows, width = second.shape
    here = pl.BlockSpec(memory_space=pltpu.VMEM)
    return pl.pallas_call(
        partial(router_back_kernel, experts),
        in_specs=[pl.BlockSpec(memory_space=pltpu.SMEM)] + [here] * 4,
        out_specs=[here] * 2,
        out_shape=[
            jax.ShapeDtypeStruct((width, 128), F32),
            jax.ShapeDtypeStruct((rows, width), F32),
        ],
        compiler_params=pltpu.CompilerParams(vmem_limit_bytes=16 * MIB),
    )(info, gates, shares, second, router)


def middle_back_kernel(own, right, left, add, middle, gain, upstream, low_out, grad_out, gain_out):
    grad = own[...].astype(F32) + right[...].astype(F32) + left[...].astype(F32) + add[...]
    rows = middle[...]
    scale = lax.rsqrt(jnp.mean(rows * rows, axis=-1, keepdims=True) + EPSILON)
    unit = rows * scale
    share = jnp.sum(grad * unit, axis=0, keepdims=True)
    gain_out[...] = share + jnp.where(pl.program_id(0) == 0, 0.0, gain_out[...])
    weighted = grad * gain[...]
    dot = jnp.mean(weighted * unit, axis=-1, keepdims=True)
    total = upstream[...].astype(F32) + scale * (weighted - unit * dot)
    grad_out[...] = total
    low_out[...] = (RES_SCALE * total).astype(BF16)


def middle_back(own, right, left, add, middle, gain, upstream):
    rows, width = middle.shape
    block = rows // 4
    some = pl.BlockSpec((block, width), lambda i: (i, 0))
    one = pl.BlockSpec((1, width), lambda i: (0, 0))
    return pl.pallas_call(
        middle_back_kernel,
        grid=(4,),
        in_specs=[some] * 5 + [one, some],
        out_specs=[some, some, one],
        out_shape=[
            jax.ShapeDtypeStruct((rows, width), BF16),
            jax.ShapeDtypeStruct((rows, width), F32),
            jax.ShapeDtypeStruct((1, width), F32),
        ],
        compiler_params=pltpu.CompilerParams(vmem_limit_bytes=BIG_VMEM),
    )(own, right, left, add, middle, gain, upstream)


def ring_add_kernel(right, left, front, back, *outs):
    half = right.shape[0]
    if half < front.shape[0]:
        right_out, left_out = outs
        right_out[:half] = add_low(right[...], front[:half])
        right_out[half:] = front[half:]
        left_out[:half] = back[:half]
        left_out[half:] = add_low(left[...], back[half:])
        return
    for came, own, places in ((right, front, outs[: len(outs) // 2]), (left, back, outs[len(outs) // 2 :])):
        at = 0
        for out in places:
            rows = out.shape[0]
            out[...] = add_low(came[at : at + rows], own[at : at + rows])
            at += rows


def add_both(right, left, front, back, halved=False):
    here = pl.BlockSpec(memory_space=pltpu.VMEM)
    rows, width = front.shape
    shapes = [(rows // 2, width)] * 4 if halved else [(rows, width)] * 2
    return pl.pallas_call(
        ring_add_kernel,
        in_specs=[here] * 4,
        out_specs=[here] * len(shapes),
        out_shape=[jax.ShapeDtypeStruct(shape, front.dtype) for shape in shapes],
        compiler_params=pltpu.CompilerParams(vmem_limit_bytes=16 * MIB),
        cost_estimate=pl.CostEstimate(flops=1, bytes_accessed=12 * front.size, transcendentals=0),
    )(right, left, front, back)


def sum_blocks_kernel(plan, starts, *refs):
    arrays, refs = refs[: 2 * len(starts)], refs[2 * len(starts) :]
    many = len(plan)
    total = sum(len(came) for _, _, _, came in plan)
    refs, outs, (scratch, sems) = refs[:total], refs[total : total + many], refs[-2:]
    copies = Copies(sems)
    made = []
    for i, (place, low, high, _) in enumerate(plan):
        made.append([])
        for start, pair in zip(starts, (arrays[k : k + 2] for k in range(0, len(arrays), 2))):
            first, last = max(low, start), min(high, start + pair[0].shape[2])
            if first >= last:
                continue
            for j, ref in enumerate(pair):
                made[-1].append(
                    copies.start(
                        ref.at[place, :, pl.ds(first - start, last - first)],
                        scratch.at[2 * i + j, :, pl.ds(first - low, last - first)],
                    )
                )
    at = 0
    for i, (_, low, high, came) in enumerate(plan):
        finish(made[i])
        wide = high - low
        value = scratch[2 * i, :, :wide].astype(F32) + scratch[2 * i + 1, :, :wide].astype(F32)
        outs[i][...] = value.astype(BF16)
        for start, stop in came:
            part = value[:, start - low : stop - low] + refs[at][...].astype(F32)
            at += 1
            if (start, stop) == (low, high):
                value = part
            outs[i][:, start - low : stop - low] = part.astype(BF16)


def sum_blocks(pairs, wanted):
    unit = pairs[0][0].shape[1]
    starts = [sum(p[0].shape[2] for p in pairs[:i]) for i in range(len(pairs))]
    every = sum(p[0].shape[2] for p in pairs)
    plan, flat = [], []
    for place, low, high, came in wanted:
        plan.append((place, low, high, [(at, at + c.shape[1]) for at, c in came]))
        flat += [c for _, c in came]
    anywhere = pl.BlockSpec(memory_space=pltpu.HBM)
    here = pl.BlockSpec(memory_space=pltpu.VMEM)
    arrays = [array for pair in pairs for array in pair]
    return pl.pallas_call(
        partial(sum_blocks_kernel, plan, starts),
        in_specs=[anywhere] * len(arrays) + [here] * len(flat),
        out_specs=[here] * len(plan),
        out_shape=[jax.ShapeDtypeStruct((unit, high - low), BF16) for _, low, high, _ in plan],
        scratch_shapes=[
            pltpu.VMEM((2 * len(plan), unit, every), BF16),
            pltpu.SemaphoreType.DMA((len(arrays) * len(plan),)),
        ],
        compiler_params=pltpu.CompilerParams(vmem_limit_bytes=16 * MIB),
        cost_estimate=pl.CostEstimate(
            flops=1, bytes_accessed=6 * len(plan) * unit * every, transcendentals=0
        ),
    )(*arrays, *flat)


def body(
    tokens,
    segment_ids,
    routes,
    norm1_gain,
    norm2_gain,
    qkv_weight,
    out_weight,
    route_weight,
    expert_in,
    expert_down,
    cotangent,
):
    rows, width = tokens.shape
    shards = lax.axis_size("shard")
    chips = lax.axis_size("chip")
    experts = 2 * chips
    length = rows * shards
    q_cols = QUERY_HEADS // shards * HEAD_SIZE
    k_cols = KEY_VALUE_HEADS // shards * HEAD_SIZE
    own_cols = q_cols + 2 * k_cols
    query_width = QUERY_HEADS * HEAD_SIZE
    pair_width = KEY_VALUE_HEADS * HEAD_SIZE
    ffe = expert_down.shape[1]
    cut = width // shards
    shard = lax.axis_index("shard")
    core = lax.axis_index("core")
    chip = lax.axis_index("chip")
    walk = ring_chips(chips)
    ahead = [(walk[i], walk[(i + 1) % chips]) for i in range(chips)]
    behind = [(b, a) for a, b in ahead]
    half_ring = chips // 2
    order = [0]
    for step in range(1, half_ring):
        order += [-step, step]
    order.append(half_ring)
    place_of = {c: i for i, c in enumerate(walk)}
    chip_tables = np.array([[walk[(place_of[c] + o) % chips] for o in order] for c in range(chips)])
    senders = jnp.asarray(chip_tables, jnp.int32)[chip]
    info = jnp.concatenate(
        [
            jnp.stack([2 * chip + core, 2 * chip + 1 - core]),
            (shard - jnp.arange(shards) + shards) % shards,
            senders,
        ]
    ).astype(jnp.int32)
    slot_of = lambda i: 2 + shards + i
    both_cores = jnp.concatenate([2 * senders + core, 2 * senders + 1 - core])
    rel_tables = np.array([[list(row).index(c) for c in range(chips)] for row in chip_tables])
    chip_places = jnp.asarray(rel_tables, jnp.int32)[chip]

    def to_shard(value, step):
        return lax.ppermute(value, "shard", [(i, (i + step) % shards) for i in range(shards)])

    def to_core(value):
        return lax.ppermute(value, "core", [(0, 1), (1, 0)])

    def in_order(pieces):
        out = []
        for j in range(shards):
            value = pieces[0]
            for s in range(1, shards):
                value = jnp.where((shard - j + shards) % shards == s, pieces[s], value)
            out.append(value)
        return out

    def exchange_shards(piece_for):
        got = [piece_for(shard)]
        for s in range(1, shards):
            got.append(to_shard(piece_for(lax.rem(shard + s, shards)), s))
        return got

    def sum_shards(piece_for):
        got = exchange_shards(piece_for)
        total = got[0].astype(F32)
        for piece in got[1:]:
            total = total + piece.astype(F32)
        return total

    def to_holders(parts):
        return [parts[0]] + [to_shard(parts[s], s) for s in range(1, shards)]

    def ring_step(pair, cut_far=False):
        right, left = pair
        if cut_far:
            right, left = right[: rows // 2], left[rows // 2 :]
        return lax.ppermute(right, "chip", ahead), lax.ppermute(left, "chip", behind)

    def ring_gather(value):
        out, pair = [value], (value, value)
        for step in range(1, half_ring + 1):
            pair = ring_step(pair, step == half_ring)
            out += pair
        return out

    def ring_start(parts):
        return lax.ppermute(parts[-2], "chip", ahead), lax.ppermute(parts[-1], "chip", behind)

    def ring_add(parts, step, got):
        return tuple(add_both(*got, parts[2 * step], parts[2 * step - 1]))

    def ring_send(sent):
        return lax.ppermute(sent[0], "chip", ahead), lax.ppermute(sent[1], "chip", behind)

    def ring_end(parts, got):
        return parts[0].astype(F32) + got[0].astype(F32) + got[1].astype(F32)

    def plane_gather(value, beside, use_early):
        right = left = value
        got = [value]
        half = value.shape[1] // 256 * 128
        for step in range(1, half_ring + 1):
            if step > 1:
                right, left, beside[step] = lax.optimization_barrier(
                    (right, left, beside.get(step, ()))
                )
            if step == half_ring:
                right, left = right[:, :half], left[:, half:]
            right = lax.ppermute(right, "chip", ahead)
            left = lax.ppermute(left, "chip", behind)
            if step < half_ring:
                got += [right, left]
        early = 2 * half_ring - 3
        used = use_early(got[:early] + [to_core(v) for v in got[:early]])
        right, left, used = lax.optimization_barrier((right, left, used))
        late = got[early:] + [jnp.concatenate([right, left], axis=1)]
        return used, late + [to_core(v) for v in late]

    def block_ring(values, beside):
        right = left = values
        got = [values]
        for step in range(1, half_ring + 1):
            if step > 1:
                right, left, beside = lax.optimization_barrier(
                    (right, left, beside)
                ) if step == 3 else (*lax.optimization_barrier((right, left)), beside)
            right = [lax.ppermute(v, "chip", ahead) for v in right]
            got.append(right)
            if step < half_ring:
                left = [lax.ppermute(v, "chip", behind) for v in left]
                got.append(left)
        return got + [[to_core(v) for v in values] for values in got], beside

    def own_columns(rows_at, count, target):
        return jnp.concatenate(
            [
                lax.dynamic_slice(qkv_weight, (rows_at, at + target * cols), (count, cols))
                for at, cols in (
                    (0, q_cols),
                    (query_width, k_cols),
                    (query_width + pair_width, k_cols),
                )
            ],
            axis=1,
        )

    unit = cut // experts
    name = 2 * chip + core
    units = [
        to_shard(own_columns(name * unit, unit, lax.rem(shard + s, shards)), s)
        for s in range(1, shards)
    ]
    tokens_got = [tokens] + [to_shard(tokens, s) for s in range(1, shards)]
    extras = jnp.concatenate(
        [norm1_gain, norm2_gain, segment_ids.astype(BF16), route_weight.reshape(-1)]
    ).reshape(-1, 256)
    extras = [extras] + [to_shard(extras, s) for s in range(1, shards)]
    named = jnp.pad(routes.T.astype(BF16), ((0, 16 - routes.shape[1]), (0, own_cols - rows)))
    together = unit % 16 == 0
    if together:
        units[0] = jnp.concatenate([units[0], named], axis=0)
    else:
        units.append(named)
    blocks, (tokens_got, extras) = block_ring(units, (tokens_got, extras))

    held_in, held_down = tie((expert_in[0], expert_down[0]), tokens_got)
    down_own = [held_down] + [to_shard(held_down, s) for s in range(1, shards)]
    in_own = [held_in] + [to_shard(held_in, s) for s in range(1, shards)]
    layouts = ([(s, 0, cut, cut) for s in range(shards)],) * 2
    extras = jnp.stack(in_order(extras)).reshape(shards, -1)
    gain_one = extras[:, :cut].reshape(1, -1).astype(F32)
    gain_two = extras[:, cut : 2 * cut].reshape(1, -1).astype(F32)
    segments = extras[:, 2 * cut : 2 * cut + rows].reshape(-1).astype(F32)
    router = extras[:, 2 * cut + rows :].reshape(width, experts)
    router_wide = jnp.pad(router, ((0, 0), (0, 128 - experts)))

    inverse = jnp.power(ROPE_BASE, -(jnp.arange(HEAD_SIZE // 2) * 2.0 / HEAD_SIZE))
    angles = jnp.arange(length).astype(F32)[:, None] * inverse[None, :]
    cosine = jnp.concatenate([jnp.cos(angles)] * 4, axis=1)
    sine = jnp.concatenate([-jnp.sin(angles), jnp.sin(angles)] * 2, axis=1)
    ready = (gain_one, gain_two, segments, router_wide, cosine, sine)
    blocks, down_own, upstream, ready = lax.optimization_barrier(
        (blocks, down_own, cotangent, ready)
    )
    gain_one, gain_two, segments, router_wide, cosine, sine = ready
    dy_pair = ring_step((upstream, upstream))
    upstream_chunks = [cotangent, *dy_pair]
    named_chunks = [b[0 if together else -1] for b in blocks[:chips]]
    named_at = unit if together else 0
    block_list = [b[s] for s in range(shards - 1) for b in blocks]
    block_places = jnp.concatenate(
        [info[2 + s] * experts + both_cores for s in range(1, shards)]
    ).astype(jnp.int32)
    inputs = tokens.astype(F32)
    if together:
        normed, qkv_cols, projected, all_tokens = project(
            info, block_places, qkv_weight, gain_one, tokens_got, block_list, shards, q_cols, k_cols, unit
        )
    else:
        placed = jnp.zeros((shards * experts, unit, own_cols), BF16)
        for i, piece in enumerate(block_list):
            placed = lax.dynamic_update_index_in_dim(placed, piece, block_places[i], 0)
        qkv_cols = lax.dynamic_update_slice(
            placed.reshape(width, own_cols), own_columns(0, cut, shard), (shard * cut, 0)
        )
        all_tokens = jnp.concatenate(in_order(tokens_got), axis=0)
        wide_tokens = all_tokens.astype(F32)
        normed = (wide_tokens * rms_scale(wide_tokens) * gain_one).astype(BF16)
        projected = nn(normed, qkv_cols)
    projected, dy_pair = lax.optimization_barrier((projected, dy_pair))
    dy_pair = ring_step(dy_pair)
    upstream_chunks += dy_pair
    qkv, probs, head_out = attend(projected, cosine, sine, segments)
    branch = nn(head_out, out_weight).astype(BF16)
    branch, in_own, dy_pair = lax.optimization_barrier((branch, in_own, dy_pair))
    dy_pair = ring_step(dy_pair)
    upstream_chunks += dy_pair
    rows_of = lambda value, j: lax.dynamic_slice(value, (j * rows, 0), (rows, value.shape[1]))
    middle = inputs + RES_SCALE * sum_shards(lambda j: rows_of(branch, j))
    middle, dy_pair = lax.optimization_barrier((middle, dy_pair))
    weights = [in_own, down_own, [to_core(w) for w in in_own], [to_core(w) for w in down_own]]
    scale_two = rms_scale(middle)
    second = (middle * scale_two * gain_two).astype(BF16)

    second_chunks, pair = [second], (second, second)
    dy_hops = 3
    row_parts, gate_parts, lows, mixeds = [], [], [], []
    for step in range(half_ring + 1):
        first = max(0, 2 * step - 1)
        picks = list(range(first, len(second_chunks)))
        if step < half_ring:
            pair = ring_step(pair, step == half_ring - 1)
            second_chunks += pair
        far = step == half_ring
        slots = [(named_at, 0, rows)] * len(picks)
        if step == half_ring:
            slots = [(named_at, 0, rows), (named_at, rows // 2, rows)]
        low, mixed, row, gate, shares = run_experts(
            slots,
            info,
            [second_chunks[i] for i in picks],
            [upstream_chunks[i] for i in picks],
            [named_chunks[min(i, chips - 1)] for i in picks],
            router_wide,
            weights,
            layouts,
        )
        if step == 0:
            own_shares = shares
        if not far:
            pair, low, dy_pair = lax.optimization_barrier((pair, low, dy_pair))
            second_chunks[-2:] = pair
            last = dy_hops == half_ring - 1
            if dy_hops < half_ring and (not last or step == half_ring - 2):
                dy_hops += 1
                dy_pair = ring_step(tie(dy_pair, pair), last)
                upstream_chunks += dy_pair
        lows.append(low)
        mixeds.append(mixed)
        row_parts += row
        gate_parts += [gate] if far else [[g] for g in gate]

    def make_in(sent, at, more=()):
        return weight_grad(
            info, shards, second_chunks, 0, width, tie(lows, sent), at, 2 * ffe, more=more
        )

    got = ring_start(row_parts)
    made = make_in((), 2 * ffe)
    got, made = lax.optimization_barrier((got, made))
    in_other = [to_core(piece) for piece in made]
    for hop, step in enumerate(range(half_ring - 1, 0, -1)):
        sent = ring_add(row_parts, step, got)
        got = ring_send(sent)
        if hop == 0:
            in_parts = make_in(sent, 0, in_other)
            got, in_parts = lax.optimization_barrier((got, in_parts))
            in_got = to_holders(in_parts)
        if hop == 1:
            out_parts = run_results(
                info, tie(mixeds, sent), weights, layouts, [p.shape[0] for p in row_parts]
            )
            gate_home = sort_gates(info, tie(gate_parts, sent), rows)
            gate_home = lax.all_to_all(
                gate_home, "chip", split_axis=0, concat_axis=0, tiled=True
            )
            got, out_parts, gate_home = lax.optimization_barrier((got, out_parts, gate_home))
        if hop == 2:
            router_add = router_back(
                info, tie(gate_home, sent), own_shares, second, router_wide, experts
            )
            down_parts = weight_grad(
                info,
                shards,
                tie(mixeds, (sent, router_add)),
                0,
                2 * ffe,
                upstream_chunks,
                0,
                width,
                RES_SCALE,
                by_rows=False,
            )
            got, down_parts = lax.optimization_barrier((got, down_parts))
    grad_route, router_add = router_add
    out_got = ring_start(tie(out_parts, got))
    attn_low, middle_grads, grad_gain_two = middle_back(
        row_parts[0], *got, router_add, middle, gain_two, cotangent
    )
    attn_low, out_got = lax.optimization_barrier((attn_low, out_got))
    attn_low, in_got = lax.optimization_barrier((attn_low, in_got))

    low = lambda value: value.astype(BF16)
    got = ring_send(ring_add(out_parts, half_ring - 1, out_got))
    attn_got = [attn_low] + [to_shard(attn_low, s) for s in range(1, shards)]
    down_other = [to_core(piece) for piece in tie(down_parts[shards:], attn_low)]
    down_parts = [add_low(a, b) for a, b in zip(down_parts[:shards], down_other)]
    attn_got, got, down_parts = lax.optimization_barrier((attn_got, got, down_parts))
    if half_ring > 2:
        got = ring_send(ring_add(out_parts, half_ring - 2, got))

    down_got = to_holders(down_parts)
    projected_grads, attn_grads = attend_back(info, qkv, probs, out_weight, cosine, sine, attn_got)
    normed_low, grad_gain_one = normed_back(projected_grads, qkv_cols, all_tokens)
    got, normed_low, grad_gain_one, down_got = lax.optimization_barrier(
        (got, normed_low, grad_gain_one, down_got)
    )
    for step in range(half_ring - 3, 0, -1):
        sent = ring_add(out_parts, step, got)
        projected_grads, sent = lax.optimization_barrier((projected_grads, sent))
        got = ring_send(sent)
    normed_got = exchange_shards(lambda j: rows_of(normed_low, j))

    mine_qkv, theirs_qkv = dense_grad(
        info, chip_places, unit, shards, normed, projected_grads, (grad_gain_one, grad_gain_two, grad_route)
    )
    mine_out, theirs_out = dense_grad(
        info, chip_places, unit, 1, head_out, tie(attn_grads, mine_qkv)
    )
    wide = own_cols + 128
    theirs_qkv = to_core(theirs_qkv)
    theirs_out = to_core(theirs_out)
    mine_out, got = lax.optimization_barrier((mine_out, got))
    pairs = ((mine_qkv, theirs_qkv), (mine_out, theirs_out))
    every = mine_qkv.shape[2] + mine_out.shape[2]
    half = every // 256 * 128
    right, left = sum_blocks(pairs, [(chips - 1, 0, half, []), (chips - 1, half, every, [])])
    right, left = lax.ppermute(right, "chip", ahead), lax.ppermute(left, "chip", behind)
    right, left = lax.optimization_barrier((right, left))
    for hop, step in enumerate(range(half_ring - 1, 0, -1)):
        right, left = sum_blocks(
            pairs,
            [
                (2 * step, 0, every, [(0, right)]),
                (2 * step - 1, 0, every, [(every - left.shape[1], left)]),
            ],
        )
        right = lax.ppermute(right, "chip", ahead)
        left = lax.ppermute(left, "chip", behind)
        right, left = lax.optimization_barrier((right, left))
        if step == half_ring - 2:
            right, left, normed_got = lax.optimization_barrier((right, left, normed_got))
    (dense,) = sum_blocks(pairs, [(0, 0, every, [(0, right), (0, left)])])
    mixed = in_order(
        [dense[:, :wide]]
        + [to_shard(dense[:, s * wide : (s + 1) * wide], s) for s in range(1, shards)]
    )
    merged = jnp.concatenate(
        [g[:, :q_cols] for g in mixed]
        + [g[:, q_cols : q_cols + k_cols] for g in mixed]
        + [g[:, q_cols + k_cols : own_cols] for g in mixed]
        + [low(sum(g[:, own_cols:].astype(F32) for g in mixed)), dense[:, shards * wide :]],
        axis=1,
    )

    total = lambda pieces: sum(p.astype(F32) for p in pieces)
    input_grads = rms_back(inputs, rms_scale(inputs), gain_one, total(normed_got))
    grad_tokens = middle_grads + input_grads
    grad_down, grad_in = total(down_got), total(in_got)

    block_out = low(middle + RES_SCALE * ring_end(out_parts, got))
    beside = {2: block_out, half_ring - 1: grad_tokens, half_ring: (grad_down, grad_in)}
    all_cols = query_width + 2 * pair_width
    widths = [all_cols, 128, width]
    cores = jnp.split(both_cores.astype(jnp.int32), 2)
    count = 2 * half_ring - 3
    places = jnp.concatenate([c[:count] for c in cores] + [c[count:] for c in cores])
    spread_out, late = plane_gather(
        merged, beside, lambda early: spread(places, 0, early, widths, experts)
    )
    block_out, grad_tokens = beside[2], beside[half_ring - 1]
    grad_down, grad_in = beside[half_ring]
    spread_out = spread(places, 2 * count, late, widths, experts, spread_out)
    grad_qkv, small, grad_out = [out.reshape(-1, out.shape[-1]) for out in spread_out]
    return (
        block_out,
        grad_tokens,
        small[:, experts],
        small[:, experts + 1],
        grad_qkv,
        grad_out,
        small[:, :experts],
        grad_in[None],
        grad_down[None],
    )


def solution(mesh):
    chips = mesh.shape["expert"] // 2
    grid = Mesh(
        mesh.devices.reshape(chips, 2, mesh.shape["shard"]), ("chip", "core", "shard")
    )
    expert = ("chip", "core")
    every = ("chip", "core", "shard")
    in_specs = (
        P(every, None),
        P(every),
        P(every, None),
        P("shard"),
        P("shard"),
        P("shard", None),
        P("shard", None),
        P("shard", None),
        P(expert, "shard", None),
        P(expert, None, "shard"),
        P(every, None),
    )
    out_specs = (
        P(every, None),
        P(every, None),
        P("shard"),
        P("shard"),
        P("shard", None),
        P("shard", None),
        P("shard", None),
        P(expert, "shard", None),
        P(expert, None, "shard"),
    )
    return jax.shard_map(body, mesh=grid, in_specs=in_specs, out_specs=out_specs, check_vma=False)
```

time: 2050 us -> 488 us (0.24)
  waiting for transfers between devices: 1360 us -> 155 us
  Pallas kernels: 0 us -> 188 us
  matrix products: 166 us -> 3.02 us
  local copies, waits for them, and re-layouts: 152 us -> 28 us
  blocking collectives: 87.6 us -> 0 us
  starting transfers between devices: 167 us -> 83.7 us
  other arithmetic: 92.4 us -> 17.6 us
    all_to_all x4 -> x1, waiting for transfers between devices: 711 us -> 0.37 us  [body(): lax.all_to_all(gate_home, 'chip', split_axis=0, concat_axis=0, tiled=True)]
    reduce_scatter x7 -> x0, waiting for transfers between devices: 384 us -> none  [the longest x1 177 us: body(): lax.psum_scatter(grad_qkv_local, 'shard', scatter_dimension=0, tiled=True)]
    all_gather x5 -> x0, waiting for transfers between devices: 197 us -> none  [the longest x1 95.4 us: body(): lax.all_gather(query_key_value_weight, 'shard', axis=0, tiled=True)]
    pallas_call x0 -> x31, Pallas kernels: none -> 188 us  [the longest x5 65.3 us: run_experts(): pl.pallas_call(partial(expert_kernel, slots, *layouts), in_specs=[pl.Bloc...]
    all_to_all x4 -> x1, starting transfers between devices: 166 us -> 3.34 us  [body(): lax.all_to_all(gate_home, 'chip', split_axis=0, concat_axis=0, tiled=True)]
    dot_general x21 -> x1, matrix products: 166 us -> 3.02 us  [mm(): return lax.dot_general(a, b, (dims, ((), ())), preferred_element_type=F32)]
    ppermute x0 -> x92, waiting for transfers between devices: none -> 155 us  [the longest x11 46.1 us: to_shard(): lax.ppermute(value, 'shard', [(i, (i + step) % shards) for i in range(sha...]
    gather x7 -> x0, local copies, waits for them, and re-layouts: 109 us -> none  [the longest x1 46.3 us: body(): back_home[flat_routes, slot_of].astype(jnp.float32)]
  transfers between devices with their start and end apart: 17 -> 93, of which waited for: 16 -> 50; matrix products, arithmetic and copies ran while one was open for 11% -> 6% of each run, Pallas kernels for 0% -> 33%
where the time goes in v1:
time: 488 us; the launch traced here: 478 us
  Pallas kernels  188 us (39%)
  waiting for transfers between devices  155 us (32%)
  starting transfers between devices  83.7 us (17%)
  local copies, waits for them, and re-layouts  28 us (6%)
  other arithmetic  17.6 us (4%)
    pallas_call x5, Pallas kernels, run_experts(): pl.pallas_call(partial(expert_kernel, slots, *layouts), in_specs=[pl.Bloc...  65.3 us
    ppermute x11, waiting for transfers between devices, to_shard(): lax.ppermute(value, 'shard', [(i, (i + step) % shards) for i in range(sha...  46.1 us
    pallas_call x3, Pallas kernels, weight_grad(): pl.pallas_call(partial(weight_grad_kernel, heights, a_at, b_at, scale, by...  42.3 us
    ppermute x4, waiting for transfers between devices, plane_gather(): right = lax.ppermute(right, 'chip', ahead)  19.9 us
    ppermute x6, waiting for transfers between devices, ring_send(): lax.ppermute(sent[0], 'chip', ahead)  19.2 us
    ppermute x3, waiting for transfers between devices, body(): right = lax.ppermute(right, 'chip', ahead)  17.4 us
    unnamed x180, local copies, waits for them, and re-layouts  16.8 us
    ppermute x11, starting transfers between devices, to_shard(): lax.ppermute(value, 'shard', [(i, (i + step) % shards) for i in range(sha...  16.7 us
  transfers between devices with their start and end apart: 93, of which 50 were waited for; matrix products, arithmetic and copies ran while one was open for 6% of the time, Pallas kernels for 33%

profile of v1, /device:TPU:0, one launch (start us, length us, event | category | flops | bytes accessed | tf_op | source)
XLA Modules:
  0.0 478.2 jit_solution(771218030005978061)
XLA Ops:
  2.3 3.0 collective-permute-start
  7.9 2.0 collective-permute-start.6
  10.7 1.6 collective-permute-start.1
  12.8 3.4 collective-permute-done.1.refs_3_.refs_4_
  17.7 1.6 collective-permute-start.3
  21.3 4.8 %collective-permute-done.6 = bf16[55,256]{1,0:T(8,128)(2,1)S(1)} collective-permute-done((bf16[55,256]{1,0:T(8,128)(2,1)S(1)}, bf16[55,256]{1,0:T(8,128)(2,1)S(1)}, u32[]{:S(2)}, u32[]{:S(2)}) %collective-permute-start.6) | collective-permute-done | bytes 28192 | tf_op jit(solution)/shard_map/ppermute | solution.py:1090
  26.7 1.8 collective-permute-start.7
  28.9 4.1 collective-permute-done.7.refs_7_.refs_4_
  36.1 1.6 collective-permute-start.9
  38.5 3.2 collective-permute-done.9.refs_9_.refs_4_.refs_5_
  43.6 9.7 %collective-permute-done.18.refs_9_.refs_12_.refs_6_ = bf16[512,768]{1,0:T(8,128)(2,1)} collective-permute-done((bf16[512,768]{1,0:T(8,128)(2,1)}, bf16[512,768]{1,0:T(8,128)(2,1)}, u32[]{:S(2)}, u32[]{:S(2)}) %collective-permute-start.18) | collective-permute-done | bytes 786464 | tf_op jit(solution)/shard_map/ppermute | solution.py:1090
  53.3 1.8 collective-permute-start.19
  55.3 1.7 collective-permute-start.21
  61.0 7.9 %shard_map.196 = (bf16[512,1536]{1,0:T(8,128)(2,1)}, bf16[1536,1280]{1,0:T(8,128)(2,1)}, f32[512,1280]{1,0:T(8,128)}, bf16[512,1536]{1,0:T(8,128)(2,1)}) custom-call(s32[12]{0:T(128)} %pad_add_fusion.info, s32[16]{0:T(128)} %add_add_fusion.places, bf16[768,2560]{1,0:T(8,128)(2,1)} %own_ref.1, f32[1,1536]{1,0:T(1,128)} %bitcast.60, bf16[256,1536]{1,0:T(8,128)(2,1)} %refs_0_, ...), custom_call_target="tpu_custom_call" | custom-call | flops 2013265920 | bytes 9699328 | tf_op jit(solution)/shard_map/pallas_call | solution.py:857
  68.9 3.6 collective-permute-done.19.refs_2_.refs_6_
  74.9 1.7 copy-done.29
  76.6 6.7 %shard_map.197 = (bf16[512,1280]{1,0:T(8,128)(2,1)S(1)}, bf16[4,512,1536]{2,1,0:T(8,128)(2,1)S(1)}, bf16[512,768]{1,0:T(8,128)(2,1)S(1)}) custom-call(f32[512,1280]{1,0:T(8,128)S(1)} %copy-done.29, f32[512,1280]{1,0:T(8,128)S(1)} %copy-done.29, f32[512,1280]{1,0:T(8,128)S(1)} %copy-done.29, f32[512,128]{1,0:T(8,128)S(1)} %get-tuple-element.311.cos_ref, ...), custom_call_target="tpu_custom_call" | custom-call | flops 3221225472 | bytes 6291456 | tf_op jit(solution)/shard_map/pallas_call | solution.py:137
  84.4 3.0 convolution_convert_fusion
  87.8 3.2 collective-permute-done.21.refs_5_.refs_8_
  91.0 1.6 collective-permute-done.23.refs_3_.refs_9_
  93.8 1.6 collective-permute-start.24
  95.4 2.0 collective-permute-start.25
  98.3 12.2 %collective-permute-done.24 = bf16[256,1536]{1,0:T(8,128)(2,1)S(1)} collective-permute-done((bf16[256,1536]{1,0:T(8,128)(2,1)S(1)}, bf16[256,1536]{1,0:T(8,128)(2,1)S(1)}, u32[]{:S(2)}, u32[]{:S(2)}) %collective-permute-start.24) | collective-permute-done | bytes 786464 | tf_op jit(solution)/shard_map/ppermute | solution.py:1090
  114.4 1.8 collective-permute-start.31
  117.4 9.9 %shard_map.198 = (bf16[256,2048]{1,0:T(8,128)(2,1)}, bf16[256,1024]{1,0:T(8,128)(2,1)}, bf16[256,1536]{1,0:T(8,128)(2,1)}, f32[8,256]{1,0:T(8,128)}, f32[256,128]{1,0:T(8,128)}) custom-call(s32[12]{0:T(128)} %pad_add_fusion.info, bf16[256,1536]{1,0:T(8,128)(2,1)} %copy-done.5, bf16[256,1536]{1,0:T(8,128)(2,1)} %upstream.1, bf16[64,1280]{1,0:T(8,128)(2,1)} %copy-done.66, ...), custom_call_target="tpu_custom_call" | custom-call | flops 4026531840 | bytes 14155776 | tf_op jit(solution)/shard_map/pallas_call | solution.py:435
  127.3 6.0 %collective-permute-done.31.refs_0_.refs_1_ = bf16[256,1536]{1,0:T(8,128)(2,1)} collective-permute-done((bf16[256,1536]{1,0:T(8,128)(2,1)S(1)}, bf16[256,1536]{1,0:T(8,128)(2,1)}, u32[]{:S(2)}, u32[]{:S(2)}) %collective-permute-start.31) | collective-permute-done | bytes 786464 | tf_op jit(solution)/shard_map/ppermute | solution.py:1124
  133.3 1.6 collective-permute-done.32.refs_1_.refs_2_
  134.9 1.7 collective-permute-start.33
  137.1 15.0 %shard_map.199 = (bf16[512,2048]{1,0:T(8,128)(2,1)}, bf16[512,1024]{1,0:T(8,128)(2,1)}, bf16[256,1536]{1,0:T(8,128)(2,1)}, bf16[256,1536]{1,0:T(8,128)(2,1)}, f3...) custom-call(s32[12]{0:T(128)} %pad_add_fusion.info, ...), custom_call_target="tpu_custom_call" | custom-call | flops 8053063680 | bytes 18874368 | tf_op jit(solution)/shard_map/pallas_call | solution.py:435
  153.3 2.1 collective-permute-done.34.refs_1_.refs_4_
  157.0 1.8 collective-permute-start.36
  158.7 15.0 %shard_map.200 = (bf16[512,2048]{1,0:T(8,128)(2,1)}, bf16[512,1024]{1,0:T(8,128)(2,1)}, bf16[256,1536]{1,0:T(8,128)(2,1)}, bf16[256,1536]{1,0:T(8,128)(2,1)}, f3...) custom-call(s32[12]{0:T(128)} %pad_add_fusion.info, bf16[256,1536]{1,0:T(8,128)(2,1)} %copy-done.79, ...), custom_call_target="tpu_custom_call" | custom-call | flops 8053063680 | bytes 18874368 | tf_op jit(solution)/shard_map/pallas_call | solution.py:435
  181.7 15.0 %shard_map.201 = (bf16[512,2048]{1,0:T(8,128)(2,1)}, bf16[512,1024]{1,0:T(8,128)(2,1)}, bf16[256,1536]{1,0:T(8,128)(2,1)}, bf16[256,1536]{1,0:T(8,128)(2,1)}, f3...) custom-call(s32[12]{0:T(128)} %pad_add_fusion.info, bf16[256,1536]{1,0:T(8,128)(2,1)} %copy-done.67, ...), custom_call_target="tpu_custom_call" | custom-call | flops 8053063680 | bytes 18874368 | tf_op jit(solution)/shard_map/pallas_call | solution.py:435
  197.5 10.3 %shard_map.202 = (bf16[256,2048]{1,0:T(8,128)(2,1)}, bf16[256,1024]{1,0:T(8,128)(2,1)}, bf16[128,1536]{1,0:T(8,128)(2,1)}, bf16[128,1536]{1,0:T(8,128)(2,1)}, f3...) custom-call(s32[12]{0:T(128)} %pad_add_fusion.info, ...), custom_call_target="tpu_custom_call" | custom-call | flops 4026531840 | bytes 14155776 | tf_op jit(solution)/shard_map/pallas_call | solution.py:435
  209.9 13.5 %shard_map.203 = (bf16[768,1024]{1,0:T(8,128)(2,1)}, bf16[768,1024]{1,0:T(8,128)(2,1)}) custom-call(s32[12]{0:T(128)} %pad_add_fusion.info, bf16[256,1536]{1,0:T(8,128)(2,1)} %copy-done.5, bf16[256,1536]{1,0:T(8,128)(2,1)} %collective-permute-done.31.refs_0_.refs_1_, bf16[256,1536]{1,0:T(8,128)(2,1)} %copy-done.78, bf16[256,1536]{1,0:T(8,128)(2,1)} %copy-done.79, ...), custom_call_target="tpu_custom_call" | custom-call | flops 6442450944 | bytes 13631488 | tf_op jit(solution)/shard_map/pallas_call | solution.py:666
  227.3 2.2 collective-permute-done.46.refs_15_
  229.5 14.8 %shard_map.205 = (bf16[768,1024]{1,0:T(8,128)(2,1)}, bf16[768,1024]{1,0:T(8,128)(2,1)}) custom-call(s32[12]{0:T(128)} %pad_add_fusion.info, bf16[256,1536]{1,0:T(8,128)(2,1)} %copy-done.5, bf16[256,1536]{1,0:T(8,128)(2,1)} %collective-permute-done.31.refs_0_.refs_1_, bf16[256,1536]{1,0:T(8,128)(2,1)} %copy-done.78, bf16[256,1536]{1,0:T(8,128)(2,1)} %copy-done.79, ...), custom_call_target="tpu_custom_call" | custom-call | flops 6442450944 | bytes 13631488 | tf_op jit(solution)/shard_map/pallas_call | solution.py:666
  250.8 3.3 all-to-all-start
  254.1 1.6 collective-permute-start.53
  255.7 11.1 %shard_map.207 = (bf16[256,1536]{1,0:T(8,128)(2,1)}, bf16[256,1536]{1,0:T(8,128)(2,1)}, bf16[256,1536]{1,0:T(8,128)(2,1)}, bf16[256,1536]{1,0:T(8,128)(2,1)}, bf...) custom-call(s32[12]{0:T(128)} %pad_add_fusion.info, ...), custom_call_target="tpu_custom_call" | custom-call | flops 6442450944 | bytes 13631488 | tf_op jit(solution)/shard_map/pallas_call | solution.py:504
  274.2 14.1 %shard_map.211 = (bf16[512,768]{1,0:T(8,128)(2,1)}, bf16[512,768]{1,0:T(8,128)(2,1)}, bf16[512,768]{1,0:T(8,128)(2,1)}, bf16[512,768]{1,0:T(8,128)(2,1)}) custom-call(s32[12]{0:T(128)} %pad_add_fusion.info, bf16[256,1024]{1,0:T(8,128)(2,1)} %get-tuple-element.436.refs_0_, bf16[512,1024]{1,0:T(8,128)(2,1)} %get-tuple-element.437.refs_1_, ...), custom_call_target="tpu_custom_call" | custom-call | flops 6442450944 | bytes 13631488 | tf_op jit(solution)/shard_map/pallas_call | solution.py:666
  290.4 5.5 %shard_map.212 = (bf16[256,1536]{1,0:T(8,128)(2,1)}, f32[256,1536]{1,0:T(8,128)}, f32[1,1536]{1,0:T(1,128)}) custom-call(bf16[256,1536]{1,0:T(8,128)(2,1)} %get-tuple-element.330.own, bf16[256,1536]{1,0:T(8,128)(2,1)} %copy-done.60, bf16[256,1536]{1,0:T(8,128)(2,1)} %copy-done.61, f32[256,1536]{1,0:T(8,128)} %copy-done.9, f32[256,1536]{1,0:T(8,128)} %copy-done.43, ...), custom_call_target="tpu_custom_call" | custom-call | tf_op jit(solution)/shard_map/pallas_call | solution.py:932
  304.2 13.8 %collective-permute-done.54.refs_1_ = bf16[256,1536]{1,0:T(8,128)(2,1)S(1)} collective-permute-done((bf16[256,1536]{1,0:T(8,128)(2,1)}, bf16[256,1536]{1,0:T(8,128)(2,1)S(1)}, u32[]{:S(2)}, u32[]{:S(2)}) %collective-permute-start.54) | collective-permute-done | bytes 786464 | tf_op jit(solution)/shard_map/ppermute | solution.py:1090
  323.7 11.5 %shard_map.214 = (bf16[512,1280]{1,0:T(8,128)(2,1)S(1)}, bf16[512,1536]{1,0:T(8,128)(2,1)S(1)}) custom-call(s32[12]{0:T(128)S(1)} %copy-done.27, bf16[512,1280]{1,0:T(8,128)(2,1)S(1)} %copy-done.41, bf16[512,1280]{1,0:T(8,128)(2,1)S(1)} %copy-done.41, bf16[512,1280]{1,0:T(8,128)(2,1)S(1)} %copy-done.41, bf16[4,512,1536]{2,1,0:T(8,128)(2,1)} %copy-done.37, ...), custom_call_target="tpu_custom_call" | custom-call | flops 7650410496 | bytes 6291456 | tf_op jit(solution)/shard_map/pallas_call | solution.py:261
  336.3 2.4 shard_map.216
  341.7 6.4 %shard_map.218 = (bf16[8,48,2816]{2,1,0:T(8,128)(2,1)}, bf16[8,48,2816]{2,1,0:T(8,128)(2,1)}) custom-call(s32[12]{0:T(128)} %pad_add_fusion.info, s32[8]{0:T(128)} %fusion.9.places, bf16[512,1536]{1,0:T(8,128)(2,1)} %get-tuple-element.307.refs_0_, bf16[512,1280]{1,0:T(8,128)(2,1)} %copy-done.36, f32[1,1536]{1,0:T(1,128)} %copy-done.42, ...), custom_call_target="tpu_custom_call" | custom-call | flops 2013265920 | bytes 2883584 | tf_op jit(solution)/shard_map/pallas_call | solution.py:771
  348.2 4.9 %shard_map.219 = (bf16[8,48,1536]{2,1,0:T(8,128)(2,1)}, bf16[8,48,1536]{2,1,0:T(8,128)(2,1)}) custom-call(s32[12]{0:T(128)} %pad_add_fusion.info, s32[8]{0:T(128)} %fusion.9.places, bf16[512,768]{1,0:T(8,128)(2,1)} %copy-done.39, bf16[512,1536]{1,0:T(8,128)(2,1)} %copy-done.38), custom_call_target="tpu_custom_call" | custom-call | flops 1207959552 | bytes 2359296 | tf_op jit(solution)/shard_map/pallas_call | solution.py:771
  355.7 17.7 %collective-permute-done.63 = bf16[256,1536]{1,0:T(8,128)(2,1)S(1)} collective-permute-done((bf16[256,1536]{1,0:T(8,128)(2,1)}, bf16[256,1536]{1,0:T(8,128)(2,1)S(1)}, u32[]{:S(2)}, u32[]{:S(2)}) %collective-permute-start.63) | collective-permute-done | bytes 786464 | tf_op jit(solution)/shard_map/ppermute | solution.py:1140
  375.3 1.7 copy-done.1
  380.2 3.9 collective-permute-done.66.refs_4_
  391.2 4.7 collective-permute-done.68.refs_4_
  400.5 6.3 %collective-permute-done.70.refs_4_ = bf16[48,4352]{1,0:T(8,128)(2,1)S(1)} collective-permute-done((bf16[48,4352]{1,0:T(8,128)(2,1)S(1)}, bf16[48,4352]{1,0:T(8,128)(2,1)S(1)}, u32[]{:S(2)}, u32[]{:S(2)}) %collective-permute-start.70) | collective-permute-done | bytes 417824 | tf_op jit(solution)/shard_map/ppermute | solution.py:1405
  407.2 2.4 shard_map.223
  411.8 6.3 %collective-permute-done.73.refs_4_ = bf16[48,4352]{1,0:T(8,128)(2,1)} collective-permute-done((bf16[48,4352]{1,0:T(8,128)(2,1)}, bf16[48,4352]{1,0:T(8,128)(2,1)}, u32[]{:S(2)}, u32[]{:S(2)}) %collective-permute-start.73) | collective-permute-done | bytes 417824 | tf_op jit(solution)/shard_map/ppermute | solution.py:1405
  419.9 2.6 shard_map.224
  425.4 2.2 collective-permute-done.75
  430.5 9.4 %collective-permute-done.76.refs_1_ = bf16[48,4224]{1,0:T(8,128)(2,1)S(1)} collective-permute-done((bf16[48,4224]{1,0:T(8,128)(2,1)S(1)}, bf16[48,4224]{1,0:T(8,128)(2,1)S(1)}, u32[]{:S(2)}, u32[]{:S(2)}) %collective-permute-start.76) | collective-permute-done | bytes 405536 | tf_op jit(solution)/shard_map/ppermute | solution.py:1156
  442.5 1.7 fusion.3
  444.1 7.6 %collective-permute-done.78.refs_3_ = bf16[48,4224]{1,0:T(8,128)(2,1)S(1)} collective-permute-done((bf16[48,4224]{1,0:T(8,128)(2,1)S(1)}, bf16[48,4224]{1,0:T(8,128)(2,1)S(1)}, u32[]{:S(2)}, u32[]{:S(2)}) %collective-permute-start.78) | collective-permute-done | bytes 405536 | tf_op jit(solution)/shard_map/ppermute | solution.py:1156
  455.4 3.7 convert_add_fusion
  459.1 1.7 collective-permute-done.80.refs_0_
  466.2 4.0 shard_map.225
  471.5 1.7 collective-permute-done.91.refs_5_
  473.2 2.9 shard_map.226
  (392 shorter events, 125.6 us)
Async XLA Ops:
  2.3 8.3 %collective-permute-start = (bf16[48,1280]{1,0:T(8,128)(2,1)S(1)}, bf16[48,1280]{1,0:T(8,128)(2,1)S(1)}, u32[]{:S(2)}, u32[]{:S(2)}) collective-permute-start(bf16[48,1280]{1,0:T(8,128)(2,1)S(1)} %pad_maximum_fusion.2), channel_id=1, source_target_pairs={{0,1},{1,0},{2,3},{3,2},{4,5},{5,4},{6,7},{7,6},{8,9},{9,8},{10,11... | collective-permute-start | bytes 368648 | tf_op jit(solution)/shard_map/ppermute | solution.py:1090
  5.4 21.3 %collective-permute-start.5 = (bf16[256,1536]{1,0:T(8,128)(2,1)}, bf16[256,1536]{1,0:T(8,128)(2,1)S(1)}, u32[]{:S(2)}, u32[]{:S(2)}) collective-permute-start(bf16[256,1536]{1,0:T(8,128)(2,1)} %refs_0_), channel_id=1, source_target_pairs={{0,1},{1,0},{2,3},{3,2},{4,5},{5,4},{6,7},{7,6},{8,9},{9,8},{10,11... | collective-permute-start | bytes 2359304 | tf_op jit(solution)/shard_map/ppermute | solution.py:1090
  7.9 18.2 %collective-permute-start.6 = (bf16[55,256]{1,0:T(8,128)(2,1)S(1)}, bf16[55,256]{1,0:T(8,128)(2,1)S(1)}, u32[]{:S(2)}, u32[]{:S(2)}) collective-permute-start(bf16[55,256]{1,0:T(8,128)(2,1)S(1)} %reshape.116), channel_id=1, source_target_pairs={{0,1},{1,0},{2,3},{3,2},{4,5},{5,4},{6,7},{7,6},{8,9},{9,8},{10,11... | collective-permute-start | bytes 84488 | tf_op jit(solution)/shard_map/ppermute | solution.py:1090
  17.7 8.4 %collective-permute-start.3 = (bf16[64,1280]{1,0:T(8,128)(2,1)}, bf16[64,1280]{1,0:T(8,128)(2,1)S(1)}, u32[]{:S(2)}, u32[]{:S(2)}) collective-permute-start(bf16[64,1280]{1,0:T(8,128)(2,1)} %collective-permute-done.1.refs_3_.refs_4_), channel_id=1, source_target_pairs={{0,8},{8,16},{16,24},{24,28},{28,20},{20,12},{12,4},{4,0},{1,9},{9... | collective-permute-start | bytes 491528 | tf_op jit(solution)/shard_map/ppermute | solution.py:1174
  21.3 14.8 %collective-permute-start.10 = (bf16[64,1280]{1,0:T(8,128)(2,1)S(1)}, bf16[64,1280]{1,0:T(8,128)(2,1)S(1)}, u32[]{:S(2)}, u32[]{:S(2)}) collective-permute-start(bf16[64,1280]{1,0:T(8,128)(2,1)S(1)} %fusion.5.refs_2_), channel_id=1, source_target_pairs={{0,2},{2,0},{1,3},{3,1},{4,6},{6,4},{5,7},{7,5},{8,10},{10,8},{9,1... | collective-permute-start | bytes 491528 | tf_op jit(solution)/shard_map/ppermute | solution.py:1093
  26.1 11.6 %collective-permute-start.11 = (bf16[64,1280]{1,0:T(8,128)(2,1)}, bf16[64,1280]{1,0:T(8,128)(2,1)S(1)}, u32[]{:S(2)}, u32[]{:S(2)}) collective-permute-start(bf16[64,1280]{1,0:T(8,128)(2,1)} %collective-permute-done.1.refs_3_.refs_4_), channel_id=1, source_target_pairs={{0,2},{2,0},{1,3},{3,1},{4,6},{6,4},{5,7},{7,5},{8,10},{10,8},{9,1... | collective-permute-start | bytes 491528 | tf_op jit(solution)/shard_map/ppermute | solution.py:1093
  26.2 11.7 %collective-permute-start.12 = (bf16[64,1280]{1,0:T(8,128)(2,1)}, bf16[64,1280]{1,0:T(8,128)(2,1)S(1)}, u32[]{:S(2)}, u32[]{:S(2)}) collective-permute-start(bf16[64,1280]{1,0:T(8,128)(2,1)} %collective-permute-done.2.refs_4_.refs_5_), channel_id=1, source_target_pairs={{0,2},{2,0},{1,3},{3,1},{4,6},{6,4},{5,7},{7,5},{8,10},{10,8},{9,1... | collective-permute-start | bytes 491528 | tf_op jit(solution)/shard_map/ppermute | solution.py:1093
  34.5 18.8 %collective-permute-start.18 = (bf16[512,768]{1,0:T(8,128)(2,1)}, bf16[512,768]{1,0:T(8,128)(2,1)}, u32[]{:S(2)}, u32[]{:S(2)}) collective-permute-start(bf16[512,768]{1,0:T(8,128)(2,1)} %bitcast.7.refs_8_.refs_11_.refs_5_), channel_id=1, source_target_pairs={{0,1},{1,0},{2,3},{3,2},{4,5},{5,4},{6,7},{7,6},{8,9},{9,8},{10,11... | collective-permute-start | bytes 2359304 | tf_op jit(solution)/shard_map/ppermute | solution.py:1090
  53.3 19.2 %collective-permute-start.19 = (bf16[256,1536]{1,0:T(8,128)(2,1)S(1)}, bf16[256,1536]{1,0:T(8,128)(2,1)}, u32[]{:S(2)}, u32[]{:S(2)}) collective-permute-start(bf16[256,1536]{1,0:T(8,128)(2,1)S(1)} %copy-done.53), channel_id=1, source_target_pairs={{0,8},{8,16},{16,24},{24,28},{28,20},{20,12},{12,4},{4,0},{1,9},{9... | collective-permute-start | bytes 2359304 | tf_op jit(solution)/shard_map/ppermute | solution.py:1124
  55.1 17.6 %collective-permute-start.20 = (bf16[256,1536]{1,0:T(8,128)(2,1)S(1)}, bf16[256,1536]{1,0:T(8,128)(2,1)}, u32[]{:S(2)}, u32[]{:S(2)}) collective-permute-start(bf16[256,1536]{1,0:T(8,128)(2,1)S(1)} %copy-done.53), channel_id=1, source_target_pairs={{8,0},{16,8},{24,16},{28,24},{20,28},{12,20},{4,12},{0,4},{9,1},{1... | collective-permute-start | bytes 2359304 | tf_op jit(solution)/shard_map/ppermute | solution.py:1124
  55.3 35.7 %collective-permute-start.21 = (bf16[768,1024]{1,0:T(8,128)(2,1)}, bf16[768,1024]{1,0:T(8,128)(2,1)}, u32[]{:S(2)}, u32[]{:S(2)}) collective-permute-start(bf16[768,1024]{1,0:T(8,128)(2,1)} %bitcast.66), channel_id=1, source_target_pairs={{0,1},{1,0},{2,3},{3,2},{4,5},{5,4},{6,7},{7,6},{8,9},{9,8},{10,11... | collective-permute-start | bytes 4718600 | tf_op jit(solution)/shard_map/ppermute | solution.py:1090
  72.7 18.4 %collective-permute-start.22 = (bf16[256,1536]{1,0:T(8,128)(2,1)}, bf16[256,1536]{1,0:T(8,128)(2,1)}, u32[]{:S(2)}, u32[]{:S(2)}) collective-permute-start(bf16[256,1536]{1,0:T(8,128)(2,1)} %collective-permute-done.19.refs_2_.refs_6_), channel_id=1, source_target_pairs={{0,8},{8,16},{16,24},{24,28},{28,20},{20,12},{12,4},{4,0},{1,9},{9... | collective-permute-start | bytes 2359304 | tf_op jit(solution)/shard_map/ppermute | solution.py:1124
  74.2 18.4 %collective-permute-start.23 = (bf16[256,1536]{1,0:T(8,128)(2,1)}, bf16[256,1536]{1,0:T(8,128)(2,1)}, u32[]{:S(2)}, u32[]{:S(2)}) collective-permute-start(bf16[256,1536]{1,0:T(8,128)(2,1)} %collective-permute-done.20.refs_3_.refs_7_), channel_id=1, source_target_pairs={{8,0},{16,8},{24,16},{28,24},{20,28},{12,20},{4,12},{0,4},{9,1},{1... | collective-permute-start | bytes 2359304 | tf_op jit(solution)/shard_map/ppermute | solution.py:1124
  93.8 16.7 %collective-permute-start.24 = (bf16[256,1536]{1,0:T(8,128)(2,1)S(1)}, bf16[256,1536]{1,0:T(8,128)(2,1)S(1)}, u32[]{:S(2)}, u32[]{:S(2)}) collective-permute-start(bf16[256,1536]{1,0:T(8,128)(2,1)S(1)} %constant_dynamic-slice_fusion.2), channel_id=1, source_target_pairs={{0,1},{1,0},{2,3},{3,2},{4,5},{5,4},{6,7},{7,6},{8,9},{9,8},{10,11... | collective-permute-start | bytes 2359304 | tf_op jit(solution)/shard_map/ppermute | solution.py:1090
  95.4 16.7 %collective-permute-start.25 = (bf16[256,1536]{1,0:T(8,128)(2,1)}, bf16[256,1536]{1,0:T(8,128)(2,1)}, u32[]{:S(2)}, u32[]{:S(2)}) collective-permute-start(bf16[256,1536]{1,0:T(8,128)(2,1)} %collective-permute-done.22.refs_2_.refs_8_), channel_id=1, source_target_pairs={{0,8},{8,16},{16,24},{24,28},{28,20},{20,12},{12,4},{4,0},{1,9},{9... | collective-permute-start | bytes 2359304 | tf_op jit(solution)/shard_map/ppermute | solution.py:1124
  97.4 16.5 %collective-permute-start.26 = (bf16[256,1536]{1,0:T(8,128)(2,1)}, bf16[256,1536]{1,0:T(8,128)(2,1)}, u32[]{:S(2)}, u32[]{:S(2)}) collective-permute-start(bf16[256,1536]{1,0:T(8,128)(2,1)} %collective-permute-done.23.refs_3_.refs_9_), channel_id=1, source_target_pairs={{8,0},{16,8},{24,16},{28,24},{20,28},{12,20},{4,12},{0,4},{9,1},{1... | collective-permute-start | bytes 2359304 | tf_op jit(solution)/shard_map/ppermute | solution.py:1124
  97.6 18.5 %collective-permute-start.29 = (bf16[512,768]{1,0:T(8,128)(2,1)}, bf16[512,768]{1,0:T(8,128)(2,1)}, u32[]{:S(2)}, u32[]{:S(2)}) collective-permute-start(bf16[512,768]{1,0:T(8,128)(2,1)} %bitcast.7.refs_8_.refs_11_.refs_5_), channel_id=1, source_target_pairs={{0,2},{2,0},{1,3},{3,1},{4,6},{6,4},{5,7},{7,5},{8,10},{10,8},{9,1... | collective-permute-start | bytes 2359304 | tf_op jit(solution)/shard_map/ppermute | solution.py:1093
  97.7 18.7 %collective-permute-start.27 = (bf16[768,1024]{1,0:T(8,128)(2,1)}, bf16[768,1024]{1,0:T(8,128)(2,1)}, u32[]{:S(2)}, u32[]{:S(2)}) collective-permute-start(bf16[768,1024]{1,0:T(8,128)(2,1)} %bitcast.67), channel_id=1, source_target_pairs={{0,2},{2,0},{1,3},{3,1},{4,6},{6,4},{5,7},{7,5},{8,10},{10,8},{9,1... | collective-permute-start | bytes 4718600 | tf_op jit(solution)/shard_map/ppermute | solution.py:1093
  114.4 18.9 %collective-permute-start.31 = (bf16[256,1536]{1,0:T(8,128)(2,1)S(1)}, bf16[256,1536]{1,0:T(8,128)(2,1)}, u32[]{:S(2)}, u32[]{:S(2)}) collective-permute-start(bf16[256,1536]{1,0:T(8,128)(2,1)S(1)} %multiply_convert_fusion.refs_0_.second_ref), channel_id=1, source_target_pairs={{0,8},{8,16},{16,24},{24,28},{28,20},{20,12},{12,4},{4,0},{1,9},{9... | collective-permute-start | bytes 2359304 | tf_op jit(solution)/shard_map/ppermute | solution.py:1124
  116.2 18.7 %collective-permute-start.32 = (bf16[256,1536]{1,0:T(8,128)(2,1)S(1)}, bf16[256,1536]{1,0:T(8,128)(2,1)S(1)}, u32[]{:S(2)}, u32[]{:S(2)}) collective-permute-start(bf16[256,1536]{1,0:T(8,128)(2,1)S(1)} %multiply_convert_fusion.refs_0_.second_ref), channel_id=1, source_target_pairs={{8,0},{16,8},{24,16},{28,24},{20,28},{12,20},{4,12},{0,4},{9,1},{1... | collective-permute-start | bytes 2359304 | tf_op jit(solution)/shard_map/ppermute | solution.py:1124
  134.9 18.4 %collective-permute-start.33 = (bf16[256,1536]{1,0:T(8,128)(2,1)}, bf16[256,1536]{1,0:T(8,128)(2,1)S(1)}, u32[]{:S(2)}, u32[]{:S(2)}) collective-permute-start(bf16[256,1536]{1,0:T(8,128)(2,1)} %collective-permute-done.31.refs_0_.refs_1_), channel_id=1, source_target_pairs={{0,8},{8,16},{16,24},{24,28},{28,20},{20,12},{12,4},{4,0},{1,9},{9... | collective-permute-start | bytes 2359304 | tf_op jit(solution)/shard_map/ppermute | solution.py:1124
  136.6 18.8 %collective-permute-start.34 = (bf16[256,1536]{1,0:T(8,128)(2,1)S(1)}, bf16[256,1536]{1,0:T(8,128)(2,1)S(1)}, u32[]{:S(2)}, u32[]{:S(2)}) collective-permute-start(bf16[256,1536]{1,0:T(8,128)(2,1)S(1)} %collective-permute-done.32.refs_1_.refs_2_), channel_id=1, source_target_pairs={{8,0},{16,8},{24,16},{28,24},{20,28},{12,20},{4,12},{0,4},{9,1},{1... | collective-permute-start | bytes 2359304 | tf_op jit(solution)/shard_map/ppermute | solution.py:1124
  156.3 17.7 %collective-permute-start.35 = (bf16[256,1536]{1,0:T(8,128)(2,1)S(1)}, bf16[256,1536]{1,0:T(8,128)(2,1)S(1)}, u32[]{:S(2)}, u32[]{:S(2)}) collective-permute-start(bf16[256,1536]{1,0:T(8,128)(2,1)S(1)} %collective-permute-done.33.refs_0_.refs_3_), channel_id=1, source_target_pairs={{0,8},{8,16},{16,24},{24,28},{28,20},{20,12},{12,4},{4,0},{1,9},{9... | collective-permute-start | bytes 2359304 | tf_op jit(solution)/shard_map/ppermute | solution.py:1124
  157.0 18.1 %collective-permute-start.36 = (bf16[256,1536]{1,0:T(8,128)(2,1)}, bf16[256,1536]{1,0:T(8,128)(2,1)S(1)}, u32[]{:S(2)}, u32[]{:S(2)}) collective-permute-start(bf16[256,1536]{1,0:T(8,128)(2,1)} %copy-done.80), channel_id=1, source_target_pairs={{8,0},{16,8},{24,16},{28,24},{20,28},{12,20},{4,12},{0,4},{9,1},{1... | collective-permute-start | bytes 2359304 | tf_op jit(solution)/shard_map/ppermute | solution.py:1124
  175.1 21.6 %collective-permute-start.37 = (bf16[128,1536]{1,0:T(8,128)(2,1)S(1)}, bf16[128,1536]{1,0:T(8,128)(2,1)}, u32[]{:S(2)}, u32[]{:S(2)}) collective-permute-start(bf16[128,1536]{1,0:T(8,128)(2,1)S(1)} %slice.92), channel_id=1, source_target_pairs={{0,8},{8,16},{16,24},{24,28},{28,20},{20,12},{12,4},{4,0},{1,9},{9... | collective-permute-start | bytes 1179656 | tf_op jit(solution)/shard_map/ppermute | solution.py:1124
  176.3 20.4 %collective-permute-start.38 = (bf16[128,1536]{1,0:T(8,128)(2,1)S(1)}, bf16[128,1536]{1,0:T(8,128)(2,1)}, u32[]{:S(2)}, u32[]{:S(2)}) collective-permute-start(bf16[128,1536]{1,0:T(8,128)(2,1)S(1)} %slice.93), channel_id=1, source_target_pairs={{8,0},{16,8},{24,16},{28,24},{20,28},{12,20},{4,12},{0,4},{9,1},{1... | collective-permute-start | bytes 1179656 | tf_op jit(solution)/shard_map/ppermute | solution.py:1124
  178.3 18.4 %collective-permute-start.39 = (bf16[128,1536]{1,0:T(8,128)(2,1)S(1)}, bf16[128,1536]{1,0:T(8,128)(2,1)S(1)}, u32[]{:S(2)}, u32[]{:S(2)}) collective-permute-start(bf16[128,1536]{1,0:T(8,128)(2,1)S(1)} %slice.94), channel_id=1, source_target_pairs={{0,8},{8,16},{16,24},{24,28},{28,20},{20,12},{12,4},{4,0},{1,9},{9... | collective-permute-start | bytes 1179656 | tf_op jit(solution)/shard_map/ppermute | solution.py:1124
  180.5 16.2 %collective-permute-start.40 = (bf16[128,1536]{1,0:T(8,128)(2,1)S(1)}, bf16[128,1536]{1,0:T(8,128)(2,1)}, u32[]{:S(2)}, u32[]{:S(2)}) collective-permute-start(bf16[128,1536]{1,0:T(8,128)(2,1)S(1)} %slice.95), channel_id=1, source_target_pairs={{8,0},{16,8},{24,16},{28,24},{20,28},{12,20},{4,12},{0,4},{9,1},{1... | collective-permute-start | bytes 1179656 | tf_op jit(solution)/shard_map/ppermute | solution.py:1124
  207.9 15.5 %collective-permute-start.41 = (bf16[128,1536]{1,0:T(8,128)(2,1)}, bf16[128,1536]{1,0:T(8,128)(2,1)S(1)}, u32[]{:S(2)}, u32[]{:S(2)}) collective-permute-start(bf16[128,1536]{1,0:T(8,128)(2,1)} %get-tuple-element.353), channel_id=1, source_target_pairs={{0,8},{8,16},{16,24},{24,28},{28,20},{20,12},{12,4},{4,0},{1,9},{9... | collective-permute-start | bytes 1179656 | tf_op jit(solution)/shard_map/ppermute | solution.py:1134
  209.0 14.4 %collective-permute-start.42 = (bf16[128,1536]{1,0:T(8,128)(2,1)}, bf16[128,1536]{1,0:T(8,128)(2,1)S(1)}, u32[]{:S(2)}, u32[]{:S(2)}) collective-permute-start(bf16[128,1536]{1,0:T(8,128)(2,1)} %get-tuple-element.354), channel_id=1, source_target_pairs={{8,0},{16,8},{24,16},{28,24},{20,28},{12,20},{4,12},{0,4},{9,1},{1... | collective-permute-start | bytes 1179656 | tf_op jit(solution)/shard_map/ppermute | solution.py:1134
  225.3 19.7 %collective-permute-start.43 = (bf16[256,1536]{1,0:T(8,128)(2,1)}, bf16[256,1536]{1,0:T(8,128)(2,1)S(1)}, u32[]{:S(2)}, u32[]{:S(2)}) collective-permute-start(bf16[256,1536]{1,0:T(8,128)(2,1)} %get-tuple-element.371), channel_id=1, source_target_pairs={{0,8},{8,16},{16,24},{24,28},{28,20},{20,12},{12,4},{4,0},{1,9},{9... | collective-permute-start | bytes 2359304 | tf_op jit(solution)/shard_map/ppermute | solution.py:1140
  226.4 19.5 %collective-permute-start.44 = (bf16[256,1536]{1,0:T(8,128)(2,1)}, bf16[256,1536]{1,0:T(8,128)(2,1)S(1)}, u32[]{:S(2)}, u32[]{:S(2)}) collective-permute-start(bf16[256,1536]{1,0:T(8,128)(2,1)} %get-tuple-element.372), channel_id=1, source_target_pairs={{8,0},{16,8},{24,16},{28,24},{20,28},{12,20},{4,12},{0,4},{9,1},{1... | collective-permute-start | bytes 2359304 | tf_op jit(solution)/shard_map/ppermute | solution.py:1140
  247.3 19.9 %collective-permute-start.47 = (bf16[256,1536]{1,0:T(8,128)(2,1)}, bf16[256,1536]{1,0:T(8,128)(2,1)S(1)}, u32[]{:S(2)}, u32[]{:S(2)}) collective-permute-start(bf16[256,1536]{1,0:T(8,128)(2,1)} %get-tuple-element.386), channel_id=1, source_target_pairs={{0,8},{8,16},{16,24},{24,28},{28,20},{20,12},{12,4},{4,0},{1,9},{9... | collective-permute-start | bytes 2359304 | tf_op jit(solution)/shard_map/ppermute | solution.py:1140
  248.3 18.9 %collective-permute-start.48 = (bf16[256,1536]{1,0:T(8,128)(2,1)}, bf16[256,1536]{1,0:T(8,128)(2,1)S(1)}, u32[]{:S(2)}, u32[]{:S(2)}) collective-permute-start(bf16[256,1536]{1,0:T(8,128)(2,1)} %get-tuple-element.387), channel_id=1, source_target_pairs={{8,0},{16,8},{24,16},{28,24},{20,28},{12,20},{4,12},{0,4},{9,1},{1... | collective-permute-start | bytes 2359304 | tf_op jit(solution)/shard_map/ppermute | solution.py:1140
  250.8 16.4 %all-to-all-start = ((f32[8,2,256]{2,1,0:T(2,128)}), f32[8,2,256]{2,1,0:T(2,128)S(1)}, u32[]{:S(2)}, u32[]{:S(2)}) async-start(f32[8,2,256]{2,1,0:T(2,128)} %shard_map.208), calls=%async_computation | async-start | bytes 32768 | tf_op jit(solution)/shard_map/all_to_all | solution.py:1331
  254.1 43.7 %collective-permute-start.53 = (bf16[768,1024]{1,0:T(8,128)(2,1)}, bf16[768,1024]{1,0:T(8,128)(2,1)}, u32[]{:S(2)}, u32[]{:S(2)}) collective-permute-start(bf16[768,1024]{1,0:T(8,128)(2,1)} %get-tuple-element.461), channel_id=1, source_target_pairs={{0,1},{1,0},{2,3},{3,2},{4,5},{5,4},{6,7},{7,6},{8,9},{9,8},{10,11... | collective-permute-start | bytes 4718600 | tf_op jit(solution)/shard_map/ppermute | solution.py:1090
  268.8 19.5 %collective-permute-start.49 = (bf16[256,1536]{1,0:T(8,128)(2,1)}, bf16[256,1536]{1,0:T(8,128)(2,1)S(1)}, u32[]{:S(2)}, u32[]{:S(2)}) collective-permute-start(bf16[256,1536]{1,0:T(8,128)(2,1)} %get-tuple-element.429), channel_id=1, source_target_pairs={{0,8},{8,16},{16,24},{24,28},{28,20},{20,12},{12,4},{4,0},{1,9},{9... | collective-permute-start | bytes 2359304 | tf_op jit(solution)/shard_map/ppermute | solution.py:1140
  270.3 18.0 %collective-permute-start.50 = (bf16[256,1536]{1,0:T(8,128)(2,1)}, bf16[256,1536]{1,0:T(8,128)(2,1)S(1)}, u32[]{:S(2)}, u32[]{:S(2)}) collective-permute-start(bf16[256,1536]{1,0:T(8,128)(2,1)} %get-tuple-element.430), channel_id=1, source_target_pairs={{8,0},{16,8},{24,16},{28,24},{20,28},{12,20},{4,12},{0,4},{9,1},{1... | collective-permute-start | bytes 2359304 | tf_op jit(solution)/shard_map/ppermute | solution.py:1140
  288.3 8.5 %collective-permute-start.51 = (bf16[128,1536]{1,0:T(8,128)(2,1)}, bf16[128,1536]{1,0:T(8,128)(2,1)S(1)}, u32[]{:S(2)}, u32[]{:S(2)}) collective-permute-start(bf16[128,1536]{1,0:T(8,128)(2,1)} %get-tuple-element.457), channel_id=1, source_target_pairs={{0,8},{8,16},{16,24},{24,28},{28,20},{20,12},{12,4},{4,0},{1,9},{9... | collective-permute-start | bytes 1179656 | tf_op jit(solution)/shard_map/ppermute | solution.py:1134
  289.9 8.0 %collective-permute-start.52 = (bf16[128,1536]{1,0:T(8,128)(2,1)S(1)}, bf16[128,1536]{1,0:T(8,128)(2,1)S(1)}, u32[]{:S(2)}, u32[]{:S(2)}) collective-permute-start(bf16[128,1536]{1,0:T(8,128)(2,1)S(1)} %copy-done.82), channel_id=1, source_target_pairs={{8,0},{16,8},{24,16},{28,24},{20,28},{12,20},{4,12},{0,4},{9,1},{1... | collective-permute-start | bytes 1179656 | tf_op jit(solution)/shard_map/ppermute | solution.py:1134
  298.4 19.7 %collective-permute-start.54 = (bf16[256,1536]{1,0:T(8,128)(2,1)}, bf16[256,1536]{1,0:T(8,128)(2,1)S(1)}, u32[]{:S(2)}, u32[]{:S(2)}) collective-permute-start(bf16[256,1536]{1,0:T(8,128)(2,1)} %get-tuple-element.473.refs_0_), channel_id=1, source_target_pairs={{0,1},{1,0},{2,3},{3,2},{4,5},{5,4},{6,7},{7,6},{8,9},{9,8},{10,11... | collective-permute-start | bytes 2359304 | tf_op jit(solution)/shard_map/ppermute | solution.py:1090
  299.6 19.2 %collective-permute-start.55 = (bf16[256,1536]{1,0:T(8,128)(2,1)S(1)}, bf16[256,1536]{1,0:T(8,128)(2,1)S(1)}, u32[]{:S(2)}, u32[]{:S(2)}) collective-permute-start(bf16[256,1536]{1,0:T(8,128)(2,1)S(1)} %get-tuple-element.465), channel_id=1, source_target_pairs={{0,8},{8,16},{16,24},{24,28},{28,20},{20,12},{12,4},{4,0},{1,9},{9... | collective-permute-start | bytes 2359304 | tf_op jit(solution)/shard_map/ppermute | solution.py:1140
  301.0 18.9 %collective-permute-start.56 = (bf16[256,1536]{1,0:T(8,128)(2,1)S(1)}, bf16[256,1536]{1,0:T(8,128)(2,1)S(1)}, u32[]{:S(2)}, u32[]{:S(2)}) collective-permute-start(bf16[256,1536]{1,0:T(8,128)(2,1)S(1)} %get-tuple-element.466), channel_id=1, source_target_pairs={{8,0},{16,8},{24,16},{28,24},{20,28},{12,20},{4,12},{0,4},{9,1},{1... | collective-permute-start | bytes 2359304 | tf_op jit(solution)/shard_map/ppermute | solution.py:1140
  320.3 18.6 %collective-permute-start.59 = (bf16[256,1536]{1,0:T(8,128)(2,1)S(1)}, bf16[256,1536]{1,0:T(8,128)(2,1)S(1)}, u32[]{:S(2)}, u32[]{:S(2)}) collective-permute-start(bf16[256,1536]{1,0:T(8,128)(2,1)S(1)} %get-tuple-element.478), channel_id=1, source_target_pairs={{0,8},{8,16},{16,24},{24,28},{28,20},{20,12},{12,4},{4,0},{1,9},{9... | collective-permute-start | bytes 2359304 | tf_op jit(solution)/shard_map/ppermute | solution.py:1140
  321.8 17.8 %collective-permute-start.60 = (bf16[256,1536]{1,0:T(8,128)(2,1)S(1)}, bf16[256,1536]{1,0:T(8,128)(2,1)S(1)}, u32[]{:S(2)}, u32[]{:S(2)}) collective-permute-start(bf16[256,1536]{1,0:T(8,128)(2,1)S(1)} %get-tuple-element.479), channel_id=1, source_target_pairs={{8,0},{16,8},{24,16},{28,24},{20,28},{12,20},{4,12},{0,4},{9,1},{1... | collective-permute-start | bytes 2359304 | tf_op jit(solution)/shard_map/ppermute | solution.py:1140
  322.5 17.4 %collective-permute-start.61 = (bf16[512,768]{1,0:T(8,128)(2,1)S(1)}, bf16[512,768]{1,0:T(8,128)(2,1)S(1)}, u32[]{:S(2)}, u32[]{:S(2)}) collective-permute-start(bf16[512,768]{1,0:T(8,128)(2,1)S(1)} %add_convert_fusion.1), channel_id=1, source_target_pairs={{0,1},{1,0},{2,3},{3,2},{4,5},{5,4},{6,7},{7,6},{8,9},{9,8},{10,11... | collective-permute-start | bytes 2359304 | tf_op jit(solution)/shard_map/ppermute | solution.py:1090
  348.1 27.2 %collective-permute-start.62 = (bf16[8,48,2816]{2,1,0:T(8,128)(2,1)}, bf16[8,48,2816]{2,1,0:T(8,128)(2,1)}, u32[]{:S(2)}, u32[]{:S(2)}) collective-permute-start(bf16[8,48,2816]{2,1,0:T(8,128)(2,1)} %get-tuple-element.494), channel_id=1, source_target_pairs={{0,2},{2,0},{1,3},{3,1},{4,6},{6,4},{5,7},{7,5},{8,10},{10,8},{9,1... | collective-permute-start | bytes 6488072 | tf_op jit(solution)/shard_map/ppermute | solution.py:1093
  353.1 21.3 %collective-permute-start.65 = (bf16[8,48,1536]{2,1,0:T(8,128)(2,1)}, bf16[8,48,1536]{2,1,0:T(8,128)(2,1)S(1)}, u32[]{:S(2)}, u32[]{:S(2)}) collective-permute-start(bf16[8,48,1536]{2,1,0:T(8,128)(2,1)} %get-tuple-element.501), channel_id=1, source_target_pairs={{0,2},{2,0},{1,3},{3,1},{4,6},{6,4},{5,7},{7,5},{8,10},{10,8},{9,1... | collective-permute-start | bytes 3538952 | tf_op jit(solution)/shard_map/ppermute | solution.py:1093
  353.7 19.7 %collective-permute-start.63 = (bf16[256,1536]{1,0:T(8,128)(2,1)}, bf16[256,1536]{1,0:T(8,128)(2,1)S(1)}, u32[]{:S(2)}, u32[]{:S(2)}) collective-permute-start(bf16[256,1536]{1,0:T(8,128)(2,1)} %copy-done.35), channel_id=1, source_target_pairs={{0,8},{8,16},{16,24},{24,28},{28,20},{20,12},{12,4},{4,0},{1,9},{9... | collective-permute-start | bytes 2359304 | tf_op jit(solution)/shard_map/ppermute | solution.py:1140
  355.2 19.2 %collective-permute-start.64 = (bf16[256,1536]{1,0:T(8,128)(2,1)S(1)}, bf16[256,1536]{1,0:T(8,128)(2,1)S(1)}, u32[]{:S(2)}, u32[]{:S(2)}) collective-permute-start(bf16[256,1536]{1,0:T(8,128)(2,1)S(1)} %get-tuple-element.499), channel_id=1, source_target_pairs={{8,0},{16,8},{24,16},{28,24},{20,28},{12,20},{4,12},{0,4},{9,1},{1... | collective-permute-start | bytes 2359304 | tf_op jit(solution)/shard_map/ppermute | solution.py:1140
  386.5 9.4 %collective-permute-start.68 = (bf16[48,4352]{1,0:T(8,128)(2,1)S(1)}, bf16[48,4352]{1,0:T(8,128)(2,1)S(1)}, u32[]{:S(2)}, u32[]{:S(2)}) collective-permute-start(bf16[48,4352]{1,0:T(8,128)(2,1)S(1)} %get-tuple-element.506), channel_id=1, source_target_pairs={{0,8},{8,16},{16,24},{24,28},{28,20},{20,12},{12,4},{4,0},{1,9},{9... | collective-permute-start | bytes 1253384 | tf_op jit(solution)/shard_map/ppermute | solution.py:1405
  387.5 9.5 %collective-permute-start.69 = (bf16[48,4352]{1,0:T(8,128)(2,1)S(1)}, bf16[48,4352]{1,0:T(8,128)(2,1)S(1)}, u32[]{:S(2)}, u32[]{:S(2)}) collective-permute-start(bf16[48,4352]{1,0:T(8,128)(2,1)S(1)} %get-tuple-element.507), channel_id=1, source_target_pairs={{8,0},{16,8},{24,16},{28,24},{20,28},{12,20},{4,12},{0,4},{9,1},{1... | collective-permute-start | bytes 1253384 | tf_op jit(solution)/shard_map/ppermute | solution.py:1406
  389.8 17.4 %collective-permute-start.72 = (bf16[256,1536]{1,0:T(8,128)(2,1)S(1)}, bf16[256,1536]{1,0:T(8,128)(2,1)S(1)}, u32[]{:S(2)}, u32[]{:S(2)}) collective-permute-start(bf16[256,1536]{1,0:T(8,128)(2,1)S(1)} %get-tuple-element.557), channel_id=1, source_target_pairs={{0,1},{1,0},{2,3},{3,2},{4,5},{5,4},{6,7},{7,6},{8,9},{9,8},{10,11... | collective-permute-start | bytes 2359304 | tf_op jit(solution)/shard_map/ppermute | solution.py:1090
  398.5 8.4 %collective-permute-start.70 = (bf16[48,4352]{1,0:T(8,128)(2,1)S(1)}, bf16[48,4352]{1,0:T(8,128)(2,1)S(1)}, u32[]{:S(2)}, u32[]{:S(2)}) collective-permute-start(bf16[48,4352]{1,0:T(8,128)(2,1)S(1)} %get-tuple-element.510), channel_id=1, source_target_pairs={{0,8},{8,16},{16,24},{24,28},{28,20},{20,12},{12,4},{4,0},{1,9},{9... | collective-permute-start | bytes 1253384 | tf_op jit(solution)/shard_map/ppermute | solution.py:1405
  399.1 8.1 %collective-permute-start.71 = (bf16[48,4352]{1,0:T(8,128)(2,1)S(1)}, bf16[48,4352]{1,0:T(8,128)(2,1)S(1)}, u32[]{:S(2)}, u32[]{:S(2)}) collective-permute-start(bf16[48,4352]{1,0:T(8,128)(2,1)S(1)} %get-tuple-element.511), channel_id=1, source_target_pairs={{8,0},{16,8},{24,16},{28,24},{20,28},{12,20},{4,12},{0,4},{9,1},{1... | collective-permute-start | bytes 1253384 | tf_op jit(solution)/shard_map/ppermute | solution.py:1406
  409.7 8.4 %collective-permute-start.73 = (bf16[48,4352]{1,0:T(8,128)(2,1)}, bf16[48,4352]{1,0:T(8,128)(2,1)}, u32[]{:S(2)}, u32[]{:S(2)}) collective-permute-start(bf16[48,4352]{1,0:T(8,128)(2,1)} %get-tuple-element.517), channel_id=1, source_target_pairs={{0,8},{8,16},{16,24},{24,28},{28,20},{20,12},{12,4},{4,0},{1,9},{9... | collective-permute-start | bytes 1253384 | tf_op jit(solution)/shard_map/ppermute | solution.py:1405
  410.3 8.4 %collective-permute-start.74 = (bf16[48,4352]{1,0:T(8,128)(2,1)}, bf16[48,4352]{1,0:T(8,128)(2,1)}, u32[]{:S(2)}, u32[]{:S(2)}) collective-permute-start(bf16[48,4352]{1,0:T(8,128)(2,1)} %get-tuple-element.518), channel_id=1, source_target_pairs={{8,0},{16,8},{24,16},{28,24},{20,28},{12,20},{4,12},{0,4},{9,1},{1... | collective-permute-start | bytes 1253384 | tf_op jit(solution)/shard_map/ppermute | solution.py:1406
  427.8 12.0 %collective-permute-start.76 = (bf16[48,4224]{1,0:T(8,128)(2,1)S(1)}, bf16[48,4224]{1,0:T(8,128)(2,1)S(1)}, u32[]{:S(2)}, u32[]{:S(2)}) collective-permute-start(bf16[48,4224]{1,0:T(8,128)(2,1)S(1)} %slice_dynamic-update-slice_fusion.refs_0_), channel_id=1, source_target_pairs={{0,8},{8,16},{16,24},{24,28},{28,20},{20,12},{12,4},{4,0},{1,9},{9... | collective-permute-start | bytes 1216520 | tf_op jit(solution)/shard_map/ppermute | solution.py:1156
  429.0 11.4 %collective-permute-start.77 = (bf16[48,4224]{1,0:T(8,128)(2,1)S(1)}, bf16[48,4224]{1,0:T(8,128)(2,1)S(1)}, u32[]{:S(2)}, u32[]{:S(2)}) collective-permute-start(bf16[48,4224]{1,0:T(8,128)(2,1)S(1)} %slice_dynamic-update-slice_fusion.refs_0_), channel_id=1, source_target_pairs={{8,0},{16,8},{24,16},{28,24},{20,28},{12,20},{4,12},{0,4},{9,1},{1... | collective-permute-start | bytes 1216520 | tf_op jit(solution)/shard_map/ppermute | solution.py:1157
  440.5 11.3 %collective-permute-start.78 = (bf16[48,4224]{1,0:T(8,128)(2,1)S(1)}, bf16[48,4224]{1,0:T(8,128)(2,1)S(1)}, u32[]{:S(2)}, u32[]{:S(2)}) collective-permute-start(bf16[48,4224]{1,0:T(8,128)(2,1)S(1)} %collective-permute-done.76.refs_1_), channel_id=1, source_target_pairs={{0,8},{8,16},{16,24},{24,28},{28,20},{20,12},{12,4},{4,0},{1,9},{9... | collective-permute-start | bytes 1216520 | tf_op jit(solution)/shard_map/ppermute | solution.py:1156
  441.8 11.1 %collective-permute-start.79 = (bf16[48,4224]{1,0:T(8,128)(2,1)S(1)}, bf16[48,4224]{1,0:T(8,128)(2,1)S(1)}, u32[]{:S(2)}, u32[]{:S(2)}) collective-permute-start(bf16[48,4224]{1,0:T(8,128)(2,1)S(1)} %collective-permute-done.77.refs_2_), channel_id=1, source_target_pairs={{8,0},{16,8},{24,16},{28,24},{20,28},{12,20},{4,12},{0,4},{9,1},{1... | collective-permute-start | bytes 1216520 | tf_op jit(solution)/shard_map/ppermute | solution.py:1157
  454.9 8.4 %collective-permute-start.84 = (bf16[48,4224]{1,0:T(8,128)(2,1)S(1)}, bf16[48,4224]{1,0:T(8,128)(2,1)S(1)}, u32[]{:S(2)}, u32[]{:S(2)}) collective-permute-start(bf16[48,4224]{1,0:T(8,128)(2,1)S(1)} %slice_dynamic-update-slice_fusion.refs_0_), channel_id=1, source_target_pairs={{0,2},{2,0},{1,3},{3,1},{4,6},{6,4},{5,7},{7,5},{8,10},{10,8},{9,1... | collective-permute-start | bytes 1216520 | tf_op jit(solution)/shard_map/ppermute | solution.py:1093
  454.9 9.4 %collective-permute-start.85 = (bf16[48,4224]{1,0:T(8,128)(2,1)S(1)}, bf16[48,4224]{1,0:T(8,128)(2,1)S(1)}, u32[]{:S(2)}, u32[]{:S(2)}) collective-permute-start(bf16[48,4224]{1,0:T(8,128)(2,1)S(1)} %collective-permute-done.76.refs_1_), channel_id=1, source_target_pairs={{0,2},{2,0},{1,3},{3,1},{4,6},{6,4},{5,7},{7,5},{8,10},{10,8},{9,1... | collective-permute-start | bytes 1216520 | tf_op jit(solution)/shard_map/ppermute | solution.py:1093
  463.3 8.1 %collective-permute-start.83 = (bf16[48,2176]{1,0:T(8,128)(2,1)S(1)}, bf16[48,2176]{1,0:T(8,128)(2,1)S(1)}, u32[]{:S(2)}, u32[]{:S(2)}) collective-permute-start(bf16[48,2176]{1,0:T(8,128)(2,1)S(1)} %slice.112), channel_id=1, source_target_pairs={{8,0},{16,8},{24,16},{28,24},{20,28},{12,20},{4,12},{0,4},{9,1},{1... | collective-permute-start | bytes 626696 | tf_op jit(solution)/shard_map/ppermute | solution.py:1157
  (112 other events, 1039.7 us)

commit v2 on v1

--- a/solution.py
+++ b/solution.py
@@ -776,7 +776,7 @@
         scratch_shapes=scratch,
         compiler_params=pltpu.CompilerParams(vmem_limit_bytes=BIG_VMEM),
         cost_estimate=pl.CostEstimate(
-            flops=2 * length * rows * cols,
+            flops=6 * length * rows * cols,
             bytes_accessed=2 * length * (rows + cols),
             transcendentals=0,
         ),
@@ -1214,22 +1214,7 @@
     down_own = [held_down] + [to_shard(held_down, s) for s in range(1, shards)]
     in_own = [held_in] + [to_shard(held_in, s) for s in range(1, shards)]
     layouts = ([(s, 0, cut, cut) for s in range(shards)],) * 2
-    extras = jnp.stack(in_order(extras)).reshape(shards, -1)
-    gain_one = extras[:, :cut].reshape(1, -1).astype(F32)
-    gain_two = extras[:, cut : 2 * cut].reshape(1, -1).astype(F32)
-    segments = extras[:, 2 * cut : 2 * cut + rows].reshape(-1).astype(F32)
-    router = extras[:, 2 * cut + rows :].reshape(width, experts)
-    router_wide = jnp.pad(router, ((0, 0), (0, 128 - experts)))
-
-    inverse = jnp.power(ROPE_BASE, -(jnp.arange(HEAD_SIZE // 2) * 2.0 / HEAD_SIZE))
-    angles = jnp.arange(length).astype(F32)[:, None] * inverse[None, :]
-    cosine = jnp.concatenate([jnp.cos(angles)] * 4, axis=1)
-    sine = jnp.concatenate([-jnp.sin(angles), jnp.sin(angles)] * 2, axis=1)
-    ready = (gain_one, gain_two, segments, router_wide, cosine, sine)
-    blocks, down_own, upstream, ready = lax.optimization_barrier(
-        (blocks, down_own, cotangent, ready)
-    )
-    gain_one, gain_two, segments, router_wide, cosine, sine = ready
+    blocks, down_own, upstream = lax.optimization_barrier((blocks, down_own, cotangent))
     dy_pair = ring_step((upstream, upstream))
     upstream_chunks = [cotangent, *dy_pair]
     named_chunks = [b[0 if together else -1] for b in blocks[:chips]]
@@ -1238,6 +1223,13 @@
     block_places = jnp.concatenate(
         [info[2 + s] * experts + both_cores for s in range(1, shards)]
     ).astype(jnp.int32)
+    extras = jnp.stack(in_order(extras)).reshape(shards, -1)
+    gain_one = extras[:, :cut].reshape(1, -1).astype(F32)
+    gain_two = extras[:, cut : 2 * cut].reshape(1, -1).astype(F32)
+    segments = extras[:, 2 * cut : 2 * cut + rows].reshape(-1).astype(F32)
+    router = extras[:, 2 * cut + rows :].reshape(width, experts)
+    router_wide = jnp.pad(router, ((0, 0), (0, 128 - experts)))
+
     inputs = tokens.astype(F32)
     if together:
         normed, qkv_cols, projected, all_tokens = project(
@@ -1254,6 +1246,11 @@
         wide_tokens = all_tokens.astype(F32)
         normed = (wide_tokens * rms_scale(wide_tokens) * gain_one).astype(BF16)
         projected = nn(normed, qkv_cols)
+    places = jnp.arange(length)
+    inverse = jnp.power(ROPE_BASE, -(jnp.arange(HEAD_SIZE // 2) * 2.0 / HEAD_SIZE))
+    angles = places.astype(F32)[:, None] * inverse[None, :]
+    cosine = jnp.concatenate([jnp.cos(angles)] * 4, axis=1)
+    sine = jnp.concatenate([-jnp.sin(angles), jnp.sin(angles)] * 2, axis=1)
     projected, dy_pair = lax.optimization_barrier((projected, dy_pair))
     dy_pair = ring_step(dy_pair)
     upstream_chunks += dy_pair
@@ -1358,9 +1355,10 @@
     attn_low, in_got = lax.optimization_barrier((attn_low, in_got))
 
     low = lambda value: value.astype(BF16)
-    got = ring_send(ring_add(out_parts, half_ring - 1, out_got))
+    sent = ring_add(out_parts, half_ring - 1, out_got)
+    got = ring_send(sent)
     attn_got = [attn_low] + [to_shard(attn_low, s) for s in range(1, shards)]
-    down_other = [to_core(piece) for piece in tie(down_parts[shards:], attn_low)]
+    down_other = [to_core(piece) for piece in tie(down_parts[shards:], (attn_low, sent))]
     down_parts = [add_low(a, b) for a, b in zip(down_parts[:shards], down_other)]
     attn_got, got, down_parts = lax.optimization_barrier((attn_got, got, down_parts))
     if half_ring > 2:
@@ -1376,24 +1374,30 @@
         sent = ring_add(out_parts, step, got)
         projected_grads, sent = lax.optimization_barrier((projected_grads, sent))
         got = ring_send(sent)
-    normed_got = exchange_shards(lambda j: rows_of(normed_low, j))
-
+
+    mine_out, theirs_out = dense_grad(info, chip_places, unit, 1, head_out, attn_grads)
+    theirs_out = to_core(theirs_out)
     mine_qkv, theirs_qkv = dense_grad(
-        info, chip_places, unit, shards, normed, projected_grads, (grad_gain_one, grad_gain_two, grad_route)
-    )
-    mine_out, theirs_out = dense_grad(
-        info, chip_places, unit, 1, head_out, tie(attn_grads, mine_qkv)
+        info,
+        chip_places,
+        unit,
+        shards,
+        tie(normed, mine_out),
+        projected_grads,
+        (grad_gain_one, grad_gain_two, grad_route),
     )
     wide = own_cols + 128
+    mine_qkv, theirs_qkv, theirs_out, got = lax.optimization_barrier(
+        (mine_qkv, theirs_qkv, theirs_out, got)
+    )
     theirs_qkv = to_core(theirs_qkv)
-    theirs_out = to_core(theirs_out)
-    mine_out, got = lax.optimization_barrier((mine_out, got))
     pairs = ((mine_qkv, theirs_qkv), (mine_out, theirs_out))
     every = mine_qkv.shape[2] + mine_out.shape[2]
     half = every // 256 * 128
     right, left = sum_blocks(pairs, [(chips - 1, 0, half, []), (chips - 1, half, every, [])])
     right, left = lax.ppermute(right, "chip", ahead), lax.ppermute(left, "chip", behind)
-    right, left = lax.optimization_barrier((right, left))
+    right, left, normed_low = lax.optimization_barrier((right, left, normed_low))
+    normed_got = exchange_shards(lambda j: rows_of(normed_low, j))
     for hop, step in enumerate(range(half_ring - 1, 0, -1)):
         right, left = sum_blocks(
             pairs,

time: 488 us -> 481 us (0.986)
  waiting for transfers between devices: 155 us -> 144 us
  local copies, waits for them, and re-layouts: 28 us -> 33.1 us
    ppermute x11, waiting for transfers between devices: 46.1 us -> 39.8 us  [to_shard(): lax.ppermute(value, 'shard', [(i, (i + step) % shards) for i in range(sha...]
    ppermute x6, waiting for transfers between devices: 19.2 us -> 12.9 us  [ring_send(): lax.ppermute(sent[0], 'chip', ahead)]
    unnamed x180 -> x175, local copies, waits for them, and re-layouts: 16.8 us -> 22 us
  transfers between devices with their start and end apart: 93 -> 93, of which waited for: 50 -> 47; matrix products, arithmetic and copies ran while one was open for 6% -> 7% of each run, Pallas kernels for 33% -> 35%
where the time goes in v2:
time: 481 us; the launch traced here: 472 us
  Pallas kernels  186 us (39%)
  waiting for transfers between devices  144 us (30%)
  starting transfers between devices  81.8 us (17%)
  local copies, waits for them, and re-layouts  33.1 us (7%)
  other arithmetic  21 us (4%)
    pallas_call x5, Pallas kernels, run_experts(): pl.pallas_call(partial(expert_kernel, slots, *layouts), in_specs=[pl.Bloc...  65.2 us
    pallas_call x3, Pallas kernels, weight_grad(): pl.pallas_call(partial(weight_grad_kernel, heights, a_at, b_at, scale, by...  42.4 us
    ppermute x11, waiting for transfers between devices, to_shard(): lax.ppermute(value, 'shard', [(i, (i + step) % shards) for i in range(sha...  39.8 us
    unnamed x175, local copies, waits for them, and re-layouts  22 us
    ppermute x3, waiting for transfers between devices, body(): right = lax.ppermute(right, 'chip', ahead)  20.4 us
    ppermute x4, waiting for transfers between devices, plane_gather(): right = lax.ppermute(right, 'chip', ahead)  19.9 us
    ppermute x11, starting transfers between devices, to_shard(): lax.ppermute(value, 'shard', [(i, (i + step) % shards) for i in range(sha...  14.9 us
    ppermute x6, waiting for transfers between devices, ring_send(): lax.ppermute(sent[0], 'chip', ahead)  12.9 us
  transfers between devices with their start and end apart: 93, of which 47 were waited for; matrix products, arithmetic and copies ran while one was open for 7% of the time, Pallas kernels for 35%

profile of v2, /device:TPU:0, one launch (start us, length us, event | category | flops | bytes accessed | tf_op | source)
XLA Modules:
  0.0 471.8 jit_solution(14868118484150038220)
XLA Ops:
  2.4 3.0 collective-permute-start
  6.2 3.4 collective-permute-done
  9.6 2.2 collective-permute-start.1
  15.1 2.1 collective-permute-done.2.refs_4_.refs_5_
  20.0 1.6 collective-permute-start.6
  21.6 4.7 collective-permute-done.6
  26.3 1.8 collective-permute-start.7
  28.4 1.7 collective-permute-start.18
  31.7 1.7 collective-permute-done.8.refs_8_.refs_5_
  37.5 3.2 collective-permute-done.9.refs_9_.refs_4_.refs_5_
  43.7 4.4 collective-permute-done.18.refs_9_.refs_12_.refs_6_
  54.4 7.9 %shard_map.196 = (bf16[512,1536]{1,0:T(8,128)(2,1)}, bf16[1536,1280]{1,0:T(8,128)(2,1)}, f32[512,1280]{1,0:T(8,128)}, bf16[512,1536]{1,0:T(8,128)(2,1)}) custom-call(s32[12]{0:T(128)} %pad_add_fusion.info, s32[16]{0:T(128)} %add_add_fusion.places, bf16[768,2560]{1,0:T(8,128)(2,1)} %own_ref.1, f32[1,1536]{1,0:T(1,128)} %bitcast.64, bf16[256,1536]{1,0:T(8,128)(2,1)} %refs_0_, ...), custom_call_target="tpu_custom_call" | custom-call | flops 2013265920 | bytes 9699328 | tf_op jit(solution)/shard_map/pallas_call | solution.py:857
  62.3 2.9 collective-permute-done.19.refs_2_.refs_6_
  65.6 2.2 collective-permute-start.22
  68.0 1.7 copy-done.32
  69.8 6.7 %shard_map.197 = (bf16[512,1280]{1,0:T(8,128)(2,1)S(1)}, bf16[4,512,1536]{2,1,0:T(8,128)(2,1)S(1)}, bf16[512,768]{1,0:T(8,128)(2,1)S(1)}) custom-call(f32[512,1280]{1,0:T(8,128)S(1)} %copy-done.32, f32[512,1280]{1,0:T(8,128)S(1)} %copy-done.32, f32[512,1280]{1,0:T(8,128)S(1)} %copy-done.32, f32[512,128]{1,0:T(8,128)S(1)} %get-tuple-element.566.cos_ref, ...), custom_call_target="tpu_custom_call" | custom-call | flops 3221225472 | bytes 6291456 | tf_op jit(solution)/shard_map/pallas_call | solution.py:137
  77.6 3.0 convolution_convert_fusion
  87.4 12.8 %collective-permute-done.24 = bf16[256,1536]{1,0:T(8,128)(2,1)} collective-permute-done((bf16[256,1536]{1,0:T(8,128)(2,1)S(1)}, bf16[256,1536]{1,0:T(8,128)(2,1)}, u32[]{:S(2)}, u32[]{:S(2)}) %collective-permute-start.24) | collective-permute-done | bytes 786464 | tf_op jit(solution)/shard_map/ppermute | solution.py:1090
  100.2 1.7 convert_add_fusion.1.middle
  103.6 1.6 collective-permute-start.31
  107.4 9.8 %shard_map.198 = (bf16[256,2048]{1,0:T(8,128)(2,1)}, bf16[256,1024]{1,0:T(8,128)(2,1)}, bf16[256,1536]{1,0:T(8,128)(2,1)}, f32[8,256]{1,0:T(8,128)}, f32[256,128]{1,0:T(8,128)}) custom-call(s32[12]{0:T(128)} %pad_add_fusion.info, bf16[256,1536]{1,0:T(8,128)(2,1)} %copy-done.8, bf16[256,1536]{1,0:T(8,128)(2,1)} %upstream.1, bf16[64,1280]{1,0:T(8,128)(2,1)} %copy-done.65, ...), custom_call_target="tpu_custom_call" | custom-call | flops 4026531840 | bytes 14155776 | tf_op jit(solution)/shard_map/pallas_call | solution.py:435
  117.3 6.0 %collective-permute-done.31.refs_0_.refs_1_ = bf16[256,1536]{1,0:T(8,128)(2,1)} collective-permute-done((bf16[256,1536]{1,0:T(8,128)(2,1)S(1)}, bf16[256,1536]{1,0:T(8,128)(2,1)}, u32[]{:S(2)}, u32[]{:S(2)}) %collective-permute-start.31) | collective-permute-done | bytes 786464 | tf_op jit(solution)/shard_map/ppermute | solution.py:1124
  126.7 15.0 %shard_map.199 = (bf16[512,2048]{1,0:T(8,128)(2,1)}, bf16[512,1024]{1,0:T(8,128)(2,1)}, bf16[256,1536]{1,0:T(8,128)(2,1)}, bf16[256,1536]{1,0:T(8,128)(2,1)}, f3...) custom-call(s32[12]{0:T(128)} %pad_add_fusion.info, ...), custom_call_target="tpu_custom_call" | custom-call | flops 8053063680 | bytes 18874368 | tf_op jit(solution)/shard_map/pallas_call | solution.py:435
  144.6 1.7 collective-permute-start.35
  147.1 15.0 %shard_map.200 = (bf16[512,2048]{1,0:T(8,128)(2,1)}, bf16[512,1024]{1,0:T(8,128)(2,1)}, bf16[256,1536]{1,0:T(8,128)(2,1)}, bf16[256,1536]{1,0:T(8,128)(2,1)}, f3...) custom-call(s32[12]{0:T(128)} %pad_add_fusion.info, bf16[256,1536]{1,0:T(8,128)(2,1)} %copy-done.76, ...), custom_call_target="tpu_custom_call" | custom-call | flops 8053063680 | bytes 18874368 | tf_op jit(solution)/shard_map/pallas_call | solution.py:435
  162.0 2.1 collective-permute-done.36.refs_1_.refs_6_
  170.7 15.0 %shard_map.201 = (bf16[512,2048]{1,0:T(8,128)(2,1)}, bf16[512,1024]{1,0:T(8,128)(2,1)}, bf16[256,1536]{1,0:T(8,128)(2,1)}, bf16[256,1536]{1,0:T(8,128)(2,1)}, f3...) custom-call(s32[12]{0:T(128)} %pad_add_fusion.info, bf16[256,1536]{1,0:T(8,128)(2,1)} %copy-done.66, ...), custom_call_target="tpu_custom_call" | custom-call | flops 8053063680 | bytes 18874368 | tf_op jit(solution)/shard_map/pallas_call | solution.py:435
  186.5 10.3 %shard_map.202 = (bf16[256,2048]{1,0:T(8,128)(2,1)}, bf16[256,1024]{1,0:T(8,128)(2,1)}, bf16[128,1536]{1,0:T(8,128)(2,1)}, bf16[128,1536]{1,0:T(8,128)(2,1)}, f3...) custom-call(s32[12]{0:T(128)} %pad_add_fusion.info, ...), custom_call_target="tpu_custom_call" | custom-call | flops 4026531840 | bytes 14155776 | tf_op jit(solution)/shard_map/pallas_call | solution.py:435
  198.9 13.5 %shard_map.203 = (bf16[768,1024]{1,0:T(8,128)(2,1)}, bf16[768,1024]{1,0:T(8,128)(2,1)}) custom-call(s32[12]{0:T(128)} %pad_add_fusion.info, bf16[256,1536]{1,0:T(8,128)(2,1)} %copy-done.8, bf16[256,1536]{1,0:T(8,128)(2,1)} %collective-permute-done.31.refs_0_.refs_1_, bf16[256,1536]{1,0:T(8,128)(2,1)} %copy-done.75, bf16[256,1536]{1,0:T(8,128)(2,1)} %copy-done.76, ...), custom_call_target="tpu_custom_call" | custom-call | flops 6442450944 | bytes 13631488 | tf_op jit(solution)/shard_map/pallas_call | solution.py:666
  216.3 2.2 collective-permute-done.46.refs_15_
  218.5 15.0 %shard_map.205 = (bf16[768,1024]{1,0:T(8,128)(2,1)}, bf16[768,1024]{1,0:T(8,128)(2,1)}) custom-call(s32[12]{0:T(128)} %pad_add_fusion.info, bf16[256,1536]{1,0:T(8,128)(2,1)} %copy-done.8, bf16[256,1536]{1,0:T(8,128)(2,1)} %collective-permute-done.31.refs_0_.refs_1_, bf16[256,1536]{1,0:T(8,128)(2,1)} %copy-done.75, bf16[256,1536]{1,0:T(8,128)(2,1)} %copy-done.76, ...), custom_call_target="tpu_custom_call" | custom-call | flops 6442450944 | bytes 13631488 | tf_op jit(solution)/shard_map/pallas_call | solution.py:666
  239.7 3.3 all-to-all-start
  244.6 11.1 %shard_map.207 = (bf16[256,1536]{1,0:T(8,128)(2,1)}, bf16[256,1536]{1,0:T(8,128)(2,1)}, bf16[256,1536]{1,0:T(8,128)(2,1)}, bf16[256,1536]{1,0:T(8,128)(2,1)}, bf...) custom-call(s32[12]{0:T(128)} %pad_add_fusion.info, ...), custom_call_target="tpu_custom_call" | custom-call | flops 6442450944 | bytes 13631488 | tf_op jit(solution)/shard_map/pallas_call | solution.py:504
  257.4 1.7 collective-permute-start.49
  262.8 13.9 %shard_map.211 = (bf16[512,768]{1,0:T(8,128)(2,1)}, bf16[512,768]{1,0:T(8,128)(2,1)}, bf16[512,768]{1,0:T(8,128)(2,1)}, bf16[512,768]{1,0:T(8,128)(2,1)}) custom-call(s32[12]{0:T(128)} %pad_add_fusion.info, bf16[256,1024]{1,0:T(8,128)(2,1)} %get-tuple-element.427.refs_0_, bf16[512,1024]{1,0:T(8,128)(2,1)} %get-tuple-element.428.refs_1_, ...), custom_call_target="tpu_custom_call" | custom-call | flops 6442450944 | bytes 13631488 | tf_op jit(solution)/shard_map/pallas_call | solution.py:666
  276.8 1.7 collective-permute-start.51
  279.4 5.5 %shard_map.212 = (bf16[256,1536]{1,0:T(8,128)(2,1)}, f32[256,1536]{1,0:T(8,128)}, f32[1,1536]{1,0:T(1,128)}) custom-call(bf16[256,1536]{1,0:T(8,128)(2,1)} %get-tuple-element.321.own, bf16[256,1536]{1,0:T(8,128)(2,1)} %copy-done.61, bf16[256,1536]{1,0:T(8,128)(2,1)} %copy-done.62, f32[256,1536]{1,0:T(8,128)} %copy-done.12, f32[256,1536]{1,0:T(8,128)} %copy-done.46, ...), custom_call_target="tpu_custom_call" | custom-call | tf_op jit(solution)/shard_map/pallas_call | solution.py:932
  294.0 13.1 %collective-permute-done.54.refs_1_ = bf16[256,1536]{1,0:T(8,128)(2,1)S(1)} collective-permute-done((bf16[256,1536]{1,0:T(8,128)(2,1)S(1)}, bf16[256,1536]{1,0:T(8,128)(2,1)S(1)}, u32[]{:S(2)}, u32[]{:S(2)}) %collective-permute-start.54) | collective-permute-done | bytes 786464 | tf_op jit(solution)/shard_map/ppermute | solution.py:1090
  313.6 11.3 %shard_map.214 = (bf16[512,1280]{1,0:T(8,128)(2,1)S(1)}, bf16[512,1536]{1,0:T(8,128)(2,1)S(1)}) custom-call(s32[12]{0:T(128)S(1)} %copy-done.30, bf16[512,1280]{1,0:T(8,128)(2,1)S(1)} %copy-done.42, bf16[512,1280]{1,0:T(8,128)(2,1)S(1)} %copy-done.42, bf16[512,1280]{1,0:T(8,128)(2,1)S(1)} %copy-done.42, bf16[4,512,1536]{2,1,0:T(8,128)(2,1)} %copy-done.40, ...), custom_call_target="tpu_custom_call" | custom-call | flops 7650410496 | bytes 6291456 | tf_op jit(solution)/shard_map/pallas_call | solution.py:261
  327.2 5.0 %shard_map.215 = (bf16[8,48,1536]{2,1,0:T(8,128)(2,1)}, bf16[8,48,1536]{2,1,0:T(8,128)(2,1)}) custom-call(s32[12]{0:T(128)} %pad_add_fusion.info, s32[8]{0:T(128)} %fusion.9.places, bf16[512,768]{1,0:T(8,128)(2,1)} %copy-done.43, bf16[512,1536]{1,0:T(8,128)(2,1)} %copy-done.45), custom_call_target="tpu_custom_call" | custom-call | flops 3623878656 | bytes 2359296 | tf_op jit(solution)/shard_map/pallas_call | solution.py:771
  332.2 2.1 copy-done.31
  335.8 2.4 shard_map.217
  338.2 1.6 shard_map.218
  341.9 6.5 %shard_map.219 = (bf16[8,48,2816]{2,1,0:T(8,128)(2,1)}, bf16[8,48,2816]{2,1,0:T(8,128)(2,1)}) custom-call(s32[12]{0:T(128)} %pad_add_fusion.info, s32[8]{0:T(128)} %fusion.9.places, bf16[512,1536]{1,0:T(8,128)(2,1)} %get-tuple-element.468.refs_0_, bf16[512,1280]{1,0:T(8,128)(2,1)} %copy-done.38, f32[1,1536]{1,0:T(1,128)} %copy-done.44, ...), custom_call_target="tpu_custom_call" | custom-call | flops 6039797760 | bytes 2883584 | tf_op jit(solution)/shard_map/pallas_call | solution.py:771
  348.4 11.6 %collective-permute-done.63 = bf16[256,1536]{1,0:T(8,128)(2,1)S(1)} collective-permute-done((bf16[256,1536]{1,0:T(8,128)(2,1)}, bf16[256,1536]{1,0:T(8,128)(2,1)S(1)}, u32[]{:S(2)}, u32[]{:S(2)}) %collective-permute-start.63) | collective-permute-done | bytes 786464 | tf_op jit(solution)/shard_map/ppermute | solution.py:1140
  361.3 4.5 collective-permute-done.65.refs_1_
  365.8 1.6 copy-done
  369.8 5.2 %collective-permute-done.66.refs_4_ = bf16[48,2176]{1,0:T(8,128)(2,1)S(1)} collective-permute-done((bf16[48,2176]{1,0:T(8,128)(2,1)S(1)}, bf16[48,2176]{1,0:T(8,128)(2,1)S(1)}, u32[]{:S(2)}, u32[]{:S(2)}) %collective-permute-start.66) | collective-permute-done | bytes 208928 | tf_op jit(solution)/shard_map/ppermute | solution.py:1398
  380.8 6.7 %collective-permute-done.68.refs_4_ = bf16[48,4352]{1,0:T(8,128)(2,1)S(1)} collective-permute-done((bf16[48,4352]{1,0:T(8,128)(2,1)S(1)}, bf16[48,4352]{1,0:T(8,128)(2,1)S(1)}, u32[]{:S(2)}, u32[]{:S(2)}) %collective-permute-start.68) | collective-permute-done | bytes 417824 | tf_op jit(solution)/shard_map/ppermute | solution.py:1409
  392.3 7.3 %collective-permute-done.70.refs_4_ = bf16[48,4352]{1,0:T(8,128)(2,1)S(1)} collective-permute-done((bf16[48,4352]{1,0:T(8,128)(2,1)S(1)}, bf16[48,4352]{1,0:T(8,128)(2,1)S(1)}, u32[]{:S(2)}, u32[]{:S(2)}) %collective-permute-start.70) | collective-permute-done | bytes 417824 | tf_op jit(solution)/shard_map/ppermute | solution.py:1409
  400.0 1.6 shard_map.223
  403.8 6.5 %collective-permute-done.73.refs_4_ = bf16[48,4352]{1,0:T(8,128)(2,1)} collective-permute-done((bf16[48,4352]{1,0:T(8,128)(2,1)}, bf16[48,4352]{1,0:T(8,128)(2,1)}, u32[]{:S(2)}, u32[]{:S(2)}) %collective-permute-start.73) | collective-permute-done | bytes 417824 | tf_op jit(solution)/shard_map/ppermute | solution.py:1409
  410.6 1.6 copy-done.3
  413.5 1.7 shard_map.224
  416.3 2.6 add_convert_fusion
  423.2 9.3 %collective-permute-done.76.refs_1_ = bf16[48,4224]{1,0:T(8,128)(2,1)S(1)} collective-permute-done((bf16[48,4224]{1,0:T(8,128)(2,1)S(1)}, bf16[48,4224]{1,0:T(8,128)(2,1)S(1)}, u32[]{:S(2)}, u32[]{:S(2)}) %collective-permute-start.76) | collective-permute-done | bytes 405536 | tf_op jit(solution)/shard_map/ppermute | solution.py:1156
  434.7 1.6 fusion.3
  436.3 8.1 %collective-permute-done.78.refs_3_ = bf16[48,4224]{1,0:T(8,128)(2,1)S(1)} collective-permute-done((bf16[48,4224]{1,0:T(8,128)(2,1)S(1)}, bf16[48,4224]{1,0:T(8,128)(2,1)S(1)}, u32[]{:S(2)}, u32[]{:S(2)}) %collective-permute-start.78) | collective-permute-done | bytes 405536 | tf_op jit(solution)/shard_map/ppermute | solution.py:1156
  447.9 3.7 convert_add_fusion
  451.6 1.7 collective-permute-done.80.refs_0_
  454.7 2.5 convert_add_fusion.2
  460.1 4.0 shard_map.225
  465.1 1.7 collective-permute-done.91.refs_5_
  466.8 2.9 shard_map.226
  (386 shorter events, 127.7 us)
Async XLA Ops:
  5.4 20.8 %collective-permute-start.5 = (bf16[256,1536]{1,0:T(8,128)(2,1)}, bf16[256,1536]{1,0:T(8,128)(2,1)S(1)}, u32[]{:S(2)}, u32[]{:S(2)}) collective-permute-start(bf16[256,1536]{1,0:T(8,128)(2,1)} %refs_0_), channel_id=1, source_target_pairs={{0,1},{1,0},{2,3},{3,2},{4,5},{5,4},{6,7},{7,6},{8,9},{9,8},{10,11... | collective-permute-start | bytes 2359304 | tf_op jit(solution)/shard_map/ppermute | solution.py:1090
  17.2 9.0 %collective-permute-start.3 = (bf16[64,1280]{1,0:T(8,128)(2,1)}, bf16[64,1280]{1,0:T(8,128)(2,1)S(1)}, u32[]{:S(2)}, u32[]{:S(2)}) collective-permute-start(bf16[64,1280]{1,0:T(8,128)(2,1)} %collective-permute-done.1.refs_3_.refs_4_), channel_id=1, source_target_pairs={{0,8},{8,16},{16,24},{24,28},{28,20},{20,12},{12,4},{4,0},{1,9},{9... | collective-permute-start | bytes 491528 | tf_op jit(solution)/shard_map/ppermute | solution.py:1174
  18.8 7.5 %collective-permute-start.4 = (bf16[64,1280]{1,0:T(8,128)(2,1)}, bf16[64,1280]{1,0:T(8,128)(2,1)S(1)}, u32[]{:S(2)}, u32[]{:S(2)}) collective-permute-start(bf16[64,1280]{1,0:T(8,128)(2,1)} %collective-permute-done.2.refs_4_.refs_5_), channel_id=1, source_target_pairs={{8,0},{16,8},{24,16},{28,24},{20,28},{12,20},{4,12},{0,4},{9,1},{1... | collective-permute-start | bytes 491528 | tf_op jit(solution)/shard_map/ppermute | solution.py:1177
  21.6 11.9 %collective-permute-start.10 = (bf16[64,1280]{1,0:T(8,128)(2,1)S(1)}, bf16[64,1280]{1,0:T(8,128)(2,1)S(1)}, u32[]{:S(2)}, u32[]{:S(2)}) collective-permute-start(bf16[64,1280]{1,0:T(8,128)(2,1)S(1)} %fusion.5.refs_2_), channel_id=1, source_target_pairs={{0,2},{2,0},{1,3},{3,1},{4,6},{6,4},{5,7},{7,5},{8,10},{10,8},{9,1... | collective-permute-start | bytes 491528 | tf_op jit(solution)/shard_map/ppermute | solution.py:1093
  28.4 19.7 %collective-permute-start.18 = (bf16[512,768]{1,0:T(8,128)(2,1)}, bf16[512,768]{1,0:T(8,128)(2,1)}, u32[]{:S(2)}, u32[]{:S(2)}) collective-permute-start(bf16[512,768]{1,0:T(8,128)(2,1)} %bitcast.7.refs_8_.refs_11_.refs_5_), channel_id=1, source_target_pairs={{0,1},{1,0},{2,3},{3,2},{4,5},{5,4},{6,7},{7,6},{8,9},{9,8},{10,11... | collective-permute-start | bytes 2359304 | tf_op jit(solution)/shard_map/ppermute | solution.py:1090
  42.1 38.9 %collective-permute-start.21 = (bf16[768,1024]{1,0:T(8,128)(2,1)}, bf16[768,1024]{1,0:T(8,128)(2,1)}, u32[]{:S(2)}, u32[]{:S(2)}) collective-permute-start(bf16[768,1024]{1,0:T(8,128)(2,1)} %bitcast.68), channel_id=1, source_target_pairs={{0,1},{1,0},{2,3},{3,2},{4,5},{5,4},{6,7},{7,6},{8,9},{9,8},{10,11... | collective-permute-start | bytes 4718600 | tf_op jit(solution)/shard_map/ppermute | solution.py:1090
  48.1 17.1 %collective-permute-start.19 = (bf16[256,1536]{1,0:T(8,128)(2,1)S(1)}, bf16[256,1536]{1,0:T(8,128)(2,1)}, u32[]{:S(2)}, u32[]{:S(2)}) collective-permute-start(bf16[256,1536]{1,0:T(8,128)(2,1)S(1)} %copy-done.56), channel_id=1, source_target_pairs={{0,8},{8,16},{16,24},{24,28},{28,20},{20,12},{12,4},{4,0},{1,9},{9... | collective-permute-start | bytes 2359304 | tf_op jit(solution)/shard_map/ppermute | solution.py:1124
  49.4 16.2 %collective-permute-start.20 = (bf16[256,1536]{1,0:T(8,128)(2,1)S(1)}, bf16[256,1536]{1,0:T(8,128)(2,1)}, u32[]{:S(2)}, u32[]{:S(2)}) collective-permute-start(bf16[256,1536]{1,0:T(8,128)(2,1)S(1)} %copy-done.56), channel_id=1, source_target_pairs={{8,0},{16,8},{24,16},{28,24},{20,28},{12,20},{4,12},{0,4},{9,1},{1... | collective-permute-start | bytes 2359304 | tf_op jit(solution)/shard_map/ppermute | solution.py:1124
  65.6 15.4 %collective-permute-start.22 = (bf16[256,1536]{1,0:T(8,128)(2,1)}, bf16[256,1536]{1,0:T(8,128)(2,1)}, u32[]{:S(2)}, u32[]{:S(2)}) collective-permute-start(bf16[256,1536]{1,0:T(8,128)(2,1)} %collective-permute-done.19.refs_2_.refs_6_), channel_id=1, source_target_pairs={{0,8},{8,16},{16,24},{24,28},{28,20},{20,12},{12,4},{4,0},{1,9},{9... | collective-permute-start | bytes 2359304 | tf_op jit(solution)/shard_map/ppermute | solution.py:1124
  67.8 14.1 %collective-permute-start.23 = (bf16[256,1536]{1,0:T(8,128)(2,1)}, bf16[256,1536]{1,0:T(8,128)(2,1)}, u32[]{:S(2)}, u32[]{:S(2)}) collective-permute-start(bf16[256,1536]{1,0:T(8,128)(2,1)} %collective-permute-done.20.refs_3_.refs_7_), channel_id=1, source_target_pairs={{8,0},{16,8},{24,16},{28,24},{20,28},{12,20},{4,12},{0,4},{9,1},{1... | collective-permute-start | bytes 2359304 | tf_op jit(solution)/shard_map/ppermute | solution.py:1124
  83.1 17.1 %collective-permute-start.24 = (bf16[256,1536]{1,0:T(8,128)(2,1)S(1)}, bf16[256,1536]{1,0:T(8,128)(2,1)}, u32[]{:S(2)}, u32[]{:S(2)}) collective-permute-start(bf16[256,1536]{1,0:T(8,128)(2,1)S(1)} %constant_dynamic-slice_fusion.2), channel_id=1, source_target_pairs={{0,1},{1,0},{2,3},{3,2},{4,5},{5,4},{6,7},{7,6},{8,9},{9,8},{10,11... | collective-permute-start | bytes 2359304 | tf_op jit(solution)/shard_map/ppermute | solution.py:1090
  84.7 17.2 %collective-permute-start.25 = (bf16[256,1536]{1,0:T(8,128)(2,1)}, bf16[256,1536]{1,0:T(8,128)(2,1)}, u32[]{:S(2)}, u32[]{:S(2)}) collective-permute-start(bf16[256,1536]{1,0:T(8,128)(2,1)} %collective-permute-done.22.refs_2_.refs_8_), channel_id=1, source_target_pairs={{0,8},{8,16},{16,24},{24,28},{28,20},{20,12},{12,4},{4,0},{1,9},{9... | collective-permute-start | bytes 2359304 | tf_op jit(solution)/shard_map/ppermute | solution.py:1124
  86.3 16.9 %collective-permute-start.26 = (bf16[256,1536]{1,0:T(8,128)(2,1)}, bf16[256,1536]{1,0:T(8,128)(2,1)}, u32[]{:S(2)}, u32[]{:S(2)}) collective-permute-start(bf16[256,1536]{1,0:T(8,128)(2,1)} %collective-permute-done.23.refs_3_.refs_9_), channel_id=1, source_target_pairs={{8,0},{16,8},{24,16},{28,24},{20,28},{12,20},{4,12},{0,4},{9,1},{1... | collective-permute-start | bytes 2359304 | tf_op jit(solution)/shard_map/ppermute | solution.py:1124
  86.9 18.3 %collective-permute-start.29 = (bf16[512,768]{1,0:T(8,128)(2,1)}, bf16[512,768]{1,0:T(8,128)(2,1)S(1)}, u32[]{:S(2)}, u32[]{:S(2)}) collective-permute-start(bf16[512,768]{1,0:T(8,128)(2,1)} %bitcast.7.refs_8_.refs_11_.refs_5_), channel_id=1, source_target_pairs={{0,2},{2,0},{1,3},{3,1},{4,6},{6,4},{5,7},{7,5},{8,10},{10,8},{9,1... | collective-permute-start | bytes 2359304 | tf_op jit(solution)/shard_map/ppermute | solution.py:1093
  86.9 20.5 %collective-permute-start.30 = (bf16[512,768]{1,0:T(8,128)(2,1)}, bf16[512,768]{1,0:T(8,128)(2,1)}, u32[]{:S(2)}, u32[]{:S(2)}) collective-permute-start(bf16[512,768]{1,0:T(8,128)(2,1)} %collective-permute-done.18.refs_9_.refs_12_.refs_6_), channel_id=1, source_target_pairs={{0,2},{2,0},{1,3},{3,1},{4,6},{6,4},{5,7},{7,5},{8,10},{10,8},{9,1... | collective-permute-start | bytes 2359304 | tf_op jit(solution)/shard_map/ppermute | solution.py:1093
  103.6 19.6 %collective-permute-start.31 = (bf16[256,1536]{1,0:T(8,128)(2,1)S(1)}, bf16[256,1536]{1,0:T(8,128)(2,1)}, u32[]{:S(2)}, u32[]{:S(2)}) collective-permute-start(bf16[256,1536]{1,0:T(8,128)(2,1)S(1)} %multiply_convert_fusion.refs_0_.second_ref), channel_id=1, source_target_pairs={{0,8},{8,16},{16,24},{24,28},{28,20},{20,12},{12,4},{4,0},{1,9},{9... | collective-permute-start | bytes 2359304 | tf_op jit(solution)/shard_map/ppermute | solution.py:1124
  105.2 19.2 %collective-permute-start.32 = (bf16[256,1536]{1,0:T(8,128)(2,1)S(1)}, bf16[256,1536]{1,0:T(8,128)(2,1)S(1)}, u32[]{:S(2)}, u32[]{:S(2)}) collective-permute-start(bf16[256,1536]{1,0:T(8,128)(2,1)S(1)} %multiply_convert_fusion.refs_0_.second_ref), channel_id=1, source_target_pairs={{8,0},{16,8},{24,16},{28,24},{20,28},{12,20},{4,12},{0,4},{9,1},{1... | collective-permute-start | bytes 2359304 | tf_op jit(solution)/shard_map/ppermute | solution.py:1124
  124.4 18.6 %collective-permute-start.33 = (bf16[256,1536]{1,0:T(8,128)(2,1)}, bf16[256,1536]{1,0:T(8,128)(2,1)S(1)}, u32[]{:S(2)}, u32[]{:S(2)}) collective-permute-start(bf16[256,1536]{1,0:T(8,128)(2,1)} %collective-permute-done.31.refs_0_.refs_1_), channel_id=1, source_target_pairs={{0,8},{8,16},{16,24},{24,28},{28,20},{20,12},{12,4},{4,0},{1,9},{9... | collective-permute-start | bytes 2359304 | tf_op jit(solution)/shard_map/ppermute | solution.py:1124
  126.0 18.6 %collective-permute-start.34 = (bf16[256,1536]{1,0:T(8,128)(2,1)S(1)}, bf16[256,1536]{1,0:T(8,128)(2,1)S(1)}, u32[]{:S(2)}, u32[]{:S(2)}) collective-permute-start(bf16[256,1536]{1,0:T(8,128)(2,1)S(1)} %collective-permute-done.32.refs_1_.refs_2_), channel_id=1, source_target_pairs={{8,0},{16,8},{24,16},{28,24},{20,28},{12,20},{4,12},{0,4},{9,1},{1... | collective-permute-start | bytes 2359304 | tf_op jit(solution)/shard_map/ppermute | solution.py:1124
  144.6 17.5 %collective-permute-start.35 = (bf16[256,1536]{1,0:T(8,128)(2,1)S(1)}, bf16[256,1536]{1,0:T(8,128)(2,1)S(1)}, u32[]{:S(2)}, u32[]{:S(2)}) collective-permute-start(bf16[256,1536]{1,0:T(8,128)(2,1)S(1)} %collective-permute-done.33.refs_0_.refs_3_), channel_id=1, source_target_pairs={{0,8},{8,16},{16,24},{24,28},{28,20},{20,12},{12,4},{4,0},{1,9},{9... | collective-permute-start | bytes 2359304 | tf_op jit(solution)/shard_map/ppermute | solution.py:1124
  146.3 17.8 %collective-permute-start.36 = (bf16[256,1536]{1,0:T(8,128)(2,1)S(1)}, bf16[256,1536]{1,0:T(8,128)(2,1)S(1)}, u32[]{:S(2)}, u32[]{:S(2)}) collective-permute-start(bf16[256,1536]{1,0:T(8,128)(2,1)S(1)} %collective-permute-done.34.refs_1_.refs_4_), channel_id=1, source_target_pairs={{8,0},{16,8},{24,16},{28,24},{20,28},{12,20},{4,12},{0,4},{9,1},{1... | collective-permute-start | bytes 2359304 | tf_op jit(solution)/shard_map/ppermute | solution.py:1124
  164.2 21.6 %collective-permute-start.37 = (bf16[128,1536]{1,0:T(8,128)(2,1)S(1)}, bf16[128,1536]{1,0:T(8,128)(2,1)}, u32[]{:S(2)}, u32[]{:S(2)}) collective-permute-start(bf16[128,1536]{1,0:T(8,128)(2,1)S(1)} %slice.92), channel_id=1, source_target_pairs={{0,8},{8,16},{16,24},{24,28},{28,20},{20,12},{12,4},{4,0},{1,9},{9... | collective-permute-start | bytes 1179656 | tf_op jit(solution)/shard_map/ppermute | solution.py:1124
  165.2 20.5 %collective-permute-start.38 = (bf16[128,1536]{1,0:T(8,128)(2,1)S(1)}, bf16[128,1536]{1,0:T(8,128)(2,1)}, u32[]{:S(2)}, u32[]{:S(2)}) collective-permute-start(bf16[128,1536]{1,0:T(8,128)(2,1)S(1)} %slice.93), channel_id=1, source_target_pairs={{8,0},{16,8},{24,16},{28,24},{20,28},{12,20},{4,12},{0,4},{9,1},{1... | collective-permute-start | bytes 1179656 | tf_op jit(solution)/shard_map/ppermute | solution.py:1124
  167.3 18.4 %collective-permute-start.39 = (bf16[128,1536]{1,0:T(8,128)(2,1)S(1)}, bf16[128,1536]{1,0:T(8,128)(2,1)S(1)}, u32[]{:S(2)}, u32[]{:S(2)}) collective-permute-start(bf16[128,1536]{1,0:T(8,128)(2,1)S(1)} %slice.94), channel_id=1, source_target_pairs={{0,8},{8,16},{16,24},{24,28},{28,20},{20,12},{12,4},{4,0},{1,9},{9... | collective-permute-start | bytes 1179656 | tf_op jit(solution)/shard_map/ppermute | solution.py:1124
  169.4 16.4 %collective-permute-start.40 = (bf16[128,1536]{1,0:T(8,128)(2,1)S(1)}, bf16[128,1536]{1,0:T(8,128)(2,1)}, u32[]{:S(2)}, u32[]{:S(2)}) collective-permute-start(bf16[128,1536]{1,0:T(8,128)(2,1)S(1)} %slice.95), channel_id=1, source_target_pairs={{8,0},{16,8},{24,16},{28,24},{20,28},{12,20},{4,12},{0,4},{9,1},{1... | collective-permute-start | bytes 1179656 | tf_op jit(solution)/shard_map/ppermute | solution.py:1124
  196.9 15.6 %collective-permute-start.41 = (bf16[128,1536]{1,0:T(8,128)(2,1)}, bf16[128,1536]{1,0:T(8,128)(2,1)S(1)}, u32[]{:S(2)}, u32[]{:S(2)}) collective-permute-start(bf16[128,1536]{1,0:T(8,128)(2,1)} %get-tuple-element.344), channel_id=1, source_target_pairs={{0,8},{8,16},{16,24},{24,28},{28,20},{20,12},{12,4},{4,0},{1,9},{9... | collective-permute-start | bytes 1179656 | tf_op jit(solution)/shard_map/ppermute | solution.py:1134
  197.9 14.6 %collective-permute-start.42 = (bf16[128,1536]{1,0:T(8,128)(2,1)}, bf16[128,1536]{1,0:T(8,128)(2,1)S(1)}, u32[]{:S(2)}, u32[]{:S(2)}) collective-permute-start(bf16[128,1536]{1,0:T(8,128)(2,1)} %get-tuple-element.345), channel_id=1, source_target_pairs={{8,0},{16,8},{24,16},{28,24},{20,28},{12,20},{4,12},{0,4},{9,1},{1... | collective-permute-start | bytes 1179656 | tf_op jit(solution)/shard_map/ppermute | solution.py:1134
  214.3 19.7 %collective-permute-start.43 = (bf16[256,1536]{1,0:T(8,128)(2,1)}, bf16[256,1536]{1,0:T(8,128)(2,1)S(1)}, u32[]{:S(2)}, u32[]{:S(2)}) collective-permute-start(bf16[256,1536]{1,0:T(8,128)(2,1)} %get-tuple-element.362), channel_id=1, source_target_pairs={{0,8},{8,16},{16,24},{24,28},{28,20},{20,12},{12,4},{4,0},{1,9},{9... | collective-permute-start | bytes 2359304 | tf_op jit(solution)/shard_map/ppermute | solution.py:1140
  215.3 19.5 %collective-permute-start.44 = (bf16[256,1536]{1,0:T(8,128)(2,1)}, bf16[256,1536]{1,0:T(8,128)(2,1)S(1)}, u32[]{:S(2)}, u32[]{:S(2)}) collective-permute-start(bf16[256,1536]{1,0:T(8,128)(2,1)} %get-tuple-element.363), channel_id=1, source_target_pairs={{8,0},{16,8},{24,16},{28,24},{20,28},{12,20},{4,12},{0,4},{9,1},{1... | collective-permute-start | bytes 2359304 | tf_op jit(solution)/shard_map/ppermute | solution.py:1140
  236.2 19.7 %collective-permute-start.47 = (bf16[256,1536]{1,0:T(8,128)(2,1)}, bf16[256,1536]{1,0:T(8,128)(2,1)S(1)}, u32[]{:S(2)}, u32[]{:S(2)}) collective-permute-start(bf16[256,1536]{1,0:T(8,128)(2,1)} %get-tuple-element.377), channel_id=1, source_target_pairs={{0,8},{8,16},{16,24},{24,28},{28,20},{20,12},{12,4},{4,0},{1,9},{9... | collective-permute-start | bytes 2359304 | tf_op jit(solution)/shard_map/ppermute | solution.py:1140
  236.8 19.1 %collective-permute-start.48 = (bf16[256,1536]{1,0:T(8,128)(2,1)}, bf16[256,1536]{1,0:T(8,128)(2,1)S(1)}, u32[]{:S(2)}, u32[]{:S(2)}) collective-permute-start(bf16[256,1536]{1,0:T(8,128)(2,1)} %get-tuple-element.378), channel_id=1, source_target_pairs={{8,0},{16,8},{24,16},{28,24},{20,28},{12,20},{4,12},{0,4},{9,1},{1... | collective-permute-start | bytes 2359304 | tf_op jit(solution)/shard_map/ppermute | solution.py:1140
  239.7 16.2 %all-to-all-start = ((f32[8,2,256]{2,1,0:T(2,128)}), f32[8,2,256]{2,1,0:T(2,128)S(1)}, u32[]{:S(2)}, u32[]{:S(2)}) async-start(f32[8,2,256]{2,1,0:T(2,128)} %shard_map.208), calls=%async_computation | async-start | bytes 32768 | tf_op jit(solution)/shard_map/all_to_all | solution.py:1328
  243.0 43.7 %collective-permute-start.53 = (bf16[768,1024]{1,0:T(8,128)(2,1)}, bf16[768,1024]{1,0:T(8,128)(2,1)}, u32[]{:S(2)}, u32[]{:S(2)}) collective-permute-start(bf16[768,1024]{1,0:T(8,128)(2,1)} %get-tuple-element.452), channel_id=1, source_target_pairs={{0,1},{1,0},{2,3},{3,2},{4,5},{5,4},{6,7},{7,6},{8,9},{9,8},{10,11... | collective-permute-start | bytes 4718600 | tf_op jit(solution)/shard_map/ppermute | solution.py:1090
  257.4 19.4 %collective-permute-start.49 = (bf16[256,1536]{1,0:T(8,128)(2,1)}, bf16[256,1536]{1,0:T(8,128)(2,1)S(1)}, u32[]{:S(2)}, u32[]{:S(2)}) collective-permute-start(bf16[256,1536]{1,0:T(8,128)(2,1)} %get-tuple-element.420), channel_id=1, source_target_pairs={{0,8},{8,16},{16,24},{24,28},{28,20},{20,12},{12,4},{4,0},{1,9},{9... | collective-permute-start | bytes 2359304 | tf_op jit(solution)/shard_map/ppermute | solution.py:1140
  259.1 17.7 %collective-permute-start.50 = (bf16[256,1536]{1,0:T(8,128)(2,1)}, bf16[256,1536]{1,0:T(8,128)(2,1)S(1)}, u32[]{:S(2)}, u32[]{:S(2)}) collective-permute-start(bf16[256,1536]{1,0:T(8,128)(2,1)} %get-tuple-element.421), channel_id=1, source_target_pairs={{8,0},{16,8},{24,16},{28,24},{20,28},{12,20},{4,12},{0,4},{9,1},{1... | collective-permute-start | bytes 2359304 | tf_op jit(solution)/shard_map/ppermute | solution.py:1140
  276.8 8.7 %collective-permute-start.51 = (bf16[128,1536]{1,0:T(8,128)(2,1)}, bf16[128,1536]{1,0:T(8,128)(2,1)S(1)}, u32[]{:S(2)}, u32[]{:S(2)}) collective-permute-start(bf16[128,1536]{1,0:T(8,128)(2,1)} %get-tuple-element.448), channel_id=1, source_target_pairs={{0,8},{8,16},{16,24},{24,28},{28,20},{20,12},{12,4},{4,0},{1,9},{9... | collective-permute-start | bytes 1179656 | tf_op jit(solution)/shard_map/ppermute | solution.py:1134
  278.5 8.2 %collective-permute-start.52 = (bf16[128,1536]{1,0:T(8,128)(2,1)}, bf16[128,1536]{1,0:T(8,128)(2,1)S(1)}, u32[]{:S(2)}, u32[]{:S(2)}) collective-permute-start(bf16[128,1536]{1,0:T(8,128)(2,1)} %get-tuple-element.449), channel_id=1, source_target_pairs={{8,0},{16,8},{24,16},{28,24},{20,28},{12,20},{4,12},{0,4},{9,1},{1... | collective-permute-start | bytes 1179656 | tf_op jit(solution)/shard_map/ppermute | solution.py:1134
  287.5 19.5 %collective-permute-start.54 = (bf16[256,1536]{1,0:T(8,128)(2,1)S(1)}, bf16[256,1536]{1,0:T(8,128)(2,1)S(1)}, u32[]{:S(2)}, u32[]{:S(2)}) collective-permute-start(bf16[256,1536]{1,0:T(8,128)(2,1)S(1)} %copy-done.37), channel_id=1, source_target_pairs={{0,1},{1,0},{2,3},{3,2},{4,5},{5,4},{6,7},{7,6},{8,9},{9,8},{10,11... | collective-permute-start | bytes 2359304 | tf_op jit(solution)/shard_map/ppermute | solution.py:1090
  288.5 19.3 %collective-permute-start.55 = (bf16[256,1536]{1,0:T(8,128)(2,1)S(1)}, bf16[256,1536]{1,0:T(8,128)(2,1)S(1)}, u32[]{:S(2)}, u32[]{:S(2)}) collective-permute-start(bf16[256,1536]{1,0:T(8,128)(2,1)S(1)} %get-tuple-element.456), channel_id=1, source_target_pairs={{0,8},{8,16},{16,24},{24,28},{28,20},{20,12},{12,4},{4,0},{1,9},{9... | collective-permute-start | bytes 2359304 | tf_op jit(solution)/shard_map/ppermute | solution.py:1140
  289.9 19.0 %collective-permute-start.56 = (bf16[256,1536]{1,0:T(8,128)(2,1)S(1)}, bf16[256,1536]{1,0:T(8,128)(2,1)S(1)}, u32[]{:S(2)}, u32[]{:S(2)}) collective-permute-start(bf16[256,1536]{1,0:T(8,128)(2,1)S(1)} %get-tuple-element.457), channel_id=1, source_target_pairs={{8,0},{16,8},{24,16},{28,24},{20,28},{12,20},{4,12},{0,4},{9,1},{1... | collective-permute-start | bytes 2359304 | tf_op jit(solution)/shard_map/ppermute | solution.py:1140
  310.3 27.9 %collective-permute-start.59 = (bf16[256,1536]{1,0:T(8,128)(2,1)}, bf16[256,1536]{1,0:T(8,128)(2,1)S(1)}, u32[]{:S(2)}, u32[]{:S(2)}) collective-permute-start(bf16[256,1536]{1,0:T(8,128)(2,1)} %get-tuple-element.472), channel_id=1, source_target_pairs={{0,8},{8,16},{16,24},{24,28},{28,20},{20,12},{12,4},{4,0},{1,9},{9... | collective-permute-start | bytes 2359304 | tf_op jit(solution)/shard_map/ppermute | solution.py:1140
  311.9 26.3 %collective-permute-start.60 = (bf16[256,1536]{1,0:T(8,128)(2,1)}, bf16[256,1536]{1,0:T(8,128)(2,1)S(1)}, u32[]{:S(2)}, u32[]{:S(2)}) collective-permute-start(bf16[256,1536]{1,0:T(8,128)(2,1)} %get-tuple-element.473), channel_id=1, source_target_pairs={{8,0},{16,8},{24,16},{28,24},{20,28},{12,20},{4,12},{0,4},{9,1},{1... | collective-permute-start | bytes 2359304 | tf_op jit(solution)/shard_map/ppermute | solution.py:1140
  312.5 25.7 %collective-permute-start.61 = (bf16[512,768]{1,0:T(8,128)(2,1)}, bf16[512,768]{1,0:T(8,128)(2,1)}, u32[]{:S(2)}, u32[]{:S(2)}) collective-permute-start(bf16[512,768]{1,0:T(8,128)(2,1)} %add_convert_fusion.1), channel_id=1, source_target_pairs={{0,1},{1,0},{2,3},{3,2},{4,5},{5,4},{6,7},{7,6},{8,9},{9,8},{10,11... | collective-permute-start | bytes 2359304 | tf_op jit(solution)/shard_map/ppermute | solution.py:1090
  332.1 16.2 %collective-permute-start.62 = (bf16[8,48,1536]{2,1,0:T(8,128)(2,1)}, bf16[8,48,1536]{2,1,0:T(8,128)(2,1)S(1)}, u32[]{:S(2)}, u32[]{:S(2)}) collective-permute-start(bf16[8,48,1536]{2,1,0:T(8,128)(2,1)} %get-tuple-element.489), channel_id=1, source_target_pairs={{0,2},{2,0},{1,3},{3,1},{4,6},{6,4},{5,7},{7,5},{8,10},{10,8},{9,1... | collective-permute-start | bytes 3538952 | tf_op jit(solution)/shard_map/ppermute | solution.py:1093
  339.9 20.1 %collective-permute-start.63 = (bf16[256,1536]{1,0:T(8,128)(2,1)}, bf16[256,1536]{1,0:T(8,128)(2,1)S(1)}, u32[]{:S(2)}, u32[]{:S(2)}) collective-permute-start(bf16[256,1536]{1,0:T(8,128)(2,1)} %get-tuple-element.490), channel_id=1, source_target_pairs={{0,8},{8,16},{16,24},{24,28},{28,20},{20,12},{12,4},{4,0},{1,9},{9... | collective-permute-start | bytes 2359304 | tf_op jit(solution)/shard_map/ppermute | solution.py:1140
  341.3 20.0 %collective-permute-start.64 = (bf16[256,1536]{1,0:T(8,128)(2,1)}, bf16[256,1536]{1,0:T(8,128)(2,1)}, u32[]{:S(2)}, u32[]{:S(2)}) collective-permute-start(bf16[256,1536]{1,0:T(8,128)(2,1)} %get-tuple-element.491), channel_id=1, source_target_pairs={{8,0},{16,8},{24,16},{28,24},{20,28},{12,20},{4,12},{0,4},{9,1},{1... | collective-permute-start | bytes 2359304 | tf_op jit(solution)/shard_map/ppermute | solution.py:1140
  367.7 7.3 %collective-permute-start.66 = (bf16[48,2176]{1,0:T(8,128)(2,1)S(1)}, bf16[48,2176]{1,0:T(8,128)(2,1)S(1)}, u32[]{:S(2)}, u32[]{:S(2)}) collective-permute-start(bf16[48,2176]{1,0:T(8,128)(2,1)S(1)} %get-tuple-element.495), channel_id=1, source_target_pairs={{0,8},{8,16},{16,24},{24,28},{28,20},{20,12},{12,4},{4,0},{1,9},{9... | collective-permute-start | bytes 626696 | tf_op jit(solution)/shard_map/ppermute | solution.py:1398
  376.9 10.6 %collective-permute-start.68 = (bf16[48,4352]{1,0:T(8,128)(2,1)S(1)}, bf16[48,4352]{1,0:T(8,128)(2,1)S(1)}, u32[]{:S(2)}, u32[]{:S(2)}) collective-permute-start(bf16[48,4352]{1,0:T(8,128)(2,1)S(1)} %get-tuple-element.500), channel_id=1, source_target_pairs={{0,8},{8,16},{16,24},{24,28},{28,20},{20,12},{12,4},{4,0},{1,9},{9... | collective-permute-start | bytes 1253384 | tf_op jit(solution)/shard_map/ppermute | solution.py:1409
  377.7 10.4 %collective-permute-start.69 = (bf16[48,4352]{1,0:T(8,128)(2,1)S(1)}, bf16[48,4352]{1,0:T(8,128)(2,1)S(1)}, u32[]{:S(2)}, u32[]{:S(2)}) collective-permute-start(bf16[48,4352]{1,0:T(8,128)(2,1)S(1)} %get-tuple-element.501), channel_id=1, source_target_pairs={{8,0},{16,8},{24,16},{28,24},{20,28},{12,20},{4,12},{0,4},{9,1},{1... | collective-permute-start | bytes 1253384 | tf_op jit(solution)/shard_map/ppermute | solution.py:1410
  380.2 19.9 %collective-permute-start.72 = (bf16[256,1536]{1,0:T(8,128)(2,1)S(1)}, bf16[256,1536]{1,0:T(8,128)(2,1)S(1)}, u32[]{:S(2)}, u32[]{:S(2)}) collective-permute-start(bf16[256,1536]{1,0:T(8,128)(2,1)S(1)} %get-tuple-element.551), channel_id=1, source_target_pairs={{0,1},{1,0},{2,3},{3,2},{4,5},{5,4},{6,7},{7,6},{8,9},{9,8},{10,11... | collective-permute-start | bytes 2359304 | tf_op jit(solution)/shard_map/ppermute | solution.py:1090
  390.3 9.4 %collective-permute-start.70 = (bf16[48,4352]{1,0:T(8,128)(2,1)S(1)}, bf16[48,4352]{1,0:T(8,128)(2,1)S(1)}, u32[]{:S(2)}, u32[]{:S(2)}) collective-permute-start(bf16[48,4352]{1,0:T(8,128)(2,1)S(1)} %get-tuple-element.504), channel_id=1, source_target_pairs={{0,8},{8,16},{16,24},{24,28},{28,20},{20,12},{12,4},{4,0},{1,9},{9... | collective-permute-start | bytes 1253384 | tf_op jit(solution)/shard_map/ppermute | solution.py:1409
  390.9 9.1 %collective-permute-start.71 = (bf16[48,4352]{1,0:T(8,128)(2,1)S(1)}, bf16[48,4352]{1,0:T(8,128)(2,1)S(1)}, u32[]{:S(2)}, u32[]{:S(2)}) collective-permute-start(bf16[48,4352]{1,0:T(8,128)(2,1)S(1)} %get-tuple-element.505), channel_id=1, source_target_pairs={{8,0},{16,8},{24,16},{28,24},{20,28},{12,20},{4,12},{0,4},{9,1},{1... | collective-permute-start | bytes 1253384 | tf_op jit(solution)/shard_map/ppermute | solution.py:1410
  401.7 8.6 %collective-permute-start.73 = (bf16[48,4352]{1,0:T(8,128)(2,1)}, bf16[48,4352]{1,0:T(8,128)(2,1)}, u32[]{:S(2)}, u32[]{:S(2)}) collective-permute-start(bf16[48,4352]{1,0:T(8,128)(2,1)} %get-tuple-element.511), channel_id=1, source_target_pairs={{0,8},{8,16},{16,24},{24,28},{28,20},{20,12},{12,4},{4,0},{1,9},{9... | collective-permute-start | bytes 1253384 | tf_op jit(solution)/shard_map/ppermute | solution.py:1409
  402.3 8.4 %collective-permute-start.74 = (bf16[48,4352]{1,0:T(8,128)(2,1)}, bf16[48,4352]{1,0:T(8,128)(2,1)}, u32[]{:S(2)}, u32[]{:S(2)}) collective-permute-start(bf16[48,4352]{1,0:T(8,128)(2,1)} %get-tuple-element.512), channel_id=1, source_target_pairs={{8,0},{16,8},{24,16},{28,24},{20,28},{12,20},{4,12},{0,4},{9,1},{1... | collective-permute-start | bytes 1253384 | tf_op jit(solution)/shard_map/ppermute | solution.py:1410
  420.5 11.9 %collective-permute-start.76 = (bf16[48,4224]{1,0:T(8,128)(2,1)S(1)}, bf16[48,4224]{1,0:T(8,128)(2,1)S(1)}, u32[]{:S(2)}, u32[]{:S(2)}) collective-permute-start(bf16[48,4224]{1,0:T(8,128)(2,1)S(1)} %slice_dynamic-update-slice_fusion.refs_0_), channel_id=1, source_target_pairs={{0,8},{8,16},{16,24},{24,28},{28,20},{20,12},{12,4},{4,0},{1,9},{9... | collective-permute-start | bytes 1216520 | tf_op jit(solution)/shard_map/ppermute | solution.py:1156
  421.1 11.6 %collective-permute-start.77 = (bf16[48,4224]{1,0:T(8,128)(2,1)S(1)}, bf16[48,4224]{1,0:T(8,128)(2,1)S(1)}, u32[]{:S(2)}, u32[]{:S(2)}) collective-permute-start(bf16[48,4224]{1,0:T(8,128)(2,1)S(1)} %slice_dynamic-update-slice_fusion.refs_0_), channel_id=1, source_target_pairs={{8,0},{16,8},{24,16},{28,24},{20,28},{12,20},{4,12},{0,4},{9,1},{1... | collective-permute-start | bytes 1216520 | tf_op jit(solution)/shard_map/ppermute | solution.py:1157
  432.6 11.8 %collective-permute-start.78 = (bf16[48,4224]{1,0:T(8,128)(2,1)S(1)}, bf16[48,4224]{1,0:T(8,128)(2,1)S(1)}, u32[]{:S(2)}, u32[]{:S(2)}) collective-permute-start(bf16[48,4224]{1,0:T(8,128)(2,1)S(1)} %collective-permute-done.76.refs_1_), channel_id=1, source_target_pairs={{0,8},{8,16},{16,24},{24,28},{28,20},{20,12},{12,4},{4,0},{1,9},{9... | collective-permute-start | bytes 1216520 | tf_op jit(solution)/shard_map/ppermute | solution.py:1156
  433.5 11.8 %collective-permute-start.79 = (bf16[48,4224]{1,0:T(8,128)(2,1)S(1)}, bf16[48,4224]{1,0:T(8,128)(2,1)S(1)}, u32[]{:S(2)}, u32[]{:S(2)}) collective-permute-start(bf16[48,4224]{1,0:T(8,128)(2,1)S(1)} %collective-permute-done.77.refs_2_), channel_id=1, source_target_pairs={{8,0},{16,8},{24,16},{28,24},{20,28},{12,20},{4,12},{0,4},{9,1},{1... | collective-permute-start | bytes 1216520 | tf_op jit(solution)/shard_map/ppermute | solution.py:1157
  445.3 7.9 %collective-permute-start.80 = (bf16[48,4224]{1,0:T(8,128)(2,1)S(1)}, bf16[48,4224]{1,0:T(8,128)(2,1)S(1)}, u32[]{:S(2)}, u32[]{:S(2)}) collective-permute-start(bf16[48,4224]{1,0:T(8,128)(2,1)S(1)} %collective-permute-done.78.refs_3_), channel_id=1, source_target_pairs={{0,8},{8,16},{16,24},{24,28},{28,20},{20,12},{12,4},{4,0},{1,9},{9... | collective-permute-start | bytes 1216520 | tf_op jit(solution)/shard_map/ppermute | solution.py:1156
  446.8 7.9 %collective-permute-start.81 = (bf16[48,4224]{1,0:T(8,128)(2,1)S(1)}, bf16[48,4224]{1,0:T(8,128)(2,1)S(1)}, u32[]{:S(2)}, u32[]{:S(2)}) collective-permute-start(bf16[48,4224]{1,0:T(8,128)(2,1)S(1)} %collective-permute-done.79.refs_4_), channel_id=1, source_target_pairs={{8,0},{16,8},{24,16},{28,24},{20,28},{12,20},{4,12},{0,4},{9,1},{1... | collective-permute-start | bytes 1216520 | tf_op jit(solution)/shard_map/ppermute | solution.py:1157
  447.4 9.9 %collective-permute-start.84 = (bf16[48,4224]{1,0:T(8,128)(2,1)S(1)}, bf16[48,4224]{1,0:T(8,128)(2,1)S(1)}, u32[]{:S(2)}, u32[]{:S(2)}) collective-permute-start(bf16[48,4224]{1,0:T(8,128)(2,1)S(1)} %slice_dynamic-update-slice_fusion.refs_0_), channel_id=1, source_target_pairs={{0,2},{2,0},{1,3},{3,1},{4,6},{6,4},{5,7},{7,5},{8,10},{10,8},{9,1... | collective-permute-start | bytes 1216520 | tf_op jit(solution)/shard_map/ppermute | solution.py:1093
  447.4 10.5 %collective-permute-start.85 = (bf16[48,4224]{1,0:T(8,128)(2,1)S(1)}, bf16[48,4224]{1,0:T(8,128)(2,1)S(1)}, u32[]{:S(2)}, u32[]{:S(2)}) collective-permute-start(bf16[48,4224]{1,0:T(8,128)(2,1)S(1)} %collective-permute-done.76.refs_1_), channel_id=1, source_target_pairs={{0,2},{2,0},{1,3},{3,1},{4,6},{6,4},{5,7},{7,5},{8,10},{10,8},{9,1... | collective-permute-start | bytes 1216520 | tf_op jit(solution)/shard_map/ppermute | solution.py:1093
  451.6 8.0 %collective-permute-start.86 = (bf16[48,4224]{1,0:T(8,128)(2,1)S(1)}, bf16[48,4224]{1,0:T(8,128)(2,1)S(1)}, u32[]{:S(2)}, u32[]{:S(2)}) collective-permute-start(bf16[48,4224]{1,0:T(8,128)(2,1)S(1)} %collective-permute-done.77.refs_2_), channel_id=1, source_target_pairs={{0,2},{2,0},{1,3},{3,1},{4,6},{6,4},{5,7},{7,5},{8,10},{10,8},{9,1... | collective-permute-start | bytes 1216520 | tf_op jit(solution)/shard_map/ppermute | solution.py:1093
  457.2 7.7 %collective-permute-start.83 = (bf16[48,2176]{1,0:T(8,128)(2,1)S(1)}, bf16[48,2176]{1,0:T(8,128)(2,1)S(1)}, u32[]{:S(2)}, u32[]{:S(2)}) collective-permute-start(bf16[48,2176]{1,0:T(8,128)(2,1)S(1)} %slice.112), channel_id=1, source_target_pairs={{8,0},{16,8},{24,16},{28,24},{20,28},{12,20},{4,12},{0,4},{9,1},{1... | collective-permute-start | bytes 626696 | tf_op jit(solution)/shard_map/ppermute | solution.py:1157
  (109 other events, 935.4 us)

commit v3 on v2

--- a/solution.py
+++ b/solution.py
@@ -1372,7 +1372,9 @@
     )
     for step in range(half_ring - 3, 0, -1):
         sent = ring_add(out_parts, step, got)
-        projected_grads, sent = lax.optimization_barrier((projected_grads, sent))
+        projected_grads, attn_grads, sent = lax.optimization_barrier(
+            (projected_grads, attn_grads, sent)
+        )
         got = ring_send(sent)
 
     mine_out, theirs_out = dense_grad(info, chip_places, unit, 1, head_out, attn_grads)
@@ -1387,9 +1389,7 @@
         (grad_gain_one, grad_gain_two, grad_route),
     )
     wide = own_cols + 128
-    mine_qkv, theirs_qkv, theirs_out, got = lax.optimization_barrier(
-        (mine_qkv, theirs_qkv, theirs_out, got)
-    )
+    mine_qkv, theirs_qkv, got = lax.optimization_barrier((mine_qkv, theirs_qkv, got))
     theirs_qkv = to_core(theirs_qkv)
     pairs = ((mine_qkv, theirs_qkv), (mine_out, theirs_out))
     every = mine_qkv.shape[2] + mine_out.shape[2]

time: 481 us -> 465 us (0.967)
  local copies, waits for them, and re-layouts: 33.1 us -> 26.5 us
  waiting for transfers between devices: 144 us -> 139 us
    ppermute x6, waiting for transfers between devices: 12.9 us -> 5.72 us  [ring_send(): lax.ppermute(sent[0], 'chip', ahead)]
    unnamed x175 -> x169, local copies, waits for them, and re-layouts: 22 us -> 16.5 us
  transfers between devices with their start and end apart: 93 -> 93, of which waited for: 47 -> 50; matrix products, arithmetic and copies ran while one was open for 7% -> 7% of each run, Pallas kernels for 35% -> 36%
where the time goes in v3:
time: 465 us; the launch traced here: 456 us
  Pallas kernels  184 us (40%)
  waiting for transfers between devices  139 us (30%)
  starting transfers between devices  82.3 us (18%)
  local copies, waits for them, and re-layouts  26.5 us (6%)
  other arithmetic  21 us (5%)
    pallas_call x5, Pallas kernels, run_experts(): pl.pallas_call(partial(expert_kernel, slots, *layouts), in_specs=[pl.Bloc...  65 us
    pallas_call x3, Pallas kernels, weight_grad(): pl.pallas_call(partial(weight_grad_kernel, heights, a_at, b_at, scale, by...  42.3 us
    ppermute x11, waiting for transfers between devices, to_shard(): lax.ppermute(value, 'shard', [(i, (i + step) % shards) for i in range(sha...  41.4 us
    ppermute x3, waiting for transfers between devices, body(): right = lax.ppermute(right, 'chip', ahead)  20.5 us
    ppermute x4, waiting for transfers between devices, plane_gather(): right = lax.ppermute(right, 'chip', ahead)  17.1 us
    unnamed x169, local copies, waits for them, and re-layouts  16.5 us
    ppermute x11, starting transfers between devices, to_shard(): lax.ppermute(value, 'shard', [(i, (i + step) % shards) for i in range(sha...  15.3 us
    pallas_call x1, Pallas kernels, attend_back(): pl.pallas_call(partial(attend_back_kernel, shards), grid=(pairs,), in_spe...  11.5 us
  transfers between devices with their start and end apart: 93, of which 50 were waited for; matrix products, arithmetic and copies ran while one was open for 7% of the time, Pallas kernels for 36%

profile of v3, /device:TPU:0, one launch (start us, length us, event | category | flops | bytes accessed | tf_op | source)
XLA Modules:
  0.0 456.4 jit_solution(12183277044082059244)
XLA Ops:
  2.4 3.0 collective-permute-start
  6.2 3.4 collective-permute-done
  9.6 2.2 collective-permute-start.1
  15.1 2.1 collective-permute-done.2.refs_4_.refs_5_
  20.0 1.6 collective-permute-start.6
  21.6 4.7 %collective-permute-done.6 = bf16[55,256]{1,0:T(8,128)(2,1)S(1)} collective-permute-done((bf16[55,256]{1,0:T(8,128)(2,1)S(1)}, bf16[55,256]{1,0:T(8,128)(2,1)S(1)}, u32[]{:S(2)}, u32[]{:S(2)}) %collective-permute-start.6) | collective-permute-done | bytes 28192 | tf_op jit(solution)/shard_map/ppermute | solution.py:1090
  26.3 1.8 collective-permute-start.7
  28.4 1.7 collective-permute-start.18
  31.7 1.7 collective-permute-done.8.refs_8_.refs_5_
  33.5 1.6 collective-permute-start.9
  36.9 3.2 collective-permute-done.9.refs_9_.refs_4_.refs_5_
  43.0 5.7 %collective-permute-done.18.refs_9_.refs_12_.refs_6_ = bf16[512,768]{1,0:T(8,128)(2,1)} collective-permute-done((bf16[512,768]{1,0:T(8,128)(2,1)}, bf16[512,768]{1,0:T(8,128)(2,1)}, u32[]{:S(2)}, u32[]{:S(2)}) %collective-permute-start.18) | collective-permute-done | bytes 786464 | tf_op jit(solution)/shard_map/ppermute | solution.py:1090
  54.5 7.9 %shard_map.196 = (bf16[512,1536]{1,0:T(8,128)(2,1)}, bf16[1536,1280]{1,0:T(8,128)(2,1)}, f32[512,1280]{1,0:T(8,128)}, bf16[512,1536]{1,0:T(8,128)(2,1)}) custom-call(s32[12]{0:T(128)} %pad_add_fusion.info, s32[16]{0:T(128)} %add_add_fusion.places, bf16[768,2560]{1,0:T(8,128)(2,1)} %own_ref.1, f32[1,1536]{1,0:T(1,128)} %bitcast.64, bf16[256,1536]{1,0:T(8,128)(2,1)} %refs_0_, ...), custom_call_target="tpu_custom_call" | custom-call | flops 2013265920 | bytes 9699328 | tf_op jit(solution)/shard_map/pallas_call | solution.py:857
  62.5 3.4 collective-permute-done.19.refs_2_.refs_6_
  66.3 1.9 collective-permute-start.22
  68.5 1.7 copy-done.31
  70.3 6.7 %shard_map.197 = (bf16[512,1280]{1,0:T(8,128)(2,1)S(1)}, bf16[4,512,1536]{2,1,0:T(8,128)(2,1)S(1)}, bf16[512,768]{1,0:T(8,128)(2,1)S(1)}) custom-call(f32[512,1280]{1,0:T(8,128)S(1)} %copy-done.31, f32[512,1280]{1,0:T(8,128)S(1)} %copy-done.31, f32[512,1280]{1,0:T(8,128)S(1)} %copy-done.31, f32[512,128]{1,0:T(8,128)S(1)} %get-tuple-element.566.cos_ref, ...), custom_call_target="tpu_custom_call" | custom-call | flops 3221225472 | bytes 6291456 | tf_op jit(solution)/shard_map/pallas_call | solution.py:137
  82.0 1.6 collective-permute-start.24
  86.3 12.1 %collective-permute-done.24 = bf16[256,1536]{1,0:T(8,128)(2,1)} collective-permute-done((bf16[256,1536]{1,0:T(8,128)(2,1)S(1)}, bf16[256,1536]{1,0:T(8,128)(2,1)}, u32[]{:S(2)}, u32[]{:S(2)}) %collective-permute-start.24) | collective-permute-done | bytes 786464 | tf_op jit(solution)/shard_map/ppermute | solution.py:1090
  101.8 1.6 collective-permute-start.31
  105.7 9.8 %shard_map.198 = (bf16[256,2048]{1,0:T(8,128)(2,1)}, bf16[256,1024]{1,0:T(8,128)(2,1)}, bf16[256,1536]{1,0:T(8,128)(2,1)}, f32[8,256]{1,0:T(8,128)}, f32[256,128]{1,0:T(8,128)}) custom-call(s32[12]{0:T(128)} %pad_add_fusion.info, bf16[256,1536]{1,0:T(8,128)(2,1)} %copy-done.7, bf16[256,1536]{1,0:T(8,128)(2,1)} %upstream.1, bf16[64,1280]{1,0:T(8,128)(2,1)} %copy-done.62, ...), custom_call_target="tpu_custom_call" | custom-call | flops 4026531840 | bytes 14155776 | tf_op jit(solution)/shard_map/pallas_call | solution.py:435
  115.5 5.6 %collective-permute-done.31.refs_0_.refs_1_ = bf16[256,1536]{1,0:T(8,128)(2,1)S(1)} collective-permute-done((bf16[256,1536]{1,0:T(8,128)(2,1)S(1)}, bf16[256,1536]{1,0:T(8,128)(2,1)S(1)}, u32[]{:S(2)}, u32[]{:S(2)}) %collective-permute-start.31) | collective-permute-done | bytes 786464 | tf_op jit(solution)/shard_map/ppermute | solution.py:1124
  124.7 15.0 %shard_map.199 = (bf16[512,2048]{1,0:T(8,128)(2,1)}, bf16[512,1024]{1,0:T(8,128)(2,1)}, bf16[256,1536]{1,0:T(8,128)(2,1)}, bf16[256,1536]{1,0:T(8,128)(2,1)}, f3...) custom-call(s32[12]{0:T(128)} %pad_add_fusion.info, bf16[256,1536]{1,0:T(8,128)(2,1)} %copy-done.71, ...), custom_call_target="tpu_custom_call" | custom-call | flops 8053063680 | bytes 18874368 | tf_op jit(solution)/shard_map/pallas_call | solution.py:435
  140.4 2.2 collective-permute-done.34.refs_1_.refs_4_
  142.6 1.7 collective-permute-start.35
  145.1 15.0 %shard_map.200 = (bf16[512,2048]{1,0:T(8,128)(2,1)}, bf16[512,1024]{1,0:T(8,128)(2,1)}, bf16[256,1536]{1,0:T(8,128)(2,1)}, bf16[256,1536]{1,0:T(8,128)(2,1)}, f3...) custom-call(s32[12]{0:T(128)} %pad_add_fusion.info, bf16[256,1536]{1,0:T(8,128)(2,1)} %copy-done.73, ...), custom_call_target="tpu_custom_call" | custom-call | flops 8053063680 | bytes 18874368 | tf_op jit(solution)/shard_map/pallas_call | solution.py:435
  160.1 2.3 collective-permute-done.36.refs_1_.refs_6_
  169.0 15.0 %shard_map.201 = (bf16[512,2048]{1,0:T(8,128)(2,1)}, bf16[512,1024]{1,0:T(8,128)(2,1)}, bf16[256,1536]{1,0:T(8,128)(2,1)}, bf16[256,1536]{1,0:T(8,128)(2,1)}, f3...) custom-call(s32[12]{0:T(128)} %pad_add_fusion.info, bf16[256,1536]{1,0:T(8,128)(2,1)} %copy-done.63, ...), custom_call_target="tpu_custom_call" | custom-call | flops 8053063680 | bytes 18874368 | tf_op jit(solution)/shard_map/pallas_call | solution.py:435
  184.8 10.1 %shard_map.202 = (bf16[256,2048]{1,0:T(8,128)(2,1)}, bf16[256,1024]{1,0:T(8,128)(2,1)}, bf16[128,1536]{1,0:T(8,128)(2,1)}, bf16[128,1536]{1,0:T(8,128)(2,1)}, f3...) custom-call(s32[12]{0:T(128)} %pad_add_fusion.info, ...), custom_call_target="tpu_custom_call" | custom-call | flops 4026531840 | bytes 14155776 | tf_op jit(solution)/shard_map/pallas_call | solution.py:435
  197.1 13.5 %shard_map.203 = (bf16[768,1024]{1,0:T(8,128)(2,1)}, bf16[768,1024]{1,0:T(8,128)(2,1)}) custom-call(s32[12]{0:T(128)} %pad_add_fusion.info, bf16[256,1536]{1,0:T(8,128)(2,1)} %copy-done.7, bf16[256,1536]{1,0:T(8,128)(2,1)} %copy-done.71, bf16[256,1536]{1,0:T(8,128)(2,1)} %copy-done.72, bf16[256,1536]{1,0:T(8,128)(2,1)} %copy-done.73, ...), custom_call_target="tpu_custom_call" | custom-call | flops 6442450944 | bytes 13631488 | tf_op jit(solution)/shard_map/pallas_call | solution.py:666
  214.5 2.2 collective-permute-done.46.refs_15_
  216.6 14.8 %shard_map.205 = (bf16[768,1024]{1,0:T(8,128)(2,1)}, bf16[768,1024]{1,0:T(8,128)(2,1)}) custom-call(s32[12]{0:T(128)} %pad_add_fusion.info, bf16[256,1536]{1,0:T(8,128)(2,1)} %copy-done.7, bf16[256,1536]{1,0:T(8,128)(2,1)} %copy-done.71, bf16[256,1536]{1,0:T(8,128)(2,1)} %copy-done.72, bf16[256,1536]{1,0:T(8,128)(2,1)} %copy-done.73, ...), custom_call_target="tpu_custom_call" | custom-call | flops 6442450944 | bytes 13631488 | tf_op jit(solution)/shard_map/pallas_call | solution.py:666
  237.5 3.3 all-to-all-start
  240.9 1.6 collective-permute-start.53
  242.5 11.1 %shard_map.207 = (bf16[256,1536]{1,0:T(8,128)(2,1)}, bf16[256,1536]{1,0:T(8,128)(2,1)}, bf16[256,1536]{1,0:T(8,128)(2,1)}, bf16[256,1536]{1,0:T(8,128)(2,1)}, bf...) custom-call(s32[12]{0:T(128)} %pad_add_fusion.info, ...), custom_call_target="tpu_custom_call" | custom-call | flops 6442450944 | bytes 13631488 | tf_op jit(solution)/shard_map/pallas_call | solution.py:504
  255.3 1.6 collective-permute-start.49
  261.2 14.0 %shard_map.211 = (bf16[512,768]{1,0:T(8,128)(2,1)}, bf16[512,768]{1,0:T(8,128)(2,1)}, bf16[512,768]{1,0:T(8,128)(2,1)}, bf16[512,768]{1,0:T(8,128)(2,1)}) custom-call(s32[12]{0:T(128)} %pad_add_fusion.info, bf16[256,1024]{1,0:T(8,128)(2,1)} %get-tuple-element.427.refs_0_, bf16[512,1024]{1,0:T(8,128)(2,1)} %get-tuple-element.428.refs_1_, ...), custom_call_target="tpu_custom_call" | custom-call | flops 6442450944 | bytes 13631488 | tf_op jit(solution)/shard_map/pallas_call | solution.py:666
  275.2 1.7 collective-permute-start.51
  277.9 5.5 %shard_map.212 = (bf16[256,1536]{1,0:T(8,128)(2,1)}, f32[256,1536]{1,0:T(8,128)}, f32[1,1536]{1,0:T(1,128)}) custom-call(bf16[256,1536]{1,0:T(8,128)(2,1)} %get-tuple-element.321.own, bf16[256,1536]{1,0:T(8,128)(2,1)} %copy-done.57, bf16[256,1536]{1,0:T(8,128)(2,1)} %collective-permute-done.50.left, f32[256,1536]{1,0:T(8,128)} %copy-done.11, ...), custom_call_target="tpu_custom_call" | custom-call | tf_op jit(solution)/shard_map/pallas_call | solution.py:932
  291.5 13.8 %collective-permute-done.54.refs_1_ = bf16[256,1536]{1,0:T(8,128)(2,1)S(1)} collective-permute-done((bf16[256,1536]{1,0:T(8,128)(2,1)S(1)}, bf16[256,1536]{1,0:T(8,128)(2,1)S(1)}, u32[]{:S(2)}, u32[]{:S(2)}) %collective-permute-start.54) | collective-permute-done | bytes 786464 | tf_op jit(solution)/shard_map/ppermute | solution.py:1090
  310.8 11.5 %shard_map.214 = (bf16[512,1280]{1,0:T(8,128)(2,1)S(1)}, bf16[512,1536]{1,0:T(8,128)(2,1)S(1)}) custom-call(s32[12]{0:T(128)S(1)} %copy-done.29, bf16[512,1280]{1,0:T(8,128)(2,1)S(1)} %copy-done.40, bf16[512,1280]{1,0:T(8,128)(2,1)S(1)} %copy-done.40, bf16[512,1280]{1,0:T(8,128)(2,1)S(1)} %copy-done.40, bf16[4,512,1536]{2,1,0:T(8,128)(2,1)} %copy-done.38, ...), custom_call_target="tpu_custom_call" | custom-call | flops 7650410496 | bytes 6291456 | tf_op jit(solution)/shard_map/pallas_call | solution.py:261
  322.3 2.4 shard_map.216
  330.4 4.8 %shard_map.218 = (bf16[8,48,1536]{2,1,0:T(8,128)(2,1)}, bf16[8,48,1536]{2,1,0:T(8,128)(2,1)}) custom-call(s32[12]{0:T(128)} %pad_add_fusion.info, s32[8]{0:T(128)} %fusion.9.places, bf16[512,768]{1,0:T(8,128)(2,1)} %copy-done.41, bf16[512,1536]{1,0:T(8,128)(2,1)} %copy-done.43), custom_call_target="tpu_custom_call" | custom-call | flops 3623878656 | bytes 2359296 | tf_op jit(solution)/shard_map/pallas_call | solution.py:771
  335.2 6.5 %shard_map.219 = (bf16[8,48,2816]{2,1,0:T(8,128)(2,1)}, bf16[8,48,2816]{2,1,0:T(8,128)(2,1)}) custom-call(s32[12]{0:T(128)} %pad_add_fusion.info, s32[8]{0:T(128)} %fusion.9.places, bf16[512,1536]{1,0:T(8,128)(2,1)} %get-tuple-element.484.refs_0_, bf16[512,1280]{1,0:T(8,128)(2,1)} %copy-done.37, f32[1,1536]{1,0:T(1,128)} %copy-done.42, ...), custom_call_target="tpu_custom_call" | custom-call | flops 6039797760 | bytes 2883584 | tf_op jit(solution)/shard_map/pallas_call | solution.py:771
  341.7 3.1 collective-permute-done.62
  346.8 5.6 %collective-permute-done.65.refs_3_ = bf16[8,48,1536]{2,1,0:T(8,128)(2,1)S(1)} collective-permute-done((bf16[8,48,1536]{2,1,0:T(8,128)(2,1)}, bf16[8,48,1536]{2,1,0:T(8,128)(2,1)S(1)}, u32[]{:S(2)}, u32[]{:S(2)}) %collective-permute-start.65) | collective-permute-done | bytes 1179680 | tf_op jit(solution)/shard_map/ppermute | solution.py:1093
  352.4 2.0 copy-done
  356.9 5.2 %collective-permute-done.66.refs_4_ = bf16[48,2176]{1,0:T(8,128)(2,1)S(1)} collective-permute-done((bf16[48,2176]{1,0:T(8,128)(2,1)S(1)}, bf16[48,2176]{1,0:T(8,128)(2,1)S(1)}, u32[]{:S(2)}, u32[]{:S(2)}) %collective-permute-start.66) | collective-permute-done | bytes 208928 | tf_op jit(solution)/shard_map/ppermute | solution.py:1398
  368.0 6.5 %collective-permute-done.68.refs_4_ = bf16[48,4352]{1,0:T(8,128)(2,1)S(1)} collective-permute-done((bf16[48,4352]{1,0:T(8,128)(2,1)S(1)}, bf16[48,4352]{1,0:T(8,128)(2,1)S(1)}, u32[]{:S(2)}, u32[]{:S(2)}) %collective-permute-start.68) | collective-permute-done | bytes 417824 | tf_op jit(solution)/shard_map/ppermute | solution.py:1409
  377.8 7.4 %collective-permute-done.70.refs_4_ = bf16[48,4352]{1,0:T(8,128)(2,1)S(1)} collective-permute-done((bf16[48,4352]{1,0:T(8,128)(2,1)S(1)}, bf16[48,4352]{1,0:T(8,128)(2,1)S(1)}, u32[]{:S(2)}, u32[]{:S(2)}) %collective-permute-start.70) | collective-permute-done | bytes 417824 | tf_op jit(solution)/shard_map/ppermute | solution.py:1409
  389.5 6.6 %collective-permute-done.73.refs_4_ = bf16[48,4352]{1,0:T(8,128)(2,1)} collective-permute-done((bf16[48,4352]{1,0:T(8,128)(2,1)}, bf16[48,4352]{1,0:T(8,128)(2,1)}, u32[]{:S(2)}, u32[]{:S(2)}) %collective-permute-start.73) | collective-permute-done | bytes 417824 | tf_op jit(solution)/shard_map/ppermute | solution.py:1409
  397.0 1.6 copy-done.3
  399.8 1.7 shard_map.224
  402.6 2.5 add_convert_fusion
  408.9 1.7 fusion
  410.6 7.8 %collective-permute-done.76.refs_1_ = bf16[48,4224]{1,0:T(8,128)(2,1)S(1)} collective-permute-done((bf16[48,4224]{1,0:T(8,128)(2,1)S(1)}, bf16[48,4224]{1,0:T(8,128)(2,1)S(1)}, u32[]{:S(2)}, u32[]{:S(2)}) %collective-permute-start.76) | collective-permute-done | bytes 405536 | tf_op jit(solution)/shard_map/ppermute | solution.py:1156
  419.4 1.9 collective-permute-start.79
  421.4 2.9 fusion.3
  424.3 6.5 %collective-permute-done.78.refs_3_ = bf16[48,4224]{1,0:T(8,128)(2,1)S(1)} collective-permute-done((bf16[48,4224]{1,0:T(8,128)(2,1)S(1)}, bf16[48,4224]{1,0:T(8,128)(2,1)S(1)}, u32[]{:S(2)}, u32[]{:S(2)}) %collective-permute-start.78) | collective-permute-done | bytes 405536 | tf_op jit(solution)/shard_map/ppermute | solution.py:1156
  433.7 3.7 convert_add_fusion
  437.4 1.7 collective-permute-done.80.refs_0_
  444.6 4.0 shard_map.225
  449.8 1.7 collective-permute-done.91.refs_5_
  451.5 2.9 shard_map.226
  (380 shorter events, 121.8 us)
Async XLA Ops:
  2.4 7.2 %collective-permute-start = (bf16[48,1280]{1,0:T(8,128)(2,1)S(1)}, bf16[48,1280]{1,0:T(8,128)(2,1)S(1)}, u32[]{:S(2)}, u32[]{:S(2)}) collective-permute-start(bf16[48,1280]{1,0:T(8,128)(2,1)S(1)} %pad_maximum_fusion.2), channel_id=1, source_target_pairs={{0,1},{1,0},{2,3},{3,2},{4,5},{5,4},{6,7},{7,6},{8,9},{9,8},{10,11... | collective-permute-start | bytes 368648 | tf_op jit(solution)/shard_map/ppermute | solution.py:1090
  5.4 20.8 %collective-permute-start.5 = (bf16[256,1536]{1,0:T(8,128)(2,1)}, bf16[256,1536]{1,0:T(8,128)(2,1)S(1)}, u32[]{:S(2)}, u32[]{:S(2)}) collective-permute-start(bf16[256,1536]{1,0:T(8,128)(2,1)} %refs_0_), channel_id=1, source_target_pairs={{0,1},{1,0},{2,3},{3,2},{4,5},{5,4},{6,7},{7,6},{8,9},{9,8},{10,11... | collective-permute-start | bytes 2359304 | tf_op jit(solution)/shard_map/ppermute | solution.py:1090
  17.2 9.0 %collective-permute-start.3 = (bf16[64,1280]{1,0:T(8,128)(2,1)}, bf16[64,1280]{1,0:T(8,128)(2,1)S(1)}, u32[]{:S(2)}, u32[]{:S(2)}) collective-permute-start(bf16[64,1280]{1,0:T(8,128)(2,1)} %collective-permute-done.1.refs_3_.refs_4_), channel_id=1, source_target_pairs={{0,8},{8,16},{16,24},{24,28},{28,20},{20,12},{12,4},{4,0},{1,9},{9... | collective-permute-start | bytes 491528 | tf_op jit(solution)/shard_map/ppermute | solution.py:1174
  18.8 7.5 %collective-permute-start.4 = (bf16[64,1280]{1,0:T(8,128)(2,1)}, bf16[64,1280]{1,0:T(8,128)(2,1)S(1)}, u32[]{:S(2)}, u32[]{:S(2)}) collective-permute-start(bf16[64,1280]{1,0:T(8,128)(2,1)} %collective-permute-done.2.refs_4_.refs_5_), channel_id=1, source_target_pairs={{8,0},{16,8},{24,16},{28,24},{20,28},{12,20},{4,12},{0,4},{9,1},{1... | collective-permute-start | bytes 491528 | tf_op jit(solution)/shard_map/ppermute | solution.py:1177
  21.6 11.9 %collective-permute-start.10 = (bf16[64,1280]{1,0:T(8,128)(2,1)S(1)}, bf16[64,1280]{1,0:T(8,128)(2,1)}, u32[]{:S(2)}, u32[]{:S(2)}) collective-permute-start(bf16[64,1280]{1,0:T(8,128)(2,1)S(1)} %fusion.5.refs_2_), channel_id=1, source_target_pairs={{0,2},{2,0},{1,3},{3,1},{4,6},{6,4},{5,7},{7,5},{8,10},{10,8},{9,1... | collective-permute-start | bytes 491528 | tf_op jit(solution)/shard_map/ppermute | solution.py:1093
  28.4 20.4 %collective-permute-start.18 = (bf16[512,768]{1,0:T(8,128)(2,1)}, bf16[512,768]{1,0:T(8,128)(2,1)}, u32[]{:S(2)}, u32[]{:S(2)}) collective-permute-start(bf16[512,768]{1,0:T(8,128)(2,1)} %bitcast.75), channel_id=1, source_target_pairs={{0,1},{1,0},{2,3},{3,2},{4,5},{5,4},{6,7},{7,6},{8,9},{9,8},{10,11... | collective-permute-start | bytes 2359304 | tf_op jit(solution)/shard_map/ppermute | solution.py:1090
  41.5 39.6 %collective-permute-start.21 = (bf16[768,1024]{1,0:T(8,128)(2,1)}, bf16[768,1024]{1,0:T(8,128)(2,1)}, u32[]{:S(2)}, u32[]{:S(2)}) collective-permute-start(bf16[768,1024]{1,0:T(8,128)(2,1)} %bitcast.68), channel_id=1, source_target_pairs={{0,1},{1,0},{2,3},{3,2},{4,5},{5,4},{6,7},{7,6},{8,9},{9,8},{10,11... | collective-permute-start | bytes 4718600 | tf_op jit(solution)/shard_map/ppermute | solution.py:1090
  48.7 17.1 %collective-permute-start.19 = (bf16[256,1536]{1,0:T(8,128)(2,1)S(1)}, bf16[256,1536]{1,0:T(8,128)(2,1)}, u32[]{:S(2)}, u32[]{:S(2)}) collective-permute-start(bf16[256,1536]{1,0:T(8,128)(2,1)S(1)} %copy-done.52), channel_id=1, source_target_pairs={{0,8},{8,16},{16,24},{24,28},{28,20},{20,12},{12,4},{4,0},{1,9},{9... | collective-permute-start | bytes 2359304 | tf_op jit(solution)/shard_map/ppermute | solution.py:1124
  50.1 16.2 %collective-permute-start.20 = (bf16[256,1536]{1,0:T(8,128)(2,1)S(1)}, bf16[256,1536]{1,0:T(8,128)(2,1)}, u32[]{:S(2)}, u32[]{:S(2)}) collective-permute-start(bf16[256,1536]{1,0:T(8,128)(2,1)S(1)} %copy-done.52), channel_id=1, source_target_pairs={{8,0},{16,8},{24,16},{28,24},{20,28},{12,20},{4,12},{0,4},{9,1},{1... | collective-permute-start | bytes 2359304 | tf_op jit(solution)/shard_map/ppermute | solution.py:1124
  66.3 14.7 %collective-permute-start.22 = (bf16[256,1536]{1,0:T(8,128)(2,1)}, bf16[256,1536]{1,0:T(8,128)(2,1)}, u32[]{:S(2)}, u32[]{:S(2)}) collective-permute-start(bf16[256,1536]{1,0:T(8,128)(2,1)} %collective-permute-done.19.refs_2_.refs_6_), channel_id=1, source_target_pairs={{0,8},{8,16},{16,24},{24,28},{28,20},{20,12},{12,4},{4,0},{1,9},{9... | collective-permute-start | bytes 2359304 | tf_op jit(solution)/shard_map/ppermute | solution.py:1124
  68.2 13.7 %collective-permute-start.23 = (bf16[256,1536]{1,0:T(8,128)(2,1)}, bf16[256,1536]{1,0:T(8,128)(2,1)}, u32[]{:S(2)}, u32[]{:S(2)}) collective-permute-start(bf16[256,1536]{1,0:T(8,128)(2,1)} %collective-permute-done.20.refs_3_.refs_7_), channel_id=1, source_target_pairs={{8,0},{16,8},{24,16},{28,24},{20,28},{12,20},{4,12},{0,4},{9,1},{1... | collective-permute-start | bytes 2359304 | tf_op jit(solution)/shard_map/ppermute | solution.py:1124
  82.0 16.5 %collective-permute-start.24 = (bf16[256,1536]{1,0:T(8,128)(2,1)S(1)}, bf16[256,1536]{1,0:T(8,128)(2,1)}, u32[]{:S(2)}, u32[]{:S(2)}) collective-permute-start(bf16[256,1536]{1,0:T(8,128)(2,1)S(1)} %constant_dynamic-slice_fusion.2), channel_id=1, source_target_pairs={{0,1},{1,0},{2,3},{3,2},{4,5},{5,4},{6,7},{7,6},{8,9},{9,8},{10,11... | collective-permute-start | bytes 2359304 | tf_op jit(solution)/shard_map/ppermute | solution.py:1090
  83.6 16.3 %collective-permute-start.25 = (bf16[256,1536]{1,0:T(8,128)(2,1)}, bf16[256,1536]{1,0:T(8,128)(2,1)}, u32[]{:S(2)}, u32[]{:S(2)}) collective-permute-start(bf16[256,1536]{1,0:T(8,128)(2,1)} %collective-permute-done.22.refs_2_.refs_8_), channel_id=1, source_target_pairs={{0,8},{8,16},{16,24},{24,28},{28,20},{20,12},{12,4},{4,0},{1,9},{9... | collective-permute-start | bytes 2359304 | tf_op jit(solution)/shard_map/ppermute | solution.py:1124
  85.1 16.2 %collective-permute-start.26 = (bf16[256,1536]{1,0:T(8,128)(2,1)}, bf16[256,1536]{1,0:T(8,128)(2,1)}, u32[]{:S(2)}, u32[]{:S(2)}) collective-permute-start(bf16[256,1536]{1,0:T(8,128)(2,1)} %collective-permute-done.23.refs_3_.refs_9_), channel_id=1, source_target_pairs={{8,0},{16,8},{24,16},{28,24},{20,28},{12,20},{4,12},{0,4},{9,1},{1... | collective-permute-start | bytes 2359304 | tf_op jit(solution)/shard_map/ppermute | solution.py:1124
  85.8 17.6 %collective-permute-start.29 = (bf16[512,768]{1,0:T(8,128)(2,1)}, bf16[512,768]{1,0:T(8,128)(2,1)S(1)}, u32[]{:S(2)}, u32[]{:S(2)}) collective-permute-start(bf16[512,768]{1,0:T(8,128)(2,1)} %bitcast.76), channel_id=1, source_target_pairs={{0,2},{2,0},{1,3},{3,1},{4,6},{6,4},{5,7},{7,5},{8,10},{10,8},{9,1... | collective-permute-start | bytes 2359304 | tf_op jit(solution)/shard_map/ppermute | solution.py:1093
  85.8 19.9 %collective-permute-start.30 = (bf16[512,768]{1,0:T(8,128)(2,1)}, bf16[512,768]{1,0:T(8,128)(2,1)}, u32[]{:S(2)}, u32[]{:S(2)}) collective-permute-start(bf16[512,768]{1,0:T(8,128)(2,1)} %collective-permute-done.18.refs_9_.refs_12_.refs_6_), channel_id=1, source_target_pairs={{0,2},{2,0},{1,3},{3,1},{4,6},{6,4},{5,7},{7,5},{8,10},{10,8},{9,1... | collective-permute-start | bytes 2359304 | tf_op jit(solution)/shard_map/ppermute | solution.py:1093
  98.4 7.2 %collective-permute-start.27 = (bf16[768,1024]{1,0:T(8,128)(2,1)}, bf16[768,1024]{1,0:T(8,128)(2,1)}, u32[]{:S(2)}, u32[]{:S(2)}) collective-permute-start(bf16[768,1024]{1,0:T(8,128)(2,1)} %bitcast.69), channel_id=1, source_target_pairs={{0,2},{2,0},{1,3},{3,1},{4,6},{6,4},{5,7},{7,5},{8,10},{10,8},{9,1... | collective-permute-start | bytes 4718600 | tf_op jit(solution)/shard_map/ppermute | solution.py:1093
  101.8 19.3 %collective-permute-start.31 = (bf16[256,1536]{1,0:T(8,128)(2,1)S(1)}, bf16[256,1536]{1,0:T(8,128)(2,1)S(1)}, u32[]{:S(2)}, u32[]{:S(2)}) collective-permute-start(bf16[256,1536]{1,0:T(8,128)(2,1)S(1)} %multiply_convert_fusion.refs_0_.second_ref), channel_id=1, source_target_pairs={{0,8},{8,16},{16,24},{24,28},{28,20},{20,12},{12,4},{4,0},{1,9},{9... | collective-permute-start | bytes 2359304 | tf_op jit(solution)/shard_map/ppermute | solution.py:1124
  103.4 19.0 %collective-permute-start.32 = (bf16[256,1536]{1,0:T(8,128)(2,1)S(1)}, bf16[256,1536]{1,0:T(8,128)(2,1)S(1)}, u32[]{:S(2)}, u32[]{:S(2)}) collective-permute-start(bf16[256,1536]{1,0:T(8,128)(2,1)S(1)} %multiply_convert_fusion.refs_0_.second_ref), channel_id=1, source_target_pairs={{8,0},{16,8},{24,16},{28,24},{20,28},{12,20},{4,12},{0,4},{9,1},{1... | collective-permute-start | bytes 2359304 | tf_op jit(solution)/shard_map/ppermute | solution.py:1124
  122.4 18.0 %collective-permute-start.33 = (bf16[256,1536]{1,0:T(8,128)(2,1)S(1)}, bf16[256,1536]{1,0:T(8,128)(2,1)S(1)}, u32[]{:S(2)}, u32[]{:S(2)}) collective-permute-start(bf16[256,1536]{1,0:T(8,128)(2,1)S(1)} %collective-permute-done.31.refs_0_.refs_1_), channel_id=1, source_target_pairs={{0,8},{8,16},{16,24},{24,28},{28,20},{20,12},{12,4},{4,0},{1,9},{9... | collective-permute-start | bytes 2359304 | tf_op jit(solution)/shard_map/ppermute | solution.py:1124
  124.0 18.7 %collective-permute-start.34 = (bf16[256,1536]{1,0:T(8,128)(2,1)S(1)}, bf16[256,1536]{1,0:T(8,128)(2,1)}, u32[]{:S(2)}, u32[]{:S(2)}) collective-permute-start(bf16[256,1536]{1,0:T(8,128)(2,1)S(1)} %collective-permute-done.32.refs_1_.refs_2_), channel_id=1, source_target_pairs={{8,0},{16,8},{24,16},{28,24},{20,28},{12,20},{4,12},{0,4},{9,1},{1... | collective-permute-start | bytes 2359304 | tf_op jit(solution)/shard_map/ppermute | solution.py:1124
  142.6 17.5 %collective-permute-start.35 = (bf16[256,1536]{1,0:T(8,128)(2,1)S(1)}, bf16[256,1536]{1,0:T(8,128)(2,1)S(1)}, u32[]{:S(2)}, u32[]{:S(2)}) collective-permute-start(bf16[256,1536]{1,0:T(8,128)(2,1)S(1)} %collective-permute-done.33.refs_0_.refs_3_), channel_id=1, source_target_pairs={{0,8},{8,16},{16,24},{24,28},{28,20},{20,12},{12,4},{4,0},{1,9},{9... | collective-permute-start | bytes 2359304 | tf_op jit(solution)/shard_map/ppermute | solution.py:1124
  144.4 18.0 %collective-permute-start.36 = (bf16[256,1536]{1,0:T(8,128)(2,1)}, bf16[256,1536]{1,0:T(8,128)(2,1)S(1)}, u32[]{:S(2)}, u32[]{:S(2)}) collective-permute-start(bf16[256,1536]{1,0:T(8,128)(2,1)} %collective-permute-done.34.refs_1_.refs_4_), channel_id=1, source_target_pairs={{8,0},{16,8},{24,16},{28,24},{20,28},{12,20},{4,12},{0,4},{9,1},{1... | collective-permute-start | bytes 2359304 | tf_op jit(solution)/shard_map/ppermute | solution.py:1124
  162.4 21.6 %collective-permute-start.37 = (bf16[128,1536]{1,0:T(8,128)(2,1)S(1)}, bf16[128,1536]{1,0:T(8,128)(2,1)}, u32[]{:S(2)}, u32[]{:S(2)}) collective-permute-start(bf16[128,1536]{1,0:T(8,128)(2,1)S(1)} %slice.92), channel_id=1, source_target_pairs={{0,8},{8,16},{16,24},{24,28},{28,20},{20,12},{12,4},{4,0},{1,9},{9... | collective-permute-start | bytes 1179656 | tf_op jit(solution)/shard_map/ppermute | solution.py:1124
  163.3 20.8 %collective-permute-start.38 = (bf16[128,1536]{1,0:T(8,128)(2,1)S(1)}, bf16[128,1536]{1,0:T(8,128)(2,1)}, u32[]{:S(2)}, u32[]{:S(2)}) collective-permute-start(bf16[128,1536]{1,0:T(8,128)(2,1)S(1)} %slice.93), channel_id=1, source_target_pairs={{8,0},{16,8},{24,16},{28,24},{20,28},{12,20},{4,12},{0,4},{9,1},{1... | collective-permute-start | bytes 1179656 | tf_op jit(solution)/shard_map/ppermute | solution.py:1124
  165.6 18.4 %collective-permute-start.39 = (bf16[128,1536]{1,0:T(8,128)(2,1)S(1)}, bf16[128,1536]{1,0:T(8,128)(2,1)S(1)}, u32[]{:S(2)}, u32[]{:S(2)}) collective-permute-start(bf16[128,1536]{1,0:T(8,128)(2,1)S(1)} %slice.94), channel_id=1, source_target_pairs={{0,8},{8,16},{16,24},{24,28},{28,20},{20,12},{12,4},{4,0},{1,9},{9... | collective-permute-start | bytes 1179656 | tf_op jit(solution)/shard_map/ppermute | solution.py:1124
  167.5 16.6 %collective-permute-start.40 = (bf16[128,1536]{1,0:T(8,128)(2,1)S(1)}, bf16[128,1536]{1,0:T(8,128)(2,1)}, u32[]{:S(2)}, u32[]{:S(2)}) collective-permute-start(bf16[128,1536]{1,0:T(8,128)(2,1)S(1)} %slice.95), channel_id=1, source_target_pairs={{8,0},{16,8},{24,16},{28,24},{20,28},{12,20},{4,12},{0,4},{9,1},{1... | collective-permute-start | bytes 1179656 | tf_op jit(solution)/shard_map/ppermute | solution.py:1124
  195.0 15.6 %collective-permute-start.41 = (bf16[128,1536]{1,0:T(8,128)(2,1)}, bf16[128,1536]{1,0:T(8,128)(2,1)S(1)}, u32[]{:S(2)}, u32[]{:S(2)}) collective-permute-start(bf16[128,1536]{1,0:T(8,128)(2,1)} %get-tuple-element.344), channel_id=1, source_target_pairs={{0,8},{8,16},{16,24},{24,28},{28,20},{20,12},{12,4},{4,0},{1,9},{9... | collective-permute-start | bytes 1179656 | tf_op jit(solution)/shard_map/ppermute | solution.py:1134
  195.7 14.8 %collective-permute-start.42 = (bf16[128,1536]{1,0:T(8,128)(2,1)}, bf16[128,1536]{1,0:T(8,128)(2,1)S(1)}, u32[]{:S(2)}, u32[]{:S(2)}) collective-permute-start(bf16[128,1536]{1,0:T(8,128)(2,1)} %get-tuple-element.345), channel_id=1, source_target_pairs={{8,0},{16,8},{24,16},{28,24},{20,28},{12,20},{4,12},{0,4},{9,1},{1... | collective-permute-start | bytes 1179656 | tf_op jit(solution)/shard_map/ppermute | solution.py:1134
  212.4 19.7 %collective-permute-start.43 = (bf16[256,1536]{1,0:T(8,128)(2,1)}, bf16[256,1536]{1,0:T(8,128)(2,1)S(1)}, u32[]{:S(2)}, u32[]{:S(2)}) collective-permute-start(bf16[256,1536]{1,0:T(8,128)(2,1)} %get-tuple-element.362), channel_id=1, source_target_pairs={{0,8},{8,16},{16,24},{24,28},{28,20},{20,12},{12,4},{4,0},{1,9},{9... | collective-permute-start | bytes 2359304 | tf_op jit(solution)/shard_map/ppermute | solution.py:1140
  213.2 19.5 %collective-permute-start.44 = (bf16[256,1536]{1,0:T(8,128)(2,1)}, bf16[256,1536]{1,0:T(8,128)(2,1)S(1)}, u32[]{:S(2)}, u32[]{:S(2)}) collective-permute-start(bf16[256,1536]{1,0:T(8,128)(2,1)} %get-tuple-element.363), channel_id=1, source_target_pairs={{8,0},{16,8},{24,16},{28,24},{20,28},{12,20},{4,12},{0,4},{9,1},{1... | collective-permute-start | bytes 2359304 | tf_op jit(solution)/shard_map/ppermute | solution.py:1140
  234.1 19.8 %collective-permute-start.47 = (bf16[256,1536]{1,0:T(8,128)(2,1)}, bf16[256,1536]{1,0:T(8,128)(2,1)S(1)}, u32[]{:S(2)}, u32[]{:S(2)}) collective-permute-start(bf16[256,1536]{1,0:T(8,128)(2,1)} %get-tuple-element.377), channel_id=1, source_target_pairs={{0,8},{8,16},{16,24},{24,28},{28,20},{20,12},{12,4},{4,0},{1,9},{9... | collective-permute-start | bytes 2359304 | tf_op jit(solution)/shard_map/ppermute | solution.py:1140
  234.9 18.9 %collective-permute-start.48 = (bf16[256,1536]{1,0:T(8,128)(2,1)}, bf16[256,1536]{1,0:T(8,128)(2,1)S(1)}, u32[]{:S(2)}, u32[]{:S(2)}) collective-permute-start(bf16[256,1536]{1,0:T(8,128)(2,1)} %get-tuple-element.378), channel_id=1, source_target_pairs={{8,0},{16,8},{24,16},{28,24},{20,28},{12,20},{4,12},{0,4},{9,1},{1... | collective-permute-start | bytes 2359304 | tf_op jit(solution)/shard_map/ppermute | solution.py:1140
  237.5 16.3 %all-to-all-start = ((f32[8,2,256]{2,1,0:T(2,128)}), f32[8,2,256]{2,1,0:T(2,128)S(1)}, u32[]{:S(2)}, u32[]{:S(2)}) async-start(f32[8,2,256]{2,1,0:T(2,128)} %shard_map.208), calls=%async_computation | async-start | bytes 32768 | tf_op jit(solution)/shard_map/all_to_all | solution.py:1328
  240.9 44.1 %collective-permute-start.53 = (bf16[768,1024]{1,0:T(8,128)(2,1)}, bf16[768,1024]{1,0:T(8,128)(2,1)}, u32[]{:S(2)}, u32[]{:S(2)}) collective-permute-start(bf16[768,1024]{1,0:T(8,128)(2,1)} %get-tuple-element.452), channel_id=1, source_target_pairs={{0,1},{1,0},{2,3},{3,2},{4,5},{5,4},{6,7},{7,6},{8,9},{9,8},{10,11... | collective-permute-start | bytes 4718600 | tf_op jit(solution)/shard_map/ppermute | solution.py:1090
  255.3 19.9 %collective-permute-start.49 = (bf16[256,1536]{1,0:T(8,128)(2,1)}, bf16[256,1536]{1,0:T(8,128)(2,1)S(1)}, u32[]{:S(2)}, u32[]{:S(2)}) collective-permute-start(bf16[256,1536]{1,0:T(8,128)(2,1)} %get-tuple-element.420), channel_id=1, source_target_pairs={{0,8},{8,16},{16,24},{24,28},{28,20},{20,12},{12,4},{4,0},{1,9},{9... | collective-permute-start | bytes 2359304 | tf_op jit(solution)/shard_map/ppermute | solution.py:1140
  257.0 18.3 %collective-permute-start.50 = (bf16[256,1536]{1,0:T(8,128)(2,1)}, bf16[256,1536]{1,0:T(8,128)(2,1)}, u32[]{:S(2)}, u32[]{:S(2)}) collective-permute-start(bf16[256,1536]{1,0:T(8,128)(2,1)} %get-tuple-element.421), channel_id=1, source_target_pairs={{8,0},{16,8},{24,16},{28,24},{20,28},{12,20},{4,12},{0,4},{9,1},{1... | collective-permute-start | bytes 2359304 | tf_op jit(solution)/shard_map/ppermute | solution.py:1140
  275.2 8.7 %collective-permute-start.51 = (bf16[128,1536]{1,0:T(8,128)(2,1)}, bf16[128,1536]{1,0:T(8,128)(2,1)S(1)}, u32[]{:S(2)}, u32[]{:S(2)}) collective-permute-start(bf16[128,1536]{1,0:T(8,128)(2,1)} %get-tuple-element.448), channel_id=1, source_target_pairs={{0,8},{8,16},{16,24},{24,28},{28,20},{20,12},{12,4},{4,0},{1,9},{9... | collective-permute-start | bytes 1179656 | tf_op jit(solution)/shard_map/ppermute | solution.py:1134
  276.9 8.1 %collective-permute-start.52 = (bf16[128,1536]{1,0:T(8,128)(2,1)S(1)}, bf16[128,1536]{1,0:T(8,128)(2,1)S(1)}, u32[]{:S(2)}, u32[]{:S(2)}) collective-permute-start(bf16[128,1536]{1,0:T(8,128)(2,1)S(1)} %copy-done.76), channel_id=1, source_target_pairs={{8,0},{16,8},{24,16},{28,24},{20,28},{12,20},{4,12},{0,4},{9,1},{1... | collective-permute-start | bytes 1179656 | tf_op jit(solution)/shard_map/ppermute | solution.py:1134
  285.8 19.5 %collective-permute-start.54 = (bf16[256,1536]{1,0:T(8,128)(2,1)S(1)}, bf16[256,1536]{1,0:T(8,128)(2,1)S(1)}, u32[]{:S(2)}, u32[]{:S(2)}) collective-permute-start(bf16[256,1536]{1,0:T(8,128)(2,1)S(1)} %copy-done.36), channel_id=1, source_target_pairs={{0,1},{1,0},{2,3},{3,2},{4,5},{5,4},{6,7},{7,6},{8,9},{9,8},{10,11... | collective-permute-start | bytes 2359304 | tf_op jit(solution)/shard_map/ppermute | solution.py:1090
  287.0 19.3 %collective-permute-start.55 = (bf16[256,1536]{1,0:T(8,128)(2,1)S(1)}, bf16[256,1536]{1,0:T(8,128)(2,1)S(1)}, u32[]{:S(2)}, u32[]{:S(2)}) collective-permute-start(bf16[256,1536]{1,0:T(8,128)(2,1)S(1)} %get-tuple-element.456), channel_id=1, source_target_pairs={{0,8},{8,16},{16,24},{24,28},{28,20},{20,12},{12,4},{4,0},{1,9},{9... | collective-permute-start | bytes 2359304 | tf_op jit(solution)/shard_map/ppermute | solution.py:1140
  288.3 19.0 %collective-permute-start.56 = (bf16[256,1536]{1,0:T(8,128)(2,1)S(1)}, bf16[256,1536]{1,0:T(8,128)(2,1)S(1)}, u32[]{:S(2)}, u32[]{:S(2)}) collective-permute-start(bf16[256,1536]{1,0:T(8,128)(2,1)S(1)} %get-tuple-element.457), channel_id=1, source_target_pairs={{8,0},{16,8},{24,16},{28,24},{20,28},{12,20},{4,12},{0,4},{9,1},{1... | collective-permute-start | bytes 2359304 | tf_op jit(solution)/shard_map/ppermute | solution.py:1140
  307.7 18.1 %collective-permute-start.59 = (bf16[256,1536]{1,0:T(8,128)(2,1)S(1)}, bf16[256,1536]{1,0:T(8,128)(2,1)S(1)}, u32[]{:S(2)}, u32[]{:S(2)}) collective-permute-start(bf16[256,1536]{1,0:T(8,128)(2,1)S(1)} %get-tuple-element.470), channel_id=1, source_target_pairs={{0,8},{8,16},{16,24},{24,28},{28,20},{20,12},{12,4},{4,0},{1,9},{9... | collective-permute-start | bytes 2359304 | tf_op jit(solution)/shard_map/ppermute | solution.py:1140
  309.3 17.8 %collective-permute-start.60 = (bf16[256,1536]{1,0:T(8,128)(2,1)S(1)}, bf16[256,1536]{1,0:T(8,128)(2,1)S(1)}, u32[]{:S(2)}, u32[]{:S(2)}) collective-permute-start(bf16[256,1536]{1,0:T(8,128)(2,1)S(1)} %get-tuple-element.471), channel_id=1, source_target_pairs={{8,0},{16,8},{24,16},{28,24},{20,28},{12,20},{4,12},{0,4},{9,1},{1... | collective-permute-start | bytes 2359304 | tf_op jit(solution)/shard_map/ppermute | solution.py:1140
  309.8 17.5 %collective-permute-start.61 = (bf16[512,768]{1,0:T(8,128)(2,1)S(1)}, bf16[512,768]{1,0:T(8,128)(2,1)S(1)}, u32[]{:S(2)}, u32[]{:S(2)}) collective-permute-start(bf16[512,768]{1,0:T(8,128)(2,1)S(1)} %add_convert_fusion.1), channel_id=1, source_target_pairs={{0,1},{1,0},{2,3},{3,2},{4,5},{5,4},{6,7},{7,6},{8,9},{9,8},{10,11... | collective-permute-start | bytes 2359304 | tf_op jit(solution)/shard_map/ppermute | solution.py:1090
  328.2 16.6 %collective-permute-start.62 = (bf16[256,1536]{1,0:T(8,128)(2,1)S(1)}, bf16[256,1536]{1,0:T(8,128)(2,1)S(1)}, u32[]{:S(2)}, u32[]{:S(2)}) collective-permute-start(bf16[256,1536]{1,0:T(8,128)(2,1)S(1)} %get-tuple-element.490), channel_id=1, source_target_pairs={{0,8},{8,16},{16,24},{24,28},{28,20},{20,12},{12,4},{4,0},{1,9},{9... | collective-permute-start | bytes 2359304 | tf_op jit(solution)/shard_map/ppermute | solution.py:1140
  329.7 16.6 %collective-permute-start.63 = (bf16[256,1536]{1,0:T(8,128)(2,1)S(1)}, bf16[256,1536]{1,0:T(8,128)(2,1)}, u32[]{:S(2)}, u32[]{:S(2)}) collective-permute-start(bf16[256,1536]{1,0:T(8,128)(2,1)S(1)} %get-tuple-element.491), channel_id=1, source_target_pairs={{8,0},{16,8},{24,16},{28,24},{20,28},{12,20},{4,12},{0,4},{9,1},{1... | collective-permute-start | bytes 2359304 | tf_op jit(solution)/shard_map/ppermute | solution.py:1140
  354.8 7.3 %collective-permute-start.66 = (bf16[48,2176]{1,0:T(8,128)(2,1)S(1)}, bf16[48,2176]{1,0:T(8,128)(2,1)S(1)}, u32[]{:S(2)}, u32[]{:S(2)}) collective-permute-start(bf16[48,2176]{1,0:T(8,128)(2,1)S(1)} %get-tuple-element.495), channel_id=1, source_target_pairs={{0,8},{8,16},{16,24},{24,28},{28,20},{20,12},{12,4},{4,0},{1,9},{9... | collective-permute-start | bytes 626696 | tf_op jit(solution)/shard_map/ppermute | solution.py:1398
  363.9 10.6 %collective-permute-start.68 = (bf16[48,4352]{1,0:T(8,128)(2,1)S(1)}, bf16[48,4352]{1,0:T(8,128)(2,1)S(1)}, u32[]{:S(2)}, u32[]{:S(2)}) collective-permute-start(bf16[48,4352]{1,0:T(8,128)(2,1)S(1)} %get-tuple-element.500), channel_id=1, source_target_pairs={{0,8},{8,16},{16,24},{24,28},{28,20},{20,12},{12,4},{4,0},{1,9},{9... | collective-permute-start | bytes 1253384 | tf_op jit(solution)/shard_map/ppermute | solution.py:1409
  364.7 10.2 %collective-permute-start.69 = (bf16[48,4352]{1,0:T(8,128)(2,1)S(1)}, bf16[48,4352]{1,0:T(8,128)(2,1)S(1)}, u32[]{:S(2)}, u32[]{:S(2)}) collective-permute-start(bf16[48,4352]{1,0:T(8,128)(2,1)S(1)} %get-tuple-element.501), channel_id=1, source_target_pairs={{8,0},{16,8},{24,16},{28,24},{20,28},{12,20},{4,12},{0,4},{9,1},{1... | collective-permute-start | bytes 1253384 | tf_op jit(solution)/shard_map/ppermute | solution.py:1410
  367.0 18.9 %collective-permute-start.72 = (bf16[256,1536]{1,0:T(8,128)(2,1)S(1)}, bf16[256,1536]{1,0:T(8,128)(2,1)}, u32[]{:S(2)}, u32[]{:S(2)}) collective-permute-start(bf16[256,1536]{1,0:T(8,128)(2,1)S(1)} %get-tuple-element.551), channel_id=1, source_target_pairs={{0,1},{1,0},{2,3},{3,2},{4,5},{5,4},{6,7},{7,6},{8,9},{9,8},{10,11... | collective-permute-start | bytes 2359304 | tf_op jit(solution)/shard_map/ppermute | solution.py:1090
  375.7 9.5 %collective-permute-start.70 = (bf16[48,4352]{1,0:T(8,128)(2,1)S(1)}, bf16[48,4352]{1,0:T(8,128)(2,1)S(1)}, u32[]{:S(2)}, u32[]{:S(2)}) collective-permute-start(bf16[48,4352]{1,0:T(8,128)(2,1)S(1)} %get-tuple-element.504), channel_id=1, source_target_pairs={{0,8},{8,16},{16,24},{24,28},{28,20},{20,12},{12,4},{4,0},{1,9},{9... | collective-permute-start | bytes 1253384 | tf_op jit(solution)/shard_map/ppermute | solution.py:1409
  376.7 9.2 %collective-permute-start.71 = (bf16[48,4352]{1,0:T(8,128)(2,1)S(1)}, bf16[48,4352]{1,0:T(8,128)(2,1)S(1)}, u32[]{:S(2)}, u32[]{:S(2)}) collective-permute-start(bf16[48,4352]{1,0:T(8,128)(2,1)S(1)} %get-tuple-element.505), channel_id=1, source_target_pairs={{8,0},{16,8},{24,16},{28,24},{20,28},{12,20},{4,12},{0,4},{9,1},{1... | collective-permute-start | bytes 1253384 | tf_op jit(solution)/shard_map/ppermute | solution.py:1410
  387.4 8.7 %collective-permute-start.73 = (bf16[48,4352]{1,0:T(8,128)(2,1)}, bf16[48,4352]{1,0:T(8,128)(2,1)}, u32[]{:S(2)}, u32[]{:S(2)}) collective-permute-start(bf16[48,4352]{1,0:T(8,128)(2,1)} %get-tuple-element.511), channel_id=1, source_target_pairs={{0,8},{8,16},{16,24},{24,28},{28,20},{20,12},{12,4},{4,0},{1,9},{9... | collective-permute-start | bytes 1253384 | tf_op jit(solution)/shard_map/ppermute | solution.py:1409
  388.3 8.6 %collective-permute-start.74 = (bf16[48,4352]{1,0:T(8,128)(2,1)}, bf16[48,4352]{1,0:T(8,128)(2,1)}, u32[]{:S(2)}, u32[]{:S(2)}) collective-permute-start(bf16[48,4352]{1,0:T(8,128)(2,1)} %get-tuple-element.512), channel_id=1, source_target_pairs={{8,0},{16,8},{24,16},{28,24},{20,28},{12,20},{4,12},{0,4},{9,1},{1... | collective-permute-start | bytes 1253384 | tf_op jit(solution)/shard_map/ppermute | solution.py:1410
  406.8 11.6 %collective-permute-start.76 = (bf16[48,4224]{1,0:T(8,128)(2,1)S(1)}, bf16[48,4224]{1,0:T(8,128)(2,1)S(1)}, u32[]{:S(2)}, u32[]{:S(2)}) collective-permute-start(bf16[48,4224]{1,0:T(8,128)(2,1)S(1)} %slice_dynamic-update-slice_fusion.refs_0_), channel_id=1, source_target_pairs={{0,8},{8,16},{16,24},{24,28},{28,20},{20,12},{12,4},{4,0},{1,9},{9... | collective-permute-start | bytes 1216520 | tf_op jit(solution)/shard_map/ppermute | solution.py:1156
  407.4 11.9 %collective-permute-start.77 = (bf16[48,4224]{1,0:T(8,128)(2,1)S(1)}, bf16[48,4224]{1,0:T(8,128)(2,1)S(1)}, u32[]{:S(2)}, u32[]{:S(2)}) collective-permute-start(bf16[48,4224]{1,0:T(8,128)(2,1)S(1)} %slice_dynamic-update-slice_fusion.refs_0_), channel_id=1, source_target_pairs={{8,0},{16,8},{24,16},{28,24},{20,28},{12,20},{4,12},{0,4},{9,1},{1... | collective-permute-start | bytes 1216520 | tf_op jit(solution)/shard_map/ppermute | solution.py:1157
  419.3 11.4 %collective-permute-start.78 = (bf16[48,4224]{1,0:T(8,128)(2,1)S(1)}, bf16[48,4224]{1,0:T(8,128)(2,1)S(1)}, u32[]{:S(2)}, u32[]{:S(2)}) collective-permute-start(bf16[48,4224]{1,0:T(8,128)(2,1)S(1)} %collective-permute-done.76.refs_1_), channel_id=1, source_target_pairs={{0,8},{8,16},{16,24},{24,28},{28,20},{20,12},{12,4},{4,0},{1,9},{9... | collective-permute-start | bytes 1216520 | tf_op jit(solution)/shard_map/ppermute | solution.py:1156
  419.4 11.8 %collective-permute-start.79 = (bf16[48,4224]{1,0:T(8,128)(2,1)S(1)}, bf16[48,4224]{1,0:T(8,128)(2,1)S(1)}, u32[]{:S(2)}, u32[]{:S(2)}) collective-permute-start(bf16[48,4224]{1,0:T(8,128)(2,1)S(1)} %collective-permute-done.77.refs_2_), channel_id=1, source_target_pairs={{8,0},{16,8},{24,16},{28,24},{20,28},{12,20},{4,12},{0,4},{9,1},{1... | collective-permute-start | bytes 1216520 | tf_op jit(solution)/shard_map/ppermute | solution.py:1157
  431.2 7.9 %collective-permute-start.80 = (bf16[48,4224]{1,0:T(8,128)(2,1)S(1)}, bf16[48,4224]{1,0:T(8,128)(2,1)S(1)}, u32[]{:S(2)}, u32[]{:S(2)}) collective-permute-start(bf16[48,4224]{1,0:T(8,128)(2,1)S(1)} %collective-permute-done.78.refs_3_), channel_id=1, source_target_pairs={{0,8},{8,16},{16,24},{24,28},{28,20},{20,12},{12,4},{4,0},{1,9},{9... | collective-permute-start | bytes 1216520 | tf_op jit(solution)/shard_map/ppermute | solution.py:1156
  432.4 7.9 %collective-permute-start.81 = (bf16[48,4224]{1,0:T(8,128)(2,1)S(1)}, bf16[48,4224]{1,0:T(8,128)(2,1)S(1)}, u32[]{:S(2)}, u32[]{:S(2)}) collective-permute-start(bf16[48,4224]{1,0:T(8,128)(2,1)S(1)} %collective-permute-done.79.refs_4_), channel_id=1, source_target_pairs={{8,0},{16,8},{24,16},{28,24},{20,28},{12,20},{4,12},{0,4},{9,1},{1... | collective-permute-start | bytes 1216520 | tf_op jit(solution)/shard_map/ppermute | solution.py:1157
  433.2 8.5 %collective-permute-start.84 = (bf16[48,4224]{1,0:T(8,128)(2,1)S(1)}, bf16[48,4224]{1,0:T(8,128)(2,1)S(1)}, u32[]{:S(2)}, u32[]{:S(2)}) collective-permute-start(bf16[48,4224]{1,0:T(8,128)(2,1)S(1)} %slice_dynamic-update-slice_fusion.refs_0_), channel_id=1, source_target_pairs={{0,2},{2,0},{1,3},{3,1},{4,6},{6,4},{5,7},{7,5},{8,10},{10,8},{9,1... | collective-permute-start | bytes 1216520 | tf_op jit(solution)/shard_map/ppermute | solution.py:1093
  433.2 9.3 %collective-permute-start.85 = (bf16[48,4224]{1,0:T(8,128)(2,1)S(1)}, bf16[48,4224]{1,0:T(8,128)(2,1)S(1)}, u32[]{:S(2)}, u32[]{:S(2)}) collective-permute-start(bf16[48,4224]{1,0:T(8,128)(2,1)S(1)} %collective-permute-done.76.refs_1_), channel_id=1, source_target_pairs={{0,2},{2,0},{1,3},{3,1},{4,6},{6,4},{5,7},{7,5},{8,10},{10,8},{9,1... | collective-permute-start | bytes 1216520 | tf_op jit(solution)/shard_map/ppermute | solution.py:1093
  441.7 8.0 %collective-permute-start.83 = (bf16[48,2176]{1,0:T(8,128)(2,1)S(1)}, bf16[48,2176]{1,0:T(8,128)(2,1)S(1)}, u32[]{:S(2)}, u32[]{:S(2)}) collective-permute-start(bf16[48,2176]{1,0:T(8,128)(2,1)S(1)} %slice.112), channel_id=1, source_target_pairs={{8,0},{16,8},{24,16},{28,24},{20,28},{12,20},{4,12},{0,4},{9,1},{1... | collective-permute-start | bytes 626696 | tf_op jit(solution)/shard_map/ppermute | solution.py:1157
  (106 other events, 975.9 us)

commit v4 on v3

--- a/solution.py
+++ b/solution.py
@@ -1398,20 +1398,20 @@
     right, left = lax.ppermute(right, "chip", ahead), lax.ppermute(left, "chip", behind)
     right, left, normed_low = lax.optimization_barrier((right, left, normed_low))
     normed_got = exchange_shards(lambda j: rows_of(normed_low, j))
-    for hop, step in enumerate(range(half_ring - 1, 0, -1)):
-        right, left = sum_blocks(
-            pairs,
-            [
-                (2 * step, 0, every, [(0, right)]),
-                (2 * step - 1, 0, every, [(every - left.shape[1], left)]),
-            ],
-        )
+    for step in range(half_ring - 1, 0, -1):
+        wanted = [
+            (2 * step, 0, every, [(0, right)]),
+            (2 * step - 1, 0, every, [(every - left.shape[1], left)]),
+        ]
+        if step == 1:
+            wanted.append((0, 0, every, []))
+        right, left, *own = sum_blocks(pairs, wanted)
         right = lax.ppermute(right, "chip", ahead)
         left = lax.ppermute(left, "chip", behind)
         right, left = lax.optimization_barrier((right, left))
         if step == half_ring - 2:
             right, left, normed_got = lax.optimization_barrier((right, left, normed_got))
-    (dense,) = sum_blocks(pairs, [(0, 0, every, [(0, right), (0, left)])])
+    dense = low(own[0].astype(F32) + right.astype(F32) + left.astype(F32))
     mixed = in_order(
         [dense[:, :wide]]
         + [to_shard(dense[:, s * wide : (s + 1) * wide], s) for s in range(1, shards)]

time: 465 us -> 461 us (level)
    unnamed x169 -> x155, local copies, waits for them, and re-layouts: 16.5 us -> 13.8 us
  transfers between devices with their start and end apart: 93 -> 93, of which waited for: 50 -> 49; matrix products, arithmetic and copies ran while one was open for 7% -> 7% of each run, Pallas kernels for 36% -> 36%
where the time goes in v4:
time: 461 us; the launch traced here: 452 us
  Pallas kernels  182 us (39%)
  waiting for transfers between devices  139 us (30%)
  starting transfers between devices  82.5 us (18%)
  local copies, waits for them, and re-layouts  23.8 us (5%)
  other arithmetic  20.4 us (4%)
    pallas_call x5, Pallas kernels, run_experts(): pl.pallas_call(partial(expert_kernel, slots, *layouts), in_specs=[pl.Bloc...  65 us
    pallas_call x3, Pallas kernels, weight_grad(): pl.pallas_call(partial(weight_grad_kernel, heights, a_at, b_at, scale, by...  42.2 us
    ppermute x11, waiting for transfers between devices, to_shard(): lax.ppermute(value, 'shard', [(i, (i + step) % shards) for i in range(sha...  40.7 us
    ppermute x3, waiting for transfers between devices, body(): right = lax.ppermute(right, 'chip', ahead)  20.1 us
    ppermute x4, waiting for transfers between devices, plane_gather(): right = lax.ppermute(right, 'chip', ahead)  19.5 us
    ppermute x11, starting transfers between devices, to_shard(): lax.ppermute(value, 'shard', [(i, (i + step) % shards) for i in range(sha...  15.5 us
    unnamed x155, local copies, waits for them, and re-layouts  13.8 us
    pallas_call x1, Pallas kernels, attend_back(): pl.pallas_call(partial(attend_back_kernel, shards), grid=(pairs,), in_spe...  11.5 us
  transfers between devices with their start and end apart: 93, of which 49 were waited for; matrix products, arithmetic and copies ran while one was open for 7% of the time, Pallas kernels for 36%

profile of v4, /device:TPU:0, one launch (start us, length us, event | category | flops | bytes accessed | tf_op | source)
XLA Modules:
  0.0 452.0 jit_solution(10067368780830754257)
XLA Ops:
  2.4 3.0 collective-permute-start
  6.2 3.4 collective-permute-done
  9.6 2.2 collective-permute-start.1
  15.1 2.1 collective-permute-done.2.refs_4_.refs_5_
  17.2 1.6 collective-permute-start.3
  20.0 1.6 collective-permute-start.6
  21.6 4.7 %collective-permute-done.6 = bf16[55,256]{1,0:T(8,128)(2,1)S(1)} collective-permute-done((bf16[55,256]{1,0:T(8,128)(2,1)S(1)}, bf16[55,256]{1,0:T(8,128)(2,1)S(1)}, u32[]{:S(2)}, u32[]{:S(2)}) %collective-permute-start.6) | collective-permute-done | bytes 28192 | tf_op jit(solution)/shard_map/ppermute | solution.py:1090
  26.3 1.8 collective-permute-start.7
  28.4 1.7 collective-permute-start.18
  31.7 1.7 collective-permute-done.8.refs_8_.refs_5_
  33.5 1.6 collective-permute-start.9
  36.9 3.2 collective-permute-done.9.refs_9_.refs_4_.refs_5_
  43.0 5.7 %collective-permute-done.18.refs_9_.refs_12_.refs_6_ = bf16[512,768]{1,0:T(8,128)(2,1)} collective-permute-done((bf16[512,768]{1,0:T(8,128)(2,1)}, bf16[512,768]{1,0:T(8,128)(2,1)}, u32[]{:S(2)}, u32[]{:S(2)}) %collective-permute-start.18) | collective-permute-done | bytes 786464 | tf_op jit(solution)/shard_map/ppermute | solution.py:1090
  54.6 7.9 %shard_map.196 = (bf16[512,1536]{1,0:T(8,128)(2,1)}, bf16[1536,1280]{1,0:T(8,128)(2,1)}, f32[512,1280]{1,0:T(8,128)}, bf16[512,1536]{1,0:T(8,128)(2,1)}) custom-call(s32[12]{0:T(128)} %pad_add_fusion.info, s32[16]{0:T(128)} %add_add_fusion.places, bf16[768,2560]{1,0:T(8,128)(2,1)} %own_ref.1, f32[1,1536]{1,0:T(1,128)} %bitcast.64, bf16[256,1536]{1,0:T(8,128)(2,1)} %refs_0_, ...), custom_call_target="tpu_custom_call" | custom-call | flops 2013265920 | bytes 9699328 | tf_op jit(solution)/shard_map/pallas_call | solution.py:857
  62.5 3.3 collective-permute-done.19.refs_2_.refs_6_
  66.3 1.9 collective-permute-start.22
  68.5 1.7 copy-done.25
  70.3 6.7 %shard_map.197 = (bf16[512,1280]{1,0:T(8,128)(2,1)S(1)}, bf16[4,512,1536]{2,1,0:T(8,128)(2,1)S(1)}, bf16[512,768]{1,0:T(8,128)(2,1)S(1)}) custom-call(f32[512,1280]{1,0:T(8,128)S(1)} %copy-done.25, f32[512,1280]{1,0:T(8,128)S(1)} %copy-done.25, f32[512,1280]{1,0:T(8,128)S(1)} %copy-done.25, f32[512,128]{1,0:T(8,128)S(1)} %get-tuple-element.568.cos_ref, ...), custom_call_target="tpu_custom_call" | custom-call | flops 3221225472 | bytes 6291456 | tf_op jit(solution)/shard_map/pallas_call | solution.py:137
  82.0 1.6 collective-permute-start.24
  83.6 1.6 collective-permute-start.25
  86.3 12.1 %collective-permute-done.24 = bf16[256,1536]{1,0:T(8,128)(2,1)} collective-permute-done((bf16[256,1536]{1,0:T(8,128)(2,1)S(1)}, bf16[256,1536]{1,0:T(8,128)(2,1)}, u32[]{:S(2)}, u32[]{:S(2)}) %collective-permute-start.24) | collective-permute-done | bytes 786464 | tf_op jit(solution)/shard_map/ppermute | solution.py:1090
  101.8 1.6 collective-permute-start.31
  105.7 9.8 %shard_map.198 = (bf16[256,2048]{1,0:T(8,128)(2,1)}, bf16[256,1024]{1,0:T(8,128)(2,1)}, bf16[256,1536]{1,0:T(8,128)(2,1)}, f32[8,256]{1,0:T(8,128)}, f32[256,128]{1,0:T(8,128)}) custom-call(s32[12]{0:T(128)} %pad_add_fusion.info, bf16[256,1536]{1,0:T(8,128)(2,1)} %copy-done.3, bf16[256,1536]{1,0:T(8,128)(2,1)} %upstream.1, bf16[64,1280]{1,0:T(8,128)(2,1)} %copy-done.55, ...), custom_call_target="tpu_custom_call" | custom-call | flops 4026531840 | bytes 14155776 | tf_op jit(solution)/shard_map/pallas_call | solution.py:435
  115.5 5.6 %collective-permute-done.31.refs_0_.refs_1_ = bf16[256,1536]{1,0:T(8,128)(2,1)S(1)} collective-permute-done((bf16[256,1536]{1,0:T(8,128)(2,1)S(1)}, bf16[256,1536]{1,0:T(8,128)(2,1)S(1)}, u32[]{:S(2)}, u32[]{:S(2)}) %collective-permute-start.31) | collective-permute-done | bytes 786464 | tf_op jit(solution)/shard_map/ppermute | solution.py:1124
  122.4 1.6 collective-permute-start.33
  124.7 15.0 %shard_map.199 = (bf16[512,2048]{1,0:T(8,128)(2,1)}, bf16[512,1024]{1,0:T(8,128)(2,1)}, bf16[256,1536]{1,0:T(8,128)(2,1)}, bf16[256,1536]{1,0:T(8,128)(2,1)}, f3...) custom-call(s32[12]{0:T(128)} %pad_add_fusion.info, bf16[256,1536]{1,0:T(8,128)(2,1)} %copy-done.64, ...), custom_call_target="tpu_custom_call" | custom-call | flops 8053063680 | bytes 18874368 | tf_op jit(solution)/shard_map/pallas_call | solution.py:435
  140.4 2.2 collective-permute-done.34.refs_1_.refs_4_
  142.6 1.7 collective-permute-start.35
  145.1 14.9 %shard_map.200 = (bf16[512,2048]{1,0:T(8,128)(2,1)}, bf16[512,1024]{1,0:T(8,128)(2,1)}, bf16[256,1536]{1,0:T(8,128)(2,1)}, bf16[256,1536]{1,0:T(8,128)(2,1)}, f3...) custom-call(s32[12]{0:T(128)} %pad_add_fusion.info, bf16[256,1536]{1,0:T(8,128)(2,1)} %copy-done.66, ...), custom_call_target="tpu_custom_call" | custom-call | flops 8053063680 | bytes 18874368 | tf_op jit(solution)/shard_map/pallas_call | solution.py:435
  160.1 2.3 collective-permute-done.36.refs_1_.refs_6_
  169.0 15.0 %shard_map.201 = (bf16[512,2048]{1,0:T(8,128)(2,1)}, bf16[512,1024]{1,0:T(8,128)(2,1)}, bf16[256,1536]{1,0:T(8,128)(2,1)}, bf16[256,1536]{1,0:T(8,128)(2,1)}, f3...) custom-call(s32[12]{0:T(128)} %pad_add_fusion.info, bf16[256,1536]{1,0:T(8,128)(2,1)} %copy-done.56, ...), custom_call_target="tpu_custom_call" | custom-call | flops 8053063680 | bytes 18874368 | tf_op jit(solution)/shard_map/pallas_call | solution.py:435
  184.7 10.2 %shard_map.202 = (bf16[256,2048]{1,0:T(8,128)(2,1)}, bf16[256,1024]{1,0:T(8,128)(2,1)}, bf16[128,1536]{1,0:T(8,128)(2,1)}, bf16[128,1536]{1,0:T(8,128)(2,1)}, f3...) custom-call(s32[12]{0:T(128)} %pad_add_fusion.info, ...), custom_call_target="tpu_custom_call" | custom-call | flops 4026531840 | bytes 14155776 | tf_op jit(solution)/shard_map/pallas_call | solution.py:435
  197.0 13.4 %shard_map.203 = (bf16[768,1024]{1,0:T(8,128)(2,1)}, bf16[768,1024]{1,0:T(8,128)(2,1)}) custom-call(s32[12]{0:T(128)} %pad_add_fusion.info, bf16[256,1536]{1,0:T(8,128)(2,1)} %copy-done.3, bf16[256,1536]{1,0:T(8,128)(2,1)} %copy-done.64, bf16[256,1536]{1,0:T(8,128)(2,1)} %copy-done.65, bf16[256,1536]{1,0:T(8,128)(2,1)} %copy-done.66, ...), custom_call_target="tpu_custom_call" | custom-call | flops 6442450944 | bytes 13631488 | tf_op jit(solution)/shard_map/pallas_call | solution.py:666
  214.3 2.2 collective-permute-done.46.refs_15_
  216.5 14.8 %shard_map.205 = (bf16[768,1024]{1,0:T(8,128)(2,1)}, bf16[768,1024]{1,0:T(8,128)(2,1)}) custom-call(s32[12]{0:T(128)} %pad_add_fusion.info, bf16[256,1536]{1,0:T(8,128)(2,1)} %copy-done.3, bf16[256,1536]{1,0:T(8,128)(2,1)} %copy-done.64, bf16[256,1536]{1,0:T(8,128)(2,1)} %copy-done.65, bf16[256,1536]{1,0:T(8,128)(2,1)} %copy-done.66, ...), custom_call_target="tpu_custom_call" | custom-call | flops 6442450944 | bytes 13631488 | tf_op jit(solution)/shard_map/pallas_call | solution.py:666
  237.4 3.3 all-to-all-start
  240.8 1.6 collective-permute-start.53
  242.4 11.1 %shard_map.207 = (bf16[256,1536]{1,0:T(8,128)(2,1)}, bf16[256,1536]{1,0:T(8,128)(2,1)}, bf16[256,1536]{1,0:T(8,128)(2,1)}, bf16[256,1536]{1,0:T(8,128)(2,1)}, bf...) custom-call(s32[12]{0:T(128)} %pad_add_fusion.info, ...), custom_call_target="tpu_custom_call" | custom-call | flops 6442450944 | bytes 13631488 | tf_op jit(solution)/shard_map/pallas_call | solution.py:504
  255.2 1.6 collective-permute-start.49
  261.0 14.0 %shard_map.211 = (bf16[512,768]{1,0:T(8,128)(2,1)}, bf16[512,768]{1,0:T(8,128)(2,1)}, bf16[512,768]{1,0:T(8,128)(2,1)}, bf16[512,768]{1,0:T(8,128)(2,1)}) custom-call(s32[12]{0:T(128)} %pad_add_fusion.info, bf16[256,1024]{1,0:T(8,128)(2,1)} %get-tuple-element.428.refs_0_, bf16[512,1024]{1,0:T(8,128)(2,1)} %get-tuple-element.429.refs_1_, ...), custom_call_target="tpu_custom_call" | custom-call | flops 6442450944 | bytes 13631488 | tf_op jit(solution)/shard_map/pallas_call | solution.py:666
  275.1 1.7 collective-permute-start.51
  277.8 5.5 %shard_map.212 = (bf16[256,1536]{1,0:T(8,128)(2,1)}, f32[256,1536]{1,0:T(8,128)}, f32[1,1536]{1,0:T(1,128)}) custom-call(bf16[256,1536]{1,0:T(8,128)(2,1)} %get-tuple-element.322.own, bf16[256,1536]{1,0:T(8,128)(2,1)} %copy-done.50, bf16[256,1536]{1,0:T(8,128)(2,1)} %collective-permute-done.50.left, f32[256,1536]{1,0:T(8,128)} %copy-done.5, ...), custom_call_target="tpu_custom_call" | custom-call | tf_op jit(solution)/shard_map/pallas_call | solution.py:932
  291.4 13.8 %collective-permute-done.54.refs_1_ = bf16[256,1536]{1,0:T(8,128)(2,1)S(1)} collective-permute-done((bf16[256,1536]{1,0:T(8,128)(2,1)S(1)}, bf16[256,1536]{1,0:T(8,128)(2,1)S(1)}, u32[]{:S(2)}, u32[]{:S(2)}) %collective-permute-start.54) | collective-permute-done | bytes 786464 | tf_op jit(solution)/shard_map/ppermute | solution.py:1090
  307.5 1.6 collective-permute-start.59
  310.6 11.5 %shard_map.214 = (bf16[512,1280]{1,0:T(8,128)(2,1)S(1)}, bf16[512,1536]{1,0:T(8,128)(2,1)S(1)}) custom-call(s32[12]{0:T(128)S(1)} %copy-done.23, bf16[512,1280]{1,0:T(8,128)(2,1)S(1)} %copy-done.34, bf16[512,1280]{1,0:T(8,128)(2,1)S(1)} %copy-done.34, bf16[512,1280]{1,0:T(8,128)(2,1)S(1)} %copy-done.34, bf16[4,512,1536]{2,1,0:T(8,128)(2,1)} %copy-done.32, ...), custom_call_target="tpu_custom_call" | custom-call | flops 7650410496 | bytes 6291456 | tf_op jit(solution)/shard_map/pallas_call | solution.py:261
  323.2 2.4 shard_map.216
  330.4 4.8 %shard_map.218 = (bf16[8,48,1536]{2,1,0:T(8,128)(2,1)}, bf16[8,48,1536]{2,1,0:T(8,128)(2,1)}) custom-call(s32[12]{0:T(128)} %pad_add_fusion.info, s32[8]{0:T(128)} %fusion.9.places, bf16[512,768]{1,0:T(8,128)(2,1)} %copy-done.35, bf16[512,1536]{1,0:T(8,128)(2,1)} %copy-done.37), custom_call_target="tpu_custom_call" | custom-call | flops 3623878656 | bytes 2359296 | tf_op jit(solution)/shard_map/pallas_call | solution.py:771
  335.2 6.5 %shard_map.219 = (bf16[8,48,2816]{2,1,0:T(8,128)(2,1)}, bf16[8,48,2816]{2,1,0:T(8,128)(2,1)}) custom-call(s32[12]{0:T(128)} %pad_add_fusion.info, s32[8]{0:T(128)} %fusion.9.places, bf16[512,1536]{1,0:T(8,128)(2,1)} %get-tuple-element.485.refs_0_, bf16[512,1280]{1,0:T(8,128)(2,1)} %copy-done.31, f32[1,1536]{1,0:T(1,128)} %copy-done.36, ...), custom_call_target="tpu_custom_call" | custom-call | flops 6039797760 | bytes 2883584 | tf_op jit(solution)/shard_map/pallas_call | solution.py:771
  341.7 3.5 collective-permute-done.62
  346.8 5.6 %collective-permute-done.65.refs_3_ = bf16[8,48,1536]{2,1,0:T(8,128)(2,1)S(1)} collective-permute-done((bf16[8,48,1536]{2,1,0:T(8,128)(2,1)}, bf16[8,48,1536]{2,1,0:T(8,128)(2,1)S(1)}, u32[]{:S(2)}, u32[]{:S(2)}) %collective-permute-start.65) | collective-permute-done | bytes 1179680 | tf_op jit(solution)/shard_map/ppermute | solution.py:1093
  352.5 1.6 copy-done
  356.5 5.2 %collective-permute-done.66.refs_4_ = bf16[48,2176]{1,0:T(8,128)(2,1)S(1)} collective-permute-done((bf16[48,2176]{1,0:T(8,128)(2,1)S(1)}, bf16[48,2176]{1,0:T(8,128)(2,1)S(1)}, u32[]{:S(2)}, u32[]{:S(2)}) %collective-permute-start.66) | collective-permute-done | bytes 208928 | tf_op jit(solution)/shard_map/ppermute | solution.py:1398
  367.6 6.6 %collective-permute-done.68.refs_4_ = bf16[48,4352]{1,0:T(8,128)(2,1)S(1)} collective-permute-done((bf16[48,4352]{1,0:T(8,128)(2,1)S(1)}, bf16[48,4352]{1,0:T(8,128)(2,1)S(1)}, u32[]{:S(2)}, u32[]{:S(2)}) %collective-permute-start.68) | collective-permute-done | bytes 417824 | tf_op jit(solution)/shard_map/ppermute | solution.py:1409
  377.4 7.3 %collective-permute-done.70.refs_4_ = bf16[48,4352]{1,0:T(8,128)(2,1)S(1)} collective-permute-done((bf16[48,4352]{1,0:T(8,128)(2,1)S(1)}, bf16[48,4352]{1,0:T(8,128)(2,1)S(1)}, u32[]{:S(2)}, u32[]{:S(2)}) %collective-permute-start.70) | collective-permute-done | bytes 417824 | tf_op jit(solution)/shard_map/ppermute | solution.py:1409
  388.5 6.3 %collective-permute-done.73 = bf16[48,4352]{1,0:T(8,128)(2,1)} collective-permute-done((bf16[48,4352]{1,0:T(8,128)(2,1)S(1)}, bf16[48,4352]{1,0:T(8,128)(2,1)}, u32[]{:S(2)}, u32[]{:S(2)}) %collective-permute-start.73) | collective-permute-done | bytes 417824 | tf_op jit(solution)/shard_map/ppermute | solution.py:1409
  398.2 3.0 add_convert_fusion
  404.8 8.8 %collective-permute-done.76.refs_1_ = bf16[48,4224]{1,0:T(8,128)(2,1)S(1)} collective-permute-done((bf16[48,4224]{1,0:T(8,128)(2,1)S(1)}, bf16[48,4224]{1,0:T(8,128)(2,1)S(1)}, u32[]{:S(2)}, u32[]{:S(2)}) %collective-permute-start.76) | collective-permute-done | bytes 405536 | tf_op jit(solution)/shard_map/ppermute | solution.py:1156
  416.7 1.6 fusion.3
  418.3 8.0 %collective-permute-done.78.refs_3_ = bf16[48,4224]{1,0:T(8,128)(2,1)S(1)} collective-permute-done((bf16[48,4224]{1,0:T(8,128)(2,1)S(1)}, bf16[48,4224]{1,0:T(8,128)(2,1)S(1)}, u32[]{:S(2)}, u32[]{:S(2)}) %collective-permute-start.78) | collective-permute-done | bytes 405536 | tf_op jit(solution)/shard_map/ppermute | solution.py:1156
  429.3 3.7 convert_add_fusion
  433.0 1.7 collective-permute-done.80.refs_0_
  440.2 4.0 shard_map.224
  445.3 1.7 collective-permute-done.91.refs_5_
  447.0 2.9 shard_map.225
  (366 shorter events, 117.0 us)
Async XLA Ops:
  2.4 7.2 %collective-permute-start = (bf16[48,1280]{1,0:T(8,128)(2,1)S(1)}, bf16[48,1280]{1,0:T(8,128)(2,1)S(1)}, u32[]{:S(2)}, u32[]{:S(2)}) collective-permute-start(bf16[48,1280]{1,0:T(8,128)(2,1)S(1)} %pad_maximum_fusion.2), channel_id=1, source_target_pairs={{0,1},{1,0},{2,3},{3,2},{4,5},{5,4},{6,7},{7,6},{8,9},{9,8},{10,11... | collective-permute-start | bytes 368648 | tf_op jit(solution)/shard_map/ppermute | solution.py:1090
  5.4 20.8 %collective-permute-start.5 = (bf16[256,1536]{1,0:T(8,128)(2,1)}, bf16[256,1536]{1,0:T(8,128)(2,1)S(1)}, u32[]{:S(2)}, u32[]{:S(2)}) collective-permute-start(bf16[256,1536]{1,0:T(8,128)(2,1)} %refs_0_), channel_id=1, source_target_pairs={{0,1},{1,0},{2,3},{3,2},{4,5},{5,4},{6,7},{7,6},{8,9},{9,8},{10,11... | collective-permute-start | bytes 2359304 | tf_op jit(solution)/shard_map/ppermute | solution.py:1090
  17.2 9.0 %collective-permute-start.3 = (bf16[64,1280]{1,0:T(8,128)(2,1)}, bf16[64,1280]{1,0:T(8,128)(2,1)S(1)}, u32[]{:S(2)}, u32[]{:S(2)}) collective-permute-start(bf16[64,1280]{1,0:T(8,128)(2,1)} %collective-permute-done.1.refs_3_.refs_4_), channel_id=1, source_target_pairs={{0,8},{8,16},{16,24},{24,28},{28,20},{20,12},{12,4},{4,0},{1,9},{9... | collective-permute-start | bytes 491528 | tf_op jit(solution)/shard_map/ppermute | solution.py:1174
  18.8 7.5 %collective-permute-start.4 = (bf16[64,1280]{1,0:T(8,128)(2,1)}, bf16[64,1280]{1,0:T(8,128)(2,1)S(1)}, u32[]{:S(2)}, u32[]{:S(2)}) collective-permute-start(bf16[64,1280]{1,0:T(8,128)(2,1)} %collective-permute-done.2.refs_4_.refs_5_), channel_id=1, source_target_pairs={{8,0},{16,8},{24,16},{28,24},{20,28},{12,20},{4,12},{0,4},{9,1},{1... | collective-permute-start | bytes 491528 | tf_op jit(solution)/shard_map/ppermute | solution.py:1177
  21.6 11.9 %collective-permute-start.10 = (bf16[64,1280]{1,0:T(8,128)(2,1)S(1)}, bf16[64,1280]{1,0:T(8,128)(2,1)}, u32[]{:S(2)}, u32[]{:S(2)}) collective-permute-start(bf16[64,1280]{1,0:T(8,128)(2,1)S(1)} %fusion.5.refs_2_), channel_id=1, source_target_pairs={{0,2},{2,0},{1,3},{3,1},{4,6},{6,4},{5,7},{7,5},{8,10},{10,8},{9,1... | collective-permute-start | bytes 491528 | tf_op jit(solution)/shard_map/ppermute | solution.py:1093
  28.4 20.4 %collective-permute-start.18 = (bf16[512,768]{1,0:T(8,128)(2,1)}, bf16[512,768]{1,0:T(8,128)(2,1)}, u32[]{:S(2)}, u32[]{:S(2)}) collective-permute-start(bf16[512,768]{1,0:T(8,128)(2,1)} %bitcast.75), channel_id=1, source_target_pairs={{0,1},{1,0},{2,3},{3,2},{4,5},{5,4},{6,7},{7,6},{8,9},{9,8},{10,11... | collective-permute-start | bytes 2359304 | tf_op jit(solution)/shard_map/ppermute | solution.py:1090
  41.5 39.6 %collective-permute-start.21 = (bf16[768,1024]{1,0:T(8,128)(2,1)}, bf16[768,1024]{1,0:T(8,128)(2,1)}, u32[]{:S(2)}, u32[]{:S(2)}) collective-permute-start(bf16[768,1024]{1,0:T(8,128)(2,1)} %bitcast.68), channel_id=1, source_target_pairs={{0,1},{1,0},{2,3},{3,2},{4,5},{5,4},{6,7},{7,6},{8,9},{9,8},{10,11... | collective-permute-start | bytes 4718600 | tf_op jit(solution)/shard_map/ppermute | solution.py:1090
  48.7 17.1 %collective-permute-start.19 = (bf16[256,1536]{1,0:T(8,128)(2,1)S(1)}, bf16[256,1536]{1,0:T(8,128)(2,1)}, u32[]{:S(2)}, u32[]{:S(2)}) collective-permute-start(bf16[256,1536]{1,0:T(8,128)(2,1)S(1)} %copy-done.48), channel_id=1, source_target_pairs={{0,8},{8,16},{16,24},{24,28},{28,20},{20,12},{12,4},{4,0},{1,9},{9... | collective-permute-start | bytes 2359304 | tf_op jit(solution)/shard_map/ppermute | solution.py:1124
  50.1 16.2 %collective-permute-start.20 = (bf16[256,1536]{1,0:T(8,128)(2,1)S(1)}, bf16[256,1536]{1,0:T(8,128)(2,1)}, u32[]{:S(2)}, u32[]{:S(2)}) collective-permute-start(bf16[256,1536]{1,0:T(8,128)(2,1)S(1)} %copy-done.48), channel_id=1, source_target_pairs={{8,0},{16,8},{24,16},{28,24},{20,28},{12,20},{4,12},{0,4},{9,1},{1... | collective-permute-start | bytes 2359304 | tf_op jit(solution)/shard_map/ppermute | solution.py:1124
  66.3 14.8 %collective-permute-start.22 = (bf16[256,1536]{1,0:T(8,128)(2,1)}, bf16[256,1536]{1,0:T(8,128)(2,1)}, u32[]{:S(2)}, u32[]{:S(2)}) collective-permute-start(bf16[256,1536]{1,0:T(8,128)(2,1)} %collective-permute-done.19.refs_2_.refs_6_), channel_id=1, source_target_pairs={{0,8},{8,16},{16,24},{24,28},{28,20},{20,12},{12,4},{4,0},{1,9},{9... | collective-permute-start | bytes 2359304 | tf_op jit(solution)/shard_map/ppermute | solution.py:1124
  68.2 13.7 %collective-permute-start.23 = (bf16[256,1536]{1,0:T(8,128)(2,1)}, bf16[256,1536]{1,0:T(8,128)(2,1)}, u32[]{:S(2)}, u32[]{:S(2)}) collective-permute-start(bf16[256,1536]{1,0:T(8,128)(2,1)} %collective-permute-done.20.refs_3_.refs_7_), channel_id=1, source_target_pairs={{8,0},{16,8},{24,16},{28,24},{20,28},{12,20},{4,12},{0,4},{9,1},{1... | collective-permute-start | bytes 2359304 | tf_op jit(solution)/shard_map/ppermute | solution.py:1124
  82.0 16.5 %collective-permute-start.24 = (bf16[256,1536]{1,0:T(8,128)(2,1)S(1)}, bf16[256,1536]{1,0:T(8,128)(2,1)}, u32[]{:S(2)}, u32[]{:S(2)}) collective-permute-start(bf16[256,1536]{1,0:T(8,128)(2,1)S(1)} %constant_dynamic-slice_fusion.2), channel_id=1, source_target_pairs={{0,1},{1,0},{2,3},{3,2},{4,5},{5,4},{6,7},{7,6},{8,9},{9,8},{10,11... | collective-permute-start | bytes 2359304 | tf_op jit(solution)/shard_map/ppermute | solution.py:1090
  83.6 16.3 %collective-permute-start.25 = (bf16[256,1536]{1,0:T(8,128)(2,1)}, bf16[256,1536]{1,0:T(8,128)(2,1)}, u32[]{:S(2)}, u32[]{:S(2)}) collective-permute-start(bf16[256,1536]{1,0:T(8,128)(2,1)} %collective-permute-done.22.refs_2_.refs_8_), channel_id=1, source_target_pairs={{0,8},{8,16},{16,24},{24,28},{28,20},{20,12},{12,4},{4,0},{1,9},{9... | collective-permute-start | bytes 2359304 | tf_op jit(solution)/shard_map/ppermute | solution.py:1124
  85.1 16.2 %collective-permute-start.26 = (bf16[256,1536]{1,0:T(8,128)(2,1)}, bf16[256,1536]{1,0:T(8,128)(2,1)}, u32[]{:S(2)}, u32[]{:S(2)}) collective-permute-start(bf16[256,1536]{1,0:T(8,128)(2,1)} %collective-permute-done.23.refs_3_.refs_9_), channel_id=1, source_target_pairs={{8,0},{16,8},{24,16},{28,24},{20,28},{12,20},{4,12},{0,4},{9,1},{1... | collective-permute-start | bytes 2359304 | tf_op jit(solution)/shard_map/ppermute | solution.py:1124
  85.8 17.6 %collective-permute-start.29 = (bf16[512,768]{1,0:T(8,128)(2,1)}, bf16[512,768]{1,0:T(8,128)(2,1)S(1)}, u32[]{:S(2)}, u32[]{:S(2)}) collective-permute-start(bf16[512,768]{1,0:T(8,128)(2,1)} %bitcast.76), channel_id=1, source_target_pairs={{0,2},{2,0},{1,3},{3,1},{4,6},{6,4},{5,7},{7,5},{8,10},{10,8},{9,1... | collective-permute-start | bytes 2359304 | tf_op jit(solution)/shard_map/ppermute | solution.py:1093
  85.8 19.8 %collective-permute-start.30 = (bf16[512,768]{1,0:T(8,128)(2,1)}, bf16[512,768]{1,0:T(8,128)(2,1)}, u32[]{:S(2)}, u32[]{:S(2)}) collective-permute-start(bf16[512,768]{1,0:T(8,128)(2,1)} %collective-permute-done.18.refs_9_.refs_12_.refs_6_), channel_id=1, source_target_pairs={{0,2},{2,0},{1,3},{3,1},{4,6},{6,4},{5,7},{7,5},{8,10},{10,8},{9,1... | collective-permute-start | bytes 2359304 | tf_op jit(solution)/shard_map/ppermute | solution.py:1093
  98.4 7.2 %collective-permute-start.27 = (bf16[768,1024]{1,0:T(8,128)(2,1)}, bf16[768,1024]{1,0:T(8,128)(2,1)}, u32[]{:S(2)}, u32[]{:S(2)}) collective-permute-start(bf16[768,1024]{1,0:T(8,128)(2,1)} %bitcast.69), channel_id=1, source_target_pairs={{0,2},{2,0},{1,3},{3,1},{4,6},{6,4},{5,7},{7,5},{8,10},{10,8},{9,1... | collective-permute-start | bytes 4718600 | tf_op jit(solution)/shard_map/ppermute | solution.py:1093
  101.8 19.3 %collective-permute-start.31 = (bf16[256,1536]{1,0:T(8,128)(2,1)S(1)}, bf16[256,1536]{1,0:T(8,128)(2,1)S(1)}, u32[]{:S(2)}, u32[]{:S(2)}) collective-permute-start(bf16[256,1536]{1,0:T(8,128)(2,1)S(1)} %multiply_convert_fusion.refs_0_.second_ref), channel_id=1, source_target_pairs={{0,8},{8,16},{16,24},{24,28},{28,20},{20,12},{12,4},{4,0},{1,9},{9... | collective-permute-start | bytes 2359304 | tf_op jit(solution)/shard_map/ppermute | solution.py:1124
  103.4 19.0 %collective-permute-start.32 = (bf16[256,1536]{1,0:T(8,128)(2,1)S(1)}, bf16[256,1536]{1,0:T(8,128)(2,1)S(1)}, u32[]{:S(2)}, u32[]{:S(2)}) collective-permute-start(bf16[256,1536]{1,0:T(8,128)(2,1)S(1)} %multiply_convert_fusion.refs_0_.second_ref), channel_id=1, source_target_pairs={{8,0},{16,8},{24,16},{28,24},{20,28},{12,20},{4,12},{0,4},{9,1},{1... | collective-permute-start | bytes 2359304 | tf_op jit(solution)/shard_map/ppermute | solution.py:1124
  122.4 18.0 %collective-permute-start.33 = (bf16[256,1536]{1,0:T(8,128)(2,1)S(1)}, bf16[256,1536]{1,0:T(8,128)(2,1)S(1)}, u32[]{:S(2)}, u32[]{:S(2)}) collective-permute-start(bf16[256,1536]{1,0:T(8,128)(2,1)S(1)} %collective-permute-done.31.refs_0_.refs_1_), channel_id=1, source_target_pairs={{0,8},{8,16},{16,24},{24,28},{28,20},{20,12},{12,4},{4,0},{1,9},{9... | collective-permute-start | bytes 2359304 | tf_op jit(solution)/shard_map/ppermute | solution.py:1124
  124.0 18.7 %collective-permute-start.34 = (bf16[256,1536]{1,0:T(8,128)(2,1)S(1)}, bf16[256,1536]{1,0:T(8,128)(2,1)}, u32[]{:S(2)}, u32[]{:S(2)}) collective-permute-start(bf16[256,1536]{1,0:T(8,128)(2,1)S(1)} %collective-permute-done.32.refs_1_.refs_2_), channel_id=1, source_target_pairs={{8,0},{16,8},{24,16},{28,24},{20,28},{12,20},{4,12},{0,4},{9,1},{1... | collective-permute-start | bytes 2359304 | tf_op jit(solution)/shard_map/ppermute | solution.py:1124
  142.6 17.4 %collective-permute-start.35 = (bf16[256,1536]{1,0:T(8,128)(2,1)S(1)}, bf16[256,1536]{1,0:T(8,128)(2,1)S(1)}, u32[]{:S(2)}, u32[]{:S(2)}) collective-permute-start(bf16[256,1536]{1,0:T(8,128)(2,1)S(1)} %collective-permute-done.33.refs_0_.refs_3_), channel_id=1, source_target_pairs={{0,8},{8,16},{16,24},{24,28},{28,20},{20,12},{12,4},{4,0},{1,9},{9... | collective-permute-start | bytes 2359304 | tf_op jit(solution)/shard_map/ppermute | solution.py:1124
  144.4 18.0 %collective-permute-start.36 = (bf16[256,1536]{1,0:T(8,128)(2,1)}, bf16[256,1536]{1,0:T(8,128)(2,1)S(1)}, u32[]{:S(2)}, u32[]{:S(2)}) collective-permute-start(bf16[256,1536]{1,0:T(8,128)(2,1)} %collective-permute-done.34.refs_1_.refs_4_), channel_id=1, source_target_pairs={{8,0},{16,8},{24,16},{28,24},{20,28},{12,20},{4,12},{0,4},{9,1},{1... | collective-permute-start | bytes 2359304 | tf_op jit(solution)/shard_map/ppermute | solution.py:1124
  162.4 21.5 %collective-permute-start.37 = (bf16[128,1536]{1,0:T(8,128)(2,1)S(1)}, bf16[128,1536]{1,0:T(8,128)(2,1)}, u32[]{:S(2)}, u32[]{:S(2)}) collective-permute-start(bf16[128,1536]{1,0:T(8,128)(2,1)S(1)} %slice.92), channel_id=1, source_target_pairs={{0,8},{8,16},{16,24},{24,28},{28,20},{20,12},{12,4},{4,0},{1,9},{9... | collective-permute-start | bytes 1179656 | tf_op jit(solution)/shard_map/ppermute | solution.py:1124
  163.3 20.7 %collective-permute-start.38 = (bf16[128,1536]{1,0:T(8,128)(2,1)S(1)}, bf16[128,1536]{1,0:T(8,128)(2,1)}, u32[]{:S(2)}, u32[]{:S(2)}) collective-permute-start(bf16[128,1536]{1,0:T(8,128)(2,1)S(1)} %slice.93), channel_id=1, source_target_pairs={{8,0},{16,8},{24,16},{28,24},{20,28},{12,20},{4,12},{0,4},{9,1},{1... | collective-permute-start | bytes 1179656 | tf_op jit(solution)/shard_map/ppermute | solution.py:1124
  165.6 18.4 %collective-permute-start.39 = (bf16[128,1536]{1,0:T(8,128)(2,1)S(1)}, bf16[128,1536]{1,0:T(8,128)(2,1)S(1)}, u32[]{:S(2)}, u32[]{:S(2)}) collective-permute-start(bf16[128,1536]{1,0:T(8,128)(2,1)S(1)} %slice.94), channel_id=1, source_target_pairs={{0,8},{8,16},{16,24},{24,28},{28,20},{20,12},{12,4},{4,0},{1,9},{9... | collective-permute-start | bytes 1179656 | tf_op jit(solution)/shard_map/ppermute | solution.py:1124
  167.5 16.5 %collective-permute-start.40 = (bf16[128,1536]{1,0:T(8,128)(2,1)S(1)}, bf16[128,1536]{1,0:T(8,128)(2,1)}, u32[]{:S(2)}, u32[]{:S(2)}) collective-permute-start(bf16[128,1536]{1,0:T(8,128)(2,1)S(1)} %slice.95), channel_id=1, source_target_pairs={{8,0},{16,8},{24,16},{28,24},{20,28},{12,20},{4,12},{0,4},{9,1},{1... | collective-permute-start | bytes 1179656 | tf_op jit(solution)/shard_map/ppermute | solution.py:1124
  194.9 15.5 %collective-permute-start.41 = (bf16[128,1536]{1,0:T(8,128)(2,1)}, bf16[128,1536]{1,0:T(8,128)(2,1)S(1)}, u32[]{:S(2)}, u32[]{:S(2)}) collective-permute-start(bf16[128,1536]{1,0:T(8,128)(2,1)} %get-tuple-element.345), channel_id=1, source_target_pairs={{0,8},{8,16},{16,24},{24,28},{28,20},{20,12},{12,4},{4,0},{1,9},{9... | collective-permute-start | bytes 1179656 | tf_op jit(solution)/shard_map/ppermute | solution.py:1134
  195.7 14.7 %collective-permute-start.42 = (bf16[128,1536]{1,0:T(8,128)(2,1)}, bf16[128,1536]{1,0:T(8,128)(2,1)S(1)}, u32[]{:S(2)}, u32[]{:S(2)}) collective-permute-start(bf16[128,1536]{1,0:T(8,128)(2,1)} %get-tuple-element.346), channel_id=1, source_target_pairs={{8,0},{16,8},{24,16},{28,24},{20,28},{12,20},{4,12},{0,4},{9,1},{1... | collective-permute-start | bytes 1179656 | tf_op jit(solution)/shard_map/ppermute | solution.py:1134
  212.3 19.7 %collective-permute-start.43 = (bf16[256,1536]{1,0:T(8,128)(2,1)}, bf16[256,1536]{1,0:T(8,128)(2,1)S(1)}, u32[]{:S(2)}, u32[]{:S(2)}) collective-permute-start(bf16[256,1536]{1,0:T(8,128)(2,1)} %get-tuple-element.363), channel_id=1, source_target_pairs={{0,8},{8,16},{16,24},{24,28},{28,20},{20,12},{12,4},{4,0},{1,9},{9... | collective-permute-start | bytes 2359304 | tf_op jit(solution)/shard_map/ppermute | solution.py:1140
  213.1 19.5 %collective-permute-start.44 = (bf16[256,1536]{1,0:T(8,128)(2,1)}, bf16[256,1536]{1,0:T(8,128)(2,1)S(1)}, u32[]{:S(2)}, u32[]{:S(2)}) collective-permute-start(bf16[256,1536]{1,0:T(8,128)(2,1)} %get-tuple-element.364), channel_id=1, source_target_pairs={{8,0},{16,8},{24,16},{28,24},{20,28},{12,20},{4,12},{0,4},{9,1},{1... | collective-permute-start | bytes 2359304 | tf_op jit(solution)/shard_map/ppermute | solution.py:1140
  233.9 19.7 %collective-permute-start.47 = (bf16[256,1536]{1,0:T(8,128)(2,1)}, bf16[256,1536]{1,0:T(8,128)(2,1)S(1)}, u32[]{:S(2)}, u32[]{:S(2)}) collective-permute-start(bf16[256,1536]{1,0:T(8,128)(2,1)} %get-tuple-element.378), channel_id=1, source_target_pairs={{0,8},{8,16},{16,24},{24,28},{28,20},{20,12},{12,4},{4,0},{1,9},{9... | collective-permute-start | bytes 2359304 | tf_op jit(solution)/shard_map/ppermute | solution.py:1140
  234.8 18.9 %collective-permute-start.48 = (bf16[256,1536]{1,0:T(8,128)(2,1)}, bf16[256,1536]{1,0:T(8,128)(2,1)S(1)}, u32[]{:S(2)}, u32[]{:S(2)}) collective-permute-start(bf16[256,1536]{1,0:T(8,128)(2,1)} %get-tuple-element.379), channel_id=1, source_target_pairs={{8,0},{16,8},{24,16},{28,24},{20,28},{12,20},{4,12},{0,4},{9,1},{1... | collective-permute-start | bytes 2359304 | tf_op jit(solution)/shard_map/ppermute | solution.py:1140
  237.4 16.3 %all-to-all-start = ((f32[8,2,256]{2,1,0:T(2,128)}), f32[8,2,256]{2,1,0:T(2,128)S(1)}, u32[]{:S(2)}, u32[]{:S(2)}) async-start(f32[8,2,256]{2,1,0:T(2,128)} %shard_map.208), calls=%async_computation | async-start | bytes 32768 | tf_op jit(solution)/shard_map/all_to_all | solution.py:1328
  240.8 44.0 %collective-permute-start.53 = (bf16[768,1024]{1,0:T(8,128)(2,1)}, bf16[768,1024]{1,0:T(8,128)(2,1)}, u32[]{:S(2)}, u32[]{:S(2)}) collective-permute-start(bf16[768,1024]{1,0:T(8,128)(2,1)} %get-tuple-element.453), channel_id=1, source_target_pairs={{0,1},{1,0},{2,3},{3,2},{4,5},{5,4},{6,7},{7,6},{8,9},{9,8},{10,11... | collective-permute-start | bytes 4718600 | tf_op jit(solution)/shard_map/ppermute | solution.py:1090
  255.2 19.8 %collective-permute-start.49 = (bf16[256,1536]{1,0:T(8,128)(2,1)}, bf16[256,1536]{1,0:T(8,128)(2,1)S(1)}, u32[]{:S(2)}, u32[]{:S(2)}) collective-permute-start(bf16[256,1536]{1,0:T(8,128)(2,1)} %get-tuple-element.421), channel_id=1, source_target_pairs={{0,8},{8,16},{16,24},{24,28},{28,20},{20,12},{12,4},{4,0},{1,9},{9... | collective-permute-start | bytes 2359304 | tf_op jit(solution)/shard_map/ppermute | solution.py:1140
  256.8 18.2 %collective-permute-start.50 = (bf16[256,1536]{1,0:T(8,128)(2,1)}, bf16[256,1536]{1,0:T(8,128)(2,1)}, u32[]{:S(2)}, u32[]{:S(2)}) collective-permute-start(bf16[256,1536]{1,0:T(8,128)(2,1)} %get-tuple-element.422), channel_id=1, source_target_pairs={{8,0},{16,8},{24,16},{28,24},{20,28},{12,20},{4,12},{0,4},{9,1},{1... | collective-permute-start | bytes 2359304 | tf_op jit(solution)/shard_map/ppermute | solution.py:1140
  275.1 8.6 %collective-permute-start.51 = (bf16[128,1536]{1,0:T(8,128)(2,1)}, bf16[128,1536]{1,0:T(8,128)(2,1)S(1)}, u32[]{:S(2)}, u32[]{:S(2)}) collective-permute-start(bf16[128,1536]{1,0:T(8,128)(2,1)} %get-tuple-element.449), channel_id=1, source_target_pairs={{0,8},{8,16},{16,24},{24,28},{28,20},{20,12},{12,4},{4,0},{1,9},{9... | collective-permute-start | bytes 1179656 | tf_op jit(solution)/shard_map/ppermute | solution.py:1134
  276.7 8.1 %collective-permute-start.52 = (bf16[128,1536]{1,0:T(8,128)(2,1)S(1)}, bf16[128,1536]{1,0:T(8,128)(2,1)S(1)}, u32[]{:S(2)}, u32[]{:S(2)}) collective-permute-start(bf16[128,1536]{1,0:T(8,128)(2,1)S(1)} %copy-done.69), channel_id=1, source_target_pairs={{8,0},{16,8},{24,16},{28,24},{20,28},{12,20},{4,12},{0,4},{9,1},{1... | collective-permute-start | bytes 1179656 | tf_op jit(solution)/shard_map/ppermute | solution.py:1134
  285.6 19.5 %collective-permute-start.54 = (bf16[256,1536]{1,0:T(8,128)(2,1)S(1)}, bf16[256,1536]{1,0:T(8,128)(2,1)S(1)}, u32[]{:S(2)}, u32[]{:S(2)}) collective-permute-start(bf16[256,1536]{1,0:T(8,128)(2,1)S(1)} %copy-done.30), channel_id=1, source_target_pairs={{0,1},{1,0},{2,3},{3,2},{4,5},{5,4},{6,7},{7,6},{8,9},{9,8},{10,11... | collective-permute-start | bytes 2359304 | tf_op jit(solution)/shard_map/ppermute | solution.py:1090
  286.8 19.3 %collective-permute-start.55 = (bf16[256,1536]{1,0:T(8,128)(2,1)S(1)}, bf16[256,1536]{1,0:T(8,128)(2,1)S(1)}, u32[]{:S(2)}, u32[]{:S(2)}) collective-permute-start(bf16[256,1536]{1,0:T(8,128)(2,1)S(1)} %get-tuple-element.457), channel_id=1, source_target_pairs={{0,8},{8,16},{16,24},{24,28},{28,20},{20,12},{12,4},{4,0},{1,9},{9... | collective-permute-start | bytes 2359304 | tf_op jit(solution)/shard_map/ppermute | solution.py:1140
  288.2 19.0 %collective-permute-start.56 = (bf16[256,1536]{1,0:T(8,128)(2,1)S(1)}, bf16[256,1536]{1,0:T(8,128)(2,1)S(1)}, u32[]{:S(2)}, u32[]{:S(2)}) collective-permute-start(bf16[256,1536]{1,0:T(8,128)(2,1)S(1)} %get-tuple-element.458), channel_id=1, source_target_pairs={{8,0},{16,8},{24,16},{28,24},{20,28},{12,20},{4,12},{0,4},{9,1},{1... | collective-permute-start | bytes 2359304 | tf_op jit(solution)/shard_map/ppermute | solution.py:1140
  307.5 18.2 %collective-permute-start.59 = (bf16[256,1536]{1,0:T(8,128)(2,1)S(1)}, bf16[256,1536]{1,0:T(8,128)(2,1)S(1)}, u32[]{:S(2)}, u32[]{:S(2)}) collective-permute-start(bf16[256,1536]{1,0:T(8,128)(2,1)S(1)} %get-tuple-element.471), channel_id=1, source_target_pairs={{0,8},{8,16},{16,24},{24,28},{28,20},{20,12},{12,4},{4,0},{1,9},{9... | collective-permute-start | bytes 2359304 | tf_op jit(solution)/shard_map/ppermute | solution.py:1140
  309.1 17.8 %collective-permute-start.60 = (bf16[256,1536]{1,0:T(8,128)(2,1)S(1)}, bf16[256,1536]{1,0:T(8,128)(2,1)S(1)}, u32[]{:S(2)}, u32[]{:S(2)}) collective-permute-start(bf16[256,1536]{1,0:T(8,128)(2,1)S(1)} %get-tuple-element.472), channel_id=1, source_target_pairs={{8,0},{16,8},{24,16},{28,24},{20,28},{12,20},{4,12},{0,4},{9,1},{1... | collective-permute-start | bytes 2359304 | tf_op jit(solution)/shard_map/ppermute | solution.py:1140
  309.6 17.5 %collective-permute-start.61 = (bf16[512,768]{1,0:T(8,128)(2,1)S(1)}, bf16[512,768]{1,0:T(8,128)(2,1)S(1)}, u32[]{:S(2)}, u32[]{:S(2)}) collective-permute-start(bf16[512,768]{1,0:T(8,128)(2,1)S(1)} %add_convert_fusion.1), channel_id=1, source_target_pairs={{0,1},{1,0},{2,3},{3,2},{4,5},{5,4},{6,7},{7,6},{8,9},{9,8},{10,11... | collective-permute-start | bytes 2359304 | tf_op jit(solution)/shard_map/ppermute | solution.py:1090
  328.2 17.0 %collective-permute-start.62 = (bf16[256,1536]{1,0:T(8,128)(2,1)}, bf16[256,1536]{1,0:T(8,128)(2,1)}, u32[]{:S(2)}, u32[]{:S(2)}) collective-permute-start(bf16[256,1536]{1,0:T(8,128)(2,1)} %get-tuple-element.491), channel_id=1, source_target_pairs={{0,8},{8,16},{16,24},{24,28},{28,20},{20,12},{12,4},{4,0},{1,9},{9... | collective-permute-start | bytes 2359304 | tf_op jit(solution)/shard_map/ppermute | solution.py:1140
  329.8 16.6 %collective-permute-start.63 = (bf16[256,1536]{1,0:T(8,128)(2,1)S(1)}, bf16[256,1536]{1,0:T(8,128)(2,1)}, u32[]{:S(2)}, u32[]{:S(2)}) collective-permute-start(bf16[256,1536]{1,0:T(8,128)(2,1)S(1)} %get-tuple-element.492), channel_id=1, source_target_pairs={{8,0},{16,8},{24,16},{28,24},{20,28},{12,20},{4,12},{0,4},{9,1},{1... | collective-permute-start | bytes 2359304 | tf_op jit(solution)/shard_map/ppermute | solution.py:1140
  354.5 7.3 %collective-permute-start.66 = (bf16[48,2176]{1,0:T(8,128)(2,1)S(1)}, bf16[48,2176]{1,0:T(8,128)(2,1)S(1)}, u32[]{:S(2)}, u32[]{:S(2)}) collective-permute-start(bf16[48,2176]{1,0:T(8,128)(2,1)S(1)} %get-tuple-element.496), channel_id=1, source_target_pairs={{0,8},{8,16},{16,24},{24,28},{28,20},{20,12},{12,4},{4,0},{1,9},{9... | collective-permute-start | bytes 626696 | tf_op jit(solution)/shard_map/ppermute | solution.py:1398
  363.5 10.6 %collective-permute-start.68 = (bf16[48,4352]{1,0:T(8,128)(2,1)S(1)}, bf16[48,4352]{1,0:T(8,128)(2,1)S(1)}, u32[]{:S(2)}, u32[]{:S(2)}) collective-permute-start(bf16[48,4352]{1,0:T(8,128)(2,1)S(1)} %get-tuple-element.501), channel_id=1, source_target_pairs={{0,8},{8,16},{16,24},{24,28},{28,20},{20,12},{12,4},{4,0},{1,9},{9... | collective-permute-start | bytes 1253384 | tf_op jit(solution)/shard_map/ppermute | solution.py:1409
  364.3 10.3 %collective-permute-start.69 = (bf16[48,4352]{1,0:T(8,128)(2,1)S(1)}, bf16[48,4352]{1,0:T(8,128)(2,1)S(1)}, u32[]{:S(2)}, u32[]{:S(2)}) collective-permute-start(bf16[48,4352]{1,0:T(8,128)(2,1)S(1)} %get-tuple-element.502), channel_id=1, source_target_pairs={{8,0},{16,8},{24,16},{28,24},{20,28},{12,20},{4,12},{0,4},{9,1},{1... | collective-permute-start | bytes 1253384 | tf_op jit(solution)/shard_map/ppermute | solution.py:1410
  366.6 18.7 %collective-permute-start.72 = (bf16[256,1536]{1,0:T(8,128)(2,1)S(1)}, bf16[256,1536]{1,0:T(8,128)(2,1)S(1)}, u32[]{:S(2)}, u32[]{:S(2)}) collective-permute-start(bf16[256,1536]{1,0:T(8,128)(2,1)S(1)} %get-tuple-element.553), channel_id=1, source_target_pairs={{0,1},{1,0},{2,3},{3,2},{4,5},{5,4},{6,7},{7,6},{8,9},{9,8},{10,11... | collective-permute-start | bytes 2359304 | tf_op jit(solution)/shard_map/ppermute | solution.py:1090
  375.3 9.4 %collective-permute-start.70 = (bf16[48,4352]{1,0:T(8,128)(2,1)S(1)}, bf16[48,4352]{1,0:T(8,128)(2,1)S(1)}, u32[]{:S(2)}, u32[]{:S(2)}) collective-permute-start(bf16[48,4352]{1,0:T(8,128)(2,1)S(1)} %get-tuple-element.505), channel_id=1, source_target_pairs={{0,8},{8,16},{16,24},{24,28},{28,20},{20,12},{12,4},{4,0},{1,9},{9... | collective-permute-start | bytes 1253384 | tf_op jit(solution)/shard_map/ppermute | solution.py:1409
  376.3 9.1 %collective-permute-start.71 = (bf16[48,4352]{1,0:T(8,128)(2,1)S(1)}, bf16[48,4352]{1,0:T(8,128)(2,1)S(1)}, u32[]{:S(2)}, u32[]{:S(2)}) collective-permute-start(bf16[48,4352]{1,0:T(8,128)(2,1)S(1)} %get-tuple-element.506), channel_id=1, source_target_pairs={{8,0},{16,8},{24,16},{28,24},{20,28},{12,20},{4,12},{0,4},{9,1},{1... | collective-permute-start | bytes 1253384 | tf_op jit(solution)/shard_map/ppermute | solution.py:1410
  386.5 8.3 %collective-permute-start.73 = (bf16[48,4352]{1,0:T(8,128)(2,1)S(1)}, bf16[48,4352]{1,0:T(8,128)(2,1)}, u32[]{:S(2)}, u32[]{:S(2)}) collective-permute-start(bf16[48,4352]{1,0:T(8,128)(2,1)S(1)} %get-tuple-element.513), channel_id=1, source_target_pairs={{0,8},{8,16},{16,24},{24,28},{28,20},{20,12},{12,4},{4,0},{1,9},{9... | collective-permute-start | bytes 1253384 | tf_op jit(solution)/shard_map/ppermute | solution.py:1409
  387.4 8.2 %collective-permute-start.74 = (bf16[48,4352]{1,0:T(8,128)(2,1)S(1)}, bf16[48,4352]{1,0:T(8,128)(2,1)}, u32[]{:S(2)}, u32[]{:S(2)}) collective-permute-start(bf16[48,4352]{1,0:T(8,128)(2,1)S(1)} %get-tuple-element.514), channel_id=1, source_target_pairs={{8,0},{16,8},{24,16},{28,24},{20,28},{12,20},{4,12},{0,4},{9,1},{1... | collective-permute-start | bytes 1253384 | tf_op jit(solution)/shard_map/ppermute | solution.py:1410
  402.2 11.4 %collective-permute-start.76 = (bf16[48,4224]{1,0:T(8,128)(2,1)S(1)}, bf16[48,4224]{1,0:T(8,128)(2,1)S(1)}, u32[]{:S(2)}, u32[]{:S(2)}) collective-permute-start(bf16[48,4224]{1,0:T(8,128)(2,1)S(1)} %slice_dynamic-update-slice_fusion.refs_0_), channel_id=1, source_target_pairs={{0,8},{8,16},{16,24},{24,28},{28,20},{20,12},{12,4},{4,0},{1,9},{9... | collective-permute-start | bytes 1216520 | tf_op jit(solution)/shard_map/ppermute | solution.py:1156
  403.0 11.7 %collective-permute-start.77 = (bf16[48,4224]{1,0:T(8,128)(2,1)S(1)}, bf16[48,4224]{1,0:T(8,128)(2,1)S(1)}, u32[]{:S(2)}, u32[]{:S(2)}) collective-permute-start(bf16[48,4224]{1,0:T(8,128)(2,1)S(1)} %slice_dynamic-update-slice_fusion.refs_0_), channel_id=1, source_target_pairs={{8,0},{16,8},{24,16},{28,24},{20,28},{12,20},{4,12},{0,4},{9,1},{1... | collective-permute-start | bytes 1216520 | tf_op jit(solution)/shard_map/ppermute | solution.py:1157
  414.6 11.7 %collective-permute-start.78 = (bf16[48,4224]{1,0:T(8,128)(2,1)S(1)}, bf16[48,4224]{1,0:T(8,128)(2,1)S(1)}, u32[]{:S(2)}, u32[]{:S(2)}) collective-permute-start(bf16[48,4224]{1,0:T(8,128)(2,1)S(1)} %collective-permute-done.76.refs_1_), channel_id=1, source_target_pairs={{0,8},{8,16},{16,24},{24,28},{28,20},{20,12},{12,4},{4,0},{1,9},{9... | collective-permute-start | bytes 1216520 | tf_op jit(solution)/shard_map/ppermute | solution.py:1156
  415.1 11.6 %collective-permute-start.79 = (bf16[48,4224]{1,0:T(8,128)(2,1)S(1)}, bf16[48,4224]{1,0:T(8,128)(2,1)S(1)}, u32[]{:S(2)}, u32[]{:S(2)}) collective-permute-start(bf16[48,4224]{1,0:T(8,128)(2,1)S(1)} %collective-permute-done.77.refs_2_), channel_id=1, source_target_pairs={{8,0},{16,8},{24,16},{28,24},{20,28},{12,20},{4,12},{0,4},{9,1},{1... | collective-permute-start | bytes 1216520 | tf_op jit(solution)/shard_map/ppermute | solution.py:1157
  426.7 7.9 %collective-permute-start.80 = (bf16[48,4224]{1,0:T(8,128)(2,1)S(1)}, bf16[48,4224]{1,0:T(8,128)(2,1)S(1)}, u32[]{:S(2)}, u32[]{:S(2)}) collective-permute-start(bf16[48,4224]{1,0:T(8,128)(2,1)S(1)} %collective-permute-done.78.refs_3_), channel_id=1, source_target_pairs={{0,8},{8,16},{16,24},{24,28},{28,20},{20,12},{12,4},{4,0},{1,9},{9... | collective-permute-start | bytes 1216520 | tf_op jit(solution)/shard_map/ppermute | solution.py:1156
  428.0 7.9 %collective-permute-start.81 = (bf16[48,4224]{1,0:T(8,128)(2,1)S(1)}, bf16[48,4224]{1,0:T(8,128)(2,1)S(1)}, u32[]{:S(2)}, u32[]{:S(2)}) collective-permute-start(bf16[48,4224]{1,0:T(8,128)(2,1)S(1)} %collective-permute-done.79.refs_4_), channel_id=1, source_target_pairs={{8,0},{16,8},{24,16},{28,24},{20,28},{12,20},{4,12},{0,4},{9,1},{1... | collective-permute-start | bytes 1216520 | tf_op jit(solution)/shard_map/ppermute | solution.py:1157
  428.7 8.5 %collective-permute-start.84 = (bf16[48,4224]{1,0:T(8,128)(2,1)S(1)}, bf16[48,4224]{1,0:T(8,128)(2,1)S(1)}, u32[]{:S(2)}, u32[]{:S(2)}) collective-permute-start(bf16[48,4224]{1,0:T(8,128)(2,1)S(1)} %slice_dynamic-update-slice_fusion.refs_0_), channel_id=1, source_target_pairs={{0,2},{2,0},{1,3},{3,1},{4,6},{6,4},{5,7},{7,5},{8,10},{10,8},{9,1... | collective-permute-start | bytes 1216520 | tf_op jit(solution)/shard_map/ppermute | solution.py:1093
  428.7 9.3 %collective-permute-start.85 = (bf16[48,4224]{1,0:T(8,128)(2,1)S(1)}, bf16[48,4224]{1,0:T(8,128)(2,1)S(1)}, u32[]{:S(2)}, u32[]{:S(2)}) collective-permute-start(bf16[48,4224]{1,0:T(8,128)(2,1)S(1)} %collective-permute-done.76.refs_1_), channel_id=1, source_target_pairs={{0,2},{2,0},{1,3},{3,1},{4,6},{6,4},{5,7},{7,5},{8,10},{10,8},{9,1... | collective-permute-start | bytes 1216520 | tf_op jit(solution)/shard_map/ppermute | solution.py:1093
  437.3 7.9 %collective-permute-start.83 = (bf16[48,2176]{1,0:T(8,128)(2,1)S(1)}, bf16[48,2176]{1,0:T(8,128)(2,1)S(1)}, u32[]{:S(2)}, u32[]{:S(2)}) collective-permute-start(bf16[48,2176]{1,0:T(8,128)(2,1)S(1)} %slice.112), channel_id=1, source_target_pairs={{8,0},{16,8},{24,16},{28,24},{20,28},{12,20},{4,12},{0,4},{9,1},{1... | collective-permute-start | bytes 626696 | tf_op jit(solution)/shard_map/ppermute | solution.py:1157
  (99 other events, 896.9 us)

commit v5 on v4

--- a/solution.py
+++ b/solution.py
@@ -1430,7 +1430,7 @@
     grad_down, grad_in = total(down_got), total(in_got)
 
     block_out = low(middle + RES_SCALE * ring_end(out_parts, got))
-    beside = {2: block_out, half_ring - 1: grad_tokens, half_ring: (grad_down, grad_in)}
+    beside = {2: block_out, half_ring - 1: (grad_tokens, grad_down, grad_in)}
     all_cols = query_width + 2 * pair_width
     widths = [all_cols, 128, width]
     cores = jnp.split(both_cores.astype(jnp.int32), 2)
@@ -1439,8 +1439,8 @@
     spread_out, late = plane_gather(
         merged, beside, lambda early: spread(places, 0, early, widths, experts)
     )
-    block_out, grad_tokens = beside[2], beside[half_ring - 1]
-    grad_down, grad_in = beside[half_ring]
+    block_out = beside[2]
+    grad_tokens, grad_down, grad_in = beside[half_ring - 1]
     spread_out = spread(places, 2 * count, late, widths, experts, spread_out)
     grad_qkv, small, grad_out = [out.reshape(-1, out.shape[-1]) for out in spread_out]
     return (

time: 461 us -> 464 us (level)
    ppermute x3, waiting for transfers between devices: 20.1 us -> 15.1 us  [body(): right = lax.ppermute(right, 'chip', ahead)]
    unnamed x155 -> x169, local copies, waits for them, and re-layouts: 13.8 us -> 16.5 us
  transfers between devices with their start and end apart: 93 -> 93, of which waited for: 49 -> 50; matrix products, arithmetic and copies ran while one was open for 7% -> 7% of each run, Pallas kernels for 36% -> 36%
where the time goes in v5:
time: 464 us; the launch traced here: 455 us
  Pallas kernels  183 us (39%)
  waiting for transfers between devices  138 us (30%)
  starting transfers between devices  82.2 us (18%)
  local copies, waits for them, and re-layouts  26.7 us (6%)
  other arithmetic  21 us (5%)
    pallas_call x5, Pallas kernels, run_experts(): pl.pallas_call(partial(expert_kernel, slots, *layouts), in_specs=[pl.Bloc...  65 us
    pallas_call x3, Pallas kernels, weight_grad(): pl.pallas_call(partial(weight_grad_kernel, heights, a_at, b_at, scale, by...  42.3 us
    ppermute x11, waiting for transfers between devices, to_shard(): lax.ppermute(value, 'shard', [(i, (i + step) % shards) for i in range(sha...  41.5 us
    ppermute x4, waiting for transfers between devices, plane_gather(): right = lax.ppermute(right, 'chip', ahead)  20.9 us
    unnamed x169, local copies, waits for them, and re-layouts  16.5 us
    ppermute x11, starting transfers between devices, to_shard(): lax.ppermute(value, 'shard', [(i, (i + step) % shards) for i in range(sha...  15.3 us
    ppermute x3, waiting for transfers between devices, body(): right = lax.ppermute(right, 'chip', ahead)  15.1 us
    pallas_call x1, Pallas kernels, attend_back(): pl.pallas_call(partial(attend_back_kernel, shards), grid=(pairs,), in_spe...  11.5 us
  transfers between devices with their start and end apart: 93, of which 50 were waited for; matrix products, arithmetic and copies ran while one was open for 7% of the time, Pallas kernels for 36%

profile of v5, /device:TPU:0, one launch (start us, length us, event | category | flops | bytes accessed | tf_op | source)
XLA Modules:
  0.0 455.0 jit_solution(1150131693240811787)
XLA Ops:
  2.4 3.0 collective-permute-start
  6.2 3.4 collective-permute-done
  9.6 2.2 collective-permute-start.1
  15.1 2.1 collective-permute-done.2.refs_4_.refs_5_
  20.0 1.6 collective-permute-start.6
  21.6 4.7 %collective-permute-done.6 = bf16[55,256]{1,0:T(8,128)(2,1)S(1)} collective-permute-done((bf16[55,256]{1,0:T(8,128)(2,1)S(1)}, bf16[55,256]{1,0:T(8,128)(2,1)S(1)}, u32[]{:S(2)}, u32[]{:S(2)}) %collective-permute-start.6) | collective-permute-done | bytes 28192 | tf_op jit(solution)/shard_map/ppermute | solution.py:1090
  26.3 1.8 collective-permute-start.7
  28.4 1.7 collective-permute-start.18
  31.7 1.7 collective-permute-done.8.refs_8_.refs_5_
  33.5 1.6 collective-permute-start.9
  36.9 3.2 collective-permute-done.9.refs_9_.refs_4_.refs_5_
  43.0 5.7 %collective-permute-done.18.refs_9_.refs_12_.refs_6_ = bf16[512,768]{1,0:T(8,128)(2,1)} collective-permute-done((bf16[512,768]{1,0:T(8,128)(2,1)}, bf16[512,768]{1,0:T(8,128)(2,1)}, u32[]{:S(2)}, u32[]{:S(2)}) %collective-permute-start.18) | collective-permute-done | bytes 786464 | tf_op jit(solution)/shard_map/ppermute | solution.py:1090
  54.5 7.9 %shard_map.196 = (bf16[512,1536]{1,0:T(8,128)(2,1)}, bf16[1536,1280]{1,0:T(8,128)(2,1)}, f32[512,1280]{1,0:T(8,128)}, bf16[512,1536]{1,0:T(8,128)(2,1)}) custom-call(s32[12]{0:T(128)} %pad_add_fusion.info, s32[16]{0:T(128)} %add_add_fusion.places, bf16[768,2560]{1,0:T(8,128)(2,1)} %own_ref.1, f32[1,1536]{1,0:T(1,128)} %bitcast.64, bf16[256,1536]{1,0:T(8,128)(2,1)} %refs_0_, ...), custom_call_target="tpu_custom_call" | custom-call | flops 2013265920 | bytes 9699328 | tf_op jit(solution)/shard_map/pallas_call | solution.py:857
  62.5 3.4 collective-permute-done.19.refs_2_.refs_6_
  66.3 1.9 collective-permute-start.22
  68.5 1.7 copy-done.31
  70.3 6.7 %shard_map.197 = (bf16[512,1280]{1,0:T(8,128)(2,1)S(1)}, bf16[4,512,1536]{2,1,0:T(8,128)(2,1)S(1)}, bf16[512,768]{1,0:T(8,128)(2,1)S(1)}) custom-call(f32[512,1280]{1,0:T(8,128)S(1)} %copy-done.31, f32[512,1280]{1,0:T(8,128)S(1)} %copy-done.31, f32[512,1280]{1,0:T(8,128)S(1)} %copy-done.31, f32[512,128]{1,0:T(8,128)S(1)} %get-tuple-element.568.cos_ref, ...), custom_call_target="tpu_custom_call" | custom-call | flops 3221225472 | bytes 6291456 | tf_op jit(solution)/shard_map/pallas_call | solution.py:137
  82.0 1.6 collective-permute-start.24
  86.3 12.1 %collective-permute-done.24 = bf16[256,1536]{1,0:T(8,128)(2,1)} collective-permute-done((bf16[256,1536]{1,0:T(8,128)(2,1)S(1)}, bf16[256,1536]{1,0:T(8,128)(2,1)}, u32[]{:S(2)}, u32[]{:S(2)}) %collective-permute-start.24) | collective-permute-done | bytes 786464 | tf_op jit(solution)/shard_map/ppermute | solution.py:1090
  101.8 1.6 collective-permute-start.31
  105.7 9.8 %shard_map.198 = (bf16[256,2048]{1,0:T(8,128)(2,1)}, bf16[256,1024]{1,0:T(8,128)(2,1)}, bf16[256,1536]{1,0:T(8,128)(2,1)}, f32[8,256]{1,0:T(8,128)}, f32[256,128]{1,0:T(8,128)}) custom-call(s32[12]{0:T(128)} %pad_add_fusion.info, bf16[256,1536]{1,0:T(8,128)(2,1)} %copy-done.7, bf16[256,1536]{1,0:T(8,128)(2,1)} %upstream.1, bf16[64,1280]{1,0:T(8,128)(2,1)} %copy-done.62, ...), custom_call_target="tpu_custom_call" | custom-call | flops 4026531840 | bytes 14155776 | tf_op jit(solution)/shard_map/pallas_call | solution.py:435
  115.5 5.6 %collective-permute-done.31.refs_0_.refs_1_ = bf16[256,1536]{1,0:T(8,128)(2,1)S(1)} collective-permute-done((bf16[256,1536]{1,0:T(8,128)(2,1)S(1)}, bf16[256,1536]{1,0:T(8,128)(2,1)S(1)}, u32[]{:S(2)}, u32[]{:S(2)}) %collective-permute-start.31) | collective-permute-done | bytes 786464 | tf_op jit(solution)/shard_map/ppermute | solution.py:1124
  124.7 15.0 %shard_map.199 = (bf16[512,2048]{1,0:T(8,128)(2,1)}, bf16[512,1024]{1,0:T(8,128)(2,1)}, bf16[256,1536]{1,0:T(8,128)(2,1)}, bf16[256,1536]{1,0:T(8,128)(2,1)}, f3...) custom-call(s32[12]{0:T(128)} %pad_add_fusion.info, bf16[256,1536]{1,0:T(8,128)(2,1)} %copy-done.71, ...), custom_call_target="tpu_custom_call" | custom-call | flops 8053063680 | bytes 18874368 | tf_op jit(solution)/shard_map/pallas_call | solution.py:435
  140.4 2.2 collective-permute-done.34.refs_1_.refs_4_
  142.6 1.7 collective-permute-start.35
  145.1 15.0 %shard_map.200 = (bf16[512,2048]{1,0:T(8,128)(2,1)}, bf16[512,1024]{1,0:T(8,128)(2,1)}, bf16[256,1536]{1,0:T(8,128)(2,1)}, bf16[256,1536]{1,0:T(8,128)(2,1)}, f3...) custom-call(s32[12]{0:T(128)} %pad_add_fusion.info, bf16[256,1536]{1,0:T(8,128)(2,1)} %copy-done.73, ...), custom_call_target="tpu_custom_call" | custom-call | flops 8053063680 | bytes 18874368 | tf_op jit(solution)/shard_map/pallas_call | solution.py:435
  160.1 2.3 collective-permute-done.36.refs_1_.refs_6_
  169.0 15.0 %shard_map.201 = (bf16[512,2048]{1,0:T(8,128)(2,1)}, bf16[512,1024]{1,0:T(8,128)(2,1)}, bf16[256,1536]{1,0:T(8,128)(2,1)}, bf16[256,1536]{1,0:T(8,128)(2,1)}, f3...) custom-call(s32[12]{0:T(128)} %pad_add_fusion.info, bf16[256,1536]{1,0:T(8,128)(2,1)} %copy-done.63, ...), custom_call_target="tpu_custom_call" | custom-call | flops 8053063680 | bytes 18874368 | tf_op jit(solution)/shard_map/pallas_call | solution.py:435
  184.8 10.1 %shard_map.202 = (bf16[256,2048]{1,0:T(8,128)(2,1)}, bf16[256,1024]{1,0:T(8,128)(2,1)}, bf16[128,1536]{1,0:T(8,128)(2,1)}, bf16[128,1536]{1,0:T(8,128)(2,1)}, f3...) custom-call(s32[12]{0:T(128)} %pad_add_fusion.info, ...), custom_call_target="tpu_custom_call" | custom-call | flops 4026531840 | bytes 14155776 | tf_op jit(solution)/shard_map/pallas_call | solution.py:435
  197.1 13.5 %shard_map.203 = (bf16[768,1024]{1,0:T(8,128)(2,1)}, bf16[768,1024]{1,0:T(8,128)(2,1)}) custom-call(s32[12]{0:T(128)} %pad_add_fusion.info, bf16[256,1536]{1,0:T(8,128)(2,1)} %copy-done.7, bf16[256,1536]{1,0:T(8,128)(2,1)} %copy-done.71, bf16[256,1536]{1,0:T(8,128)(2,1)} %copy-done.72, bf16[256,1536]{1,0:T(8,128)(2,1)} %copy-done.73, ...), custom_call_target="tpu_custom_call" | custom-call | flops 6442450944 | bytes 13631488 | tf_op jit(solution)/shard_map/pallas_call | solution.py:666
  214.5 2.2 collective-permute-done.46.refs_15_
  216.6 14.8 %shard_map.205 = (bf16[768,1024]{1,0:T(8,128)(2,1)}, bf16[768,1024]{1,0:T(8,128)(2,1)}) custom-call(s32[12]{0:T(128)} %pad_add_fusion.info, bf16[256,1536]{1,0:T(8,128)(2,1)} %copy-done.7, bf16[256,1536]{1,0:T(8,128)(2,1)} %copy-done.71, bf16[256,1536]{1,0:T(8,128)(2,1)} %copy-done.72, bf16[256,1536]{1,0:T(8,128)(2,1)} %copy-done.73, ...), custom_call_target="tpu_custom_call" | custom-call | flops 6442450944 | bytes 13631488 | tf_op jit(solution)/shard_map/pallas_call | solution.py:666
  237.5 3.3 all-to-all-start
  240.9 1.6 collective-permute-start.53
  242.5 11.1 %shard_map.207 = (bf16[256,1536]{1,0:T(8,128)(2,1)}, bf16[256,1536]{1,0:T(8,128)(2,1)}, bf16[256,1536]{1,0:T(8,128)(2,1)}, bf16[256,1536]{1,0:T(8,128)(2,1)}, bf...) custom-call(s32[12]{0:T(128)} %pad_add_fusion.info, ...), custom_call_target="tpu_custom_call" | custom-call | flops 6442450944 | bytes 13631488 | tf_op jit(solution)/shard_map/pallas_call | solution.py:504
  255.3 1.6 collective-permute-start.49
  261.2 14.0 %shard_map.211 = (bf16[512,768]{1,0:T(8,128)(2,1)}, bf16[512,768]{1,0:T(8,128)(2,1)}, bf16[512,768]{1,0:T(8,128)(2,1)}, bf16[512,768]{1,0:T(8,128)(2,1)}) custom-call(s32[12]{0:T(128)} %pad_add_fusion.info, bf16[256,1024]{1,0:T(8,128)(2,1)} %get-tuple-element.428.refs_0_, bf16[512,1024]{1,0:T(8,128)(2,1)} %get-tuple-element.429.refs_1_, ...), custom_call_target="tpu_custom_call" | custom-call | flops 6442450944 | bytes 13631488 | tf_op jit(solution)/shard_map/pallas_call | solution.py:666
  275.2 1.7 collective-permute-start.51
  277.9 5.5 %shard_map.212 = (bf16[256,1536]{1,0:T(8,128)(2,1)}, f32[256,1536]{1,0:T(8,128)}, f32[1,1536]{1,0:T(1,128)}) custom-call(bf16[256,1536]{1,0:T(8,128)(2,1)} %get-tuple-element.322.own, bf16[256,1536]{1,0:T(8,128)(2,1)} %copy-done.57, bf16[256,1536]{1,0:T(8,128)(2,1)} %collective-permute-done.50.left, f32[256,1536]{1,0:T(8,128)} %copy-done.11, ...), custom_call_target="tpu_custom_call" | custom-call | tf_op jit(solution)/shard_map/pallas_call | solution.py:932
  291.5 13.8 %collective-permute-done.54.refs_1_ = bf16[256,1536]{1,0:T(8,128)(2,1)S(1)} collective-permute-done((bf16[256,1536]{1,0:T(8,128)(2,1)S(1)}, bf16[256,1536]{1,0:T(8,128)(2,1)S(1)}, u32[]{:S(2)}, u32[]{:S(2)}) %collective-permute-start.54) | collective-permute-done | bytes 786464 | tf_op jit(solution)/shard_map/ppermute | solution.py:1090
  307.7 1.6 collective-permute-start.59
  310.8 11.5 %shard_map.214 = (bf16[512,1280]{1,0:T(8,128)(2,1)S(1)}, bf16[512,1536]{1,0:T(8,128)(2,1)S(1)}) custom-call(s32[12]{0:T(128)S(1)} %copy-done.29, bf16[512,1280]{1,0:T(8,128)(2,1)S(1)} %copy-done.40, bf16[512,1280]{1,0:T(8,128)(2,1)S(1)} %copy-done.40, bf16[512,1280]{1,0:T(8,128)(2,1)S(1)} %copy-done.40, bf16[4,512,1536]{2,1,0:T(8,128)(2,1)} %copy-done.38, ...), custom_call_target="tpu_custom_call" | custom-call | flops 7650410496 | bytes 6291456 | tf_op jit(solution)/shard_map/pallas_call | solution.py:261
  322.3 2.4 shard_map.216
  330.3 4.8 %shard_map.218 = (bf16[8,48,1536]{2,1,0:T(8,128)(2,1)}, bf16[8,48,1536]{2,1,0:T(8,128)(2,1)}) custom-call(s32[12]{0:T(128)} %pad_add_fusion.info, s32[8]{0:T(128)} %fusion.9.places, bf16[512,768]{1,0:T(8,128)(2,1)} %copy-done.41, bf16[512,1536]{1,0:T(8,128)(2,1)} %copy-done.43), custom_call_target="tpu_custom_call" | custom-call | flops 3623878656 | bytes 2359296 | tf_op jit(solution)/shard_map/pallas_call | solution.py:771
  335.2 6.5 %shard_map.219 = (bf16[8,48,2816]{2,1,0:T(8,128)(2,1)}, bf16[8,48,2816]{2,1,0:T(8,128)(2,1)}) custom-call(s32[12]{0:T(128)} %pad_add_fusion.info, s32[8]{0:T(128)} %fusion.9.places, bf16[512,1536]{1,0:T(8,128)(2,1)} %get-tuple-element.485.refs_0_, bf16[512,1280]{1,0:T(8,128)(2,1)} %copy-done.37, f32[1,1536]{1,0:T(1,128)} %copy-done.42, ...), custom_call_target="tpu_custom_call" | custom-call | flops 6039797760 | bytes 2883584 | tf_op jit(solution)/shard_map/pallas_call | solution.py:771
  341.7 3.1 collective-permute-done.62
  346.7 5.6 %collective-permute-done.65.refs_3_ = bf16[8,48,1536]{2,1,0:T(8,128)(2,1)S(1)} collective-permute-done((bf16[8,48,1536]{2,1,0:T(8,128)(2,1)}, bf16[8,48,1536]{2,1,0:T(8,128)(2,1)S(1)}, u32[]{:S(2)}, u32[]{:S(2)}) %collective-permute-start.65) | collective-permute-done | bytes 1179680 | tf_op jit(solution)/shard_map/ppermute | solution.py:1093
  352.4 2.0 copy-done
  356.9 5.2 %collective-permute-done.66.refs_4_ = bf16[48,2176]{1,0:T(8,128)(2,1)S(1)} collective-permute-done((bf16[48,2176]{1,0:T(8,128)(2,1)S(1)}, bf16[48,2176]{1,0:T(8,128)(2,1)S(1)}, u32[]{:S(2)}, u32[]{:S(2)}) %collective-permute-start.66) | collective-permute-done | bytes 208928 | tf_op jit(solution)/shard_map/ppermute | solution.py:1398
  368.2 6.3 %collective-permute-done.68.refs_4_ = bf16[48,4352]{1,0:T(8,128)(2,1)S(1)} collective-permute-done((bf16[48,4352]{1,0:T(8,128)(2,1)S(1)}, bf16[48,4352]{1,0:T(8,128)(2,1)S(1)}, u32[]{:S(2)}, u32[]{:S(2)}) %collective-permute-start.68) | collective-permute-done | bytes 417824 | tf_op jit(solution)/shard_map/ppermute | solution.py:1409
  378.6 7.7 %collective-permute-done.70.refs_4_ = bf16[48,4352]{1,0:T(8,128)(2,1)} collective-permute-done((bf16[48,4352]{1,0:T(8,128)(2,1)}, bf16[48,4352]{1,0:T(8,128)(2,1)}, u32[]{:S(2)}, u32[]{:S(2)}) %collective-permute-start.70) | collective-permute-done | bytes 417824 | tf_op jit(solution)/shard_map/ppermute | solution.py:1409
  386.9 1.6 copy-done.3
  389.8 2.3 shard_map.223
  394.2 3.7 convert_add_fusion
  402.5 2.5 add_convert_fusion
  408.8 1.7 fusion
  410.5 7.6 %collective-permute-done.76.refs_1_ = bf16[48,4224]{1,0:T(8,128)(2,1)S(1)} collective-permute-done((bf16[48,4224]{1,0:T(8,128)(2,1)S(1)}, bf16[48,4224]{1,0:T(8,128)(2,1)S(1)}, u32[]{:S(2)}, u32[]{:S(2)}) %collective-permute-start.76) | collective-permute-done | bytes 405536 | tf_op jit(solution)/shard_map/ppermute | solution.py:1156
  419.0 2.0 collective-permute-start.79
  421.0 2.8 fusion.3
  423.8 6.9 %collective-permute-done.78.refs_3_ = bf16[48,4224]{1,0:T(8,128)(2,1)S(1)} collective-permute-done((bf16[48,4224]{1,0:T(8,128)(2,1)S(1)}, bf16[48,4224]{1,0:T(8,128)(2,1)S(1)}, u32[]{:S(2)}, u32[]{:S(2)}) %collective-permute-start.78) | collective-permute-done | bytes 405536 | tf_op jit(solution)/shard_map/ppermute | solution.py:1156
  433.6 5.4 %collective-permute-done.80.refs_0_ = bf16[48,4224]{1,0:T(8,128)(2,1)S(1)} collective-permute-done((bf16[48,4224]{1,0:T(8,128)(2,1)S(1)}, bf16[48,4224]{1,0:T(8,128)(2,1)S(1)}, u32[]{:S(2)}, u32[]{:S(2)}) %collective-permute-start.80) | collective-permute-done | bytes 405536 | tf_op jit(solution)/shard_map/ppermute | solution.py:1156
  443.2 4.0 shard_map.224
  448.4 1.7 collective-permute-done.91.refs_5_
  450.1 2.9 shard_map.225
  (380 shorter events, 120.9 us)
Async XLA Ops:
  5.4 20.8 %collective-permute-start.5 = (bf16[256,1536]{1,0:T(8,128)(2,1)}, bf16[256,1536]{1,0:T(8,128)(2,1)S(1)}, u32[]{:S(2)}, u32[]{:S(2)}) collective-permute-start(bf16[256,1536]{1,0:T(8,128)(2,1)} %refs_0_), channel_id=1, source_target_pairs={{0,1},{1,0},{2,3},{3,2},{4,5},{5,4},{6,7},{7,6},{8,9},{9,8},{10,11... | collective-permute-start | bytes 2359304 | tf_op jit(solution)/shard_map/ppermute | solution.py:1090
  17.2 9.0 %collective-permute-start.3 = (bf16[64,1280]{1,0:T(8,128)(2,1)}, bf16[64,1280]{1,0:T(8,128)(2,1)S(1)}, u32[]{:S(2)}, u32[]{:S(2)}) collective-permute-start(bf16[64,1280]{1,0:T(8,128)(2,1)} %collective-permute-done.1.refs_3_.refs_4_), channel_id=1, source_target_pairs={{0,8},{8,16},{16,24},{24,28},{28,20},{20,12},{12,4},{4,0},{1,9},{9... | collective-permute-start | bytes 491528 | tf_op jit(solution)/shard_map/ppermute | solution.py:1174
  18.8 7.5 %collective-permute-start.4 = (bf16[64,1280]{1,0:T(8,128)(2,1)}, bf16[64,1280]{1,0:T(8,128)(2,1)S(1)}, u32[]{:S(2)}, u32[]{:S(2)}) collective-permute-start(bf16[64,1280]{1,0:T(8,128)(2,1)} %collective-permute-done.2.refs_4_.refs_5_), channel_id=1, source_target_pairs={{8,0},{16,8},{24,16},{28,24},{20,28},{12,20},{4,12},{0,4},{9,1},{1... | collective-permute-start | bytes 491528 | tf_op jit(solution)/shard_map/ppermute | solution.py:1177
  21.6 11.9 %collective-permute-start.10 = (bf16[64,1280]{1,0:T(8,128)(2,1)S(1)}, bf16[64,1280]{1,0:T(8,128)(2,1)}, u32[]{:S(2)}, u32[]{:S(2)}) collective-permute-start(bf16[64,1280]{1,0:T(8,128)(2,1)S(1)} %fusion.5.refs_2_), channel_id=1, source_target_pairs={{0,2},{2,0},{1,3},{3,1},{4,6},{6,4},{5,7},{7,5},{8,10},{10,8},{9,1... | collective-permute-start | bytes 491528 | tf_op jit(solution)/shard_map/ppermute | solution.py:1093
  28.4 20.4 %collective-permute-start.18 = (bf16[512,768]{1,0:T(8,128)(2,1)}, bf16[512,768]{1,0:T(8,128)(2,1)}, u32[]{:S(2)}, u32[]{:S(2)}) collective-permute-start(bf16[512,768]{1,0:T(8,128)(2,1)} %bitcast.75), channel_id=1, source_target_pairs={{0,1},{1,0},{2,3},{3,2},{4,5},{5,4},{6,7},{7,6},{8,9},{9,8},{10,11... | collective-permute-start | bytes 2359304 | tf_op jit(solution)/shard_map/ppermute | solution.py:1090
  41.5 39.6 %collective-permute-start.21 = (bf16[768,1024]{1,0:T(8,128)(2,1)}, bf16[768,1024]{1,0:T(8,128)(2,1)}, u32[]{:S(2)}, u32[]{:S(2)}) collective-permute-start(bf16[768,1024]{1,0:T(8,128)(2,1)} %bitcast.68), channel_id=1, source_target_pairs={{0,1},{1,0},{2,3},{3,2},{4,5},{5,4},{6,7},{7,6},{8,9},{9,8},{10,11... | collective-permute-start | bytes 4718600 | tf_op jit(solution)/shard_map/ppermute | solution.py:1090
  48.7 17.1 %collective-permute-start.19 = (bf16[256,1536]{1,0:T(8,128)(2,1)S(1)}, bf16[256,1536]{1,0:T(8,128)(2,1)}, u32[]{:S(2)}, u32[]{:S(2)}) collective-permute-start(bf16[256,1536]{1,0:T(8,128)(2,1)S(1)} %copy-done.52), channel_id=1, source_target_pairs={{0,8},{8,16},{16,24},{24,28},{28,20},{20,12},{12,4},{4,0},{1,9},{9... | collective-permute-start | bytes 2359304 | tf_op jit(solution)/shard_map/ppermute | solution.py:1124
  50.1 16.2 %collective-permute-start.20 = (bf16[256,1536]{1,0:T(8,128)(2,1)S(1)}, bf16[256,1536]{1,0:T(8,128)(2,1)}, u32[]{:S(2)}, u32[]{:S(2)}) collective-permute-start(bf16[256,1536]{1,0:T(8,128)(2,1)S(1)} %copy-done.52), channel_id=1, source_target_pairs={{8,0},{16,8},{24,16},{28,24},{20,28},{12,20},{4,12},{0,4},{9,1},{1... | collective-permute-start | bytes 2359304 | tf_op jit(solution)/shard_map/ppermute | solution.py:1124
  66.3 14.7 %collective-permute-start.22 = (bf16[256,1536]{1,0:T(8,128)(2,1)}, bf16[256,1536]{1,0:T(8,128)(2,1)}, u32[]{:S(2)}, u32[]{:S(2)}) collective-permute-start(bf16[256,1536]{1,0:T(8,128)(2,1)} %collective-permute-done.19.refs_2_.refs_6_), channel_id=1, source_target_pairs={{0,8},{8,16},{16,24},{24,28},{28,20},{20,12},{12,4},{4,0},{1,9},{9... | collective-permute-start | bytes 2359304 | tf_op jit(solution)/shard_map/ppermute | solution.py:1124
  68.2 13.7 %collective-permute-start.23 = (bf16[256,1536]{1,0:T(8,128)(2,1)}, bf16[256,1536]{1,0:T(8,128)(2,1)}, u32[]{:S(2)}, u32[]{:S(2)}) collective-permute-start(bf16[256,1536]{1,0:T(8,128)(2,1)} %collective-permute-done.20.refs_3_.refs_7_), channel_id=1, source_target_pairs={{8,0},{16,8},{24,16},{28,24},{20,28},{12,20},{4,12},{0,4},{9,1},{1... | collective-permute-start | bytes 2359304 | tf_op jit(solution)/shard_map/ppermute | solution.py:1124
  82.0 16.5 %collective-permute-start.24 = (bf16[256,1536]{1,0:T(8,128)(2,1)S(1)}, bf16[256,1536]{1,0:T(8,128)(2,1)}, u32[]{:S(2)}, u32[]{:S(2)}) collective-permute-start(bf16[256,1536]{1,0:T(8,128)(2,1)S(1)} %constant_dynamic-slice_fusion.2), channel_id=1, source_target_pairs={{0,1},{1,0},{2,3},{3,2},{4,5},{5,4},{6,7},{7,6},{8,9},{9,8},{10,11... | collective-permute-start | bytes 2359304 | tf_op jit(solution)/shard_map/ppermute | solution.py:1090
  83.6 16.3 %collective-permute-start.25 = (bf16[256,1536]{1,0:T(8,128)(2,1)}, bf16[256,1536]{1,0:T(8,128)(2,1)}, u32[]{:S(2)}, u32[]{:S(2)}) collective-permute-start(bf16[256,1536]{1,0:T(8,128)(2,1)} %collective-permute-done.22.refs_2_.refs_8_), channel_id=1, source_target_pairs={{0,8},{8,16},{16,24},{24,28},{28,20},{20,12},{12,4},{4,0},{1,9},{9... | collective-permute-start | bytes 2359304 | tf_op jit(solution)/shard_map/ppermute | solution.py:1124
  85.1 16.2 %collective-permute-start.26 = (bf16[256,1536]{1,0:T(8,128)(2,1)}, bf16[256,1536]{1,0:T(8,128)(2,1)}, u32[]{:S(2)}, u32[]{:S(2)}) collective-permute-start(bf16[256,1536]{1,0:T(8,128)(2,1)} %collective-permute-done.23.refs_3_.refs_9_), channel_id=1, source_target_pairs={{8,0},{16,8},{24,16},{28,24},{20,28},{12,20},{4,12},{0,4},{9,1},{1... | collective-permute-start | bytes 2359304 | tf_op jit(solution)/shard_map/ppermute | solution.py:1124
  85.8 17.6 %collective-permute-start.29 = (bf16[512,768]{1,0:T(8,128)(2,1)}, bf16[512,768]{1,0:T(8,128)(2,1)S(1)}, u32[]{:S(2)}, u32[]{:S(2)}) collective-permute-start(bf16[512,768]{1,0:T(8,128)(2,1)} %bitcast.76), channel_id=1, source_target_pairs={{0,2},{2,0},{1,3},{3,1},{4,6},{6,4},{5,7},{7,5},{8,10},{10,8},{9,1... | collective-permute-start | bytes 2359304 | tf_op jit(solution)/shard_map/ppermute | solution.py:1093
  85.8 19.9 %collective-permute-start.30 = (bf16[512,768]{1,0:T(8,128)(2,1)}, bf16[512,768]{1,0:T(8,128)(2,1)}, u32[]{:S(2)}, u32[]{:S(2)}) collective-permute-start(bf16[512,768]{1,0:T(8,128)(2,1)} %collective-permute-done.18.refs_9_.refs_12_.refs_6_), channel_id=1, source_target_pairs={{0,2},{2,0},{1,3},{3,1},{4,6},{6,4},{5,7},{7,5},{8,10},{10,8},{9,1... | collective-permute-start | bytes 2359304 | tf_op jit(solution)/shard_map/ppermute | solution.py:1093
  98.4 7.2 %collective-permute-start.27 = (bf16[768,1024]{1,0:T(8,128)(2,1)}, bf16[768,1024]{1,0:T(8,128)(2,1)}, u32[]{:S(2)}, u32[]{:S(2)}) collective-permute-start(bf16[768,1024]{1,0:T(8,128)(2,1)} %bitcast.69), channel_id=1, source_target_pairs={{0,2},{2,0},{1,3},{3,1},{4,6},{6,4},{5,7},{7,5},{8,10},{10,8},{9,1... | collective-permute-start | bytes 4718600 | tf_op jit(solution)/shard_map/ppermute | solution.py:1093
  101.8 19.3 %collective-permute-start.31 = (bf16[256,1536]{1,0:T(8,128)(2,1)S(1)}, bf16[256,1536]{1,0:T(8,128)(2,1)S(1)}, u32[]{:S(2)}, u32[]{:S(2)}) collective-permute-start(bf16[256,1536]{1,0:T(8,128)(2,1)S(1)} %multiply_convert_fusion.refs_0_.second_ref), channel_id=1, source_target_pairs={{0,8},{8,16},{16,24},{24,28},{28,20},{20,12},{12,4},{4,0},{1,9},{9... | collective-permute-start | bytes 2359304 | tf_op jit(solution)/shard_map/ppermute | solution.py:1124
  103.4 19.0 %collective-permute-start.32 = (bf16[256,1536]{1,0:T(8,128)(2,1)S(1)}, bf16[256,1536]{1,0:T(8,128)(2,1)S(1)}, u32[]{:S(2)}, u32[]{:S(2)}) collective-permute-start(bf16[256,1536]{1,0:T(8,128)(2,1)S(1)} %multiply_convert_fusion.refs_0_.second_ref), channel_id=1, source_target_pairs={{8,0},{16,8},{24,16},{28,24},{20,28},{12,20},{4,12},{0,4},{9,1},{1... | collective-permute-start | bytes 2359304 | tf_op jit(solution)/shard_map/ppermute | solution.py:1124
  122.4 18.0 %collective-permute-start.33 = (bf16[256,1536]{1,0:T(8,128)(2,1)S(1)}, bf16[256,1536]{1,0:T(8,128)(2,1)S(1)}, u32[]{:S(2)}, u32[]{:S(2)}) collective-permute-start(bf16[256,1536]{1,0:T(8,128)(2,1)S(1)} %collective-permute-done.31.refs_0_.refs_1_), channel_id=1, source_target_pairs={{0,8},{8,16},{16,24},{24,28},{28,20},{20,12},{12,4},{4,0},{1,9},{9... | collective-permute-start | bytes 2359304 | tf_op jit(solution)/shard_map/ppermute | solution.py:1124
  124.0 18.7 %collective-permute-start.34 = (bf16[256,1536]{1,0:T(8,128)(2,1)S(1)}, bf16[256,1536]{1,0:T(8,128)(2,1)}, u32[]{:S(2)}, u32[]{:S(2)}) collective-permute-start(bf16[256,1536]{1,0:T(8,128)(2,1)S(1)} %collective-permute-done.32.refs_1_.refs_2_), channel_id=1, source_target_pairs={{8,0},{16,8},{24,16},{28,24},{20,28},{12,20},{4,12},{0,4},{9,1},{1... | collective-permute-start | bytes 2359304 | tf_op jit(solution)/shard_map/ppermute | solution.py:1124
  142.6 17.5 %collective-permute-start.35 = (bf16[256,1536]{1,0:T(8,128)(2,1)S(1)}, bf16[256,1536]{1,0:T(8,128)(2,1)S(1)}, u32[]{:S(2)}, u32[]{:S(2)}) collective-permute-start(bf16[256,1536]{1,0:T(8,128)(2,1)S(1)} %collective-permute-done.33.refs_0_.refs_3_), channel_id=1, source_target_pairs={{0,8},{8,16},{16,24},{24,28},{28,20},{20,12},{12,4},{4,0},{1,9},{9... | collective-permute-start | bytes 2359304 | tf_op jit(solution)/shard_map/ppermute | solution.py:1124
  144.4 18.0 %collective-permute-start.36 = (bf16[256,1536]{1,0:T(8,128)(2,1)}, bf16[256,1536]{1,0:T(8,128)(2,1)S(1)}, u32[]{:S(2)}, u32[]{:S(2)}) collective-permute-start(bf16[256,1536]{1,0:T(8,128)(2,1)} %collective-permute-done.34.refs_1_.refs_4_), channel_id=1, source_target_pairs={{8,0},{16,8},{24,16},{28,24},{20,28},{12,20},{4,12},{0,4},{9,1},{1... | collective-permute-start | bytes 2359304 | tf_op jit(solution)/shard_map/ppermute | solution.py:1124
  162.4 21.6 %collective-permute-start.37 = (bf16[128,1536]{1,0:T(8,128)(2,1)S(1)}, bf16[128,1536]{1,0:T(8,128)(2,1)}, u32[]{:S(2)}, u32[]{:S(2)}) collective-permute-start(bf16[128,1536]{1,0:T(8,128)(2,1)S(1)} %slice.92), channel_id=1, source_target_pairs={{0,8},{8,16},{16,24},{24,28},{28,20},{20,12},{12,4},{4,0},{1,9},{9... | collective-permute-start | bytes 1179656 | tf_op jit(solution)/shard_map/ppermute | solution.py:1124
  163.3 20.8 %collective-permute-start.38 = (bf16[128,1536]{1,0:T(8,128)(2,1)S(1)}, bf16[128,1536]{1,0:T(8,128)(2,1)}, u32[]{:S(2)}, u32[]{:S(2)}) collective-permute-start(bf16[128,1536]{1,0:T(8,128)(2,1)S(1)} %slice.93), channel_id=1, source_target_pairs={{8,0},{16,8},{24,16},{28,24},{20,28},{12,20},{4,12},{0,4},{9,1},{1... | collective-permute-start | bytes 1179656 | tf_op jit(solution)/shard_map/ppermute | solution.py:1124
  165.6 18.4 %collective-permute-start.39 = (bf16[128,1536]{1,0:T(8,128)(2,1)S(1)}, bf16[128,1536]{1,0:T(8,128)(2,1)S(1)}, u32[]{:S(2)}, u32[]{:S(2)}) collective-permute-start(bf16[128,1536]{1,0:T(8,128)(2,1)S(1)} %slice.94), channel_id=1, source_target_pairs={{0,8},{8,16},{16,24},{24,28},{28,20},{20,12},{12,4},{4,0},{1,9},{9... | collective-permute-start | bytes 1179656 | tf_op jit(solution)/shard_map/ppermute | solution.py:1124
  167.5 16.6 %collective-permute-start.40 = (bf16[128,1536]{1,0:T(8,128)(2,1)S(1)}, bf16[128,1536]{1,0:T(8,128)(2,1)}, u32[]{:S(2)}, u32[]{:S(2)}) collective-permute-start(bf16[128,1536]{1,0:T(8,128)(2,1)S(1)} %slice.95), channel_id=1, source_target_pairs={{8,0},{16,8},{24,16},{28,24},{20,28},{12,20},{4,12},{0,4},{9,1},{1... | collective-permute-start | bytes 1179656 | tf_op jit(solution)/shard_map/ppermute | solution.py:1124
  195.0 15.6 %collective-permute-start.41 = (bf16[128,1536]{1,0:T(8,128)(2,1)}, bf16[128,1536]{1,0:T(8,128)(2,1)S(1)}, u32[]{:S(2)}, u32[]{:S(2)}) collective-permute-start(bf16[128,1536]{1,0:T(8,128)(2,1)} %get-tuple-element.345), channel_id=1, source_target_pairs={{0,8},{8,16},{16,24},{24,28},{28,20},{20,12},{12,4},{4,0},{1,9},{9... | collective-permute-start | bytes 1179656 | tf_op jit(solution)/shard_map/ppermute | solution.py:1134
  195.7 14.8 %collective-permute-start.42 = (bf16[128,1536]{1,0:T(8,128)(2,1)}, bf16[128,1536]{1,0:T(8,128)(2,1)S(1)}, u32[]{:S(2)}, u32[]{:S(2)}) collective-permute-start(bf16[128,1536]{1,0:T(8,128)(2,1)} %get-tuple-element.346), channel_id=1, source_target_pairs={{8,0},{16,8},{24,16},{28,24},{20,28},{12,20},{4,12},{0,4},{9,1},{1... | collective-permute-start | bytes 1179656 | tf_op jit(solution)/shard_map/ppermute | solution.py:1134
  212.4 19.7 %collective-permute-start.43 = (bf16[256,1536]{1,0:T(8,128)(2,1)}, bf16[256,1536]{1,0:T(8,128)(2,1)S(1)}, u32[]{:S(2)}, u32[]{:S(2)}) collective-permute-start(bf16[256,1536]{1,0:T(8,128)(2,1)} %get-tuple-element.363), channel_id=1, source_target_pairs={{0,8},{8,16},{16,24},{24,28},{28,20},{20,12},{12,4},{4,0},{1,9},{9... | collective-permute-start | bytes 2359304 | tf_op jit(solution)/shard_map/ppermute | solution.py:1140
  213.2 19.5 %collective-permute-start.44 = (bf16[256,1536]{1,0:T(8,128)(2,1)}, bf16[256,1536]{1,0:T(8,128)(2,1)S(1)}, u32[]{:S(2)}, u32[]{:S(2)}) collective-permute-start(bf16[256,1536]{1,0:T(8,128)(2,1)} %get-tuple-element.364), channel_id=1, source_target_pairs={{8,0},{16,8},{24,16},{28,24},{20,28},{12,20},{4,12},{0,4},{9,1},{1... | collective-permute-start | bytes 2359304 | tf_op jit(solution)/shard_map/ppermute | solution.py:1140
  234.1 19.8 %collective-permute-start.47 = (bf16[256,1536]{1,0:T(8,128)(2,1)}, bf16[256,1536]{1,0:T(8,128)(2,1)S(1)}, u32[]{:S(2)}, u32[]{:S(2)}) collective-permute-start(bf16[256,1536]{1,0:T(8,128)(2,1)} %get-tuple-element.378), channel_id=1, source_target_pairs={{0,8},{8,16},{16,24},{24,28},{28,20},{20,12},{12,4},{4,0},{1,9},{9... | collective-permute-start | bytes 2359304 | tf_op jit(solution)/shard_map/ppermute | solution.py:1140
  234.9 18.9 %collective-permute-start.48 = (bf16[256,1536]{1,0:T(8,128)(2,1)}, bf16[256,1536]{1,0:T(8,128)(2,1)S(1)}, u32[]{:S(2)}, u32[]{:S(2)}) collective-permute-start(bf16[256,1536]{1,0:T(8,128)(2,1)} %get-tuple-element.379), channel_id=1, source_target_pairs={{8,0},{16,8},{24,16},{28,24},{20,28},{12,20},{4,12},{0,4},{9,1},{1... | collective-permute-start | bytes 2359304 | tf_op jit(solution)/shard_map/ppermute | solution.py:1140
  237.5 16.3 %all-to-all-start = ((f32[8,2,256]{2,1,0:T(2,128)}), f32[8,2,256]{2,1,0:T(2,128)S(1)}, u32[]{:S(2)}, u32[]{:S(2)}) async-start(f32[8,2,256]{2,1,0:T(2,128)} %shard_map.208), calls=%async_computation | async-start | bytes 32768 | tf_op jit(solution)/shard_map/all_to_all | solution.py:1328
  240.9 44.1 %collective-permute-start.53 = (bf16[768,1024]{1,0:T(8,128)(2,1)}, bf16[768,1024]{1,0:T(8,128)(2,1)}, u32[]{:S(2)}, u32[]{:S(2)}) collective-permute-start(bf16[768,1024]{1,0:T(8,128)(2,1)} %get-tuple-element.453), channel_id=1, source_target_pairs={{0,1},{1,0},{2,3},{3,2},{4,5},{5,4},{6,7},{7,6},{8,9},{9,8},{10,11... | collective-permute-start | bytes 4718600 | tf_op jit(solution)/shard_map/ppermute | solution.py:1090
  255.3 19.9 %collective-permute-start.49 = (bf16[256,1536]{1,0:T(8,128)(2,1)}, bf16[256,1536]{1,0:T(8,128)(2,1)S(1)}, u32[]{:S(2)}, u32[]{:S(2)}) collective-permute-start(bf16[256,1536]{1,0:T(8,128)(2,1)} %get-tuple-element.421), channel_id=1, source_target_pairs={{0,8},{8,16},{16,24},{24,28},{28,20},{20,12},{12,4},{4,0},{1,9},{9... | collective-permute-start | bytes 2359304 | tf_op jit(solution)/shard_map/ppermute | solution.py:1140
  257.0 18.3 %collective-permute-start.50 = (bf16[256,1536]{1,0:T(8,128)(2,1)}, bf16[256,1536]{1,0:T(8,128)(2,1)}, u32[]{:S(2)}, u32[]{:S(2)}) collective-permute-start(bf16[256,1536]{1,0:T(8,128)(2,1)} %get-tuple-element.422), channel_id=1, source_target_pairs={{8,0},{16,8},{24,16},{28,24},{20,28},{12,20},{4,12},{0,4},{9,1},{1... | collective-permute-start | bytes 2359304 | tf_op jit(solution)/shard_map/ppermute | solution.py:1140
  275.2 8.7 %collective-permute-start.51 = (bf16[128,1536]{1,0:T(8,128)(2,1)}, bf16[128,1536]{1,0:T(8,128)(2,1)S(1)}, u32[]{:S(2)}, u32[]{:S(2)}) collective-permute-start(bf16[128,1536]{1,0:T(8,128)(2,1)} %get-tuple-element.449), channel_id=1, source_target_pairs={{0,8},{8,16},{16,24},{24,28},{28,20},{20,12},{12,4},{4,0},{1,9},{9... | collective-permute-start | bytes 1179656 | tf_op jit(solution)/shard_map/ppermute | solution.py:1134
  276.9 8.1 %collective-permute-start.52 = (bf16[128,1536]{1,0:T(8,128)(2,1)S(1)}, bf16[128,1536]{1,0:T(8,128)(2,1)S(1)}, u32[]{:S(2)}, u32[]{:S(2)}) collective-permute-start(bf16[128,1536]{1,0:T(8,128)(2,1)S(1)} %copy-done.76), channel_id=1, source_target_pairs={{8,0},{16,8},{24,16},{28,24},{20,28},{12,20},{4,12},{0,4},{9,1},{1... | collective-permute-start | bytes 1179656 | tf_op jit(solution)/shard_map/ppermute | solution.py:1134
  285.8 19.5 %collective-permute-start.54 = (bf16[256,1536]{1,0:T(8,128)(2,1)S(1)}, bf16[256,1536]{1,0:T(8,128)(2,1)S(1)}, u32[]{:S(2)}, u32[]{:S(2)}) collective-permute-start(bf16[256,1536]{1,0:T(8,128)(2,1)S(1)} %copy-done.36), channel_id=1, source_target_pairs={{0,1},{1,0},{2,3},{3,2},{4,5},{5,4},{6,7},{7,6},{8,9},{9,8},{10,11... | collective-permute-start | bytes 2359304 | tf_op jit(solution)/shard_map/ppermute | solution.py:1090
  287.0 19.3 %collective-permute-start.55 = (bf16[256,1536]{1,0:T(8,128)(2,1)S(1)}, bf16[256,1536]{1,0:T(8,128)(2,1)S(1)}, u32[]{:S(2)}, u32[]{:S(2)}) collective-permute-start(bf16[256,1536]{1,0:T(8,128)(2,1)S(1)} %get-tuple-element.457), channel_id=1, source_target_pairs={{0,8},{8,16},{16,24},{24,28},{28,20},{20,12},{12,4},{4,0},{1,9},{9... | collective-permute-start | bytes 2359304 | tf_op jit(solution)/shard_map/ppermute | solution.py:1140
  288.3 19.0 %collective-permute-start.56 = (bf16[256,1536]{1,0:T(8,128)(2,1)S(1)}, bf16[256,1536]{1,0:T(8,128)(2,1)S(1)}, u32[]{:S(2)}, u32[]{:S(2)}) collective-permute-start(bf16[256,1536]{1,0:T(8,128)(2,1)S(1)} %get-tuple-element.458), channel_id=1, source_target_pairs={{8,0},{16,8},{24,16},{28,24},{20,28},{12,20},{4,12},{0,4},{9,1},{1... | collective-permute-start | bytes 2359304 | tf_op jit(solution)/shard_map/ppermute | solution.py:1140
  307.7 18.1 %collective-permute-start.59 = (bf16[256,1536]{1,0:T(8,128)(2,1)S(1)}, bf16[256,1536]{1,0:T(8,128)(2,1)S(1)}, u32[]{:S(2)}, u32[]{:S(2)}) collective-permute-start(bf16[256,1536]{1,0:T(8,128)(2,1)S(1)} %get-tuple-element.471), channel_id=1, source_target_pairs={{0,8},{8,16},{16,24},{24,28},{28,20},{20,12},{12,4},{4,0},{1,9},{9... | collective-permute-start | bytes 2359304 | tf_op jit(solution)/shard_map/ppermute | solution.py:1140
  309.3 17.8 %collective-permute-start.60 = (bf16[256,1536]{1,0:T(8,128)(2,1)S(1)}, bf16[256,1536]{1,0:T(8,128)(2,1)S(1)}, u32[]{:S(2)}, u32[]{:S(2)}) collective-permute-start(bf16[256,1536]{1,0:T(8,128)(2,1)S(1)} %get-tuple-element.472), channel_id=1, source_target_pairs={{8,0},{16,8},{24,16},{28,24},{20,28},{12,20},{4,12},{0,4},{9,1},{1... | collective-permute-start | bytes 2359304 | tf_op jit(solution)/shard_map/ppermute | solution.py:1140
  309.8 17.5 %collective-permute-start.61 = (bf16[512,768]{1,0:T(8,128)(2,1)S(1)}, bf16[512,768]{1,0:T(8,128)(2,1)S(1)}, u32[]{:S(2)}, u32[]{:S(2)}) collective-permute-start(bf16[512,768]{1,0:T(8,128)(2,1)S(1)} %add_convert_fusion.1), channel_id=1, source_target_pairs={{0,1},{1,0},{2,3},{3,2},{4,5},{5,4},{6,7},{7,6},{8,9},{9,8},{10,11... | collective-permute-start | bytes 2359304 | tf_op jit(solution)/shard_map/ppermute | solution.py:1090
  328.1 16.6 %collective-permute-start.62 = (bf16[256,1536]{1,0:T(8,128)(2,1)S(1)}, bf16[256,1536]{1,0:T(8,128)(2,1)S(1)}, u32[]{:S(2)}, u32[]{:S(2)}) collective-permute-start(bf16[256,1536]{1,0:T(8,128)(2,1)S(1)} %get-tuple-element.491), channel_id=1, source_target_pairs={{0,8},{8,16},{16,24},{24,28},{28,20},{20,12},{12,4},{4,0},{1,9},{9... | collective-permute-start | bytes 2359304 | tf_op jit(solution)/shard_map/ppermute | solution.py:1140
  329.7 16.6 %collective-permute-start.63 = (bf16[256,1536]{1,0:T(8,128)(2,1)S(1)}, bf16[256,1536]{1,0:T(8,128)(2,1)}, u32[]{:S(2)}, u32[]{:S(2)}) collective-permute-start(bf16[256,1536]{1,0:T(8,128)(2,1)S(1)} %get-tuple-element.492), channel_id=1, source_target_pairs={{8,0},{16,8},{24,16},{28,24},{20,28},{12,20},{4,12},{0,4},{9,1},{1... | collective-permute-start | bytes 2359304 | tf_op jit(solution)/shard_map/ppermute | solution.py:1140
  354.8 7.3 %collective-permute-start.66 = (bf16[48,2176]{1,0:T(8,128)(2,1)S(1)}, bf16[48,2176]{1,0:T(8,128)(2,1)S(1)}, u32[]{:S(2)}, u32[]{:S(2)}) collective-permute-start(bf16[48,2176]{1,0:T(8,128)(2,1)S(1)} %get-tuple-element.496), channel_id=1, source_target_pairs={{0,8},{8,16},{16,24},{24,28},{28,20},{20,12},{12,4},{4,0},{1,9},{9... | collective-permute-start | bytes 626696 | tf_op jit(solution)/shard_map/ppermute | solution.py:1398
  363.9 10.6 %collective-permute-start.68 = (bf16[48,4352]{1,0:T(8,128)(2,1)S(1)}, bf16[48,4352]{1,0:T(8,128)(2,1)S(1)}, u32[]{:S(2)}, u32[]{:S(2)}) collective-permute-start(bf16[48,4352]{1,0:T(8,128)(2,1)S(1)} %get-tuple-element.501), channel_id=1, source_target_pairs={{0,8},{8,16},{16,24},{24,28},{28,20},{20,12},{12,4},{4,0},{1,9},{9... | collective-permute-start | bytes 1253384 | tf_op jit(solution)/shard_map/ppermute | solution.py:1409
  364.6 10.2 %collective-permute-start.69 = (bf16[48,4352]{1,0:T(8,128)(2,1)S(1)}, bf16[48,4352]{1,0:T(8,128)(2,1)S(1)}, u32[]{:S(2)}, u32[]{:S(2)}) collective-permute-start(bf16[48,4352]{1,0:T(8,128)(2,1)S(1)} %get-tuple-element.502), channel_id=1, source_target_pairs={{8,0},{16,8},{24,16},{28,24},{20,28},{12,20},{4,12},{0,4},{9,1},{1... | collective-permute-start | bytes 1253384 | tf_op jit(solution)/shard_map/ppermute | solution.py:1410
  367.2 19.7 %collective-permute-start.72 = (bf16[256,1536]{1,0:T(8,128)(2,1)}, bf16[256,1536]{1,0:T(8,128)(2,1)}, u32[]{:S(2)}, u32[]{:S(2)}) collective-permute-start(bf16[256,1536]{1,0:T(8,128)(2,1)} %get-tuple-element.553), channel_id=1, source_target_pairs={{0,1},{1,0},{2,3},{3,2},{4,5},{5,4},{6,7},{7,6},{8,9},{9,8},{10,11... | collective-permute-start | bytes 2359304 | tf_op jit(solution)/shard_map/ppermute | solution.py:1090
  376.5 9.8 %collective-permute-start.70 = (bf16[48,4352]{1,0:T(8,128)(2,1)}, bf16[48,4352]{1,0:T(8,128)(2,1)}, u32[]{:S(2)}, u32[]{:S(2)}) collective-permute-start(bf16[48,4352]{1,0:T(8,128)(2,1)} %get-tuple-element.505), channel_id=1, source_target_pairs={{0,8},{8,16},{16,24},{24,28},{28,20},{20,12},{12,4},{4,0},{1,9},{9... | collective-permute-start | bytes 1253384 | tf_op jit(solution)/shard_map/ppermute | solution.py:1409
  377.4 9.5 %collective-permute-start.71 = (bf16[48,4352]{1,0:T(8,128)(2,1)}, bf16[48,4352]{1,0:T(8,128)(2,1)}, u32[]{:S(2)}, u32[]{:S(2)}) collective-permute-start(bf16[48,4352]{1,0:T(8,128)(2,1)} %get-tuple-element.506), channel_id=1, source_target_pairs={{8,0},{16,8},{24,16},{28,24},{20,28},{12,20},{4,12},{0,4},{9,1},{1... | collective-permute-start | bytes 1253384 | tf_op jit(solution)/shard_map/ppermute | solution.py:1410
  392.1 8.3 %collective-permute-start.73 = (bf16[48,4352]{1,0:T(8,128)(2,1)S(1)}, bf16[48,4352]{1,0:T(8,128)(2,1)S(1)}, u32[]{:S(2)}, u32[]{:S(2)}) collective-permute-start(bf16[48,4352]{1,0:T(8,128)(2,1)S(1)} %get-tuple-element.513), channel_id=1, source_target_pairs={{0,8},{8,16},{16,24},{24,28},{28,20},{20,12},{12,4},{4,0},{1,9},{9... | collective-permute-start | bytes 1253384 | tf_op jit(solution)/shard_map/ppermute | solution.py:1409
  393.1 8.2 %collective-permute-start.74 = (bf16[48,4352]{1,0:T(8,128)(2,1)S(1)}, bf16[48,4352]{1,0:T(8,128)(2,1)S(1)}, u32[]{:S(2)}, u32[]{:S(2)}) collective-permute-start(bf16[48,4352]{1,0:T(8,128)(2,1)S(1)} %get-tuple-element.514), channel_id=1, source_target_pairs={{8,0},{16,8},{24,16},{28,24},{20,28},{12,20},{4,12},{0,4},{9,1},{1... | collective-permute-start | bytes 1253384 | tf_op jit(solution)/shard_map/ppermute | solution.py:1410
  406.7 11.4 %collective-permute-start.76 = (bf16[48,4224]{1,0:T(8,128)(2,1)S(1)}, bf16[48,4224]{1,0:T(8,128)(2,1)S(1)}, u32[]{:S(2)}, u32[]{:S(2)}) collective-permute-start(bf16[48,4224]{1,0:T(8,128)(2,1)S(1)} %slice_dynamic-update-slice_fusion.refs_0_), channel_id=1, source_target_pairs={{0,8},{8,16},{16,24},{24,28},{28,20},{20,12},{12,4},{4,0},{1,9},{9... | collective-permute-start | bytes 1216520 | tf_op jit(solution)/shard_map/ppermute | solution.py:1156
  407.3 11.6 %collective-permute-start.77 = (bf16[48,4224]{1,0:T(8,128)(2,1)S(1)}, bf16[48,4224]{1,0:T(8,128)(2,1)S(1)}, u32[]{:S(2)}, u32[]{:S(2)}) collective-permute-start(bf16[48,4224]{1,0:T(8,128)(2,1)S(1)} %slice_dynamic-update-slice_fusion.refs_0_), channel_id=1, source_target_pairs={{8,0},{16,8},{24,16},{28,24},{20,28},{12,20},{4,12},{0,4},{9,1},{1... | collective-permute-start | bytes 1216520 | tf_op jit(solution)/shard_map/ppermute | solution.py:1157
  419.0 11.7 %collective-permute-start.78 = (bf16[48,4224]{1,0:T(8,128)(2,1)S(1)}, bf16[48,4224]{1,0:T(8,128)(2,1)S(1)}, u32[]{:S(2)}, u32[]{:S(2)}) collective-permute-start(bf16[48,4224]{1,0:T(8,128)(2,1)S(1)} %collective-permute-done.76.refs_1_), channel_id=1, source_target_pairs={{0,8},{8,16},{16,24},{24,28},{28,20},{20,12},{12,4},{4,0},{1,9},{9... | collective-permute-start | bytes 1216520 | tf_op jit(solution)/shard_map/ppermute | solution.py:1156
  419.0 12.1 %collective-permute-start.79 = (bf16[48,4224]{1,0:T(8,128)(2,1)S(1)}, bf16[48,4224]{1,0:T(8,128)(2,1)S(1)}, u32[]{:S(2)}, u32[]{:S(2)}) collective-permute-start(bf16[48,4224]{1,0:T(8,128)(2,1)S(1)} %collective-permute-done.77.refs_2_), channel_id=1, source_target_pairs={{8,0},{16,8},{24,16},{28,24},{20,28},{12,20},{4,12},{0,4},{9,1},{1... | collective-permute-start | bytes 1216520 | tf_op jit(solution)/shard_map/ppermute | solution.py:1157
  431.1 7.9 %collective-permute-start.80 = (bf16[48,4224]{1,0:T(8,128)(2,1)S(1)}, bf16[48,4224]{1,0:T(8,128)(2,1)S(1)}, u32[]{:S(2)}, u32[]{:S(2)}) collective-permute-start(bf16[48,4224]{1,0:T(8,128)(2,1)S(1)} %collective-permute-done.78.refs_3_), channel_id=1, source_target_pairs={{0,8},{8,16},{16,24},{24,28},{28,20},{20,12},{12,4},{4,0},{1,9},{9... | collective-permute-start | bytes 1216520 | tf_op jit(solution)/shard_map/ppermute | solution.py:1156
  432.4 7.9 %collective-permute-start.81 = (bf16[48,4224]{1,0:T(8,128)(2,1)S(1)}, bf16[48,4224]{1,0:T(8,128)(2,1)S(1)}, u32[]{:S(2)}, u32[]{:S(2)}) collective-permute-start(bf16[48,4224]{1,0:T(8,128)(2,1)S(1)} %collective-permute-done.79.refs_4_), channel_id=1, source_target_pairs={{8,0},{16,8},{24,16},{28,24},{20,28},{12,20},{4,12},{0,4},{9,1},{1... | collective-permute-start | bytes 1216520 | tf_op jit(solution)/shard_map/ppermute | solution.py:1157
  433.1 7.2 %collective-permute-start.84 = (bf16[48,4224]{1,0:T(8,128)(2,1)S(1)}, bf16[48,4224]{1,0:T(8,128)(2,1)S(1)}, u32[]{:S(2)}, u32[]{:S(2)}) collective-permute-start(bf16[48,4224]{1,0:T(8,128)(2,1)S(1)} %slice_dynamic-update-slice_fusion.refs_0_), channel_id=1, source_target_pairs={{0,2},{2,0},{1,3},{3,1},{4,6},{6,4},{5,7},{7,5},{8,10},{10,8},{9,1... | collective-permute-start | bytes 1216520 | tf_op jit(solution)/shard_map/ppermute | solution.py:1093
  433.1 8.0 %collective-permute-start.85 = (bf16[48,4224]{1,0:T(8,128)(2,1)S(1)}, bf16[48,4224]{1,0:T(8,128)(2,1)S(1)}, u32[]{:S(2)}, u32[]{:S(2)}) collective-permute-start(bf16[48,4224]{1,0:T(8,128)(2,1)S(1)} %collective-permute-done.76.refs_1_), channel_id=1, source_target_pairs={{0,2},{2,0},{1,3},{3,1},{4,6},{6,4},{5,7},{7,5},{8,10},{10,8},{9,1... | collective-permute-start | bytes 1216520 | tf_op jit(solution)/shard_map/ppermute | solution.py:1093
  433.6 9.1 %collective-permute-start.86 = (bf16[48,4224]{1,0:T(8,128)(2,1)S(1)}, bf16[48,4224]{1,0:T(8,128)(2,1)S(1)}, u32[]{:S(2)}, u32[]{:S(2)}) collective-permute-start(bf16[48,4224]{1,0:T(8,128)(2,1)S(1)} %collective-permute-done.77.refs_2_), channel_id=1, source_target_pairs={{0,2},{2,0},{1,3},{3,1},{4,6},{6,4},{5,7},{7,5},{8,10},{10,8},{9,1... | collective-permute-start | bytes 1216520 | tf_op jit(solution)/shard_map/ppermute | solution.py:1093
  440.3 7.9 %collective-permute-start.83 = (bf16[48,2176]{1,0:T(8,128)(2,1)S(1)}, bf16[48,2176]{1,0:T(8,128)(2,1)S(1)}, u32[]{:S(2)}, u32[]{:S(2)}) collective-permute-start(bf16[48,2176]{1,0:T(8,128)(2,1)S(1)} %slice.112), channel_id=1, source_target_pairs={{8,0},{16,8},{24,16},{28,24},{20,28},{12,20},{4,12},{0,4},{9,1},{1... | collective-permute-start | bytes 626696 | tf_op jit(solution)/shard_map/ppermute | solution.py:1157
  (106 other events, 925.3 us)
